TPU v7x, 32 devices: a whole 2x2x4 slice. The times are simulated.
32 devices in a mesh: dp: 4 (over z), cent: 8 (over y, x, core).
Axes of the slice: x: 2, y: 2, z: 4, core: 2. Of those that a mesh axis runs over, the one named last changes fastest.
Arguments:
- embeddings: bfloat16 [8192, 1024], P(('dp', 'cent')), may hold values from -6 to 6
- codebook: float32 [4096, 1024], P(('cent', 'dp')), may hold values from -2 to 2
Outputs:
- new_codebook: float32 [4096, 1024], P(('cent', 'dp'))
- counts: float32 [4096], P(('cent', 'dp'))
- log_norm: float32 [8192], P(('dp', 'cent'))
All inputs are finite; a program needn't handle non-finite values.
Results may differ from a plain program's by a relative error of at most 0.0022.
Values may be sent and summed in bfloat16 or wider, within the bound.
No kernel may reach another device: no remote copies, remote signals or barrier semaphores. Data moves between devices by JAX's collectives and lax.ppermute only.
A program may use at most 128 MiB of HBM per device.

v0:
```python
import jax
import jax.numpy as jnp
from jax import lax
from jax.sharding import PartitionSpec as P

TEMPER = 0.8
PRIOR = 1.0


def score_block(rows, centers, squares):
    product = lax.dot_general(
        rows, centers, (((1,), (1,)), ((), ())), preferred_element_type=jnp.float32
    )
    return (product - 0.5 * squares[None, :]) / TEMPER


def local(embeddings, codebook):
    own_rows = embeddings.shape[0]
    centers = lax.all_gather(codebook.astype(jnp.bfloat16), "dp", axis=0, tiled=True)
    squares = jnp.sum(jnp.square(centers.astype(jnp.float32)), axis=1)
    gathered = lax.all_gather(embeddings, "cent", axis=0, tiled=True)
    scores = score_block(gathered, centers, squares)
    highest = jnp.max(scores, axis=1)
    summed = jnp.sum(jnp.exp(scores - highest[:, None]), axis=1)
    top_score = lax.pmax(highest, "cent")
    top_total = lax.psum(summed * jnp.exp(highest - top_score), "cent")
    lognorm = top_score + jnp.log(top_total)
    resp = jnp.exp(scores - lognorm[:, None]).astype(jnp.bfloat16)
    tally = jnp.sum(resp.astype(jnp.float32), axis=0)
    sums = lax.dot_general(
        resp, gathered, (((0,), (0,)), ((), ())), preferred_element_type=jnp.float32
    )
    owner_total, owner_tally = (
        lax.psum_scatter(sums, "dp", scatter_dimension=0, tiled=True),
        lax.psum_scatter(tally, "dp", scatter_dimension=0, tiled=True),
    )
    new_codebook = (owner_total + PRIOR * codebook) / (owner_tally + PRIOR)[:, None]
    position = lax.axis_index("cent") * own_rows
    own_norm = lax.dynamic_slice_in_dim(lognorm, position, own_rows, 0)
    return (new_codebook, owner_tally, own_norm)


def solution(mesh):
    return jax.shard_map(
        local,
        mesh=mesh,
        in_specs=(P(("dp", "cent"), None), P(("cent", "dp"), None)),
        out_specs=(P(("cent", "dp"), None), P(("cent", "dp")), P(("dp", "cent"))),
        check_vma=False,
    )
```

profile of v0, /device:TPU:0, one launch (start us, length us, event | category | flops | bytes accessed | tf_op | source)
XLA Modules:
  0.0 174.3 jit_solution(7230310930913809113)
XLA Ops:
  7.2 0.0 all-gather.5.cloned.1.call-start
  7.2 1.8 %convert_element_type.12 = bf16[128,1024]{1,0:T(8,128)(2,1)} convert(f32[128,1024]{1,0:T(8,128)} %param.3) | non-fusion elementwise | flops 131072 | bytes 786432 | tf_op jit(solution)/shard_map/convert_element_type | solution.py:19
  9.0 0.0 all-gather.5.cloned.1.call-update
  9.0 0.0 all-gather.3.cloned.1.call-start
  9.1 0.7 all-gather.3.cloned.1.call-update
  9.8 0.0 reduce-scatter.2.cloned.1.call-start
  9.8 31.0 %all-gather.5.cloned.1.call-done = bf16[512,1024]{1,0:T(8,128)(2,1)} async-done(((bf16[128,1024]{1,0:T(8,128)(2,1)}), bf16[512,1024]{1,0:T(8,128)(2,1)}) %all-gather.5.cloned.1.call-update) | async-done | bytes 1048592 | tf_op jit(solution)/shard_map/all_gather | solution.py:19
  40.8 1.5 multiply_reduce_fusion
  42.3 36.6 %all-gather.3.cloned.1.call-done = bf16[2048,1024]{1,0:T(8,128)(2,1)} async-done(((bf16[256,1024]{1,0:T(8,128)(2,1)}), bf16[2048,1024]{1,0:T(8,128)(2,1)}) %all-gather.3.cloned.1.call-update) | async-done | bytes 4194320 | tf_op jit(solution)/shard_map/all_gather | solution.py:21
  78.9 6.8 %fusion = (f32[2048]{0:T(1024)S(1)}, f32[2048,512]{0,1:T(8,128)}) fusion(f32[512]{0:T(512)S(1)} %broadcast_multiply_fusion, bf16[2048,1024]{1,0:T(8,128)(2,1)} %all-gather.3.cloned.1.call-done, bf16[512,1024]{1,0:T(8,128)(2,1)} %all-gather.5.cloned.1.call-done), kind=kOutput, calls=%fused_computation.4 | convolution fusion | flops 2150627328 | bytes 9447424 | tf_op jit(solution)/shard_map/dot_general | solution.py:11
  85.7 13.3 %pmax.7 = f32[2048]{0:T(1024)S(1)} all-reduce(f32[2048]{0:T(1024)S(1)} %get-tuple-element.5), channel_id=1, replica_groups=mesh['dp'=4,'cent'=8] {'cent'}, use_global_device_ids=true, to_apply=%region_2.0 | all-reduce | flops 2048 | bytes 16384 | tf_op jit(solution)/shard_map/pmax | solution.py:25
  99.1 3.1 %exponential_reduce_fusion = f32[2048]{0:T(1024)S(1)} fusion(f32[2048,512]{0,1:T(8,128)} %get-tuple-element.6, f32[2048]{0:T(1024)S(1)} %get-tuple-element.5, f32[512]{0:T(512)S(1)} %broadcast_multiply_fusion), kind=kLoop, calls=%fused_computation.2 | loop fusion | flops 4192256 | bytes 4212736 | tf_op jit(solution)/shard_map/reduce_sum | solution.py:24
  102.2 12.0 %psum.7 = f32[2048]{0:T(1024)S(1)} all-reduce(f32[2048]{0:T(1024)S(1)} %exponential_multiply_fusion), channel_id=1, replica_groups=mesh['dp'=4,'cent'=8] {'cent'}, use_global_device_ids=true, to_apply=%region_4.0 | all-reduce | flops 2048 | bytes 16384 | tf_op jit(solution)/shard_map/psum | solution.py:26
  114.3 0.0 copy-start.1
  114.3 7.3 %fusion.1 = f32[512,1024]{1,0:T(8,128)} fusion(bf16[2048,1024]{1,0:T(8,128)(2,1)} %all-gather.3.cloned.1.call-done, f32[2048,512]{0,1:T(8,128)} %get-tuple-element.6, f32[2048]{0:T(1024)S(1)} %log_add_fusion, f32[512]{0:T(512)S(1)} %broadcast_multiply_fusion), kind=kOutput, calls=%fused_computation.11 | convolution fusion | flops 2151677952 | bytes 10496000 | tf_op jit(solution)/shard_map/dot_general | solution.py:30
  121.5 0.0 reduce-scatter.2.cloned.1.call-update
  121.6 0.0 copy-done.1
  121.6 0.6 dynamic-slice
  122.8 0.6 dynamic_slice.3
  123.4 3.2 %convert_reduce_fusion = f32[512]{0:T(512)S(1)} fusion(f32[2048]{0:T(1024)S(1)} %log_add_fusion, f32[2048,512]{0,1:T(8,128)} %get-tuple-element.6, f32[512]{0:T(512)S(1)} %broadcast_multiply_fusion), kind=kLoop, calls=%fused_computation | loop fusion | flops 6290944 | bytes 4206592 | tf_op jit(solution)/shard_map/reduce_sum | solution.py:29
  126.6 12.1 %all-reduce = f32[512]{0:T(512)S(1)} all-reduce(f32[512]{0:T(512)S(1)} %convert_reduce_fusion), channel_id=3, replica_groups=mesh['dp'=4,'cent'=8] {'dp'}, use_global_device_ids=true, to_apply=%region_7.0.clone | all-reduce | flops 512 | bytes 4096
  138.7 0.6 broadcast_add_fusion
  139.3 26.5 %reduce-scatter.2.cloned.1.call-done = f32[128,1024]{1,0:T(8,128)} async-done(((f32[512,1024]{1,0:T(8,128)}), f32[128,1024]{1,0:T(8,128)}) %reduce-scatter.2.cloned.1.call-update) | async-done | bytes 524304 | tf_op jit(solution)/shard_map/reduce_scatter | solution.py:34
  165.8 2.0 %add_divide_fusion = f32[128,1024]{1,0:T(8,128)} fusion(f32[128,1024]{1,0:T(8,128)} %reduce-scatter.2.cloned.1.call-done, f32[128,1024]{1,0:T(8,128)S(1)} %copy-done, f32[128]{0:T(128)S(1)} %get-tuple-element.3), kind=kLoop, calls=%fused_computation.6 | loop fusion | flops 262144 | bytes 1573376 | tf_op jit(solution)/shard_map/div | solution.py:37
  (5 shorter events, 0.0 us)
Async XLA Ops:
  7.2 33.6 %all-gather.5.cloned.1.call-start = ((), (), s32[]{:S(2)}) async-start(), calls=%async_computation.2 | async-start | bytes 1310720 | tf_op jit(solution)/shard_map/all_gather | solution.py:19
  9.0 69.9 %all-gather.3.cloned.1.call-start = ((), (), s32[]{:S(2)}) async-start(), calls=%async_computation.1 | async-start | bytes 4718592 | tf_op jit(solution)/shard_map/all_gather | solution.py:21
  9.8 156.0 %reduce-scatter.2.cloned.1.call-start = ((), (), s32[]{:S(2)}) async-start(), calls=%async_computation.3 | async-start | bytes 2621440 | tf_op jit(solution)/shard_map/reduce_scatter | solution.py:34
  114.3 7.3 %copy-start.1 = (u32[32]{0:T(128)S(1)}, u32[32]{0:T(128)}, u32[]{:S(2)}) copy-start(u32[32]{0:T(128)} %constant.23) | copy-start | bytes 388
  121.5 44.3 %copy-start = (f32[128,1024]{1,0:T(8,128)S(1)}, f32[128,1024]{1,0:T(8,128)}, u32[]{:S(2)}) copy-start(f32[128,1024]{1,0:T(8,128)} %param.3) | copy-start | bytes 1572868
Sparse Core Ops, SparseCore 0:
  10.1 30.6 all-gather.4
  42.7 36.1 all-gather.2
  121.7 44.0 reduce-scatter.1
where the time goes:
time: 175 us; the launch traced here: 174 us
  waiting for transfers between devices  94.8 us (54%)
  blocking collectives  37.5 us (21%)
  between operations  14.5 us (8%)
  matrix products  14 us (8%)
  other arithmetic  12.1 us (7%)
    all_gather x1, waiting for transfers between devices, local(): gathered = lax.all_gather(embeddings, 'cent', axis=0, tiled=True)  36.6 us
    all_gather x1, waiting for transfers between devices, local(): lax.all_gather(codebook.astype(jnp.bfloat16), 'dp', axis=0, tiled=True)  31 us
    reduce_scatter x1, waiting for transfers between devices, local(): lax.psum_scatter(sums, 'dp', scatter_dimension=0, tiled=True)  26.5 us
    pmax x1, blocking collectives, local(): top_score = lax.pmax(highest, 'cent')  13.3 us
    unnamed x1, blocking collectives  12.1 us
    psum x1, blocking collectives, local(): top_total = lax.psum(summed * jnp.exp(highest - top_score), 'cent')  12 us
    dot_general x1, matrix products, local(): lax.dot_general(resp, gathered, (((0,), (0,)), ((), ())), preferred_eleme...  7.25 us
    dot_general x1, matrix products, score_block(): lax.dot_general(rows, centers, (((1,), (1,)), ((), ())), preferred_elemen...  6.79 us
  transfers between devices with their start and end apart: 3, of which 3 were waited for; matrix products, arithmetic and copies ran while one was open for 4% of the time, Pallas kernels for 0%

commit v1 on v0

v1 whole, which is shorter than its diff:
```python
import jax
import jax.numpy as jnp
from jax import lax
from jax.sharding import PartitionSpec as P

TEMPER = 0.8
PRIOR = 1.0


def swap(x, axis, size, mask):
    return lax.ppermute(x, axis, [(i, i ^ mask) for i in range(size)])


def gather_rows(own, size):
    if size != 8:
        return [own] + [swap(own, "cent", size, mask) for mask in range(1, size)]
    half = own.shape[0] // 2
    from_x = swap(own, "cent", size, 2)
    from_y = swap(own, "cent", size, 4)
    from_core = swap(own, "cent", size, 1)
    diag_top = swap(from_x[:half], "cent", size, 4)
    diag_low = swap(from_y[half:], "cent", size, 2)
    x_core = swap(from_x, "cent", size, 1)
    y_core = swap(from_y, "cent", size, 1)
    diag = jnp.concatenate([diag_top, diag_low], axis=0)
    diag_core = swap(diag, "cent", size, 1)
    return [own, from_core, from_x, x_core, from_y, y_core, diag, diag_core]


def score_block(rows, centers, squares):
    product = lax.dot_general(
        rows, centers, (((1,), (1,)), ((), ())), preferred_element_type=jnp.float32
    )
    return (product - 0.5 * squares[None, :]) / TEMPER


def local(n_dp, n_cent, embeddings, codebook):
    own_rows = embeddings.shape[0]
    own_cent = codebook.shape[0]
    rounded = codebook.astype(jnp.bfloat16)
    centers = [rounded] + [swap(rounded, "dp", n_dp, m) for m in range(1, n_dp)]
    blocks = gather_rows(embeddings, n_cent)
    centers = jnp.concatenate(centers, axis=0)
    squares = jnp.sum(jnp.square(centers.astype(jnp.float32)), axis=1)
    scores, pairs = [], []
    for rows in blocks:
        s = score_block(rows, centers, squares)
        m = jnp.max(s, axis=1)
        t = jnp.sum(jnp.exp(s - m[:, None]), axis=1)
        scores.append(s)
        pairs.append(jnp.stack([m, t]))
    pairs = jnp.stack(pairs)
    order = jnp.arange(n_cent)
    others = [pairs]
    for mask in range(1, n_cent):
        other = swap(pairs, "cent", n_cent, mask)
        others.append(jnp.stack([other[j ^ mask] for j in range(n_cent)]))
    others = jnp.stack(others)
    top = jnp.max(others[:, :, 0], axis=0)
    total = jnp.sum(others[:, :, 1] * jnp.exp(others[:, :, 0] - top[None]), axis=0)
    lognorm = top + jnp.log(total)
    resp = [jnp.exp(s - lognorm[j][:, None]).astype(jnp.bfloat16) for j, s in enumerate(scores)]
    resp = jnp.concatenate(resp, axis=0)
    gathered = jnp.concatenate(blocks, axis=0)
    tally = jnp.sum(resp.astype(jnp.float32), axis=0)
    sums = lax.dot_general(
        resp, gathered, (((0,), (0,)), ((), ())), preferred_element_type=jnp.float32
    )
    owner_total = sums[:own_cent]
    owner_tally = tally[:own_cent]
    for mask in range(1, n_dp):
        part = sums[mask * own_cent : (mask + 1) * own_cent]
        peak = jnp.max(jnp.abs(part), axis=1)
        power = jnp.exp2(jnp.clip(jnp.ceil(jnp.log2(peak)), -100.0, 100.0))
        packed = (part * (1.0 / power)[:, None]).astype(jnp.float16)
        side = jnp.stack([power, tally[mask * own_cent : (mask + 1) * own_cent]])
        packed = swap(packed, "dp", n_dp, mask)
        side = swap(side, "dp", n_dp, mask)
        owner_total = owner_total + packed.astype(jnp.float32) * side[0][:, None]
        owner_tally = owner_tally + side[1]
    new_codebook = (owner_total + PRIOR * codebook) / (owner_tally + PRIOR)[:, None]
    return (new_codebook, owner_tally, lognorm[0])


def solution(mesh):
    n_dp, n_cent = mesh.shape["dp"], mesh.shape["cent"]

    def run(embeddings, codebook):
        return local(n_dp, n_cent, embeddings, codebook)

    return jax.shard_map(
        run,
        mesh=mesh,
        in_specs=(P(("dp", "cent"), None), P(("cent", "dp"), None)),
        out_specs=(P(("cent", "dp"), None), P(("cent", "dp")), P(("dp", "cent"))),
        check_vma=False,
    )
```

time: 175 us -> 90.7 us (0.52)
  waiting for transfers between devices: 94.8 us -> 38.6 us
  blocking collectives: 37.5 us -> 0 us
  starting transfers between devices: 0.12 us -> 29.4 us
  between operations: 14.5 us -> 1.16 us
  local copies, waits for them, and re-layouts: 1.24 us -> 9.03 us
  matrix products: 14 us -> 6.3 us
  other arithmetic: 12.1 us -> 5.61 us
    all_gather x2 -> x0, waiting for transfers between devices: 67.6 us -> none  [the longest x1 36.6 us: local(): gathered = lax.all_gather(embeddings, 'cent', axis=0, tiled=True)]
    ppermute x0 -> x24, waiting for transfers between devices: none -> 38.6 us  [swap(): return lax.ppermute(x, axis, [(i, i ^ mask) for i in range(size)])]
    ppermute x0 -> x24, starting transfers between devices: none -> 29.4 us  [swap(): return lax.ppermute(x, axis, [(i, i ^ mask) for i in range(size)])]
    reduce_scatter x1 -> x0, waiting for transfers between devices: 26.5 us -> none  [local(): lax.psum_scatter(sums, 'dp', scatter_dimension=0, tiled=True)]
    pmax x1 -> x0, blocking collectives: 13.3 us -> none  [local(): top_score = lax.pmax(highest, 'cent')]
    unnamed x1 -> x0, blocking collectives: 12.1 us -> none
    psum x1 -> x0, blocking collectives: 12 us -> none  [local(): top_total = lax.psum(summed * jnp.exp(highest - top_score), 'cent')]
    unnamed x5 -> x32, local copies, waits for them, and re-layouts: 0.6 us -> 6.77 us
  transfers between devices with their start and end apart: 3 -> 24, of which waited for: 3 -> 10; matrix products, arithmetic and copies ran while one was open for 4% -> 10% of each run, Pallas kernels for 0% -> 0%
where the time goes in v1:
time: 90.7 us; the launch traced here: 90 us
  waiting for transfers between devices  38.6 us (43%)
  starting transfers between devices  29.4 us (32%)
  local copies, waits for them, and re-layouts  9.03 us (10%)
  matrix products  6.3 us (7%)
  other arithmetic  5.61 us (6%)
  between operations  1.16 us (1%)
    ppermute x24, waiting for transfers between devices, swap(): return lax.ppermute(x, axis, [(i, i ^ mask) for i in range(size)])  38.6 us
    ppermute x24, starting transfers between devices, swap(): return lax.ppermute(x, axis, [(i, i ^ mask) for i in range(size)])  29.4 us
    unnamed x32, local copies, waits for them, and re-layouts  6.77 us
    dot_general x8, matrix products, score_block(): lax.dot_general(rows, centers, (((1,), (1,)), ((), ())), preferred_elemen...  3.95 us
    dot_general x1, matrix products, local(): lax.dot_general(resp, gathered, (((0,), (0,)), ((), ())), preferred_eleme...  2.35 us
    concatenate x1, local copies, waits for them, and re-layouts, local(): gathered = jnp.concatenate(blocks, axis=0)  1.89 us
  transfers between devices with their start and end apart: 24, of which 10 were waited for; matrix products, arithmetic and copies ran while one was open for 10% of the time, Pallas kernels for 0%

profile of v1, /device:TPU:0, one launch (start us, length us, event | category | flops | bytes accessed | tf_op | source)
XLA Modules:
  0.0 90.0 jit_solution(14903618810144393853)
XLA Ops:
  1.8 3.1 %collective-permute-start = (bf16[128,1024]{1,0:T(8,128)(2,1)S(1)}, bf16[128,1024]{1,0:T(8,128)(2,1)S(1)}, u32[]{:S(2)}, u32[]{:S(2)}) collective-permute-start(bf16[128,1024]{1,0:T(8,128)(2,1)S(1)} %convert_element_type.39), channel_id=1, source_target_pairs={{0,8},{8,0},{16,24},{24,16},{1,9},{9,1},{17,25},{25,17},{2,10},{10... | collective-permute-start | bytes 786440 | tf_op jit(solution)/shard_map/ppermute | solution.py:11
  4.9 2.6 %collective-permute-start.1 = (bf16[128,1024]{1,0:T(8,128)(2,1)S(1)}, bf16[128,1024]{1,0:T(8,128)(2,1)S(1)}, u32[]{:S(2)}, u32[]{:S(2)}) collective-permute-start(bf16[128,1024]{1,0:T(8,128)(2,1)S(1)} %convert_element_type.39), channel_id=1, source_target_pairs={{0,16},{8,24},{16,0},{24,8},{1,17},{9,25},{17,1},{25,9},{2,18},{10... | collective-permute-start | bytes 786440 | tf_op jit(solution)/shard_map/ppermute | solution.py:11
  7.5 1.7 %collective-permute-start.4 = (bf16[256,1024]{1,0:T(8,128)(2,1)}, bf16[256,1024]{1,0:T(8,128)(2,1)S(1)}, u32[]{:S(2)}, u32[]{:S(2)}) collective-permute-start(bf16[256,1024]{1,0:T(8,128)(2,1)} %param.2), channel_id=1, source_target_pairs={{0,2},{1,3},{2,0},{3,1},{4,6},{5,7},{6,4},{7,5},{8,10},{9,11},{10,... | collective-permute-start | bytes 1572872 | tf_op jit(solution)/shard_map/ppermute | solution.py:11
  10.3 5.7 %collective-permute-done = bf16[128,1024]{1,0:T(8,128)(2,1)S(1)} collective-permute-done((bf16[128,1024]{1,0:T(8,128)(2,1)S(1)}, bf16[128,1024]{1,0:T(8,128)(2,1)S(1)}, u32[]{:S(2)}, u32[]{:S(2)}) %collective-permute-start) | collective-permute-done | bytes 262176 | tf_op jit(solution)/shard_map/ppermute | solution.py:11
  16.0 1.7 %collective-permute-start.6 = (bf16[256,1024]{1,0:T(8,128)(2,1)}, bf16[256,1024]{1,0:T(8,128)(2,1)S(1)}, u32[]{:S(2)}, u32[]{:S(2)}) collective-permute-start(bf16[256,1024]{1,0:T(8,128)(2,1)} %param.2), channel_id=1, source_target_pairs={{0,4},{1,5},{2,6},{3,7},{4,0},{5,1},{6,2},{7,3},{8,12},{9,13},{10,... | collective-permute-start | bytes 1572872 | tf_op jit(solution)/shard_map/ppermute | solution.py:11
  17.7 8.5 %collective-permute-done.1 = bf16[128,1024]{1,0:T(8,128)(2,1)S(1)} collective-permute-done((bf16[128,1024]{1,0:T(8,128)(2,1)S(1)}, bf16[128,1024]{1,0:T(8,128)(2,1)S(1)}, u32[]{:S(2)}, u32[]{:S(2)}) %collective-permute-start.1) | collective-permute-done | bytes 262176 | tf_op jit(solution)/shard_map/ppermute | solution.py:11
  27.2 1.6 %collective-permute-start.8 = (bf16[128,1024]{1,0:T(8,128)(2,1)S(1)}, bf16[128,1024]{1,0:T(8,128)(2,1)S(1)}, u32[]{:S(2)}, u32[]{:S(2)}) collective-permute-start(bf16[128,1024]{1,0:T(8,128)(2,1)S(1)} %slice.298), channel_id=1, source_target_pairs={{0,4},{1,5},{2,6},{3,7},{4,0},{5,1},{6,2},{7,3},{8,12},{9,13},{10,... | collective-permute-start | bytes 786440 | tf_op jit(solution)/shard_map/ppermute | solution.py:11
  28.8 2.3 %collective-permute-done.6 = bf16[256,1024]{1,0:T(8,128)(2,1)S(1)} collective-permute-done((bf16[256,1024]{1,0:T(8,128)(2,1)}, bf16[256,1024]{1,0:T(8,128)(2,1)S(1)}, u32[]{:S(2)}, u32[]{:S(2)}) %collective-permute-start.6) | collective-permute-done | bytes 524320 | tf_op jit(solution)/shard_map/ppermute | solution.py:11
  31.1 1.5 %collective-permute-start.9 = (bf16[128,1024]{1,0:T(8,128)(2,1)S(1)}, bf16[128,1024]{1,0:T(8,128)(2,1)S(1)}, u32[]{:S(2)}, u32[]{:S(2)}) collective-permute-start(bf16[128,1024]{1,0:T(8,128)(2,1)S(1)} %slice.299), channel_id=1, source_target_pairs={{0,2},{1,3},{2,0},{3,1},{4,6},{5,7},{6,4},{7,5},{8,10},{9,11},{10,... | collective-permute-start | bytes 786440 | tf_op jit(solution)/shard_map/ppermute | solution.py:11
  36.1 1.5 %collective-permute-done.9 = bf16[128,1024]{1,0:T(8,128)(2,1)S(1)} collective-permute-done((bf16[128,1024]{1,0:T(8,128)(2,1)S(1)}, bf16[128,1024]{1,0:T(8,128)(2,1)S(1)}, u32[]{:S(2)}, u32[]{:S(2)}) %collective-permute-start.9) | collective-permute-done | bytes 262176 | tf_op jit(solution)/shard_map/ppermute | solution.py:11
  38.2 1.3 %copy-done.7 = bf16[2048,1024]{1,0:T(8,128)(2,1)} copy-done((bf16[2048,1024]{1,0:T(8,128)(2,1)}, bf16[2048,1024]{1,0:T(8,128)(2,1)S(1)}, u32[]{:S(2)}) %copy-start.7) | copy-done | bytes 4194328
  43.4 1.2 %collective-permute-start.17 = (f32[8,2,256]{2,0,1:T(8,128)S(1)}, f32[8,2,256]{2,0,1:T(8,128)S(1)}, u32[]{:S(2)}, u32[]{:S(2)}) collective-permute-start(f32[8,2,256]{2,0,1:T(8,128)S(1)} %stack.203), channel_id=1, source_target_pairs={{0,7},{1,6},{2,5},{3,4},{4,3},{5,2},{6,1},{7,0},{8,15},{9,14},{10,... | collective-permute-start | bytes 49160 | tf_op jit(solution)/shard_map/ppermute | solution.py:11
  44.7 1.5 %collective-permute-start.15 = (f32[8,2,256]{2,0,1:T(8,128)S(1)}, f32[8,2,256]{2,0,1:T(8,128)S(1)}, u32[]{:S(2)}, u32[]{:S(2)}) collective-permute-start(f32[8,2,256]{2,0,1:T(8,128)S(1)} %stack.203), channel_id=1, source_target_pairs={{0,5},{1,4},{2,7},{3,6},{4,1},{5,0},{6,3},{7,2},{8,13},{9,12},{10,... | collective-permute-start | bytes 49160 | tf_op jit(solution)/shard_map/ppermute | solution.py:11
  46.8 1.5 %collective-permute-start.12 = (f32[8,2,256]{2,0,1:T(8,128)S(1)}, f32[8,2,256]{2,0,1:T(8,128)S(1)}, u32[]{:S(2)}, u32[]{:S(2)}) collective-permute-start(f32[8,2,256]{2,0,1:T(8,128)S(1)} %stack.203), channel_id=1, source_target_pairs={{0,2},{1,3},{2,0},{3,1},{4,6},{5,7},{6,4},{7,5},{8,10},{9,11},{10,... | collective-permute-start | bytes 49160 | tf_op jit(solution)/shard_map/ppermute | solution.py:11
  48.3 1.9 %constant_dynamic-update-slice_fusion.10 = bf16[2048,1024]{1,0:T(8,128)(2,1)} fusion(bf16[2048,1024]{1,0:T(8,128)(2,1)} %copy-done.7, bf16[256,1024]{1,0:T(8,128)(2,1)} %copy-done.6), kind=kLoop, calls=%fused_computation.76 | loop fusion | bytes 1048576 | tf_op jit(solution)/shard_map/concatenate | solution.py:64
  50.2 1.5 %collective-permute-start.14 = (f32[8,2,256]{2,0,1:T(8,128)S(1)}, f32[8,2,256]{2,0,1:T(8,128)S(1)}, u32[]{:S(2)}, u32[]{:S(2)}) collective-permute-start(f32[8,2,256]{2,0,1:T(8,128)S(1)} %stack.203), channel_id=1, source_target_pairs={{0,4},{1,5},{2,6},{3,7},{4,0},{5,1},{6,2},{7,3},{8,12},{9,13},{10,... | collective-permute-start | bytes 49160 | tf_op jit(solution)/shard_map/ppermute | solution.py:11
  54.0 2.5 %collective-permute-done.16 = f32[8,2,256]{2,0,1:T(8,128)S(1)} collective-permute-done((f32[8,2,256]{2,0,1:T(8,128)S(1)}, f32[8,2,256]{2,0,1:T(8,128)S(1)}, u32[]{:S(2)}, u32[]{:S(2)}) %collective-permute-start.16) | collective-permute-done | bytes 16416 | tf_op jit(solution)/shard_map/ppermute | solution.py:11
  58.4 1.6 %copy-done.8 = bf16[2048,1024]{1,0:T(8,128)(2,1)S(1)} copy-done((bf16[2048,1024]{1,0:T(8,128)(2,1)S(1)}, bf16[2048,1024]{1,0:T(8,128)(2,1)}, u32[]{:S(2)}) %copy-start.8) | copy-done | bytes 4194328
  60.0 2.3 %fusion.45 = f32[512,1024]{1,0:T(8,128)S(1)} fusion(bf16[2048,512]{0,1:T(8,128)(2,1)S(1)} %fusion.25, bf16[2048,1024]{1,0:T(8,128)(2,1)S(1)} %copy-done.8), kind=kOutput, calls=%fused_computation.133 | convolution fusion | flops 2147483648 | bytes 8388608 | tf_op jit(solution)/shard_map/dot_general | solution.py:66
  62.6 1.8 %collective-permute-start.19 = (f32[2,128]{1,0:T(2,128)S(1)}, f32[2,128]{1,0:T(2,128)S(1)}, u32[]{:S(2)}, u32[]{:S(2)}) collective-permute-start(f32[2,128]{1,0:T(2,128)S(1)} %pad_maximum_fusion.9), channel_id=1, source_target_pairs={{0,8},{8,0},{16,24},{24,16},{1,9},{9,1},{17,25},{25,17},{2,10},{10... | collective-permute-start | bytes 3080 | tf_op jit(solution)/shard_map/ppermute | solution.py:11
  64.5 2.1 %collective-permute-start.21 = (f32[2,128]{1,0:T(2,128)S(1)}, f32[2,128]{1,0:T(2,128)S(1)}, u32[]{:S(2)}, u32[]{:S(2)}) collective-permute-start(f32[2,128]{1,0:T(2,128)S(1)} %pad_maximum_fusion.10), channel_id=1, source_target_pairs={{0,16},{8,24},{16,0},{24,8},{1,17},{9,25},{17,1},{25,9},{2,18},{10... | collective-permute-start | bytes 3080 | tf_op jit(solution)/shard_map/ppermute | solution.py:11
  68.3 3.0 %collective-permute-start.20 = (f16[128,1024]{1,0:T(8,128)(2,1)S(1)}, f16[128,1024]{1,0:T(8,128)(2,1)S(1)}, u32[]{:S(2)}, u32[]{:S(2)}) collective-permute-start(f16[128,1024]{1,0:T(8,128)(2,1)S(1)} %get-tuple-element.16), channel_id=1, source_target_pairs={{0,16},{8,24},{16,0},{24,8},{1,17},{9,25},{17,1},{25,9},{2,18},{10... | collective-permute-start | bytes 786440 | tf_op jit(solution)/shard_map/ppermute | solution.py:11
  72.7 5.5 %collective-permute-done.18 = f16[128,1024]{1,0:T(8,128)(2,1)S(1)} collective-permute-done((f16[128,1024]{1,0:T(8,128)(2,1)S(1)}, f16[128,1024]{1,0:T(8,128)(2,1)S(1)}, u32[]{:S(2)}, u32[]{:S(2)}) %collective-permute-start.18) | collective-permute-done | bytes 262176 | tf_op jit(solution)/shard_map/ppermute | solution.py:11
  78.1 10.8 %collective-permute-done.20 = f16[128,1024]{1,0:T(8,128)(2,1)S(1)} collective-permute-done((f16[128,1024]{1,0:T(8,128)(2,1)S(1)}, f16[128,1024]{1,0:T(8,128)(2,1)S(1)}, u32[]{:S(2)}, u32[]{:S(2)}) %collective-permute-start.20) | collective-permute-done | bytes 262176 | tf_op jit(solution)/shard_map/ppermute | solution.py:11
  (137 shorter events, 20.2 us)
Async XLA Ops:
  1.8 14.2 %collective-permute-start = (bf16[128,1024]{1,0:T(8,128)(2,1)S(1)}, bf16[128,1024]{1,0:T(8,128)(2,1)S(1)}, u32[]{:S(2)}, u32[]{:S(2)}) collective-permute-start(bf16[128,1024]{1,0:T(8,128)(2,1)S(1)} %convert_element_type.39), channel_id=1, source_target_pairs={{0,8},{8,0},{16,24},{24,16},{1,9},{9,1},{17,25},{25,17},{2,10},{10... | collective-permute-start | bytes 786440 | tf_op jit(solution)/shard_map/ppermute | solution.py:11
  4.9 21.4 %collective-permute-start.1 = (bf16[128,1024]{1,0:T(8,128)(2,1)S(1)}, bf16[128,1024]{1,0:T(8,128)(2,1)S(1)}, u32[]{:S(2)}, u32[]{:S(2)}) collective-permute-start(bf16[128,1024]{1,0:T(8,128)(2,1)S(1)} %convert_element_type.39), channel_id=1, source_target_pairs={{0,16},{8,24},{16,0},{24,8},{1,17},{9,25},{17,1},{25,9},{2,18},{10... | collective-permute-start | bytes 786440 | tf_op jit(solution)/shard_map/ppermute | solution.py:11
  7.5 18.8 %collective-permute-start.2 = (bf16[128,1024]{1,0:T(8,128)(2,1)S(1)}, bf16[128,1024]{1,0:T(8,128)(2,1)S(1)}, u32[]{:S(2)}, u32[]{:S(2)}) collective-permute-start(bf16[128,1024]{1,0:T(8,128)(2,1)S(1)} %convert_element_type.39), channel_id=1, source_target_pairs={{0,24},{8,16},{16,8},{24,0},{1,25},{9,17},{17,9},{25,1},{2,26},{10... | collective-permute-start | bytes 786440 | tf_op jit(solution)/shard_map/ppermute | solution.py:11
  7.5 19.7 %collective-permute-start.4 = (bf16[256,1024]{1,0:T(8,128)(2,1)}, bf16[256,1024]{1,0:T(8,128)(2,1)S(1)}, u32[]{:S(2)}, u32[]{:S(2)}) collective-permute-start(bf16[256,1024]{1,0:T(8,128)(2,1)} %param.2), channel_id=1, source_target_pairs={{0,2},{1,3},{2,0},{3,1},{4,6},{5,7},{6,4},{7,5},{8,10},{9,11},{10,... | collective-permute-start | bytes 1572872 | tf_op jit(solution)/shard_map/ppermute | solution.py:11
  9.2 25.3 %collective-permute-start.3 = (bf16[256,1024]{1,0:T(8,128)(2,1)}, bf16[256,1024]{1,0:T(8,128)(2,1)S(1)}, u32[]{:S(2)}, u32[]{:S(2)}) collective-permute-start(bf16[256,1024]{1,0:T(8,128)(2,1)} %param.2), channel_id=1, source_target_pairs={{0,1},{1,0},{2,3},{3,2},{4,5},{5,4},{6,7},{7,6},{8,9},{9,8},{10,11... | collective-permute-start | bytes 1572872 | tf_op jit(solution)/shard_map/ppermute | solution.py:11
  16.0 15.1 %collective-permute-start.6 = (bf16[256,1024]{1,0:T(8,128)(2,1)}, bf16[256,1024]{1,0:T(8,128)(2,1)S(1)}, u32[]{:S(2)}, u32[]{:S(2)}) collective-permute-start(bf16[256,1024]{1,0:T(8,128)(2,1)} %param.2), channel_id=1, source_target_pairs={{0,4},{1,5},{2,6},{3,7},{4,0},{5,1},{6,2},{7,3},{8,12},{9,13},{10,... | collective-permute-start | bytes 1572872 | tf_op jit(solution)/shard_map/ppermute | solution.py:11
  27.2 8.8 %collective-permute-start.8 = (bf16[128,1024]{1,0:T(8,128)(2,1)S(1)}, bf16[128,1024]{1,0:T(8,128)(2,1)S(1)}, u32[]{:S(2)}, u32[]{:S(2)}) collective-permute-start(bf16[128,1024]{1,0:T(8,128)(2,1)S(1)} %slice.298), channel_id=1, source_target_pairs={{0,4},{1,5},{2,6},{3,7},{4,0},{5,1},{6,2},{7,3},{8,12},{9,13},{10,... | collective-permute-start | bytes 786440 | tf_op jit(solution)/shard_map/ppermute | solution.py:11
  31.1 6.4 %collective-permute-start.9 = (bf16[128,1024]{1,0:T(8,128)(2,1)S(1)}, bf16[128,1024]{1,0:T(8,128)(2,1)S(1)}, u32[]{:S(2)}, u32[]{:S(2)}) collective-permute-start(bf16[128,1024]{1,0:T(8,128)(2,1)S(1)} %slice.299), channel_id=1, source_target_pairs={{0,2},{1,3},{2,0},{3,1},{4,6},{5,7},{6,4},{7,5},{8,10},{9,11},{10,... | collective-permute-start | bytes 786440 | tf_op jit(solution)/shard_map/ppermute | solution.py:11
  33.3 2.0 %collective-permute-start.5 = (bf16[256,1024]{1,0:T(8,128)(2,1)S(1)}, bf16[256,1024]{1,0:T(8,128)(2,1)S(1)}, u32[]{:S(2)}, u32[]{:S(2)}) collective-permute-start(bf16[256,1024]{1,0:T(8,128)(2,1)S(1)} %collective-permute-done.4), channel_id=1, source_target_pairs={{0,1},{1,0},{2,3},{3,2},{4,5},{5,4},{6,7},{7,6},{8,9},{9,8},{10,11... | collective-permute-start | bytes 1572872 | tf_op jit(solution)/shard_map/ppermute | solution.py:11
  33.3 2.6 %collective-permute-start.7 = (bf16[256,1024]{1,0:T(8,128)(2,1)S(1)}, bf16[256,1024]{1,0:T(8,128)(2,1)S(1)}, u32[]{:S(2)}, u32[]{:S(2)}) collective-permute-start(bf16[256,1024]{1,0:T(8,128)(2,1)S(1)} %collective-permute-done.6), channel_id=1, source_target_pairs={{0,1},{1,0},{2,3},{3,2},{4,5},{5,4},{6,7},{7,6},{8,9},{9,8},{10,11... | collective-permute-start | bytes 1572872 | tf_op jit(solution)/shard_map/ppermute | solution.py:11
  37.6 4.0 %collective-permute-start.10 = (bf16[256,1024]{1,0:T(8,128)(2,1)S(1)}, bf16[256,1024]{1,0:T(8,128)(2,1)S(1)}, u32[]{:S(2)}, u32[]{:S(2)}) collective-permute-start(bf16[256,1024]{1,0:T(8,128)(2,1)S(1)} %get-tuple-element.18), channel_id=1, source_target_pairs={{0,1},{1,0},{2,3},{3,2},{4,5},{5,4},{6,7},{7,6},{8,9},{9,8},{10,11... | collective-permute-start | bytes 1572872 | tf_op jit(solution)/shard_map/ppermute | solution.py:11
  43.4 13.1 %collective-permute-start.17 = (f32[8,2,256]{2,0,1:T(8,128)S(1)}, f32[8,2,256]{2,0,1:T(8,128)S(1)}, u32[]{:S(2)}, u32[]{:S(2)}) collective-permute-start(f32[8,2,256]{2,0,1:T(8,128)S(1)} %stack.203), channel_id=1, source_target_pairs={{0,7},{1,6},{2,5},{3,4},{4,3},{5,2},{6,1},{7,0},{8,15},{9,14},{10,... | collective-permute-start | bytes 49160 | tf_op jit(solution)/shard_map/ppermute | solution.py:11
  44.7 9.3 %collective-permute-start.15 = (f32[8,2,256]{2,0,1:T(8,128)S(1)}, f32[8,2,256]{2,0,1:T(8,128)S(1)}, u32[]{:S(2)}, u32[]{:S(2)}) collective-permute-start(f32[8,2,256]{2,0,1:T(8,128)S(1)} %stack.203), channel_id=1, source_target_pairs={{0,5},{1,4},{2,7},{3,6},{4,1},{5,0},{6,3},{7,2},{8,13},{9,12},{10,... | collective-permute-start | bytes 49160 | tf_op jit(solution)/shard_map/ppermute | solution.py:11
  46.1 6.9 %collective-permute-start.13 = (f32[8,2,256]{2,0,1:T(8,128)S(1)}, f32[8,2,256]{2,0,1:T(8,128)S(1)}, u32[]{:S(2)}, u32[]{:S(2)}) collective-permute-start(f32[8,2,256]{2,0,1:T(8,128)S(1)} %stack.203), channel_id=1, source_target_pairs={{0,3},{1,2},{2,1},{3,0},{4,7},{5,6},{6,5},{7,4},{8,11},{9,10},{10,... | collective-permute-start | bytes 49160 | tf_op jit(solution)/shard_map/ppermute | solution.py:11
  46.3 3.9 %collective-permute-start.11 = (f32[8,2,256]{2,0,1:T(8,128)S(1)}, f32[8,2,256]{2,0,1:T(8,128)S(1)}, u32[]{:S(2)}, u32[]{:S(2)}) collective-permute-start(f32[8,2,256]{2,0,1:T(8,128)S(1)} %stack.203), channel_id=1, source_target_pairs={{0,1},{1,0},{2,3},{3,2},{4,5},{5,4},{6,7},{7,6},{8,9},{9,8},{10,11... | collective-permute-start | bytes 49160 | tf_op jit(solution)/shard_map/ppermute | solution.py:11
  46.8 4.9 %collective-permute-start.12 = (f32[8,2,256]{2,0,1:T(8,128)S(1)}, f32[8,2,256]{2,0,1:T(8,128)S(1)}, u32[]{:S(2)}, u32[]{:S(2)}) collective-permute-start(f32[8,2,256]{2,0,1:T(8,128)S(1)} %stack.203), channel_id=1, source_target_pairs={{0,2},{1,3},{2,0},{3,1},{4,6},{5,7},{6,4},{7,5},{8,10},{9,11},{10,... | collective-permute-start | bytes 49160 | tf_op jit(solution)/shard_map/ppermute | solution.py:11
  50.2 3.7 %collective-permute-start.14 = (f32[8,2,256]{2,0,1:T(8,128)S(1)}, f32[8,2,256]{2,0,1:T(8,128)S(1)}, u32[]{:S(2)}, u32[]{:S(2)}) collective-permute-start(f32[8,2,256]{2,0,1:T(8,128)S(1)} %stack.203), channel_id=1, source_target_pairs={{0,4},{1,5},{2,6},{3,7},{4,0},{5,1},{6,2},{7,3},{8,12},{9,13},{10,... | collective-permute-start | bytes 49160 | tf_op jit(solution)/shard_map/ppermute | solution.py:11
  51.8 4.7 %collective-permute-start.16 = (f32[8,2,256]{2,0,1:T(8,128)S(1)}, f32[8,2,256]{2,0,1:T(8,128)S(1)}, u32[]{:S(2)}, u32[]{:S(2)}) collective-permute-start(f32[8,2,256]{2,0,1:T(8,128)S(1)} %stack.203), channel_id=1, source_target_pairs={{0,6},{1,7},{2,4},{3,5},{4,2},{5,3},{6,0},{7,1},{8,14},{9,15},{10,... | collective-permute-start | bytes 49160 | tf_op jit(solution)/shard_map/ppermute | solution.py:11
  62.6 8.6 %collective-permute-start.19 = (f32[2,128]{1,0:T(2,128)S(1)}, f32[2,128]{1,0:T(2,128)S(1)}, u32[]{:S(2)}, u32[]{:S(2)}) collective-permute-start(f32[2,128]{1,0:T(2,128)S(1)} %pad_maximum_fusion.9), channel_id=1, source_target_pairs={{0,8},{8,0},{16,24},{24,16},{1,9},{9,1},{17,25},{25,17},{2,10},{10... | collective-permute-start | bytes 3080 | tf_op jit(solution)/shard_map/ppermute | solution.py:11
  64.5 7.4 %collective-permute-start.21 = (f32[2,128]{1,0:T(2,128)S(1)}, f32[2,128]{1,0:T(2,128)S(1)}, u32[]{:S(2)}, u32[]{:S(2)}) collective-permute-start(f32[2,128]{1,0:T(2,128)S(1)} %pad_maximum_fusion.10), channel_id=1, source_target_pairs={{0,16},{8,24},{16,0},{24,8},{1,17},{9,25},{17,1},{25,9},{2,18},{10... | collective-permute-start | bytes 3080 | tf_op jit(solution)/shard_map/ppermute | solution.py:11
  66.6 5.5 %collective-permute-start.23 = (f32[2,128]{1,0:T(2,128)S(1)}, f32[2,128]{1,0:T(2,128)S(1)}, u32[]{:S(2)}, u32[]{:S(2)}) collective-permute-start(f32[2,128]{1,0:T(2,128)S(1)} %pad_maximum_fusion.11), channel_id=1, source_target_pairs={{0,24},{8,16},{16,8},{24,0},{1,25},{9,17},{17,9},{25,1},{2,26},{10... | collective-permute-start | bytes 3080 | tf_op jit(solution)/shard_map/ppermute | solution.py:11
  67.4 10.8 %collective-permute-start.18 = (f16[128,1024]{1,0:T(8,128)(2,1)S(1)}, f16[128,1024]{1,0:T(8,128)(2,1)S(1)}, u32[]{:S(2)}, u32[]{:S(2)}) collective-permute-start(f16[128,1024]{1,0:T(8,128)(2,1)S(1)} %get-tuple-element.14), channel_id=1, source_target_pairs={{0,8},{8,0},{16,24},{24,16},{1,9},{9,1},{17,25},{25,17},{2,10},{10... | collective-permute-start | bytes 786440 | tf_op jit(solution)/shard_map/ppermute | solution.py:11
  68.3 20.6 %collective-permute-start.20 = (f16[128,1024]{1,0:T(8,128)(2,1)S(1)}, f16[128,1024]{1,0:T(8,128)(2,1)S(1)}, u32[]{:S(2)}, u32[]{:S(2)}) collective-permute-start(f16[128,1024]{1,0:T(8,128)(2,1)S(1)} %get-tuple-element.16), channel_id=1, source_target_pairs={{0,16},{8,24},{16,0},{24,8},{1,17},{9,25},{17,1},{25,9},{2,18},{10... | collective-permute-start | bytes 786440 | tf_op jit(solution)/shard_map/ppermute | solution.py:11
  71.3 17.7 %collective-permute-start.22 = (f16[128,1024]{1,0:T(8,128)(2,1)S(1)}, f16[128,1024]{1,0:T(8,128)(2,1)S(1)}, u32[]{:S(2)}, u32[]{:S(2)}) collective-permute-start(f16[128,1024]{1,0:T(8,128)(2,1)S(1)} %get-tuple-element.15), channel_id=1, source_target_pairs={{0,24},{8,16},{16,8},{24,0},{1,25},{9,17},{17,9},{25,1},{2,26},{10... | collective-permute-start | bytes 786440 | tf_op jit(solution)/shard_map/ppermute | solution.py:11
  (10 other events, 62.4 us)

commit v2 on v1

v2 whole, which is shorter than its diff:
```python
import jax
import jax.numpy as jnp
from jax import lax
from jax.sharding import PartitionSpec as P

TEMPER = 0.8
PRIOR = 1.0
SIDE = 16


def swap(x, axis, size, mask):
    return lax.ppermute(x, axis, [(i, i ^ mask) for i in range(size)])


def gather_centers(own, size):
    if size != 4:
        return [own] + [swap(own, "dp", size, mask) for mask in range(1, size)]
    far = swap(own, "dp", size, 2)
    near = swap(own, "dp", size, 1)
    return [own, near, far, swap(far, "dp", size, 1)]


def gather_rows(own, size):
    if size != 8:
        return [own] + [swap(own, "cent", size, mask) for mask in range(1, size)]
    half = own.shape[0] // 2
    from_x = swap(own, "cent", size, 2)
    from_y = swap(own, "cent", size, 4)
    from_core = swap(own, "cent", size, 1)
    diag_top = swap(from_x[:half], "cent", size, 4)
    diag_low = swap(from_y[half:], "cent", size, 2)
    x_core = swap(from_x, "cent", size, 1)
    y_core = swap(from_y, "cent", size, 1)
    diag = jnp.concatenate([diag_top, diag_low], axis=0)
    diag_core = swap(diag, "cent", size, 1)
    return [own, from_core, from_x, x_core, from_y, y_core, diag, diag_core]


def score_block(rows, centers, squares):
    product = lax.dot_general(
        centers, rows, (((1,), (1,)), ((), ())), preferred_element_type=jnp.float32
    )
    return (product - 0.5 * squares[:, None]) / TEMPER


def join(pairs, other, mask, size):
    other = jnp.concatenate([other[:, j ^ mask : (j ^ mask) + 1] for j in range(size)], axis=1)
    top = jnp.maximum(pairs[0], other[0])
    total = pairs[1] * jnp.exp(pairs[0] - top) + other[1] * jnp.exp(other[0] - top)
    return jnp.stack([top, total])


def encode(part, tally, power, unit):
    count = tally * unit
    high = count.astype(jnp.float16)
    low = ((count - high.astype(jnp.float32)) * 2048.0).astype(jnp.float16)
    tag = jnp.full(high.shape, 1.0, jnp.float32) * power
    side = jnp.stack([high, low, tag.astype(jnp.float16)])
    side = jnp.pad(side, ((0, SIDE - 3), (0, part.shape[1] - side.shape[1])))
    body = (part * jnp.exp2(14.0 - power)).astype(jnp.float16)
    return jnp.concatenate([body, side], axis=0)


def decode(message, unit):
    rows = message.shape[0] - SIDE
    side = message[rows:, :rows].astype(jnp.float32)
    power = side[2, 0]
    tally = (side[0] + side[1] * (1.0 / 2048.0)) * (1.0 / unit)
    return message[:rows].astype(jnp.float32) * jnp.exp2(power - 14.0), tally, power


def local(n_dp, n_cent, embeddings, codebook):
    own_rows = embeddings.shape[0]
    own_cent = codebook.shape[0]
    n_rows = own_rows * n_cent
    blocks = gather_rows(embeddings, n_cent)
    centers = gather_centers(codebook.astype(jnp.bfloat16), n_dp)
    centers = jnp.concatenate(centers, axis=0)
    squares = jnp.sum(jnp.square(centers.astype(jnp.float32)), axis=1)
    scores, tops, totals = [], [], []
    for rows in blocks:
        s = score_block(rows, centers, squares)
        m = jnp.max(s, axis=0)
        scores.append(s)
        tops.append(m)
        totals.append(jnp.sum(jnp.exp(s - m[None, :]), axis=0))
    pairs = jnp.stack([jnp.stack(tops), jnp.stack(totals)])
    mask = 1
    while mask < n_cent:
        pairs = join(pairs, swap(pairs, "cent", n_cent, mask), mask, n_cent)
        mask *= 2
    lognorm = pairs[0] + jnp.log(pairs[1])
    resp = [jnp.exp(s - lognorm[j][None, :]).astype(jnp.bfloat16) for j, s in enumerate(scores)]
    resp = jnp.concatenate(resp, axis=1)
    gathered = jnp.concatenate(blocks, axis=0)
    tally = jnp.sum(resp.astype(jnp.float32), axis=1)
    bound = jnp.max(jnp.stack([jnp.max(jnp.abs(b)) for b in blocks])).astype(jnp.float32)
    power = jnp.clip(jnp.ceil(jnp.log2(bound * n_rows)), -100.0, 100.0)
    unit = 16384.0 / n_rows

    def chunk(j):
        part = slice(j * own_cent, (j + 1) * own_cent)
        sums = lax.dot_general(
            resp[part], gathered, (((1,), (0,)), ((), ())), preferred_element_type=jnp.float32
        )
        return sums, tally[part]

    if n_dp == 4:
        first = swap(encode(*chunk(3), power, unit), "dp", n_dp, 1)
        near = swap(encode(*chunk(1), power, unit), "dp", n_dp, 1)
        part, count = chunk(2)
        more, more_count, more_power = decode(first, unit)
        far = encode(part + more, count + more_count, jnp.maximum(power, more_power) + 1.0, unit * 0.5)
        far = swap(far, "dp", n_dp, 2)
        owner_total, owner_tally = chunk(0)
        got = [decode(near, unit), decode(far, unit * 0.5)]
    else:
        owner_total, owner_tally = chunk(0)
        got = [
            decode(swap(encode(*chunk(j), power, unit), "dp", n_dp, j), unit)
            for j in range(1, n_dp)
        ]
    for more, more_count, _ in got:
        owner_total = owner_total + more
        owner_tally = owner_tally + more_count
    new_codebook = (owner_total + PRIOR * codebook) / (owner_tally + PRIOR)[:, None]
    return (new_codebook, owner_tally, lognorm[0])


def solution(mesh):
    n_dp, n_cent = mesh.shape["dp"], mesh.shape["cent"]

    def run(embeddings, codebook):
        return local(n_dp, n_cent, embeddings, codebook)

    return jax.shard_map(
        run,
        mesh=mesh,
        in_specs=(P(("dp", "cent"), None), P(("cent", "dp"), None)),
        out_specs=(P(("cent", "dp"), None), P(("cent", "dp")), P(("dp", "cent"))),
        check_vma=False,
    )
```

time: 90.7 us -> 91.8 us (1.012)
  other arithmetic: 5.61 us -> 18.3 us
  starting transfers between devices: 29.4 us -> 18.1 us
  waiting for transfers between devices: 38.6 us -> 29.8 us
  between operations: 1.16 us -> 9.17 us
  matrix products: 6.3 us -> 11.2 us
  local copies, waits for them, and re-layouts: 9.03 us -> 4.58 us
    ppermute x24 -> x17, starting transfers between devices: 29.4 us -> 18.1 us  [swap(): return lax.ppermute(x, axis, [(i, i ^ mask) for i in range(size)])]
    reduce_max x2 -> x8, other arithmetic: 0.21 us -> 9 us  [local(): jnp.max(jnp.abs(b))]
    ppermute x24 -> x17, waiting for transfers between devices: 38.6 us -> 29.8 us  [swap(): return lax.ppermute(x, axis, [(i, i ^ mask) for i in range(size)])]
    dot_general x9 -> x12, matrix products: 6.3 us -> 11.2 us  [the longest x4 7.27 us: chunk(): lax.dot_general(resp[part], gathered, (((1,), (0,)), ((), ())), preferred...]
    unnamed x10 -> x7, other arithmetic: 0.6 us -> 4.94 us
    unnamed x32 -> x33, local copies, waits for them, and re-layouts: 6.77 us -> 2.57 us
    concatenate x1 -> x2, local copies, waits for them, and re-layouts: 1.89 us -> 0.08 us  [the longest x1 0.04 us: join(): jnp.concatenate([other[:, j ^ mask:(j ^ mask) + 1] for j in range(size)],...]
    slice x8 -> x7, local copies, waits for them, and re-layouts: 0.08 us -> 1.63 us  [the longest x3 1.59 us: decode(): power = side[2, 0]]
  transfers between devices with their start and end apart: 24 -> 17, of which waited for: 10 -> 4; matrix products, arithmetic and copies ran while one was open for 10% -> 23% of each run, Pallas kernels for 0% -> 0%
where the time goes in v2:
time: 91.8 us; the launch traced here: 91.3 us
  waiting for transfers between devices  29.8 us (32%)
  other arithmetic  18.3 us (20%)
  starting transfers between devices  18.1 us (20%)
  matrix products  11.2 us (12%)
  between operations  9.17 us (10%)
  local copies, waits for them, and re-layouts  4.58 us (5%)
    ppermute x17, waiting for transfers between devices, swap(): return lax.ppermute(x, axis, [(i, i ^ mask) for i in range(size)])  29.8 us
    ppermute x17, starting transfers between devices, swap(): return lax.ppermute(x, axis, [(i, i ^ mask) for i in range(size)])  18.1 us
    reduce_max x8, other arithmetic, local(): jnp.max(jnp.abs(b))  9 us
    dot_general x4, matrix products, chunk(): lax.dot_general(resp[part], gathered, (((1,), (0,)), ((), ())), preferred...  7.27 us
    unnamed x7, other arithmetic  4.94 us
    dot_general x8, matrix products, score_block(): lax.dot_general(centers, rows, (((1,), (1,)), ((), ())), preferred_elemen...  3.97 us
    unnamed x33, local copies, waits for them, and re-layouts  2.57 us
  transfers between devices with their start and end apart: 17, of which 4 were waited for; matrix products, arithmetic and copies ran while one was open for 23% of the time, Pallas kernels for 0%

profile of v2, /device:TPU:0, one launch (start us, length us, event | category | flops | bytes accessed | tf_op | source)
XLA Modules:
  0.0 91.3 jit_solution(9704818119003334440)
XLA Ops:
  0.6 3.0 %collective-permute-start.4 = (bf16[256,1024]{1,0:T(8,128)(2,1)}, bf16[256,1024]{1,0:T(8,128)(2,1)S(1)}, u32[]{:S(2)}, u32[]{:S(2)}) collective-permute-start(bf16[256,1024]{1,0:T(8,128)(2,1)} %param.2), channel_id=1, source_target_pairs={{0,2},{1,3},{2,0},{3,1},{4,6},{5,7},{6,4},{7,5},{8,10},{9,11},{10,... | collective-permute-start | bytes 1572872 | tf_op jit(solution)/shard_map/ppermute | solution.py:12
  3.6 1.5 %collective-permute-start.6 = (bf16[256,1024]{1,0:T(8,128)(2,1)}, bf16[256,1024]{1,0:T(8,128)(2,1)S(1)}, u32[]{:S(2)}, u32[]{:S(2)}) collective-permute-start(bf16[256,1024]{1,0:T(8,128)(2,1)} %param.2), channel_id=1, source_target_pairs={{0,4},{1,5},{2,6},{3,7},{4,0},{5,1},{6,2},{7,3},{8,12},{9,13},{10,... | collective-permute-start | bytes 1572872 | tf_op jit(solution)/shard_map/ppermute | solution.py:12
  5.2 1.1 %convert_element_type.103 = bf16[128,1024]{1,0:T(8,128)(2,1)S(1)} convert(f32[128,1024]{1,0:T(8,128)} %param.3) | non-fusion elementwise | flops 131072 | bytes 786432 | tf_op jit(solution)/shard_map/convert_element_type | solution.py:77
  6.2 2.7 %collective-permute-start.1 = (bf16[128,1024]{1,0:T(8,128)(2,1)S(1)}, bf16[128,1024]{1,0:T(8,128)(2,1)S(1)}, u32[]{:S(2)}, u32[]{:S(2)}) collective-permute-start(bf16[128,1024]{1,0:T(8,128)(2,1)S(1)} %convert_element_type.103), channel_id=1, source_target_pairs={{0,16},{8,24},{16,0},{24,8},{1,17},{9,25},{17,1},{25,9},{2,18},{10... | collective-permute-start | bytes 786440 | tf_op jit(solution)/shard_map/ppermute | solution.py:12
  8.9 1.6 %collective-permute-start = (bf16[128,1024]{1,0:T(8,128)(2,1)S(1)}, bf16[128,1024]{1,0:T(8,128)(2,1)S(1)}, u32[]{:S(2)}, u32[]{:S(2)}) collective-permute-start(bf16[128,1024]{1,0:T(8,128)(2,1)S(1)} %convert_element_type.103), channel_id=1, source_target_pairs={{0,8},{8,0},{16,24},{24,16},{1,9},{9,1},{17,25},{25,17},{2,10},{10... | collective-permute-start | bytes 786440 | tf_op jit(solution)/shard_map/ppermute | solution.py:12
  10.5 9.9 %collective-permute-done.1 = bf16[128,1024]{1,0:T(8,128)(2,1)S(1)} collective-permute-done((bf16[128,1024]{1,0:T(8,128)(2,1)S(1)}, bf16[128,1024]{1,0:T(8,128)(2,1)S(1)}, u32[]{:S(2)}, u32[]{:S(2)}) %collective-permute-start.1) | collective-permute-done | bytes 262176 | tf_op jit(solution)/shard_map/ppermute | solution.py:12
  21.0 1.9 %abs_reduce_fusion.7 = (bf16[]{:T(256)}, bf16[2048,1024]{1,0:T(8,128)(2,1)S(1)}) fusion(bf16[256,1024]{1,0:T(8,128)(2,1)} %param.2), kind=kLoop, calls=%fused_computation.45 | loop fusion | flops 1048574 | bytes 1048578 | tf_op jit(solution)/shard_map/reduce_max | solution.py:97
  24.1 3.4 %collective-permute-done.2 = bf16[128,1024]{1,0:T(8,128)(2,1)S(1)} collective-permute-done((bf16[128,1024]{1,0:T(8,128)(2,1)S(1)}, bf16[128,1024]{1,0:T(8,128)(2,1)S(1)}, u32[]{:S(2)}, u32[]{:S(2)}) %collective-permute-start.2) | collective-permute-done | bytes 262176 | tf_op jit(solution)/shard_map/ppermute | solution.py:12
  30.8 0.8 abs_reduce_fusion.5
  33.8 0.8 abs_reduce_fusion.2
  35.3 1.3 %copy-done = bf16[2048,1024]{1,0:T(8,128)(2,1)} copy-done((bf16[2048,1024]{1,0:T(8,128)(2,1)}, bf16[2048,1024]{1,0:T(8,128)(2,1)S(1)}, u32[]{:S(2)}) %copy-start) | copy-done | bytes 4194328
  46.1 2.8 %abs_reduce_fusion = (bf16[]{:T(256)}, bf16[2048,1024]{1,0:T(8,128)(2,1)}) fusion(bf16[256,1024]{1,0:T(8,128)(2,1)} %copy-done.13, bf16[2048,1024]{1,0:T(8,128)(2,1)} %copy-done), kind=kLoop, calls=%fused_computation.38 | loop fusion | flops 1048575 | bytes 1049088 | tf_op jit(solution)/shard_map/reduce_max | solution.py:97
  50.0 1.2 %fusion.27 = bf16[512,2048]{1,0:T(8,128)(2,1)S(1)} fusion(bf16[512,2048]{1,0:T(8,128)(2,1)S(1)} %fusion.26, f32[512,256]{1,0:T(8,128)} %copy-done.3, f32[256]{0:T(256)S(1)} %bitcast.193), kind=kLoop, calls=%fused_computation.67 | loop fusion | flops 262144 | bytes 787456
  51.2 1.1 %fusion.28 = bf16[512,2048]{1,0:T(8,128)(2,1)S(1)} fusion(bf16[512,2048]{1,0:T(8,128)(2,1)S(1)} %fusion.27, f32[512,256]{1,0:T(8,128)} %copy-done.6, f32[256]{0:T(256)S(1)} %bitcast.192), kind=kLoop, calls=%fused_computation.68 | loop fusion | flops 262144 | bytes 787456
  52.3 1.1 %fusion.29 = bf16[512,2048]{1,0:T(8,128)(2,1)S(1)} fusion(bf16[512,2048]{1,0:T(8,128)(2,1)S(1)} %fusion.28, f32[512,256]{1,0:T(8,128)} %copy-done.4, f32[256]{0:T(256)S(1)} %bitcast.191), kind=kLoop, calls=%fused_computation.69 | loop fusion | flops 262144 | bytes 787456
  53.5 1.3 %fusion.30 = bf16[512,2048]{1,0:T(8,128)(2,1)S(1)} fusion(bf16[512,2048]{1,0:T(8,128)(2,1)S(1)} %fusion.29, f32[512,256]{1,0:T(8,128)} %copy-done.5, f32[256]{0:T(256)S(1)} %bitcast.190), kind=kLoop, calls=%fused_computation.70 | loop fusion | flops 262144 | bytes 787456
  55.8 0.8 fusion.14
  56.7 1.8 %collective-permute-start.15 = (f16[144,1024]{1,0:T(8,128)(2,1)S(1)}, f16[144,1024]{1,0:T(8,128)(2,1)S(1)}, u32[]{:S(2)}, u32[]{:S(2)}) collective-permute-start(f16[144,1024]{1,0:T(8,128)(2,1)S(1)} %fusion.23), channel_id=1, source_target_pairs={{0,8},{8,0},{16,24},{24,16},{1,9},{9,1},{17,25},{25,17},{2,10},{10... | collective-permute-start | bytes 884744 | tf_op jit(solution)/shard_map/ppermute | solution.py:12
  58.5 0.8 fusion.13
  59.7 7.0 %collective-permute-done.15 = f16[144,1024]{1,0:T(8,128)(2,1)S(1)} collective-permute-done((f16[144,1024]{1,0:T(8,128)(2,1)S(1)}, f16[144,1024]{1,0:T(8,128)(2,1)S(1)}, u32[]{:S(2)}, u32[]{:S(2)}) %collective-permute-start.15) | collective-permute-done | bytes 294944 | tf_op jit(solution)/shard_map/ppermute | solution.py:12
  68.7 3.1 %fusion.12 = f16[128,1024]{1,0:T(8,128)(2,1)S(1)} fusion(bf16[2048,1024]{1,0:T(8,128)(2,1)} %get-tuple-element.10, bf16[512,2048]{1,0:T(8,128)(2,1)S(1)} %fusion.32, f16[144,1024]{1,0:T(8,128)(2,1)} %copy-done.14, f32[]{:T(128)S(6)} %exp2.48, f32[]{:T(128)S(6)} %exp2.46), kind=kOutput, calls=%fused_computation.26 | convolution fusion | flops 537526272 | bytes 5242888 | tf_op jit(solution)/shard_map/dot_general | solution.py:103
  72.0 3.5 %collective-permute-start.16 = (f16[144,1024]{1,0:T(8,128)(2,1)S(1)}, f16[144,1024]{1,0:T(8,128)(2,1)S(1)}, u32[]{:S(2)}, u32[]{:S(2)}) collective-permute-start(f16[144,1024]{1,0:T(8,128)(2,1)S(1)} %fusion.24), channel_id=1, source_target_pairs={{0,16},{8,24},{16,0},{24,8},{1,17},{9,25},{17,1},{25,9},{2,18},{10... | collective-permute-start | bytes 884744 | tf_op jit(solution)/shard_map/ppermute | solution.py:12
  77.4 9.5 %collective-permute-done.16 = f16[144,1024]{1,0:T(8,128)(2,1)S(1)} collective-permute-done((f16[144,1024]{1,0:T(8,128)(2,1)S(1)}, f16[144,1024]{1,0:T(8,128)(2,1)S(1)}, u32[]{:S(2)}, u32[]{:S(2)}) %collective-permute-start.16) | collective-permute-done | bytes 294944 | tf_op jit(solution)/shard_map/ppermute | solution.py:12
  88.6 2.6 %fusion.11 = f32[128,1024]{1,0:T(8,128)} fusion(f32[128,1024]{1,0:T(8,128)S(1)} %copy-done.11, bf16[2048,1024]{1,0:T(8,128)(2,1)S(1)} %copy-done.2, bf16[512,2048]{1,0:T(8,128)(2,1)S(1)} %fusion.32, f16[144,1024]{1,0:T(8,128)(2,1)S(1)} %collective-permute-done.16, f16[144,1024]{1,0:T(8,128)(2,1)} %collective-permute-done.14, f32[128]{0:T(128)S(1)} %get-tuple-element.3, ...), kind=kOutput, calls=%fused_computation.25 | convolution fusion | flops 537919488 | bytes 6291976 | tf_op jit(solution)/shard_map/dot_general | solution.py:103
  (119 shorter events, 17.7 us)
Async XLA Ops:
  0.6 27.2 %copy-start.12 = (bf16[256,1024]{1,0:T(8,128)(2,1)S(1)}, bf16[256,1024]{1,0:T(8,128)(2,1)}, u32[]{:S(2)}) copy-start(bf16[256,1024]{1,0:T(8,128)(2,1)} %param.2) | copy-start | bytes 1572868
  0.6 22.3 %collective-permute-start.4 = (bf16[256,1024]{1,0:T(8,128)(2,1)}, bf16[256,1024]{1,0:T(8,128)(2,1)S(1)}, u32[]{:S(2)}, u32[]{:S(2)}) collective-permute-start(bf16[256,1024]{1,0:T(8,128)(2,1)} %param.2), channel_id=1, source_target_pairs={{0,2},{1,3},{2,0},{3,1},{4,6},{5,7},{6,4},{7,5},{8,10},{9,11},{10,... | collective-permute-start | bytes 1572872 | tf_op jit(solution)/shard_map/ppermute | solution.py:12
  3.6 19.9 %collective-permute-start.6 = (bf16[256,1024]{1,0:T(8,128)(2,1)}, bf16[256,1024]{1,0:T(8,128)(2,1)S(1)}, u32[]{:S(2)}, u32[]{:S(2)}) collective-permute-start(bf16[256,1024]{1,0:T(8,128)(2,1)} %param.2), channel_id=1, source_target_pairs={{0,4},{1,5},{2,6},{3,7},{4,0},{5,1},{6,2},{7,3},{8,12},{9,13},{10,... | collective-permute-start | bytes 1572872 | tf_op jit(solution)/shard_map/ppermute | solution.py:12
  6.2 14.2 %collective-permute-start.1 = (bf16[128,1024]{1,0:T(8,128)(2,1)S(1)}, bf16[128,1024]{1,0:T(8,128)(2,1)S(1)}, u32[]{:S(2)}, u32[]{:S(2)}) collective-permute-start(bf16[128,1024]{1,0:T(8,128)(2,1)S(1)} %convert_element_type.103), channel_id=1, source_target_pairs={{0,16},{8,24},{16,0},{24,8},{1,17},{9,25},{17,1},{25,9},{2,18},{10... | collective-permute-start | bytes 786440 | tf_op jit(solution)/shard_map/ppermute | solution.py:12
  8.9 15.2 %collective-permute-start = (bf16[128,1024]{1,0:T(8,128)(2,1)S(1)}, bf16[128,1024]{1,0:T(8,128)(2,1)S(1)}, u32[]{:S(2)}, u32[]{:S(2)}) collective-permute-start(bf16[128,1024]{1,0:T(8,128)(2,1)S(1)} %convert_element_type.103), channel_id=1, source_target_pairs={{0,8},{8,0},{16,24},{24,16},{1,9},{9,1},{17,25},{25,17},{2,10},{10... | collective-permute-start | bytes 786440 | tf_op jit(solution)/shard_map/ppermute | solution.py:12
  20.4 7.1 %collective-permute-start.2 = (bf16[128,1024]{1,0:T(8,128)(2,1)S(1)}, bf16[128,1024]{1,0:T(8,128)(2,1)S(1)}, u32[]{:S(2)}, u32[]{:S(2)}) collective-permute-start(bf16[128,1024]{1,0:T(8,128)(2,1)S(1)} %collective-permute-done.1), channel_id=1, source_target_pairs={{0,8},{8,0},{16,24},{24,16},{1,9},{9,1},{17,25},{25,17},{2,10},{10... | collective-permute-start | bytes 786440 | tf_op jit(solution)/shard_map/ppermute | solution.py:12
  21.0 7.4 %collective-permute-start.3 = (bf16[256,1024]{1,0:T(8,128)(2,1)}, bf16[256,1024]{1,0:T(8,128)(2,1)S(1)}, u32[]{:S(2)}, u32[]{:S(2)}) collective-permute-start(bf16[256,1024]{1,0:T(8,128)(2,1)} %param.2), channel_id=1, source_target_pairs={{0,1},{1,0},{2,3},{3,2},{4,5},{5,4},{6,7},{7,6},{8,9},{9,8},{10,11... | collective-permute-start | bytes 1572872 | tf_op jit(solution)/shard_map/ppermute | solution.py:12
  22.9 11.6 %collective-permute-start.8 = (bf16[128,1024]{1,0:T(8,128)(2,1)S(1)}, bf16[128,1024]{1,0:T(8,128)(2,1)S(1)}, u32[]{:S(2)}, u32[]{:S(2)}) collective-permute-start(bf16[128,1024]{1,0:T(8,128)(2,1)S(1)} %slice.232), channel_id=1, source_target_pairs={{0,4},{1,5},{2,6},{3,7},{4,0},{5,1},{6,2},{7,3},{8,12},{9,13},{10,... | collective-permute-start | bytes 786440 | tf_op jit(solution)/shard_map/ppermute | solution.py:12
  23.5 11.1 %collective-permute-start.9 = (bf16[128,1024]{1,0:T(8,128)(2,1)S(1)}, bf16[128,1024]{1,0:T(8,128)(2,1)S(1)}, u32[]{:S(2)}, u32[]{:S(2)}) collective-permute-start(bf16[128,1024]{1,0:T(8,128)(2,1)S(1)} %slice.233), channel_id=1, source_target_pairs={{0,2},{1,3},{2,0},{3,1},{4,6},{5,7},{6,4},{7,5},{8,10},{9,11},{10,... | collective-permute-start | bytes 786440 | tf_op jit(solution)/shard_map/ppermute | solution.py:12
  29.1 4.7 %collective-permute-start.7 = (bf16[256,1024]{1,0:T(8,128)(2,1)S(1)}, bf16[256,1024]{1,0:T(8,128)(2,1)S(1)}, u32[]{:S(2)}, u32[]{:S(2)}) collective-permute-start(bf16[256,1024]{1,0:T(8,128)(2,1)S(1)} %collective-permute-done.6), channel_id=1, source_target_pairs={{0,1},{1,0},{2,3},{3,2},{4,5},{5,4},{6,7},{7,6},{8,9},{9,8},{10,11... | collective-permute-start | bytes 1572872 | tf_op jit(solution)/shard_map/ppermute | solution.py:12
  29.1 3.2 %collective-permute-start.5 = (bf16[256,1024]{1,0:T(8,128)(2,1)S(1)}, bf16[256,1024]{1,0:T(8,128)(2,1)S(1)}, u32[]{:S(2)}, u32[]{:S(2)}) collective-permute-start(bf16[256,1024]{1,0:T(8,128)(2,1)S(1)} %collective-permute-done.4), channel_id=1, source_target_pairs={{0,1},{1,0},{2,3},{3,2},{4,5},{5,4},{6,7},{7,6},{8,9},{9,8},{10,11... | collective-permute-start | bytes 1572872 | tf_op jit(solution)/shard_map/ppermute | solution.py:12
  34.7 3.7 %collective-permute-start.10 = (bf16[256,1024]{1,0:T(8,128)(2,1)S(1)}, bf16[256,1024]{1,0:T(8,128)(2,1)S(1)}, u32[]{:S(2)}, u32[]{:S(2)}) collective-permute-start(bf16[256,1024]{1,0:T(8,128)(2,1)S(1)} %get-tuple-element.23), channel_id=1, source_target_pairs={{0,1},{1,0},{2,3},{3,2},{4,5},{5,4},{6,7},{7,6},{8,9},{9,8},{10,11... | collective-permute-start | bytes 1572872 | tf_op jit(solution)/shard_map/ppermute | solution.py:12
  39.2 10.6 %copy-start.9 = (f32[512,256]{1,0:T(8,128)}, f32[512,256]{1,0:T(8,128)S(1)}, u32[]{:S(2)}) copy-start(f32[512,256]{1,0:T(8,128)S(1)} %get-tuple-element.72) | copy-start | bytes 1572868
  39.4 2.2 %collective-permute-start.11 = (f32[2,8,256]{2,1,0:T(8,128)S(1)}, f32[2,8,256]{2,1,0:T(8,128)S(1)}, u32[]{:S(2)}, u32[]{:S(2)}) collective-permute-start(f32[2,8,256]{2,1,0:T(8,128)S(1)} %pad_maximum_fusion.1), channel_id=1, source_target_pairs={{0,1},{1,0},{2,3},{3,2},{4,5},{5,4},{6,7},{7,6},{8,9},{9,8},{10,11... | collective-permute-start | bytes 49160 | tf_op jit(solution)/shard_map/ppermute | solution.py:12
  41.7 3.8 %collective-permute-start.12 = (f32[2,8,256]{2,1,0:T(8,128)S(1)}, f32[2,8,256]{2,1,0:T(8,128)S(1)}, u32[]{:S(2)}, u32[]{:S(2)}) collective-permute-start(f32[2,8,256]{2,1,0:T(8,128)S(1)} %pad_maximum_fusion.2), channel_id=1, source_target_pairs={{0,2},{1,3},{2,0},{3,1},{4,6},{5,7},{6,4},{7,5},{8,10},{9,11},{10,... | collective-permute-start | bytes 49160 | tf_op jit(solution)/shard_map/ppermute | solution.py:12
  45.6 4.1 %collective-permute-start.13 = (f32[2,8,256]{2,1,0:T(8,128)S(1)}, f32[2,8,256]{2,1,0:T(8,128)S(1)}, u32[]{:S(2)}, u32[]{:S(2)}) collective-permute-start(f32[2,8,256]{2,1,0:T(8,128)S(1)} %pad_maximum_fusion.4), channel_id=1, source_target_pairs={{0,4},{1,5},{2,6},{3,7},{4,0},{5,1},{6,2},{7,3},{8,12},{9,13},{10,... | collective-permute-start | bytes 49160 | tf_op jit(solution)/shard_map/ppermute | solution.py:12
  49.8 4.9 %copy-start.15 = (f32[1,256]{1,0:T(1,128)}, f32[1,256]{1,0:T(1,128)S(1)}, u32[]{:S(2)}) copy-start(f32[1,256]{1,0:T(1,128)S(1)} %get-tuple-element.50) | copy-start | bytes 3076
  49.9 4.8 %copy-start.8 = (f32[512,256]{1,0:T(8,128)S(1)}, f32[512,256]{1,0:T(8,128)}, u32[]{:S(2)}) copy-start(f32[512,256]{1,0:T(8,128)} %copy-done.7) | copy-start | bytes 1572868
  50.0 4.8 %copy-start.10 = (f32[512,256]{1,0:T(8,128)S(1)}, f32[512,256]{1,0:T(8,128)}, u32[]{:S(2)}) copy-start(f32[512,256]{1,0:T(8,128)} %copy-done.9) | copy-start | bytes 1572868
  56.7 10.0 %collective-permute-start.15 = (f16[144,1024]{1,0:T(8,128)(2,1)S(1)}, f16[144,1024]{1,0:T(8,128)(2,1)S(1)}, u32[]{:S(2)}, u32[]{:S(2)}) collective-permute-start(f16[144,1024]{1,0:T(8,128)(2,1)S(1)} %fusion.23), channel_id=1, source_target_pairs={{0,8},{8,0},{16,24},{24,16},{1,9},{9,1},{17,25},{25,17},{2,10},{10... | collective-permute-start | bytes 884744 | tf_op jit(solution)/shard_map/ppermute | solution.py:12
  59.3 16.2 %collective-permute-start.14 = (f16[144,1024]{1,0:T(8,128)(2,1)S(1)}, f16[144,1024]{1,0:T(8,128)(2,1)}, u32[]{:S(2)}, u32[]{:S(2)}) collective-permute-start(f16[144,1024]{1,0:T(8,128)(2,1)S(1)} %fusion.22), channel_id=1, source_target_pairs={{0,8},{8,0},{16,24},{24,16},{1,9},{9,1},{17,25},{25,17},{2,10},{10... | collective-permute-start | bytes 884744 | tf_op jit(solution)/shard_map/ppermute | solution.py:12
  68.7 19.9 %copy-start.2 = (bf16[2048,1024]{1,0:T(8,128)(2,1)S(1)}, bf16[2048,1024]{1,0:T(8,128)(2,1)}, u32[]{:S(2)}) copy-start(bf16[2048,1024]{1,0:T(8,128)(2,1)} %get-tuple-element.10) | copy-start | bytes 12582916
  68.7 19.9 %copy-start.11 = (f32[128,1024]{1,0:T(8,128)S(1)}, f32[128,1024]{1,0:T(8,128)}, u32[]{:S(2)}) copy-start(f32[128,1024]{1,0:T(8,128)} %param.3) | copy-start | bytes 1572868
  72.0 14.9 %collective-permute-start.16 = (f16[144,1024]{1,0:T(8,128)(2,1)S(1)}, f16[144,1024]{1,0:T(8,128)(2,1)S(1)}, u32[]{:S(2)}, u32[]{:S(2)}) collective-permute-start(f16[144,1024]{1,0:T(8,128)(2,1)S(1)} %fusion.24), channel_id=1, source_target_pairs={{0,16},{8,24},{16,0},{24,8},{1,17},{9,25},{17,1},{25,9},{2,18},{10... | collective-permute-start | bytes 884744 | tf_op jit(solution)/shard_map/ppermute | solution.py:12
  (9 other events, 14.1 us)

commit v3 on v0

v3 whole, which is shorter than its diff:
```python
import functools

import jax
import jax.numpy as jnp
from jax import lax
from jax.experimental import pallas as pl
from jax.experimental.pallas import tpu as pltpu
from jax.sharding import PartitionSpec as P

TEMPER = 0.8
PRIOR = 1.0
SIDE = 8
VMEM = pl.BlockSpec(memory_space=pltpu.VMEM)


def swap(x, axis, size, mask):
    return lax.ppermute(x, axis, [(i, i ^ mask) for i in range(size)])


def cut(refs, r):
    return [(ref, at) for ref in refs for at in range(0, ref.shape[0], r)]


def score_kernel(n_cent, n_rows, r, *refs):
    cent_refs, row_refs = refs[:n_cent], refs[n_cent : n_cent + n_rows]
    score_ref, top_ref, total_ref = refs[n_cent + n_rows :]
    centers = jnp.concatenate([ref[...] for ref in cent_refs], axis=0)
    half = 0.5 * jnp.sum(jnp.square(centers.astype(jnp.float32)), axis=1, keepdims=True)
    for j, (ref, at) in enumerate(cut(row_refs, r)):
        product = lax.dot_general(
            centers, ref[at : at + r], (((1,), (1,)), ((), ())), preferred_element_type=jnp.float32
        )
        s = (product - half) * (1.0 / TEMPER)
        top = jnp.max(s, axis=0, keepdims=True)
        score_ref[j] = s
        top_ref[j : j + 1] = top
        total_ref[j : j + 1] = jnp.sum(jnp.exp(s - top), axis=0, keepdims=True)


def score(centers, rows, r):
    n_c, n_in = len(centers), len(rows)
    n_r = sum(x.shape[0] for x in rows) // r
    depth = rows[0].shape[1]
    c = n_c * centers[0].shape[0]
    return pl.pallas_call(
        functools.partial(score_kernel, n_c, n_in, r),
        out_shape=(
            jax.ShapeDtypeStruct((n_r, c, r), jnp.float32),
            jax.ShapeDtypeStruct((n_r, r), jnp.float32),
            jax.ShapeDtypeStruct((n_r, r), jnp.float32),
        ),
        in_specs=[VMEM] * (n_c + n_in),
        out_specs=(VMEM,) * 3,
        compiler_params=pltpu.CompilerParams(vmem_limit_bytes=32 << 20),
        cost_estimate=pl.CostEstimate(
            flops=2 * n_r * c * r * depth,
            bytes_accessed=2 * (n_r * r + c) * depth,
            transcendentals=n_r * c * r,
        ),
        name="score_rows",
    )(*centers, *rows)


def sums_kernel(n_parts, n_rows, r, parts, lognorm_ref, *refs):
    score_refs, row_refs = refs[:n_parts], refs[n_parts : n_parts + n_rows]
    outs = refs[n_parts + n_rows :]
    blocks = cut(row_refs, r)
    ones = jnp.ones((SIDE, r), jnp.bfloat16)
    for out, (k, rows_of, first, size, packed) in zip(outs, parts):
        total, tally = None, None
        for j, (row_ref, at) in enumerate(blocks):
            s = score_refs[rows_of[j][0]][rows_of[j][1], first : first + size, :]
            resp = jnp.exp(s - lognorm_ref[j : j + 1]).astype(jnp.bfloat16)
            more = jnp.dot(resp, row_ref[at : at + r], preferred_element_type=jnp.float32)
            count = lax.dot_general(
                ones, resp, (((1,), (1,)), ((), ())), preferred_element_type=jnp.float32
            )
            total = more if total is None else total + more
            tally = count if tally is None else tally + count
        wide = jnp.concatenate(
            [tally, jnp.zeros((SIDE, total.shape[1] - size), jnp.float32)], axis=1
        )
        if packed:
            total, wide = pack(total, wide[0:1], packed)
        out[0:size] = total
        out[size : size + SIDE] = wide


def pack(total, tally, unit):
    peak = jnp.max(jnp.abs(total), axis=0, keepdims=True)
    power = jnp.clip(jnp.ceil(jnp.log2(peak)), -100.0, 100.0)
    high = jnp.floor(tally * unit)
    rest = (tally * unit - high) * 1024.0
    middle = jnp.floor(rest)
    low = (rest - middle) * 1024.0
    blank = jnp.zeros((SIDE - 4, total.shape[1]), jnp.float32)
    return total * jnp.exp2(14.0 - power), jnp.concatenate([power, high, middle, low, blank])


def unpack(message, unit):
    size = message.shape[0] - SIDE
    values = message.astype(jnp.float32)
    power, high, middle, low = (values[size + i : size + i + 1] for i in range(4))
    tally = (high + (middle + low * (1.0 / 1024.0)) * (1.0 / 1024.0)) * (1.0 / unit)
    return values[:size] * jnp.exp2(power - 14.0), tally


def weighted(parts, lognorm, scores, rows):
    size = parts[0][3]
    depth = rows[0].shape[1]
    n_in, n_p = len(rows), len(scores)
    n_r, r = lognorm.shape
    return pl.pallas_call(
        functools.partial(sums_kernel, n_p, n_in, r, parts),
        out_shape=[jax.ShapeDtypeStruct((size + SIDE, depth), jnp.float32) for _ in parts],
        in_specs=[VMEM] * (1 + n_p + n_in),
        out_specs=[VMEM] * len(parts),
        compiler_params=pltpu.CompilerParams(vmem_limit_bytes=32 << 20),
        cost_estimate=pl.CostEstimate(
            flops=2 * len(parts) * n_r * size * r * depth,
            bytes_accessed=2 * n_r * r * depth,
            transcendentals=len(parts) * n_r * size * r,
        ),
        name="weighted_sums",
    )(lognorm, *scores, *rows)


def merge(a, b):
    top = jnp.maximum(a[0], b[0])
    return top, a[1] * jnp.exp(a[0] - top) + b[1] * jnp.exp(b[0] - top)


def join(pairs, mask, order):
    other = swap(jnp.stack(pairs), "cent", len(order), mask)
    places = [order.index(j ^ mask) for j in order]
    other = jnp.concatenate([other[:, p : p + 1] for p in places], axis=1)
    return merge(pairs, other)


def local(n_dp, n_cent, embeddings, codebook):
    own_rows = embeddings.shape[0]
    size = codebook.shape[0]
    n_rows = own_rows * n_cent
    unit = 1024.0 / n_rows
    rounded = codebook.astype(jnp.bfloat16)
    if n_cent == 8:
        half = own_rows // 2
        from_x = swap(embeddings, "cent", n_cent, 2)
        from_y = swap(embeddings, "cent", n_cent, 4)
    if n_dp == 4:
        far = swap(rounded, "dp", n_dp, 2)
        near = swap(rounded, "dp", n_dp, 1)
    if n_cent == 8:
        if n_dp == 4:
            from_x, from_y, near = lax.optimization_barrier((from_x, from_y, near))
        diag_top = swap(from_x[:half], "cent", n_cent, 4)
        diag_low = swap(from_y[half:], "cent", n_cent, 2)
        four = jnp.concatenate([embeddings, from_x, from_y, diag_top, diag_low], axis=0)
        give = lax.optimization_barrier((four, far))[0] if n_dp == 4 else four
        rows, order = [four, swap(give, "cent", n_cent, 1)], [0, 2, 4, 6, 1, 3, 5, 7]
        early, later = 4, 1
    else:
        rows = [embeddings] + [swap(embeddings, "cent", n_cent, m) for m in range(1, n_cent)]
        order = list(range(n_cent))
        early = later = n_cent // 2
    if n_dp == 4:
        give, near = lax.optimization_barrier((far, near))
        centers = [rounded, near, far, swap(give, "dp", n_dp, 1)]
    else:
        centers = [rounded] + [swap(rounded, "dp", n_dp, m) for m in range(1, n_dp)]
    s_a, top_a, total_a = score(centers[:-1], rows[:-later], own_rows)
    s_b, top_b, total_b = score(centers[:-1], rows[-later:], own_rows)
    s_c, top_c, total_c = score(centers[-1:], rows, own_rows)
    pairs = (jnp.concatenate([top_a, top_b]), jnp.concatenate([total_a, total_b]))
    pairs = merge(pairs, (top_c, total_c))
    mask = 1
    while mask < n_cent:
        pairs = join(pairs, mask, order)
        mask *= 2
    lognorm = pairs[0] + jnp.log(pairs[1])

    split = tuple((0, j) if j < early else (1, j - early) for j in range(n_cent))
    whole = tuple((0, j) for j in range(n_cent))

    def part(k, packed):
        return (k, split, k * size, size, packed)

    last = (n_dp - 1, whole, 0, size, unit)
    (first,) = weighted((last,), lognorm, (s_c,), rows)
    first = first.astype(jnp.float16)
    if n_dp == 4:
        first = swap(first, "dp", n_dp, 1)
        far_out, near_out, own = weighted(
            (part(2, 0), part(1, unit), part(0, 0)), lognorm, (s_a, s_b), rows
        )
        more, count = unpack(first, unit)
        total, wide = pack(far_out[:size] + more, far_out[size : size + 1] + count, unit * 0.5)
        far_out = swap(jnp.concatenate([total, wide]).astype(jnp.float16), "dp", n_dp, 2)
        near_in, _ = lax.optimization_barrier((near_out.astype(jnp.float16), first))
        near_out = swap(near_in, "dp", n_dp, 1)
        got = [unpack(near_out, unit), unpack(far_out, unit * 0.5)]
    else:
        out = weighted(
            tuple(part(k, unit if k else 0) for k in range(n_dp - 1)), lognorm, (s_a, s_b), rows
        )
        own = out[0]
        sent = [o.astype(jnp.float16) for o in out[1:]] + [first]
        got = [unpack(swap(m, "dp", n_dp, k + 1), unit) for k, m in enumerate(sent)]
    owner_total, owner_tally = own[:size], own[size, :size]
    for more, count in got:
        owner_total = owner_total + more
        owner_tally = owner_tally + count[0, :size]
    new_codebook = (owner_total + PRIOR * codebook) / (owner_tally + PRIOR)[:, None]
    return (new_codebook, owner_tally, lognorm[0])


def solution(mesh):
    n_dp, n_cent = mesh.shape["dp"], mesh.shape["cent"]

    def run(embeddings, codebook):
        return local(n_dp, n_cent, embeddings, codebook)

    return jax.shard_map(
        run,
        mesh=mesh,
        in_specs=(P(("dp", "cent"), None), P(("cent", "dp"), None)),
        out_specs=(P(("cent", "dp"), None), P(("cent", "dp")), P(("dp", "cent"))),
        check_vma=False,
    )
```

time: 175 us -> 71.2 us (0.41)
  waiting for transfers between devices: 94.8 us -> 37.2 us
  blocking collectives: 37.5 us -> 0 us
  starting transfers between devices: 0.12 us -> 17.2 us
  matrix products: 14 us -> 0 us
  between operations: 14.5 us -> 0.91 us
  other arithmetic: 12.1 us -> 3.17 us
  Pallas kernels: 0 us -> 7.52 us
  local copies, waits for them, and re-layouts: 1.24 us -> 4.92 us
    all_gather x2 -> x0, waiting for transfers between devices: 67.6 us -> none  [the longest x1 36.6 us: local(): gathered = lax.all_gather(embeddings, 'cent', axis=0, tiled=True)]
    ppermute x0 -> x14, waiting for transfers between devices: none -> 37.2 us  [swap(): return lax.ppermute(x, axis, [(i, i ^ mask) for i in range(size)])]
    reduce_scatter x1 -> x0, waiting for transfers between devices: 26.5 us -> none  [local(): lax.psum_scatter(sums, 'dp', scatter_dimension=0, tiled=True)]
    ppermute x0 -> x14, starting transfers between devices: none -> 17.2 us  [swap(): return lax.ppermute(x, axis, [(i, i ^ mask) for i in range(size)])]
    dot_general x2 -> x0, matrix products: 14 us -> none  [the longest x1 7.25 us: local(): lax.dot_general(resp, gathered, (((0,), (0,)), ((), ())), preferred_eleme...]
    pmax x1 -> x0, blocking collectives: 13.3 us -> none  [local(): top_score = lax.pmax(highest, 'cent')]
    unnamed x1 -> x0, blocking collectives: 12.1 us -> none
    psum x1 -> x0, blocking collectives: 12 us -> none  [local(): top_total = lax.psum(summed * jnp.exp(highest - top_score), 'cent')]
  transfers between devices with their start and end apart: 3 -> 14, of which waited for: 3 -> 11; matrix products, arithmetic and copies ran while one was open for 4% -> 4% of each run, Pallas kernels for 0% -> 7%
where the time goes in v3:
time: 71.2 us; the launch traced here: 70.9 us
  waiting for transfers between devices  37.2 us (52%)
  starting transfers between devices  17.2 us (24%)
  Pallas kernels  7.52 us (11%)
  local copies, waits for them, and re-layouts  4.92 us (7%)
  other arithmetic  3.17 us (4%)
  between operations  0.91 us (1%)
    ppermute x14, waiting for transfers between devices, swap(): return lax.ppermute(x, axis, [(i, i ^ mask) for i in range(size)])  37.2 us
    ppermute x14, starting transfers between devices, swap(): return lax.ppermute(x, axis, [(i, i ^ mask) for i in range(size)])  17.2 us
    pallas_call x3, Pallas kernels, score(): pl.pallas_call(functools.partial(score_kernel, n_c, n_in, r), out_shape=(...  4.16 us
    unnamed x18, local copies, waits for them, and re-layouts  4.01 us
    pallas_call x2, Pallas kernels, weighted(): pl.pallas_call(functools.partial(sums_kernel, n_p, n_in, r, parts), out_s...  3.36 us
  transfers between devices with their start and end apart: 14, of which 11 were waited for; matrix products, arithmetic and copies ran while one was open for 4% of the time, Pallas kernels for 7%

profile of v3, /device:TPU:0, one launch (start us, length us, event | category | flops | bytes accessed | tf_op | source)
XLA Modules:
  0.0 70.9 jit_solution(7380624025003411306)
XLA Ops:
  0.6 3.0 %collective-permute-start.1 = (bf16[256,1024]{1,0:T(8,128)(2,1)}, bf16[256,1024]{1,0:T(8,128)(2,1)S(1)}, u32[]{:S(2)}, u32[]{:S(2)}) collective-permute-start(bf16[256,1024]{1,0:T(8,128)(2,1)} %param.2), channel_id=1, source_target_pairs={{0,2},{1,3},{2,0},{3,1},{4,6},{5,7},{6,4},{7,5},{8,10},{9,11},{10,... | collective-permute-start | bytes 1572872 | tf_op jit(solution)/shard_map/ppermute | solution.py:17
  3.6 1.5 %collective-permute-start.2 = (bf16[256,1024]{1,0:T(8,128)(2,1)}, bf16[256,1024]{1,0:T(8,128)(2,1)S(1)}, u32[]{:S(2)}, u32[]{:S(2)}) collective-permute-start(bf16[256,1024]{1,0:T(8,128)(2,1)} %param.2), channel_id=1, source_target_pairs={{0,4},{1,5},{2,6},{3,7},{4,0},{5,1},{6,2},{7,3},{8,12},{9,13},{10,... | collective-permute-start | bytes 1572872 | tf_op jit(solution)/shard_map/ppermute | solution.py:17
  5.2 1.1 %convert_element_type.19.refs_0_ = bf16[128,1024]{1,0:T(8,128)(2,1)S(1)} convert(f32[128,1024]{1,0:T(8,128)} %param.3) | non-fusion elementwise | flops 131072 | bytes 786432 | tf_op jit(solution)/shard_map/convert_element_type | solution.py:145
  6.2 1.6 %collective-permute-start.3 = (bf16[128,1024]{1,0:T(8,128)(2,1)S(1)}, bf16[128,1024]{1,0:T(8,128)(2,1)S(1)}, u32[]{:S(2)}, u32[]{:S(2)}) collective-permute-start(bf16[128,1024]{1,0:T(8,128)(2,1)S(1)} %convert_element_type.19.refs_0_), channel_id=1, source_target_pairs={{0,8},{8,0},{16,24},{24,16},{1,9},{9,1},{17,25},{25,17},{2,10},{10... | collective-permute-start | bytes 786440 | tf_op jit(solution)/shard_map/ppermute | solution.py:17
  7.9 2.6 %collective-permute-start = (bf16[128,1024]{1,0:T(8,128)(2,1)S(1)}, bf16[128,1024]{1,0:T(8,128)(2,1)S(1)}, u32[]{:S(2)}, u32[]{:S(2)}) collective-permute-start(bf16[128,1024]{1,0:T(8,128)(2,1)S(1)} %convert_element_type.19.refs_0_), channel_id=1, source_target_pairs={{0,16},{8,24},{16,0},{24,8},{1,17},{9,25},{17,1},{25,9},{2,18},{10... | collective-permute-start | bytes 786440 | tf_op jit(solution)/shard_map/ppermute | solution.py:17
  10.5 8.8 %collective-permute-done.3.refs_1_ = bf16[128,1024]{1,0:T(8,128)(2,1)S(1)} collective-permute-done((bf16[128,1024]{1,0:T(8,128)(2,1)S(1)}, bf16[128,1024]{1,0:T(8,128)(2,1)S(1)}, u32[]{:S(2)}, u32[]{:S(2)}) %collective-permute-start.3) | collective-permute-done | bytes 262176 | tf_op jit(solution)/shard_map/ppermute | solution.py:17
  19.9 1.1 %constant_dynamic-update-slice_fusion.4 = bf16[1024,1024]{1,0:T(8,128)(2,1)S(1)} fusion(bf16[256,1024]{1,0:T(8,128)(2,1)} %param.2), kind=kLoop, calls=%fused_computation.20 | loop fusion | bytes 1048576
  21.5 4.2 %collective-permute-done.4 = bf16[128,1024]{1,0:T(8,128)(2,1)S(1)} collective-permute-done((bf16[128,1024]{1,0:T(8,128)(2,1)S(1)}, bf16[128,1024]{1,0:T(8,128)(2,1)S(1)}, u32[]{:S(2)}, u32[]{:S(2)}) %collective-permute-start.4) | collective-permute-done | bytes 262176 | tf_op jit(solution)/shard_map/ppermute | solution.py:17
  25.8 1.7 %collective-permute-done.5 = bf16[128,1024]{1,0:T(8,128)(2,1)S(1)} collective-permute-done((bf16[128,1024]{1,0:T(8,128)(2,1)S(1)}, bf16[128,1024]{1,0:T(8,128)(2,1)S(1)}, u32[]{:S(2)}, u32[]{:S(2)}) %collective-permute-start.5) | collective-permute-done | bytes 262176 | tf_op jit(solution)/shard_map/ppermute | solution.py:17
  28.3 1.3 %score_rows.3 = (f32[4,384,256]{2,1,0:T(8,128)S(1)}, f32[4,256]{1,0:T(4,128)S(1)}, f32[4,256]{1,0:T(4,128)S(1)}) custom-call(bf16[128,1024]{1,0:T(8,128)(2,1)S(1)} %convert_element_type.19.refs_0_, bf16[128,1024]{1,0:T(8,128)(2,1)S(1)} %collective-permute-done.3.refs_1_, bf16[128,1024]{1,0:T(8,128)(2,1)S(1)} %collective-permute-done.refs_2_, ...), custom_call_target="tpu_custom_call" | custom-call | flops 805306368 | bytes 2883584 | tf_op jit(solution)/shard_map/score_rows/pallas_call | solution.py:45
  29.6 1.1 %copy-done.2 = f32[4,384,256]{2,1,0:T(8,128)} copy-done((f32[4,384,256]{2,1,0:T(8,128)}, f32[4,384,256]{2,1,0:T(8,128)S(1)}, u32[]{:S(2)}) %copy-start.2) | copy-done | bytes 1572888
  31.7 1.3 %score_rows.4 = (f32[4,384,256]{2,1,0:T(8,128)S(1)}, f32[4,256]{1,0:T(4,128)S(1)}, f32[4,256]{1,0:T(4,128)S(1)}) custom-call(bf16[128,1024]{1,0:T(8,128)(2,1)S(1)} %convert_element_type.19.refs_0_, bf16[128,1024]{1,0:T(8,128)(2,1)S(1)} %collective-permute-done.3.refs_1_, bf16[128,1024]{1,0:T(8,128)(2,1)S(1)} %collective-permute-done.refs_2_, ...), custom_call_target="tpu_custom_call" | custom-call | flops 805306368 | bytes 2883584 | tf_op jit(solution)/shard_map/score_rows/pallas_call | solution.py:45
  33.0 3.3 %collective-permute-done.7.refs_0_ = bf16[128,1024]{1,0:T(8,128)(2,1)S(1)} collective-permute-done((bf16[128,1024]{1,0:T(8,128)(2,1)S(1)}, bf16[128,1024]{1,0:T(8,128)(2,1)S(1)}, u32[]{:S(2)}, u32[]{:S(2)}) %collective-permute-start.7) | collective-permute-done | bytes 262176 | tf_op jit(solution)/shard_map/ppermute | solution.py:17
  36.3 1.6 %score_rows.5 = (f32[8,128,256]{2,1,0:T(8,128)S(1)}, f32[8,256]{1,0:T(8,128)S(1)}, f32[8,256]{1,0:T(8,128)S(1)}) custom-call(bf16[128,1024]{1,0:T(8,128)(2,1)S(1)} %collective-permute-done.7.refs_0_, bf16[1024,1024]{1,0:T(8,128)(2,1)S(1)} %constant_dynamic-update-slice_fusion.refs_3_.refs_1_.refs_2_, ...), custom_call_target="tpu_custom_call" | custom-call | flops 536870912 | bytes 4456448 | tf_op jit(solution)/shard_map/score_rows/pallas_call | solution.py:45
  38.0 1.2 %collective-permute-done.8 = f32[2,8,256]{2,1,0:T(8,128)S(1)} collective-permute-done((f32[2,8,256]{2,1,0:T(8,128)S(1)}, f32[2,8,256]{2,1,0:T(8,128)S(1)}, u32[]{:S(2)}, u32[]{:S(2)}) %collective-permute-start.8) | collective-permute-done | bytes 16416 | tf_op jit(solution)/shard_map/ppermute | solution.py:17
  39.7 3.3 %collective-permute-done.9 = f32[2,8,256]{2,1,0:T(8,128)S(1)} collective-permute-done((f32[2,8,256]{2,1,0:T(8,128)S(1)}, f32[2,8,256]{2,1,0:T(8,128)S(1)}, u32[]{:S(2)}, u32[]{:S(2)}) %collective-permute-start.9) | collective-permute-done | bytes 16416 | tf_op jit(solution)/shard_map/ppermute | solution.py:17
  43.1 1.6 %collective-permute-start.10 = (f32[2,8,256]{2,1,0:T(8,128)S(1)}, f32[2,8,256]{2,1,0:T(8,128)S(1)}, u32[]{:S(2)}, u32[]{:S(2)}) collective-permute-start(f32[2,8,256]{2,1,0:T(8,128)S(1)} %pad_maximum_fusion.2), channel_id=1, source_target_pairs={{0,4},{1,5},{2,6},{3,7},{4,0},{5,1},{6,2},{7,3},{8,12},{9,13},{10,... | collective-permute-start | bytes 49160 | tf_op jit(solution)/shard_map/ppermute | solution.py:17
  44.7 2.2 %collective-permute-done.10 = f32[2,8,256]{2,1,0:T(8,128)S(1)} collective-permute-done((f32[2,8,256]{2,1,0:T(8,128)S(1)}, f32[2,8,256]{2,1,0:T(8,128)S(1)}, u32[]{:S(2)}, u32[]{:S(2)}) %collective-permute-start.10) | collective-permute-done | bytes 16416 | tf_op jit(solution)/shard_map/ppermute | solution.py:17
  47.0 1.6 %copy-done.1 = bf16[1024,1024]{1,0:T(8,128)(2,1)S(1)} copy-done((bf16[1024,1024]{1,0:T(8,128)(2,1)S(1)}, bf16[1024,1024]{1,0:T(8,128)(2,1)}, u32[]{:S(2)}) %copy-start.1) | copy-done | bytes 2097176
  50.4 2.4 %weighted_sums.2 = (f32[136,1024]{1,0:T(8,128)S(1)}, f32[136,1024]{1,0:T(8,128)S(1)}, f32[136,1024]{1,0:T(8,128)S(1)}) custom-call(f32[8,256]{1,0:T(8,128)S(1)} %fusion.10.lognorm_ref, f32[4,384,256]{2,1,0:T(8,128)S(1)} %copy-done.3, f32[4,384,256]{2,1,0:T(8,128)S(1)} %copy-done.5, ...), custom_call_target="tpu_custom_call" | custom-call | flops 1610612736 | bytes 4194304 | tf_op jit(solution)/shard_map/weighted_sums/pallas_call | solution.py:113
  52.9 3.3 %collective-permute-done.11 = f16[136,1024]{1,0:T(8,128)(2,1)S(1)} collective-permute-done((f16[136,1024]{1,0:T(8,128)(2,1)S(1)}, f16[136,1024]{1,0:T(8,128)(2,1)S(1)}, u32[]{:S(2)}, u32[]{:S(2)}) %collective-permute-start.11) | collective-permute-done | bytes 278560 | tf_op jit(solution)/shard_map/ppermute | solution.py:17
  56.7 1.8 %collective-permute-start.13 = (f16[136,1024]{1,0:T(8,128)(2,1)S(1)}, f16[136,1024]{1,0:T(8,128)(2,1)S(1)}, u32[]{:S(2)}, u32[]{:S(2)}) collective-permute-start(f16[136,1024]{1,0:T(8,128)(2,1)S(1)} %concatenate.30), channel_id=1, source_target_pairs={{0,16},{8,24},{16,0},{24,8},{1,17},{9,25},{17,1},{25,9},{2,18},{10... | collective-permute-start | bytes 835592 | tf_op jit(solution)/shard_map/ppermute | solution.py:17
  58.6 1.8 %collective-permute-start.12 = (f16[136,1024]{1,0:T(8,128)(2,1)S(1)}, f16[136,1024]{1,0:T(8,128)(2,1)S(1)}, u32[]{:S(2)}, u32[]{:S(2)}) collective-permute-start(f16[136,1024]{1,0:T(8,128)(2,1)S(1)} %convert_element_type.20), channel_id=1, source_target_pairs={{0,8},{8,0},{16,24},{24,16},{1,9},{9,1},{17,25},{25,17},{2,10},{10... | collective-permute-start | bytes 835592 | tf_op jit(solution)/shard_map/ppermute | solution.py:17
  60.9 8.1 %collective-permute-done.13 = f16[136,1024]{1,0:T(8,128)(2,1)S(1)} collective-permute-done((f16[136,1024]{1,0:T(8,128)(2,1)S(1)}, f16[136,1024]{1,0:T(8,128)(2,1)S(1)}, u32[]{:S(2)}, u32[]{:S(2)}) %collective-permute-start.13) | collective-permute-done | bytes 278560 | tf_op jit(solution)/shard_map/ppermute | solution.py:17
  (61 shorter events, 8.5 us)
Async XLA Ops:
  0.6 18.7 %collective-permute-start.1 = (bf16[256,1024]{1,0:T(8,128)(2,1)}, bf16[256,1024]{1,0:T(8,128)(2,1)S(1)}, u32[]{:S(2)}, u32[]{:S(2)}) collective-permute-start(bf16[256,1024]{1,0:T(8,128)(2,1)} %param.2), channel_id=1, source_target_pairs={{0,2},{1,3},{2,0},{3,1},{4,6},{5,7},{6,4},{7,5},{8,10},{9,11},{10,... | collective-permute-start | bytes 1572872 | tf_op jit(solution)/shard_map/ppermute | solution.py:17
  3.6 15.7 %collective-permute-start.2 = (bf16[256,1024]{1,0:T(8,128)(2,1)}, bf16[256,1024]{1,0:T(8,128)(2,1)S(1)}, u32[]{:S(2)}, u32[]{:S(2)}) collective-permute-start(bf16[256,1024]{1,0:T(8,128)(2,1)} %param.2), channel_id=1, source_target_pairs={{0,4},{1,5},{2,6},{3,7},{4,0},{5,1},{6,2},{7,3},{8,12},{9,13},{10,... | collective-permute-start | bytes 1572872 | tf_op jit(solution)/shard_map/ppermute | solution.py:17
  6.2 13.1 %collective-permute-start.3 = (bf16[128,1024]{1,0:T(8,128)(2,1)S(1)}, bf16[128,1024]{1,0:T(8,128)(2,1)S(1)}, u32[]{:S(2)}, u32[]{:S(2)}) collective-permute-start(bf16[128,1024]{1,0:T(8,128)(2,1)S(1)} %convert_element_type.19.refs_0_), channel_id=1, source_target_pairs={{0,8},{8,0},{16,24},{24,16},{1,9},{9,1},{17,25},{25,17},{2,10},{10... | collective-permute-start | bytes 786440 | tf_op jit(solution)/shard_map/ppermute | solution.py:17
  7.9 19.6 %collective-permute-start = (bf16[128,1024]{1,0:T(8,128)(2,1)S(1)}, bf16[128,1024]{1,0:T(8,128)(2,1)S(1)}, u32[]{:S(2)}, u32[]{:S(2)}) collective-permute-start(bf16[128,1024]{1,0:T(8,128)(2,1)S(1)} %convert_element_type.19.refs_0_), channel_id=1, source_target_pairs={{0,16},{8,24},{16,0},{24,8},{1,17},{9,25},{17,1},{25,9},{2,18},{10... | collective-permute-start | bytes 786440 | tf_op jit(solution)/shard_map/ppermute | solution.py:17
  19.3 6.4 %collective-permute-start.4 = (bf16[128,1024]{1,0:T(8,128)(2,1)S(1)}, bf16[128,1024]{1,0:T(8,128)(2,1)S(1)}, u32[]{:S(2)}, u32[]{:S(2)}) collective-permute-start(bf16[128,1024]{1,0:T(8,128)(2,1)S(1)} %slice.151), channel_id=1, source_target_pairs={{0,4},{1,5},{2,6},{3,7},{4,0},{5,1},{6,2},{7,3},{8,12},{9,13},{10,... | collective-permute-start | bytes 786440 | tf_op jit(solution)/shard_map/ppermute | solution.py:17
  21.0 6.4 %collective-permute-start.5 = (bf16[128,1024]{1,0:T(8,128)(2,1)S(1)}, bf16[128,1024]{1,0:T(8,128)(2,1)S(1)}, u32[]{:S(2)}, u32[]{:S(2)}) collective-permute-start(bf16[128,1024]{1,0:T(8,128)(2,1)S(1)} %slice.152), channel_id=1, source_target_pairs={{0,2},{1,3},{2,0},{3,1},{4,6},{5,7},{6,4},{7,5},{8,10},{9,11},{10,... | collective-permute-start | bytes 786440 | tf_op jit(solution)/shard_map/ppermute | solution.py:17
  27.5 4.2 %collective-permute-start.6 = (bf16[1024,1024]{1,0:T(8,128)(2,1)S(1)}, bf16[1024,1024]{1,0:T(8,128)(2,1)S(1)}, u32[]{:S(2)}, u32[]{:S(2)}) collective-permute-start(bf16[1024,1024]{1,0:T(8,128)(2,1)S(1)} %constant_dynamic-update-slice_fusion.refs_3_.refs_1_.refs_2_), channel_id=1, source_target_pairs={{0,1},{1,0},{2,3},{3,2},{4,5},{5,4},{6,7},{7,6},{8,9},{9,8},{10,11... | collective-permute-start | bytes 6291464 | tf_op jit(solution)/shard_map/ppermute | solution.py:17
  27.5 8.7 %collective-permute-start.7 = (bf16[128,1024]{1,0:T(8,128)(2,1)S(1)}, bf16[128,1024]{1,0:T(8,128)(2,1)S(1)}, u32[]{:S(2)}, u32[]{:S(2)}) collective-permute-start(bf16[128,1024]{1,0:T(8,128)(2,1)S(1)} %collective-permute-done.refs_2_), channel_id=1, source_target_pairs={{0,8},{8,0},{16,24},{24,16},{1,9},{9,1},{17,25},{25,17},{2,10},{10... | collective-permute-start | bytes 786440 | tf_op jit(solution)/shard_map/ppermute | solution.py:17
  29.6 1.2 %copy-start.2 = (f32[4,384,256]{2,1,0:T(8,128)}, f32[4,384,256]{2,1,0:T(8,128)S(1)}, u32[]{:S(2)}) copy-start(f32[4,384,256]{2,1,0:T(8,128)S(1)} %get-tuple-element.34.refs_0_) | copy-start | bytes 4718596
  31.7 6.2 %copy-start = (bf16[1024,1024]{1,0:T(8,128)(2,1)}, bf16[1024,1024]{1,0:T(8,128)(2,1)S(1)}, u32[]{:S(2)}) copy-start(bf16[1024,1024]{1,0:T(8,128)(2,1)S(1)} %collective-permute-done.6.refs_3_.refs_2_) | copy-start | bytes 6291460
  33.0 4.9 %copy-start.4 = (f32[4,384,256]{2,1,0:T(8,128)}, f32[4,384,256]{2,1,0:T(8,128)S(1)}, u32[]{:S(2)}) copy-start(f32[4,384,256]{2,1,0:T(8,128)S(1)} %get-tuple-element.35.refs_1_) | copy-start | bytes 4718596
  37.9 1.2 %collective-permute-start.8 = (f32[2,8,256]{2,1,0:T(8,128)S(1)}, f32[2,8,256]{2,1,0:T(8,128)S(1)}, u32[]{:S(2)}, u32[]{:S(2)}) collective-permute-start(f32[2,8,256]{2,1,0:T(8,128)S(1)} %pad_maximum_fusion), channel_id=1, source_target_pairs={{0,1},{1,0},{2,3},{3,2},{4,5},{5,4},{6,7},{7,6},{8,9},{9,8},{10,11... | collective-permute-start | bytes 49160 | tf_op jit(solution)/shard_map/ppermute | solution.py:17
  39.2 3.8 %collective-permute-start.9 = (f32[2,8,256]{2,1,0:T(8,128)S(1)}, f32[2,8,256]{2,1,0:T(8,128)S(1)}, u32[]{:S(2)}, u32[]{:S(2)}) collective-permute-start(f32[2,8,256]{2,1,0:T(8,128)S(1)} %pad_maximum_fusion.1), channel_id=1, source_target_pairs={{0,2},{1,3},{2,0},{3,1},{4,6},{5,7},{6,4},{7,5},{8,10},{9,11},{10,... | collective-permute-start | bytes 49160 | tf_op jit(solution)/shard_map/ppermute | solution.py:17
  43.1 3.8 %collective-permute-start.10 = (f32[2,8,256]{2,1,0:T(8,128)S(1)}, f32[2,8,256]{2,1,0:T(8,128)S(1)}, u32[]{:S(2)}, u32[]{:S(2)}) collective-permute-start(f32[2,8,256]{2,1,0:T(8,128)S(1)} %pad_maximum_fusion.2), channel_id=1, source_target_pairs={{0,4},{1,5},{2,6},{3,7},{4,0},{5,1},{6,2},{7,3},{8,12},{9,13},{10,... | collective-permute-start | bytes 49160 | tf_op jit(solution)/shard_map/ppermute | solution.py:17
  47.0 1.6 %copy-start.1 = (bf16[1024,1024]{1,0:T(8,128)(2,1)S(1)}, bf16[1024,1024]{1,0:T(8,128)(2,1)}, u32[]{:S(2)}) copy-start(bf16[1024,1024]{1,0:T(8,128)(2,1)} %copy-done) | copy-start | bytes 6291460
  48.6 1.8 %copy-start.3 = (f32[4,384,256]{2,1,0:T(8,128)S(1)}, f32[4,384,256]{2,1,0:T(8,128)}, u32[]{:S(2)}) copy-start(f32[4,384,256]{2,1,0:T(8,128)} %copy-done.2) | copy-start | bytes 4718596
  48.6 1.9 %copy-start.5 = (f32[4,384,256]{2,1,0:T(8,128)S(1)}, f32[4,384,256]{2,1,0:T(8,128)}, u32[]{:S(2)}) copy-start(f32[4,384,256]{2,1,0:T(8,128)} %copy-done.4) | copy-start | bytes 4718596
  49.5 6.6 %collective-permute-start.11 = (f16[136,1024]{1,0:T(8,128)(2,1)S(1)}, f16[136,1024]{1,0:T(8,128)(2,1)S(1)}, u32[]{:S(2)}, u32[]{:S(2)}) collective-permute-start(f16[136,1024]{1,0:T(8,128)(2,1)S(1)} %convert_element_type.21), channel_id=1, source_target_pairs={{0,8},{8,0},{16,24},{24,16},{1,9},{9,1},{17,25},{25,17},{2,10},{10... | collective-permute-start | bytes 835592 | tf_op jit(solution)/shard_map/ppermute | solution.py:17
  56.3 13.6 %copy-start.6 = (f32[128,1024]{1,0:T(8,128)S(1)}, f32[128,1024]{1,0:T(8,128)}, u32[]{:S(2)}) copy-start(f32[128,1024]{1,0:T(8,128)} %param.3) | copy-start | bytes 1572868
  56.7 12.4 %collective-permute-start.13 = (f16[136,1024]{1,0:T(8,128)(2,1)S(1)}, f16[136,1024]{1,0:T(8,128)(2,1)S(1)}, u32[]{:S(2)}, u32[]{:S(2)}) collective-permute-start(f16[136,1024]{1,0:T(8,128)(2,1)S(1)} %concatenate.30), channel_id=1, source_target_pairs={{0,16},{8,24},{16,0},{24,8},{1,17},{9,25},{17,1},{25,9},{2,18},{10... | collective-permute-start | bytes 835592 | tf_op jit(solution)/shard_map/ppermute | solution.py:17
  58.6 10.8 %collective-permute-start.12 = (f16[136,1024]{1,0:T(8,128)(2,1)S(1)}, f16[136,1024]{1,0:T(8,128)(2,1)S(1)}, u32[]{:S(2)}, u32[]{:S(2)}) collective-permute-start(f16[136,1024]{1,0:T(8,128)(2,1)S(1)} %convert_element_type.20), channel_id=1, source_target_pairs={{0,8},{8,0},{16,24},{24,16},{1,9},{9,1},{17,25},{25,17},{2,10},{10... | collective-permute-start | bytes 835592 | tf_op jit(solution)/shard_map/ppermute | solution.py:17

commit v4 on v3

v4 whole, which is shorter than its diff:
```python
import functools

import jax
import jax.numpy as jnp
from jax import lax
from jax.experimental import pallas as pl
from jax.experimental.pallas import tpu as pltpu
from jax.sharding import PartitionSpec as P

TEMPER = 0.8
PRIOR = 1.0
SIDE = 8
VMEM = pl.BlockSpec(memory_space=pltpu.VMEM)
PARAMS = pltpu.CompilerParams(vmem_limit_bytes=24 << 20)


def swap(x, axis, size, mask):
    return lax.ppermute(x, axis, [(i, i ^ mask) for i in range(size)])


def merge(a, b):
    top = jnp.maximum(a[0], b[0])
    return top, a[1] * jnp.exp(a[0] - top) + b[1] * jnp.exp(b[0] - top)


def score_kernel(n_cent, n_rows, picks, begin, starts, *refs):
    cent_refs, row_refs = refs[:n_cent], refs[n_cent : n_cent + n_rows]
    early_refs = refs[n_cent + n_rows : -2]
    score_ref, pair_ref = refs[-2:]
    r = score_ref.shape[2]
    centers = jnp.concatenate([ref[...] for ref in cent_refs], axis=0)
    half = 0.5 * jnp.sum(jnp.square(centers.astype(jnp.float32)), axis=1, keepdims=True)
    for j, (i, at) in enumerate(picks):
        product = lax.dot_general(
            centers,
            row_refs[i][at : at + r],
            (((1,), (1,)), ((), ())),
            preferred_element_type=jnp.float32,
        )
        s = (product - half) * (1.0 / TEMPER)
        top = jnp.max(s, axis=0, keepdims=True)
        score_ref[j] = s
        total = jnp.sum(jnp.exp(s - top), axis=0, keepdims=True)
        at = begin + j
        for ref, start in zip(early_refs, starts):
            if start <= at < start + ref.shape[1]:
                k = slice(at - start, at - start + 1)
                top, total = merge((top, total), (ref[0, k], ref[1, k]))
        pair_ref[0, at : at + 1] = top
        pair_ref[1, at : at + 1] = total
    for ref, start in zip(early_refs, starts):
        for k in range(ref.shape[1]):
            if not begin <= start + k < begin + len(picks):
                pair_ref[:, start + k : start + k + 1] = ref[:, k : k + 1]


def score(centers, rows, r, picks, early=(), begin=0):
    n_c, n_r = len(centers), len(picks)
    depth = rows[0].shape[1]
    c = n_c * centers[0].shape[0]
    starts = [sum(e.shape[1] for e in early[:i]) for i in range(len(early))]
    n_out = max(begin + n_r, sum(e.shape[1] for e in early))
    return pl.pallas_call(
        functools.partial(score_kernel, n_c, len(rows), picks, begin, starts),
        out_shape=(
            jax.ShapeDtypeStruct((n_r, c, r), jnp.float32),
            jax.ShapeDtypeStruct((2, n_out, r), jnp.float32),
        ),
        in_specs=[VMEM] * (n_c + len(rows) + len(early)),
        out_specs=(VMEM,) * 2,
        compiler_params=PARAMS,
        cost_estimate=pl.CostEstimate(
            flops=2 * n_r * c * r * depth,
            bytes_accessed=2 * (n_r * r + c) * depth,
            transcendentals=n_r * c * r,
        ),
        name="score_rows",
    )(*centers, *rows, *early)


def join_kernel(places, last, pair_ref, other_ref, out_ref):
    other = [jnp.concatenate([other_ref[i, p : p + 1] for p in places]) for i in range(2)]
    top, total = merge((pair_ref[0], pair_ref[1]), other)
    if last:
        out_ref[...] = top + jnp.log(total)
    else:
        out_ref[0] = top
        out_ref[1] = total


def join(pairs, mask, order, last):
    other = swap(pairs, "cent", len(order), mask)
    places = [order.index(j ^ mask) for j in order]
    return pl.pallas_call(
        functools.partial(join_kernel, places, last),
        out_shape=jax.ShapeDtypeStruct(pairs.shape[1:] if last else pairs.shape, jnp.float32),
        in_specs=[VMEM] * 2,
        out_specs=VMEM,
        compiler_params=PARAMS,
        name="join_rows",
    )(pairs, other)


def sums_kernel(n_parts, picks, parts, lognorm_ref, *refs):
    score_refs, row_refs = refs[:n_parts], refs[n_parts : -len(parts)]
    outs = refs[-len(parts) :]
    r = lognorm_ref.shape[1]
    ones = jnp.ones((SIDE, r), jnp.bfloat16)
    for out, (places, size, unit) in zip(outs, parts):
        total, tally = None, None
        for j, (i, at) in enumerate(picks):
            k, block, first = places[j]
            s = score_refs[k][block, first : first + size, :]
            resp = jnp.exp(s - lognorm_ref[j : j + 1]).astype(jnp.bfloat16)
            more = jnp.dot(resp, row_refs[i][at : at + r], preferred_element_type=jnp.float32)
            count = lax.dot_general(
                ones, resp, (((1,), (1,)), ((), ())), preferred_element_type=jnp.float32
            )
            total = more if total is None else total + more
            tally = count if tally is None else tally + count
        wide = jnp.concatenate(
            [tally, jnp.zeros((SIDE, total.shape[1] - size), jnp.float32)], axis=1
        )
        if unit:
            total, wide = pack(total, wide[0:1], unit)
        out[0:size] = total
        out[size : size + SIDE] = wide


def pack(total, tally, unit):
    peak = jnp.max(jnp.abs(total), axis=0, keepdims=True)
    power = jnp.clip(jnp.ceil(jnp.log2(peak)), -100.0, 100.0)
    high = jnp.floor(tally * unit)
    rest = (tally * unit - high) * 1024.0
    middle = jnp.floor(rest)
    low = (rest - middle) * 1024.0
    blank = jnp.zeros((SIDE - 4, total.shape[1]), jnp.float32)
    return total * jnp.exp2(14.0 - power), jnp.concatenate([power, high, middle, low, blank])


def unpack(values, unit):
    size = values.shape[0] - SIDE
    power, high, middle, low = (values[size + i : size + i + 1] for i in range(4))
    tally = (high + (middle + low * (1.0 / 1024.0)) * (1.0 / 1024.0)) * (1.0 / unit)
    return values[:size] * jnp.exp2(power - 14.0), tally


def relay_kernel(unit, own_ref, got_ref, out_ref):
    size = own_ref.shape[0] - SIDE
    more, count = unpack(got_ref[...], unit)
    total, wide = pack(own_ref[0:size] + more, own_ref[size : size + 1] + count, unit * 0.5)
    out_ref[0:size] = total
    out_ref[size : size + SIDE] = wide


def relay(own, got, unit):
    return pl.pallas_call(
        functools.partial(relay_kernel, unit),
        out_shape=jax.ShapeDtypeStruct(own.shape, jnp.float32),
        in_specs=[VMEM] * 2,
        out_specs=VMEM,
        compiler_params=PARAMS,
        name="relay_sums",
    )(own, got)


def weighted(parts, lognorm, scores, rows, picks):
    size = parts[0][1]
    depth = rows[0].shape[1]
    n_r, r = lognorm.shape
    return pl.pallas_call(
        functools.partial(sums_kernel, len(scores), picks, parts),
        out_shape=[jax.ShapeDtypeStruct((size + SIDE, depth), jnp.float32) for _ in parts],
        in_specs=[VMEM] * (1 + len(scores) + len(rows)),
        out_specs=[VMEM] * len(parts),
        compiler_params=PARAMS,
        cost_estimate=pl.CostEstimate(
            flops=2 * len(parts) * n_r * size * r * depth,
            bytes_accessed=2 * n_r * r * depth,
            transcendentals=len(parts) * n_r * size * r,
        ),
        name="weighted_sums",
    )(lognorm, *scores, *rows)


def local(n_dp, n_cent, embeddings, codebook):
    own_rows = embeddings.shape[0]
    size = codebook.shape[0]
    unit = 1024.0 / (own_rows * n_cent)
    rounded = codebook.astype(jnp.bfloat16)
    if n_cent == 8:
        half = own_rows // 2
        from_x = swap(embeddings, "cent", n_cent, 2)
        from_y = swap(embeddings, "cent", n_cent, 4)
    if n_dp == 4:
        far = swap(rounded, "dp", n_dp, 2)
        near = swap(rounded, "dp", n_dp, 1)
        centers = [rounded, near, far, swap(far, "dp", n_dp, 1)]
    else:
        centers = [rounded] + [swap(rounded, "dp", n_dp, m) for m in range(1, n_dp)]
    if n_cent == 8:
        diag_top = swap(from_x[:half], "cent", n_cent, 4)
        diag_low = swap(from_y[half:], "cent", n_cent, 2)
        s_0, pair_0 = score(
            centers[:-1], [embeddings, from_x, from_y], own_rows, [(0, 0), (1, 0), (2, 0)]
        )
        diag_top, diag_low, s_0, pair_0 = lax.optimization_barrier(
            (diag_top, diag_low, s_0, pair_0)
        )
        four = jnp.concatenate([embeddings, from_x, from_y, diag_top, diag_low], axis=0)
        rows, order = [four, swap(four, "cent", n_cent, 1)], [0, 2, 4, 6, 1, 3, 5, 7]
        picks = [(i, j * own_rows) for i in range(2) for j in range(4)]
        rows[0], centers[-1] = lax.optimization_barrier((four, centers[-1]))
        s_1, pair_1 = score(centers[:-1], rows[:1], own_rows, [(0, 3 * own_rows)])
        s_2, pairs = score(centers[-1:], rows[:1], own_rows, picks[:4], [pair_0, pair_1])
        four_core, s_2, pairs = lax.optimization_barrier((rows[1], s_2, pairs))
        rows[1] = four_core
        s_3, pairs = score(centers, rows[1:], own_rows, picks[:4], [pairs], 4)
        scores = [s_0, s_1, s_3]
        places = [(0, 0), (0, 1), (0, 2), (1, 0), (2, 0), (2, 1), (2, 2), (2, 3)]
        last_scores = [s_2, s_3]
        last_places = [(0, j, 0) for j in range(4)] + [(1, j, (n_dp - 1) * size) for j in range(4)]
    else:
        rows = [embeddings] + [swap(embeddings, "cent", n_cent, m) for m in range(1, n_cent)]
        order = list(range(n_cent))
        picks = [(j, 0) for j in order]
        s_0, pair_0 = score(centers[:-1], rows, own_rows, picks)
        scores = [s_0]
        places = [(0, j) for j in order]
        s_1, pairs = score(centers[-1:], rows, own_rows, picks, [pair_0])
        last_scores, last_places = [s_1], [(0, j, 0) for j in order]
    mask = 1
    while mask < n_cent:
        pairs = join(pairs, mask, order, 2 * mask >= n_cent)
        mask *= 2
    lognorm = pairs

    def part(k, unit):
        return [(i, j, k * size) for i, j in places], size, unit

    (first,) = weighted([(last_places, size, unit)], lognorm, last_scores, rows, picks)
    first = first.astype(jnp.float16)
    if n_dp == 4:
        first = swap(first, "dp", n_dp, 1)
        parts = [part(2, 0), part(1, unit), part(0, 0)]
        far_out, near_out, own = weighted(parts, lognorm, scores, rows, picks)
        far_out = relay(far_out, first.astype(jnp.float32), unit)
        far_out, near_out = lax.optimization_barrier((far_out, near_out))
        far_out = swap(far_out.astype(jnp.float16), "dp", n_dp, 2)
        near_out = swap(near_out.astype(jnp.float16), "dp", n_dp, 1)
        got = [(near_out, unit), (far_out, unit * 0.5)]
    else:
        parts = [part(k, unit if k else 0) for k in range(n_dp - 1)]
        out = weighted(parts, lognorm, scores, rows, picks)
        own = out[0]
        sent = [o.astype(jnp.float16) for o in out[1:]] + [first]
        got = [(swap(m, "dp", n_dp, k + 1), unit) for k, m in enumerate(sent)]
    owner_total, owner_tally = own[:size], own[size, :size]
    for message, of in got:
        more, count = unpack(message.astype(jnp.float32), of)
        owner_total = owner_total + more
        owner_tally = owner_tally + count[0, :size]
    new_codebook = (owner_total + PRIOR * codebook) / (owner_tally + PRIOR)[:, None]
    return (new_codebook, owner_tally, lognorm[0])


def solution(mesh):
    n_dp, n_cent = mesh.shape["dp"], mesh.shape["cent"]

    def run(embeddings, codebook):
        return local(n_dp, n_cent, embeddings, codebook)

    return jax.shard_map(
        run,
        mesh=mesh,
        in_specs=(P(("dp", "cent"), None), P(("cent", "dp"), None)),
        out_specs=(P(("cent", "dp"), None), P(("cent", "dp")), P(("dp", "cent"))),
        check_vma=False,
    )
```

time: 71.2 us -> 68 us (0.955)
  starting transfers between devices: 17.2 us -> 22.7 us
  waiting for transfers between devices: 37.2 us -> 31.9 us
  local copies, waits for them, and re-layouts: 4.92 us -> 1.79 us
    ppermute x14, starting transfers between devices: 17.2 us -> 22.7 us  [swap(): return lax.ppermute(x, axis, [(i, i ^ mask) for i in range(size)])]
    ppermute x14, waiting for transfers between devices: 37.2 us -> 31.9 us  [swap(): return lax.ppermute(x, axis, [(i, i ^ mask) for i in range(size)])]
    unnamed x18 -> x8, local copies, waits for them, and re-layouts: 4.01 us -> 1.18 us
    pallas_call x5 -> x10, Pallas kernels: 7.52 us -> 7.69 us  [the longest x4 4.11 us: score(): pl.pallas_call(functools.partial(score_kernel, n_c, len(rows), picks, beg...]
  transfers between devices with their start and end apart: 14 -> 14, of which waited for: 11 -> 12; matrix products, arithmetic and copies ran while one was open for 4% -> 4% of each run, Pallas kernels for 7% -> 7%
where the time goes in v4:
time: 68 us; the launch traced here: 67.8 us
  waiting for transfers between devices  31.9 us (47%)
  starting transfers between devices  22.7 us (33%)
  Pallas kernels  7.69 us (11%)
  other arithmetic  2.87 us (4%)
  local copies, waits for them, and re-layouts  1.79 us (3%)
  between operations  0.82 us (1%)
    ppermute x14, waiting for transfers between devices, swap(): return lax.ppermute(x, axis, [(i, i ^ mask) for i in range(size)])  31.9 us
    ppermute x14, starting transfers between devices, swap(): return lax.ppermute(x, axis, [(i, i ^ mask) for i in range(size)])  22.7 us
    pallas_call x4, Pallas kernels, score(): pl.pallas_call(functools.partial(score_kernel, n_c, len(rows), picks, beg...  4.11 us
    pallas_call x2, Pallas kernels, weighted(): pl.pallas_call(functools.partial(sums_kernel, len(scores), picks, parts),...  3.39 us
  transfers between devices with their start and end apart: 14, of which 12 were waited for; matrix products, arithmetic and copies ran while one was open for 4% of the time, Pallas kernels for 7%

profile of v4, /device:TPU:0, one launch (start us, length us, event | category | flops | bytes accessed | tf_op | source)
XLA Modules:
  0.0 67.8 jit_solution(18266825422214351069)
XLA Ops:
  0.6 3.0 %collective-permute-start.2 = (bf16[256,1024]{1,0:T(8,128)(2,1)}, bf16[256,1024]{1,0:T(8,128)(2,1)S(1)}, u32[]{:S(2)}, u32[]{:S(2)}) collective-permute-start(bf16[256,1024]{1,0:T(8,128)(2,1)} %refs_3_.1), channel_id=1, source_target_pairs={{0,2},{1,3},{2,0},{3,1},{4,6},{5,7},{6,4},{7,5},{8,10},{9,11},{10,... | collective-permute-start | bytes 1572872 | tf_op jit(solution)/shard_map/ppermute | solution.py:18
  3.6 1.5 %collective-permute-start.3 = (bf16[256,1024]{1,0:T(8,128)(2,1)}, bf16[256,1024]{1,0:T(8,128)(2,1)S(1)}, u32[]{:S(2)}, u32[]{:S(2)}) collective-permute-start(bf16[256,1024]{1,0:T(8,128)(2,1)} %refs_3_.1), channel_id=1, source_target_pairs={{0,4},{1,5},{2,6},{3,7},{4,0},{5,1},{6,2},{7,3},{8,12},{9,13},{10,... | collective-permute-start | bytes 1572872 | tf_op jit(solution)/shard_map/ppermute | solution.py:18
  6.2 1.6 %collective-permute-start = (bf16[128,1024]{1,0:T(8,128)(2,1)S(1)}, bf16[128,1024]{1,0:T(8,128)(2,1)S(1)}, u32[]{:S(2)}, u32[]{:S(2)}) collective-permute-start(bf16[128,1024]{1,0:T(8,128)(2,1)S(1)} %convert_element_type.21.refs_0_), channel_id=1, source_target_pairs={{0,8},{8,0},{16,24},{24,16},{1,9},{9,1},{17,25},{25,17},{2,10},{10... | collective-permute-start | bytes 786440 | tf_op jit(solution)/shard_map/ppermute | solution.py:18
  7.9 2.6 %collective-permute-start.1 = (bf16[128,1024]{1,0:T(8,128)(2,1)S(1)}, bf16[128,1024]{1,0:T(8,128)(2,1)S(1)}, u32[]{:S(2)}, u32[]{:S(2)}) collective-permute-start(bf16[128,1024]{1,0:T(8,128)(2,1)S(1)} %convert_element_type.21.refs_0_), channel_id=1, source_target_pairs={{0,16},{8,24},{16,0},{24,8},{1,17},{9,25},{17,1},{25,9},{2,18},{10... | collective-permute-start | bytes 786440 | tf_op jit(solution)/shard_map/ppermute | solution.py:18
  10.5 1.1 %constant_dynamic-update-slice_fusion.4 = bf16[1024,1024]{1,0:T(8,128)(2,1)S(1)} fusion(bf16[256,1024]{1,0:T(8,128)(2,1)} %refs_3_.1), kind=kLoop, calls=%fused_computation.10 | loop fusion | bytes 1048576
  11.6 4.2 %collective-permute-done.2.refs_4_ = bf16[256,1024]{1,0:T(8,128)(2,1)S(1)} collective-permute-done((bf16[256,1024]{1,0:T(8,128)(2,1)}, bf16[256,1024]{1,0:T(8,128)(2,1)S(1)}, u32[]{:S(2)}, u32[]{:S(2)}) %collective-permute-start.2) | collective-permute-done | bytes 524320 | tf_op jit(solution)/shard_map/ppermute | solution.py:18
  15.8 1.8 %collective-permute-start.4 = (bf16[128,1024]{1,0:T(8,128)(2,1)S(1)}, bf16[128,1024]{1,0:T(8,128)(2,1)S(1)}, u32[]{:S(2)}, u32[]{:S(2)}) collective-permute-start(bf16[128,1024]{1,0:T(8,128)(2,1)S(1)} %slice.68), channel_id=1, source_target_pairs={{0,4},{1,5},{2,6},{3,7},{4,0},{5,1},{6,2},{7,3},{8,12},{9,13},{10,... | collective-permute-start | bytes 786440 | tf_op jit(solution)/shard_map/ppermute | solution.py:18
  17.7 1.6 %collective-permute-start.5 = (bf16[128,1024]{1,0:T(8,128)(2,1)S(1)}, bf16[128,1024]{1,0:T(8,128)(2,1)S(1)}, u32[]{:S(2)}, u32[]{:S(2)}) collective-permute-start(bf16[128,1024]{1,0:T(8,128)(2,1)S(1)} %slice.69), channel_id=1, source_target_pairs={{0,2},{1,3},{2,0},{3,1},{4,6},{5,7},{6,4},{7,5},{8,10},{9,11},{10,... | collective-permute-start | bytes 786440 | tf_op jit(solution)/shard_map/ppermute | solution.py:18
  19.3 2.4 %collective-permute-done.1.refs_2_ = bf16[128,1024]{1,0:T(8,128)(2,1)S(1)} collective-permute-done((bf16[128,1024]{1,0:T(8,128)(2,1)S(1)}, bf16[128,1024]{1,0:T(8,128)(2,1)S(1)}, u32[]{:S(2)}, u32[]{:S(2)}) %collective-permute-start.1) | collective-permute-done | bytes 262176 | tf_op jit(solution)/shard_map/ppermute | solution.py:18
  23.4 1.3 %collective-permute-done.5 = bf16[128,1024]{1,0:T(8,128)(2,1)S(1)} collective-permute-done((bf16[128,1024]{1,0:T(8,128)(2,1)S(1)}, bf16[128,1024]{1,0:T(8,128)(2,1)S(1)}, u32[]{:S(2)}, u32[]{:S(2)}) %collective-permute-start.5) | collective-permute-done | bytes 262176 | tf_op jit(solution)/shard_map/ppermute | solution.py:18
  24.7 1.6 %collective-permute-start.6 = (bf16[128,1024]{1,0:T(8,128)(2,1)S(1)}, bf16[128,1024]{1,0:T(8,128)(2,1)S(1)}, u32[]{:S(2)}, u32[]{:S(2)}) collective-permute-start(bf16[128,1024]{1,0:T(8,128)(2,1)S(1)} %collective-permute-done.1.refs_2_), channel_id=1, source_target_pairs={{0,8},{8,0},{16,24},{24,16},{1,9},{9,1},{17,25},{25,17},{2,10},{10... | collective-permute-start | bytes 786440 | tf_op jit(solution)/shard_map/ppermute | solution.py:18
  26.4 7.1 %collective-permute-done.6.refs_0_.refs_3_ = bf16[128,1024]{1,0:T(8,128)(2,1)S(1)} collective-permute-done((bf16[128,1024]{1,0:T(8,128)(2,1)S(1)}, bf16[128,1024]{1,0:T(8,128)(2,1)S(1)}, u32[]{:S(2)}, u32[]{:S(2)}) %collective-permute-start.6) | collective-permute-done | bytes 262176 | tf_op jit(solution)/shard_map/ppermute | solution.py:18
  34.9 1.7 %score_rows.7 = (f32[4,512,256]{2,1,0:T(8,128)S(1)}, f32[2,8,256]{2,1,0:T(8,128)S(1)}) custom-call(bf16[128,1024]{1,0:T(8,128)(2,1)S(1)} %convert_element_type.21.refs_0_, bf16[128,1024]{1,0:T(8,128)(2,1)S(1)} %collective-permute-done.refs_1_, bf16[128,1024]{1,0:T(8,128)(2,1)S(1)} %collective-permute-done.1.refs_2_, ...), custom_call_target="tpu_custom_call" | custom-call | flops 1073741824 | bytes 3145728 | tf_op jit(solution)/shard_map/score_rows/pallas_call | solution.py:63
  36.7 1.2 %collective-permute-done.8.other_ref = f32[2,8,256]{2,1,0:T(8,128)S(1)} collective-permute-done((f32[2,8,256]{2,1,0:T(8,128)S(1)}, f32[2,8,256]{2,1,0:T(8,128)S(1)}, u32[]{:S(2)}, u32[]{:S(2)}) %collective-permute-start.8) | collective-permute-done | bytes 16416 | tf_op jit(solution)/shard_map/ppermute | solution.py:18
  37.8 1.5 %collective-permute-start.9 = (f32[2,8,256]{2,1,0:T(8,128)S(1)}, f32[2,8,256]{2,1,0:T(8,128)S(1)}, u32[]{:S(2)}, u32[]{:S(2)}) collective-permute-start(f32[2,8,256]{2,1,0:T(8,128)S(1)} %join_rows.3.pair_ref), channel_id=1, source_target_pairs={{0,2},{1,3},{2,0},{3,1},{4,6},{5,7},{6,4},{7,5},{8,10},{9,11},{10,... | collective-permute-start | bytes 49160 | tf_op jit(solution)/shard_map/ppermute | solution.py:18
  39.4 2.3 %collective-permute-done.9.other_ref = f32[2,8,256]{2,1,0:T(8,128)S(1)} collective-permute-done((f32[2,8,256]{2,1,0:T(8,128)S(1)}, f32[2,8,256]{2,1,0:T(8,128)S(1)}, u32[]{:S(2)}, u32[]{:S(2)}) %collective-permute-start.9) | collective-permute-done | bytes 16416 | tf_op jit(solution)/shard_map/ppermute | solution.py:18
  41.7 1.1 %collective-permute-start.10 = (f32[2,8,256]{2,1,0:T(8,128)S(1)}, f32[2,8,256]{2,1,0:T(8,128)S(1)}, u32[]{:S(2)}, u32[]{:S(2)}) collective-permute-start(f32[2,8,256]{2,1,0:T(8,128)S(1)} %join_rows.4.pair_ref), channel_id=1, source_target_pairs={{0,4},{1,5},{2,6},{3,7},{4,0},{5,1},{6,2},{7,3},{8,12},{9,13},{10,... | collective-permute-start | bytes 49160 | tf_op jit(solution)/shard_map/ppermute | solution.py:18
  42.8 2.7 %collective-permute-done.10.other_ref = f32[2,8,256]{2,1,0:T(8,128)S(1)} collective-permute-done((f32[2,8,256]{2,1,0:T(8,128)S(1)}, f32[2,8,256]{2,1,0:T(8,128)S(1)}, u32[]{:S(2)}, u32[]{:S(2)}) %collective-permute-start.10) | collective-permute-done | bytes 16416 | tf_op jit(solution)/shard_map/ppermute | solution.py:18
  46.5 1.6 %collective-permute-start.11 = (f16[136,1024]{1,0:T(8,128)(2,1)S(1)}, f16[136,1024]{1,0:T(8,128)(2,1)S(1)}, u32[]{:S(2)}, u32[]{:S(2)}) collective-permute-start(f16[136,1024]{1,0:T(8,128)(2,1)S(1)} %convert_element_type.22), channel_id=1, source_target_pairs={{0,8},{8,0},{16,24},{24,16},{1,9},{9,1},{17,25},{25,17},{2,10},{10... | collective-permute-start | bytes 835592 | tf_op jit(solution)/shard_map/ppermute | solution.py:18
  48.2 2.4 %weighted_sums.2 = (f32[136,1024]{1,0:T(8,128)S(1)}, f32[136,1024]{1,0:T(8,128)S(1)}, f32[136,1024]{1,0:T(8,128)S(1)}) custom-call(f32[8,256]{1,0:T(8,128)S(1)} %join_rows.5.lognorm_ref, f32[3,384,256]{2,1,0:T(8,128)S(1)} %get-tuple-element.38.refs_0_, f32[1,384,256]{2,1,0:T(8,128)S(1)} %get-tuple-element.39.refs_1_, ...), custom_call_target="tpu_custom_call" | custom-call | flops 1610612736 | bytes 4194304 | tf_op jit(solution)/shard_map/weighted_sums/pallas_call | solution.py:171
  50.6 2.5 %collective-permute-done.11 = f16[136,1024]{1,0:T(8,128)(2,1)S(1)} collective-permute-done((f16[136,1024]{1,0:T(8,128)(2,1)S(1)}, f16[136,1024]{1,0:T(8,128)(2,1)S(1)}, u32[]{:S(2)}, u32[]{:S(2)}) %collective-permute-start.11) | collective-permute-done | bytes 278560 | tf_op jit(solution)/shard_map/ppermute | solution.py:18
  53.4 3.1 %collective-permute-start.13 = (f16[136,1024]{1,0:T(8,128)(2,1)S(1)}, f16[136,1024]{1,0:T(8,128)(2,1)S(1)}, u32[]{:S(2)}, u32[]{:S(2)}) collective-permute-start(f16[136,1024]{1,0:T(8,128)(2,1)S(1)} %convert_element_type.26), channel_id=1, source_target_pairs={{0,16},{8,24},{16,0},{24,8},{1,17},{9,25},{17,1},{25,9},{2,18},{10... | collective-permute-start | bytes 835592 | tf_op jit(solution)/shard_map/ppermute | solution.py:18
  56.5 1.4 %collective-permute-start.12 = (f16[136,1024]{1,0:T(8,128)(2,1)S(1)}, f16[136,1024]{1,0:T(8,128)(2,1)S(1)}, u32[]{:S(2)}, u32[]{:S(2)}) collective-permute-start(f16[136,1024]{1,0:T(8,128)(2,1)S(1)} %convert_element_type.24), channel_id=1, source_target_pairs={{0,8},{8,0},{16,24},{24,16},{1,9},{9,1},{17,25},{25,17},{2,10},{10... | collective-permute-start | bytes 835592 | tf_op jit(solution)/shard_map/ppermute | solution.py:18
  58.4 7.3 %collective-permute-done.13 = f16[136,1024]{1,0:T(8,128)(2,1)S(1)} collective-permute-done((f16[136,1024]{1,0:T(8,128)(2,1)S(1)}, f16[136,1024]{1,0:T(8,128)(2,1)S(1)}, u32[]{:S(2)}, u32[]{:S(2)}) %collective-permute-start.13) | collective-permute-done | bytes 278560 | tf_op jit(solution)/shard_map/ppermute | solution.py:18
  (37 shorter events, 8.4 us)
Async XLA Ops:
  0.6 21.0 %copy-start = (bf16[256,1024]{1,0:T(8,128)(2,1)S(1)}, bf16[256,1024]{1,0:T(8,128)(2,1)}, u32[]{:S(2)}) copy-start(bf16[256,1024]{1,0:T(8,128)(2,1)} %refs_3_.1) | copy-start | bytes 1572868
  0.6 15.1 %collective-permute-start.2 = (bf16[256,1024]{1,0:T(8,128)(2,1)}, bf16[256,1024]{1,0:T(8,128)(2,1)S(1)}, u32[]{:S(2)}, u32[]{:S(2)}) collective-permute-start(bf16[256,1024]{1,0:T(8,128)(2,1)} %refs_3_.1), channel_id=1, source_target_pairs={{0,2},{1,3},{2,0},{3,1},{4,6},{5,7},{6,4},{7,5},{8,10},{9,11},{10,... | collective-permute-start | bytes 1572872 | tf_op jit(solution)/shard_map/ppermute | solution.py:18
  3.6 14.0 %collective-permute-start.3 = (bf16[256,1024]{1,0:T(8,128)(2,1)}, bf16[256,1024]{1,0:T(8,128)(2,1)S(1)}, u32[]{:S(2)}, u32[]{:S(2)}) collective-permute-start(bf16[256,1024]{1,0:T(8,128)(2,1)} %refs_3_.1), channel_id=1, source_target_pairs={{0,4},{1,5},{2,6},{3,7},{4,0},{5,1},{6,2},{7,3},{8,12},{9,13},{10,... | collective-permute-start | bytes 1572872 | tf_op jit(solution)/shard_map/ppermute | solution.py:18
  6.2 13.1 %collective-permute-start = (bf16[128,1024]{1,0:T(8,128)(2,1)S(1)}, bf16[128,1024]{1,0:T(8,128)(2,1)S(1)}, u32[]{:S(2)}, u32[]{:S(2)}) collective-permute-start(bf16[128,1024]{1,0:T(8,128)(2,1)S(1)} %convert_element_type.21.refs_0_), channel_id=1, source_target_pairs={{0,8},{8,0},{16,24},{24,16},{1,9},{9,1},{17,25},{25,17},{2,10},{10... | collective-permute-start | bytes 786440 | tf_op jit(solution)/shard_map/ppermute | solution.py:18
  7.9 13.8 %collective-permute-start.1 = (bf16[128,1024]{1,0:T(8,128)(2,1)S(1)}, bf16[128,1024]{1,0:T(8,128)(2,1)S(1)}, u32[]{:S(2)}, u32[]{:S(2)}) collective-permute-start(bf16[128,1024]{1,0:T(8,128)(2,1)S(1)} %convert_element_type.21.refs_0_), channel_id=1, source_target_pairs={{0,16},{8,24},{16,0},{24,8},{1,17},{9,25},{17,1},{25,9},{2,18},{10... | collective-permute-start | bytes 786440 | tf_op jit(solution)/shard_map/ppermute | solution.py:18
  15.8 7.6 %collective-permute-start.4 = (bf16[128,1024]{1,0:T(8,128)(2,1)S(1)}, bf16[128,1024]{1,0:T(8,128)(2,1)S(1)}, u32[]{:S(2)}, u32[]{:S(2)}) collective-permute-start(bf16[128,1024]{1,0:T(8,128)(2,1)S(1)} %slice.68), channel_id=1, source_target_pairs={{0,4},{1,5},{2,6},{3,7},{4,0},{5,1},{6,2},{7,3},{8,12},{9,13},{10,... | collective-permute-start | bytes 786440 | tf_op jit(solution)/shard_map/ppermute | solution.py:18
  17.7 7.0 %collective-permute-start.5 = (bf16[128,1024]{1,0:T(8,128)(2,1)S(1)}, bf16[128,1024]{1,0:T(8,128)(2,1)S(1)}, u32[]{:S(2)}, u32[]{:S(2)}) collective-permute-start(bf16[128,1024]{1,0:T(8,128)(2,1)S(1)} %slice.69), channel_id=1, source_target_pairs={{0,2},{1,3},{2,0},{3,1},{4,6},{5,7},{6,4},{7,5},{8,10},{9,11},{10,... | collective-permute-start | bytes 786440 | tf_op jit(solution)/shard_map/ppermute | solution.py:18
  24.7 10.2 %collective-permute-start.7 = (bf16[1024,1024]{1,0:T(8,128)(2,1)S(1)}, bf16[1024,1024]{1,0:T(8,128)(2,1)S(1)}, u32[]{:S(2)}, u32[]{:S(2)}) collective-permute-start(bf16[1024,1024]{1,0:T(8,128)(2,1)S(1)} %constant_dynamic-update-slice_fusion.refs_3_.refs_1_.refs_2_), channel_id=1, source_target_pairs={{0,1},{1,0},{2,3},{3,2},{4,5},{5,4},{6,7},{7,6},{8,9},{9,8},{10,11... | collective-permute-start | bytes 6291464 | tf_op jit(solution)/shard_map/ppermute | solution.py:18
  24.7 8.7 %collective-permute-start.6 = (bf16[128,1024]{1,0:T(8,128)(2,1)S(1)}, bf16[128,1024]{1,0:T(8,128)(2,1)S(1)}, u32[]{:S(2)}, u32[]{:S(2)}) collective-permute-start(bf16[128,1024]{1,0:T(8,128)(2,1)S(1)} %collective-permute-done.1.refs_2_), channel_id=1, source_target_pairs={{0,8},{8,0},{16,24},{24,16},{1,9},{9,1},{17,25},{25,17},{2,10},{10... | collective-permute-start | bytes 786440 | tf_op jit(solution)/shard_map/ppermute | solution.py:18
  36.6 1.2 %collective-permute-start.8 = (f32[2,8,256]{2,1,0:T(8,128)S(1)}, f32[2,8,256]{2,1,0:T(8,128)S(1)}, u32[]{:S(2)}, u32[]{:S(2)}) collective-permute-start(f32[2,8,256]{2,1,0:T(8,128)S(1)} %get-tuple-element.37.pair_ref), channel_id=1, source_target_pairs={{0,1},{1,0},{2,3},{3,2},{4,5},{5,4},{6,7},{7,6},{8,9},{9,8},{10,11... | collective-permute-start | bytes 49160 | tf_op jit(solution)/shard_map/ppermute | solution.py:18
  37.8 3.8 %collective-permute-start.9 = (f32[2,8,256]{2,1,0:T(8,128)S(1)}, f32[2,8,256]{2,1,0:T(8,128)S(1)}, u32[]{:S(2)}, u32[]{:S(2)}) collective-permute-start(f32[2,8,256]{2,1,0:T(8,128)S(1)} %join_rows.3.pair_ref), channel_id=1, source_target_pairs={{0,2},{1,3},{2,0},{3,1},{4,6},{5,7},{6,4},{7,5},{8,10},{9,11},{10,... | collective-permute-start | bytes 49160 | tf_op jit(solution)/shard_map/ppermute | solution.py:18
  41.7 3.8 %collective-permute-start.10 = (f32[2,8,256]{2,1,0:T(8,128)S(1)}, f32[2,8,256]{2,1,0:T(8,128)S(1)}, u32[]{:S(2)}, u32[]{:S(2)}) collective-permute-start(f32[2,8,256]{2,1,0:T(8,128)S(1)} %join_rows.4.pair_ref), channel_id=1, source_target_pairs={{0,4},{1,5},{2,6},{3,7},{4,0},{5,1},{6,2},{7,3},{8,12},{9,13},{10,... | collective-permute-start | bytes 49160 | tf_op jit(solution)/shard_map/ppermute | solution.py:18
  46.5 6.6 %collective-permute-start.11 = (f16[136,1024]{1,0:T(8,128)(2,1)S(1)}, f16[136,1024]{1,0:T(8,128)(2,1)S(1)}, u32[]{:S(2)}, u32[]{:S(2)}) collective-permute-start(f16[136,1024]{1,0:T(8,128)(2,1)S(1)} %convert_element_type.22), channel_id=1, source_target_pairs={{0,8},{8,0},{16,24},{24,16},{1,9},{9,1},{17,25},{25,17},{2,10},{10... | collective-permute-start | bytes 835592 | tf_op jit(solution)/shard_map/ppermute | solution.py:18
  53.3 13.4 %copy-start.1 = (f32[128,1024]{1,0:T(8,128)S(1)}, f32[128,1024]{1,0:T(8,128)}, u32[]{:S(2)}) copy-start(f32[128,1024]{1,0:T(8,128)} %param.3) | copy-start | bytes 1572868
  53.4 12.3 %collective-permute-start.13 = (f16[136,1024]{1,0:T(8,128)(2,1)S(1)}, f16[136,1024]{1,0:T(8,128)(2,1)S(1)}, u32[]{:S(2)}, u32[]{:S(2)}) collective-permute-start(f16[136,1024]{1,0:T(8,128)(2,1)S(1)} %convert_element_type.26), channel_id=1, source_target_pairs={{0,16},{8,24},{16,0},{24,8},{1,17},{9,25},{17,1},{25,9},{2,18},{10... | collective-permute-start | bytes 835592 | tf_op jit(solution)/shard_map/ppermute | solution.py:18
  56.5 9.7 %collective-permute-start.12 = (f16[136,1024]{1,0:T(8,128)(2,1)S(1)}, f16[136,1024]{1,0:T(8,128)(2,1)S(1)}, u32[]{:S(2)}, u32[]{:S(2)}) collective-permute-start(f16[136,1024]{1,0:T(8,128)(2,1)S(1)} %convert_element_type.24), channel_id=1, source_target_pairs={{0,8},{8,0},{16,24},{24,16},{1,9},{9,1},{17,25},{25,17},{2,10},{10... | collective-permute-start | bytes 835592 | tf_op jit(solution)/shard_map/ppermute | solution.py:18

commit v5 on v4

--- a/solution.py
+++ b/solution.py
@@ -57,7 +57,7 @@
 def score(centers, rows, r, picks, early=(), begin=0):
     n_c, n_r = len(centers), len(picks)
     depth = rows[0].shape[1]
-    c = n_c * centers[0].shape[0]
+    c = sum(x.shape[0] for x in centers)
     starts = [sum(e.shape[1] for e in early[:i]) for i in range(len(early))]
     n_out = max(begin + n_r, sum(e.shape[1] for e in early))
     return pl.pallas_call(
@@ -193,41 +193,43 @@
         from_x = swap(embeddings, "cent", n_cent, 2)
         from_y = swap(embeddings, "cent", n_cent, 4)
     if n_dp == 4:
-        far = swap(rounded, "dp", n_dp, 2)
+        far = [swap(x, "dp", n_dp, 2) for x in (rounded[: size // 2], rounded[size // 2 :])]
         near = swap(rounded, "dp", n_dp, 1)
-        centers = [rounded, near, far, swap(far, "dp", n_dp, 1)]
-    else:
-        centers = [rounded] + [swap(rounded, "dp", n_dp, m) for m in range(1, n_dp)]
+        most = [rounded, near] + far
+        final = [swap(x, "dp", n_dp, 1) for x in far]
+    else:
+        most = [rounded] + [swap(rounded, "dp", n_dp, m) for m in range(1, n_dp - 1)]
+        final = [swap(rounded, "dp", n_dp, n_dp - 1)]
+    end = (n_dp - 1) * size
     if n_cent == 8:
+        from_x, from_y, most = lax.optimization_barrier((from_x, from_y, most))
         diag_top = swap(from_x[:half], "cent", n_cent, 4)
         diag_low = swap(from_y[half:], "cent", n_cent, 2)
-        s_0, pair_0 = score(
-            centers[:-1], [embeddings, from_x, from_y], own_rows, [(0, 0), (1, 0), (2, 0)]
-        )
-        diag_top, diag_low, s_0, pair_0 = lax.optimization_barrier(
-            (diag_top, diag_low, s_0, pair_0)
-        )
-        four = jnp.concatenate([embeddings, from_x, from_y, diag_top, diag_low], axis=0)
-        rows, order = [four, swap(four, "cent", n_cent, 1)], [0, 2, 4, 6, 1, 3, 5, 7]
-        picks = [(i, j * own_rows) for i in range(2) for j in range(4)]
-        rows[0], centers[-1] = lax.optimization_barrier((four, centers[-1]))
-        s_1, pair_1 = score(centers[:-1], rows[:1], own_rows, [(0, 3 * own_rows)])
-        s_2, pairs = score(centers[-1:], rows[:1], own_rows, picks[:4], [pair_0, pair_1])
-        four_core, s_2, pairs = lax.optimization_barrier((rows[1], s_2, pairs))
-        rows[1] = four_core
-        s_3, pairs = score(centers, rows[1:], own_rows, picks[:4], [pairs], 4)
-        scores = [s_0, s_1, s_3]
-        places = [(0, 0), (0, 1), (0, 2), (1, 0), (2, 0), (2, 1), (2, 2), (2, 3)]
-        last_scores = [s_2, s_3]
-        last_places = [(0, j, 0) for j in range(4)] + [(1, j, (n_dp - 1) * size) for j in range(4)]
+        three = jnp.concatenate([embeddings, from_x, from_y], axis=0)
+        give, final[0] = lax.optimization_barrier((three, final[0]))
+        three_core = swap(give, "cent", n_cent, 1)
+        diag = jnp.concatenate([diag_top, diag_low], axis=0)
+        give, final[-1] = lax.optimization_barrier((diag, final[-1]))
+        diag_core = swap(give, "cent", n_cent, 1)
+        rows, order = [three, three_core, diag, diag_core], [0, 2, 4, 1, 3, 5, 6, 7]
+        picks = [(i, j * own_rows) for i in range(2) for j in range(3)] + [(2, 0), (3, 0)]
+        s_0, pair_0 = score(most, rows[:1], own_rows, picks[:3])
+        s_1, pair_1 = score(most, rows[1:2], own_rows, picks[:3])
+        s_2, pair_2 = score(most + final, rows[2:3], own_rows, [(0, 0)])
+        s_3, pairs = score(final, rows[:2], own_rows, picks[:6], [pair_0, pair_1])
+        s_4, pairs = score(most + final, rows[3:], own_rows, [(0, 0)], [pairs, pair_2], 7)
+        scores = [s_0, s_1, s_2, s_4]
+        places = [(i, j) for i in range(2) for j in range(3)] + [(2, 0), (3, 0)]
+        last_scores = [s_3, s_2, s_4]
+        last_places = [(0, j, 0) for j in range(6)] + [(1, 0, end), (2, 0, end)]
     else:
         rows = [embeddings] + [swap(embeddings, "cent", n_cent, m) for m in range(1, n_cent)]
         order = list(range(n_cent))
         picks = [(j, 0) for j in order]
-        s_0, pair_0 = score(centers[:-1], rows, own_rows, picks)
+        s_0, pair_0 = score(most, rows, own_rows, picks)
         scores = [s_0]
         places = [(0, j) for j in order]
-        s_1, pairs = score(centers[-1:], rows, own_rows, picks, [pair_0])
+        s_1, pairs = score(final, rows, own_rows, picks, [pair_0])
         last_scores, last_places = [s_1], [(0, j, 0) for j in order]
     mask = 1
     while mask < n_cent:

time: 68 us -> 70.8 us (1.041)
  waiting for transfers between devices: 31.9 us -> 34.5 us
  local copies, waits for them, and re-layouts: 1.79 us -> 0.77 us
  starting transfers between devices: 22.7 us -> 23.6 us
    ppermute x14 -> x17, waiting for transfers between devices: 31.9 us -> 34.5 us  [swap(): return lax.ppermute(x, axis, [(i, i ^ mask) for i in range(size)])]
    unnamed x8 -> x7, local copies, waits for them, and re-layouts: 1.18 us -> 0.1 us
    ppermute x14 -> x17, starting transfers between devices: 22.7 us -> 23.6 us  [swap(): return lax.ppermute(x, axis, [(i, i ^ mask) for i in range(size)])]
    pallas_call x4 -> x5, Pallas kernels: 4.11 us -> 4.52 us  [score(): pl.pallas_call(functools.partial(score_kernel, n_c, len(rows), picks, beg...]
  transfers between devices with their start and end apart: 14 -> 17, of which waited for: 12 -> 11; matrix products, arithmetic and copies ran while one was open for 4% -> 3% of each run, Pallas kernels for 7% -> 9%
where the time goes in v5:
time: 70.8 us; the launch traced here: 70.6 us
  waiting for transfers between devices  34.5 us (49%)
  starting transfers between devices  23.6 us (33%)
  Pallas kernels  8.11 us (11%)
  other arithmetic  2.87 us (4%)
  between operations  0.83 us (1%)
  local copies, waits for them, and re-layouts  0.77 us (1%)
    ppermute x17, waiting for transfers between devices, swap(): return lax.ppermute(x, axis, [(i, i ^ mask) for i in range(size)])  34.5 us
    ppermute x17, starting transfers between devices, swap(): return lax.ppermute(x, axis, [(i, i ^ mask) for i in range(size)])  23.6 us
    pallas_call x5, Pallas kernels, score(): pl.pallas_call(functools.partial(score_kernel, n_c, len(rows), picks, beg...  4.52 us
    pallas_call x2, Pallas kernels, weighted(): pl.pallas_call(functools.partial(sums_kernel, len(scores), picks, parts),...  3.39 us
  transfers between devices with their start and end apart: 17, of which 11 were waited for; matrix products, arithmetic and copies ran while one was open for 3% of the time, Pallas kernels for 9%

profile of v5, /device:TPU:0, one launch (start us, length us, event | category | flops | bytes accessed | tf_op | source)
XLA Modules:
  0.0 70.6 jit_solution(2688009660826920491)
XLA Ops:
  0.6 3.0 %collective-permute-start = (bf16[256,1024]{1,0:T(8,128)(2,1)}, bf16[256,1024]{1,0:T(8,128)(2,1)S(1)}, u32[]{:S(2)}, u32[]{:S(2)}) collective-permute-start(bf16[256,1024]{1,0:T(8,128)(2,1)} %param.2), channel_id=1, source_target_pairs={{0,2},{1,3},{2,0},{3,1},{4,6},{5,7},{6,4},{7,5},{8,10},{9,11},{10,... | collective-permute-start | bytes 1572872 | tf_op jit(solution)/shard_map/ppermute | solution.py:18
  3.6 1.5 %collective-permute-start.1 = (bf16[256,1024]{1,0:T(8,128)(2,1)}, bf16[256,1024]{1,0:T(8,128)(2,1)S(1)}, u32[]{:S(2)}, u32[]{:S(2)}) collective-permute-start(bf16[256,1024]{1,0:T(8,128)(2,1)} %param.2), channel_id=1, source_target_pairs={{0,4},{1,5},{2,6},{3,7},{4,0},{5,1},{6,2},{7,3},{8,12},{9,13},{10,... | collective-permute-start | bytes 1572872 | tf_op jit(solution)/shard_map/ppermute | solution.py:18
  5.2 1.1 %convert_element_type.21.refs_0_ = bf16[128,1024]{1,0:T(8,128)(2,1)S(1)} convert(f32[128,1024]{1,0:T(8,128)} %param.3) | non-fusion elementwise | flops 131072 | bytes 786432 | tf_op jit(solution)/shard_map/convert_element_type | solution.py:190
  6.2 1.6 %collective-permute-start.2 = (bf16[128,1024]{1,0:T(8,128)(2,1)S(1)}, bf16[128,1024]{1,0:T(8,128)(2,1)S(1)}, u32[]{:S(2)}, u32[]{:S(2)}) collective-permute-start(bf16[128,1024]{1,0:T(8,128)(2,1)S(1)} %convert_element_type.21.refs_0_), channel_id=1, source_target_pairs={{0,8},{8,0},{16,24},{24,16},{1,9},{9,1},{17,25},{25,17},{2,10},{10... | collective-permute-start | bytes 786440 | tf_op jit(solution)/shard_map/ppermute | solution.py:18
  7.9 2.7 %collective-permute-start.3 = (bf16[64,1024]{1,0:T(8,128)(2,1)S(1)}, bf16[64,1024]{1,0:T(8,128)(2,1)S(1)}, u32[]{:S(2)}, u32[]{:S(2)}) collective-permute-start(bf16[64,1024]{1,0:T(8,128)(2,1)S(1)} %get-tuple-element.64), channel_id=1, source_target_pairs={{0,16},{8,24},{16,0},{24,8},{1,17},{9,25},{17,1},{25,9},{2,18},{10... | collective-permute-start | bytes 393224 | tf_op jit(solution)/shard_map/ppermute | solution.py:18
  10.9 6.2 %collective-permute-done.3.refs_2_ = bf16[64,1024]{1,0:T(8,128)(2,1)S(1)} collective-permute-done((bf16[64,1024]{1,0:T(8,128)(2,1)S(1)}, bf16[64,1024]{1,0:T(8,128)(2,1)S(1)}, u32[]{:S(2)}, u32[]{:S(2)}) %collective-permute-start.3) | collective-permute-done | bytes 131104 | tf_op jit(solution)/shard_map/ppermute | solution.py:18
  17.1 3.9 %collective-permute-start.5 = (bf16[64,1024]{1,0:T(8,128)(2,1)S(1)}, bf16[64,1024]{1,0:T(8,128)(2,1)S(1)}, u32[]{:S(2)}, u32[]{:S(2)}) collective-permute-start(bf16[64,1024]{1,0:T(8,128)(2,1)S(1)} %collective-permute-done.3.refs_2_), channel_id=1, source_target_pairs={{0,8},{8,0},{16,24},{24,16},{1,9},{9,1},{17,25},{25,17},{2,10},{10... | collective-permute-start | bytes 393224 | tf_op jit(solution)/shard_map/ppermute | solution.py:18
  21.5 2.5 %collective-permute-done.5.refs_0_.refs_4_ = bf16[64,1024]{1,0:T(8,128)(2,1)S(1)} collective-permute-done((bf16[64,1024]{1,0:T(8,128)(2,1)S(1)}, bf16[64,1024]{1,0:T(8,128)(2,1)S(1)}, u32[]{:S(2)}, u32[]{:S(2)}) %collective-permute-start.5) | collective-permute-done | bytes 131104 | tf_op jit(solution)/shard_map/ppermute | solution.py:18
  25.2 2.0 %collective-permute-start.8 = (bf16[64,1024]{1,0:T(8,128)(2,1)S(1)}, bf16[64,1024]{1,0:T(8,128)(2,1)S(1)}, u32[]{:S(2)}, u32[]{:S(2)}) collective-permute-start(bf16[64,1024]{1,0:T(8,128)(2,1)S(1)} %collective-permute-done.4.refs_3_), channel_id=1, source_target_pairs={{0,8},{8,0},{16,24},{24,16},{1,9},{9,1},{17,25},{25,17},{2,10},{10... | collective-permute-start | bytes 393224 | tf_op jit(solution)/shard_map/ppermute | solution.py:18
  27.2 5.6 %collective-permute-done.6 = bf16[128,1024]{1,0:T(8,128)(2,1)S(1)} collective-permute-done((bf16[128,1024]{1,0:T(8,128)(2,1)S(1)}, bf16[128,1024]{1,0:T(8,128)(2,1)S(1)}, u32[]{:S(2)}, u32[]{:S(2)}) %collective-permute-start.6) | collective-permute-done | bytes 262176 | tf_op jit(solution)/shard_map/ppermute | solution.py:18
  33.2 1.0 %score_rows.5 = (f32[3,384,256]{2,1,0:T(8,128)S(1)}, f32[2,3,256]{2,1,0:T(4,128)S(1)}) custom-call(bf16[128,1024]{1,0:T(8,128)(2,1)S(1)} %convert_element_type.21.refs_0_, bf16[128,1024]{1,0:T(8,128)(2,1)S(1)} %collective-permute-done.2.refs_1_, bf16[64,1024]{1,0:T(8,128)(2,1)S(1)} %collective-permute-done.3.refs_2_, ...), custom_call_target="tpu_custom_call" | custom-call | flops 603979776 | bytes 2359296 | tf_op jit(solution)/shard_map/score_rows/pallas_call | solution.py:63
  34.8 1.0 %score_rows.6 = (f32[3,384,256]{2,1,0:T(8,128)S(1)}, f32[2,3,256]{2,1,0:T(4,128)S(1)}) custom-call(bf16[128,1024]{1,0:T(8,128)(2,1)S(1)} %convert_element_type.21.refs_0_, bf16[128,1024]{1,0:T(8,128)(2,1)S(1)} %collective-permute-done.2.refs_1_, bf16[64,1024]{1,0:T(8,128)(2,1)S(1)} %collective-permute-done.3.refs_2_, ...), custom_call_target="tpu_custom_call" | custom-call | flops 603979776 | bytes 2359296 | tf_op jit(solution)/shard_map/score_rows/pallas_call | solution.py:63
  35.8 1.3 %score_rows.7 = (f32[6,128,256]{2,1,0:T(8,128)S(1)}, f32[2,6,256]{2,1,0:T(8,128)S(1)}) custom-call(bf16[64,1024]{1,0:T(8,128)(2,1)S(1)} %collective-permute-done.5.refs_0_.refs_4_, bf16[64,1024]{1,0:T(8,128)(2,1)S(1)} %collective-permute-done.8.refs_1_.refs_5_, bf16[768,1024]{1,0:T(8,128)(2,1)S(1)} %constant_dynamic-update-slice_fusion.refs_4_.refs_2_.refs_3_, ...), custom_call_target="tpu_custom_call" | custom-call | flops 402653184 | bytes 3407872 | tf_op jit(solution)/shard_map/score_rows/pallas_call | solution.py:63
  39.7 3.2 %collective-permute-done.12.other_ref = f32[2,8,256]{2,1,0:T(8,128)S(1)} collective-permute-done((f32[2,8,256]{2,1,0:T(8,128)S(1)}, f32[2,8,256]{2,1,0:T(8,128)S(1)}, u32[]{:S(2)}, u32[]{:S(2)}) %collective-permute-start.12) | collective-permute-done | bytes 16416 | tf_op jit(solution)/shard_map/ppermute | solution.py:18
  43.0 1.6 %collective-permute-start.13 = (f32[2,8,256]{2,1,0:T(8,128)S(1)}, f32[2,8,256]{2,1,0:T(8,128)S(1)}, u32[]{:S(2)}, u32[]{:S(2)}) collective-permute-start(f32[2,8,256]{2,1,0:T(8,128)S(1)} %join_rows.4.pair_ref), channel_id=1, source_target_pairs={{0,4},{1,5},{2,6},{3,7},{4,0},{5,1},{6,2},{7,3},{8,12},{9,13},{10,... | collective-permute-start | bytes 49160 | tf_op jit(solution)/shard_map/ppermute | solution.py:18
  44.5 2.2 %collective-permute-done.13.other_ref = f32[2,8,256]{2,1,0:T(8,128)S(1)} collective-permute-done((f32[2,8,256]{2,1,0:T(8,128)S(1)}, f32[2,8,256]{2,1,0:T(8,128)S(1)}, u32[]{:S(2)}, u32[]{:S(2)}) %collective-permute-start.13) | collective-permute-done | bytes 16416 | tf_op jit(solution)/shard_map/ppermute | solution.py:18
  46.8 1.0 %weighted_sums.3 = f32[136,1024]{1,0:T(8,128)S(1)} custom-call(f32[8,256]{1,0:T(8,128)S(1)} %join_rows.5.lognorm_ref, f32[6,128,256]{2,1,0:T(8,128)S(1)} %get-tuple-element.49.refs_0_, f32[1,512,256]{2,1,0:T(8,128)S(1)} %get-tuple-element.45.refs_2_.refs_1_, f32[1,512,256]{2,1,0:T(8,128)S(1)} %get-tuple-element.46.refs_3_.refs_2_, ...), custom_call_target="tpu_custom_call" | custom-call | flops 536870912 | bytes 4194304 | tf_op jit(solution)/shard_map/weighted_sums/pallas_call | solution.py:171
  47.8 2.1 %collective-permute-start.14 = (f16[136,1024]{1,0:T(8,128)(2,1)S(1)}, f16[136,1024]{1,0:T(8,128)(2,1)S(1)}, u32[]{:S(2)}, u32[]{:S(2)}) collective-permute-start(f16[136,1024]{1,0:T(8,128)(2,1)S(1)} %convert_element_type.22), channel_id=1, source_target_pairs={{0,8},{8,0},{16,24},{24,16},{1,9},{9,1},{17,25},{25,17},{2,10},{10... | collective-permute-start | bytes 835592 | tf_op jit(solution)/shard_map/ppermute | solution.py:18
  49.9 2.4 %weighted_sums.2 = (f32[136,1024]{1,0:T(8,128)S(1)}, f32[136,1024]{1,0:T(8,128)S(1)}, f32[136,1024]{1,0:T(8,128)S(1)}) custom-call(f32[8,256]{1,0:T(8,128)S(1)} %join_rows.5.lognorm_ref, f32[3,384,256]{2,1,0:T(8,128)S(1)} %get-tuple-element.43.refs_0_, f32[3,384,256]{2,1,0:T(8,128)S(1)} %get-tuple-element.44.refs_1_, ...), custom_call_target="tpu_custom_call" | custom-call | flops 1610612736 | bytes 4194304 | tf_op jit(solution)/shard_map/weighted_sums/pallas_call | solution.py:171
  52.3 2.4 %collective-permute-done.14 = f16[136,1024]{1,0:T(8,128)(2,1)S(1)} collective-permute-done((f16[136,1024]{1,0:T(8,128)(2,1)S(1)}, f16[136,1024]{1,0:T(8,128)(2,1)S(1)}, u32[]{:S(2)}, u32[]{:S(2)}) %collective-permute-start.14) | collective-permute-done | bytes 278560 | tf_op jit(solution)/shard_map/ppermute | solution.py:18
  55.0 2.0 %collective-permute-start.15 = (f16[136,1024]{1,0:T(8,128)(2,1)S(1)}, f16[136,1024]{1,0:T(8,128)(2,1)S(1)}, u32[]{:S(2)}, u32[]{:S(2)}) collective-permute-start(f16[136,1024]{1,0:T(8,128)(2,1)S(1)} %convert_element_type.24), channel_id=1, source_target_pairs={{0,8},{8,0},{16,24},{24,16},{1,9},{9,1},{17,25},{25,17},{2,10},{10... | collective-permute-start | bytes 835592 | tf_op jit(solution)/shard_map/ppermute | solution.py:18
  58.1 7.5 %collective-permute-done.15 = f16[136,1024]{1,0:T(8,128)(2,1)S(1)} collective-permute-done((f16[136,1024]{1,0:T(8,128)(2,1)S(1)}, f16[136,1024]{1,0:T(8,128)(2,1)S(1)}, u32[]{:S(2)}, u32[]{:S(2)}) %collective-permute-start.15) | collective-permute-done | bytes 278560 | tf_op jit(solution)/shard_map/ppermute | solution.py:18
  65.7 3.3 %collective-permute-done.16 = f16[136,1024]{1,0:T(8,128)(2,1)S(1)} collective-permute-done((f16[136,1024]{1,0:T(8,128)(2,1)S(1)}, f16[136,1024]{1,0:T(8,128)(2,1)S(1)}, u32[]{:S(2)}, u32[]{:S(2)}) %collective-permute-start.16) | collective-permute-done | bytes 278560 | tf_op jit(solution)/shard_map/ppermute | solution.py:18
  69.6 1.0 %fusion.2 = f32[128,1024]{1,0:T(8,128)} fusion(f32[128,1024]{1,0:T(8,128)S(1)} %copy-done, f32[136,1024]{1,0:T(8,128)S(1)} %convert_element_type.27, f32[136,1024]{1,0:T(8,128)S(1)} %convert_element_type.25, f32[136,1024]{1,0:T(8,128)S(1)} %get-tuple-element.47, f32[128]{0:T(128)S(1)} %get-tuple-element.53, f32[1024]{0:T(1024)S(1)} %bitcast.7, ...), kind=kLoop, calls=%fused_computation.3 | loop fusion | flops 786432 | bytes 2630144 | tf_op jit(solution)/shard_map/div | solution.py:265
  (45 shorter events, 7.7 us)
Async XLA Ops:
  0.6 10.3 %copy-start.1 = (bf16[256,1024]{1,0:T(8,128)(2,1)S(1)}, bf16[256,1024]{1,0:T(8,128)(2,1)}, u32[]{:S(2)}) copy-start(bf16[256,1024]{1,0:T(8,128)(2,1)} %param.2) | copy-start | bytes 1572868
  0.6 20.7 %collective-permute-start = (bf16[256,1024]{1,0:T(8,128)(2,1)}, bf16[256,1024]{1,0:T(8,128)(2,1)S(1)}, u32[]{:S(2)}, u32[]{:S(2)}) collective-permute-start(bf16[256,1024]{1,0:T(8,128)(2,1)} %param.2), channel_id=1, source_target_pairs={{0,2},{1,3},{2,0},{3,1},{4,6},{5,7},{6,4},{7,5},{8,10},{9,11},{10,... | collective-permute-start | bytes 1572872 | tf_op jit(solution)/shard_map/ppermute | solution.py:18
  3.6 17.7 %collective-permute-start.1 = (bf16[256,1024]{1,0:T(8,128)(2,1)}, bf16[256,1024]{1,0:T(8,128)(2,1)S(1)}, u32[]{:S(2)}, u32[]{:S(2)}) collective-permute-start(bf16[256,1024]{1,0:T(8,128)(2,1)} %param.2), channel_id=1, source_target_pairs={{0,4},{1,5},{2,6},{3,7},{4,0},{5,1},{6,2},{7,3},{8,12},{9,13},{10,... | collective-permute-start | bytes 1572872 | tf_op jit(solution)/shard_map/ppermute | solution.py:18
  6.2 15.1 %collective-permute-start.2 = (bf16[128,1024]{1,0:T(8,128)(2,1)S(1)}, bf16[128,1024]{1,0:T(8,128)(2,1)S(1)}, u32[]{:S(2)}, u32[]{:S(2)}) collective-permute-start(bf16[128,1024]{1,0:T(8,128)(2,1)S(1)} %convert_element_type.21.refs_0_), channel_id=1, source_target_pairs={{0,8},{8,0},{16,24},{24,16},{1,9},{9,1},{17,25},{25,17},{2,10},{10... | collective-permute-start | bytes 786440 | tf_op jit(solution)/shard_map/ppermute | solution.py:18
  7.9 9.2 %collective-permute-start.3 = (bf16[64,1024]{1,0:T(8,128)(2,1)S(1)}, bf16[64,1024]{1,0:T(8,128)(2,1)S(1)}, u32[]{:S(2)}, u32[]{:S(2)}) collective-permute-start(bf16[64,1024]{1,0:T(8,128)(2,1)S(1)} %get-tuple-element.64), channel_id=1, source_target_pairs={{0,16},{8,24},{16,0},{24,8},{1,17},{9,25},{17,1},{25,9},{2,18},{10... | collective-permute-start | bytes 393224 | tf_op jit(solution)/shard_map/ppermute | solution.py:18
  10.6 10.8 %collective-permute-start.4 = (bf16[64,1024]{1,0:T(8,128)(2,1)S(1)}, bf16[64,1024]{1,0:T(8,128)(2,1)S(1)}, u32[]{:S(2)}, u32[]{:S(2)}) collective-permute-start(bf16[64,1024]{1,0:T(8,128)(2,1)S(1)} %get-tuple-element.63), channel_id=1, source_target_pairs={{0,16},{8,24},{16,0},{24,8},{1,17},{9,25},{17,1},{25,9},{2,18},{10... | collective-permute-start | bytes 393224 | tf_op jit(solution)/shard_map/ppermute | solution.py:18
  17.1 6.8 %collective-permute-start.5 = (bf16[64,1024]{1,0:T(8,128)(2,1)S(1)}, bf16[64,1024]{1,0:T(8,128)(2,1)S(1)}, u32[]{:S(2)}, u32[]{:S(2)}) collective-permute-start(bf16[64,1024]{1,0:T(8,128)(2,1)S(1)} %collective-permute-done.3.refs_2_), channel_id=1, source_target_pairs={{0,8},{8,0},{16,24},{24,16},{1,9},{9,1},{17,25},{25,17},{2,10},{10... | collective-permute-start | bytes 393224 | tf_op jit(solution)/shard_map/ppermute | solution.py:18
  23.9 10.9 %collective-permute-start.10 = (bf16[768,1024]{1,0:T(8,128)(2,1)S(1)}, bf16[768,1024]{1,0:T(8,128)(2,1)S(1)}, u32[]{:S(2)}, u32[]{:S(2)}) collective-permute-start(bf16[768,1024]{1,0:T(8,128)(2,1)S(1)} %constant_dynamic-update-slice_fusion.refs_4_.refs_2_.refs_3_), channel_id=1, source_target_pairs={{0,1},{1,0},{2,3},{3,2},{4,5},{5,4},{6,7},{7,6},{8,9},{9,8},{10,11... | collective-permute-start | bytes 4718600 | tf_op jit(solution)/shard_map/ppermute | solution.py:18
  24.0 8.8 %collective-permute-start.6 = (bf16[128,1024]{1,0:T(8,128)(2,1)S(1)}, bf16[128,1024]{1,0:T(8,128)(2,1)S(1)}, u32[]{:S(2)}, u32[]{:S(2)}) collective-permute-start(bf16[128,1024]{1,0:T(8,128)(2,1)S(1)} %slice.59), channel_id=1, source_target_pairs={{0,4},{1,5},{2,6},{3,7},{4,0},{5,1},{6,2},{7,3},{8,12},{9,13},{10,... | collective-permute-start | bytes 786440 | tf_op jit(solution)/shard_map/ppermute | solution.py:18
  24.6 8.5 %collective-permute-start.7 = (bf16[128,1024]{1,0:T(8,128)(2,1)S(1)}, bf16[128,1024]{1,0:T(8,128)(2,1)S(1)}, u32[]{:S(2)}, u32[]{:S(2)}) collective-permute-start(bf16[128,1024]{1,0:T(8,128)(2,1)S(1)} %slice.60), channel_id=1, source_target_pairs={{0,2},{1,3},{2,0},{3,1},{4,6},{5,7},{6,4},{7,5},{8,10},{9,11},{10,... | collective-permute-start | bytes 786440 | tf_op jit(solution)/shard_map/ppermute | solution.py:18
  25.2 7.9 %collective-permute-start.8 = (bf16[64,1024]{1,0:T(8,128)(2,1)S(1)}, bf16[64,1024]{1,0:T(8,128)(2,1)S(1)}, u32[]{:S(2)}, u32[]{:S(2)}) collective-permute-start(bf16[64,1024]{1,0:T(8,128)(2,1)S(1)} %collective-permute-done.4.refs_3_), channel_id=1, source_target_pairs={{0,8},{8,0},{16,24},{24,16},{1,9},{9,1},{17,25},{25,17},{2,10},{10... | collective-permute-start | bytes 393224 | tf_op jit(solution)/shard_map/ppermute | solution.py:18
  33.1 4.0 %collective-permute-start.9 = (bf16[256,1024]{1,0:T(8,128)(2,1)S(1)}, bf16[256,1024]{1,0:T(8,128)(2,1)S(1)}, u32[]{:S(2)}, u32[]{:S(2)}) collective-permute-start(bf16[256,1024]{1,0:T(8,128)(2,1)S(1)} %constant_dynamic-update-slice_fusion.3.refs_6_.refs_5_), channel_id=1, source_target_pairs={{0,1},{1,0},{2,3},{3,2},{4,5},{5,4},{6,7},{7,6},{8,9},{9,8},{10,11... | collective-permute-start | bytes 1572872 | tf_op jit(solution)/shard_map/ppermute | solution.py:18
  37.7 1.4 %collective-permute-start.11 = (f32[2,8,256]{2,1,0:T(8,128)S(1)}, f32[2,8,256]{2,1,0:T(8,128)S(1)}, u32[]{:S(2)}, u32[]{:S(2)}) collective-permute-start(f32[2,8,256]{2,1,0:T(8,128)S(1)} %get-tuple-element.42.pair_ref), channel_id=1, source_target_pairs={{0,1},{1,0},{2,3},{3,2},{4,5},{5,4},{6,7},{7,6},{8,9},{9,8},{10,11... | collective-permute-start | bytes 49160 | tf_op jit(solution)/shard_map/ppermute | solution.py:18
  39.1 3.8 %collective-permute-start.12 = (f32[2,8,256]{2,1,0:T(8,128)S(1)}, f32[2,8,256]{2,1,0:T(8,128)S(1)}, u32[]{:S(2)}, u32[]{:S(2)}) collective-permute-start(f32[2,8,256]{2,1,0:T(8,128)S(1)} %join_rows.3.pair_ref), channel_id=1, source_target_pairs={{0,2},{1,3},{2,0},{3,1},{4,6},{5,7},{6,4},{7,5},{8,10},{9,11},{10,... | collective-permute-start | bytes 49160 | tf_op jit(solution)/shard_map/ppermute | solution.py:18
  43.0 3.8 %collective-permute-start.13 = (f32[2,8,256]{2,1,0:T(8,128)S(1)}, f32[2,8,256]{2,1,0:T(8,128)S(1)}, u32[]{:S(2)}, u32[]{:S(2)}) collective-permute-start(f32[2,8,256]{2,1,0:T(8,128)S(1)} %join_rows.4.pair_ref), channel_id=1, source_target_pairs={{0,4},{1,5},{2,6},{3,7},{4,0},{5,1},{6,2},{7,3},{8,12},{9,13},{10,... | collective-permute-start | bytes 49160 | tf_op jit(solution)/shard_map/ppermute | solution.py:18
  47.8 7.0 %collective-permute-start.14 = (f16[136,1024]{1,0:T(8,128)(2,1)S(1)}, f16[136,1024]{1,0:T(8,128)(2,1)S(1)}, u32[]{:S(2)}, u32[]{:S(2)}) collective-permute-start(f16[136,1024]{1,0:T(8,128)(2,1)S(1)} %convert_element_type.22), channel_id=1, source_target_pairs={{0,8},{8,0},{16,24},{24,16},{1,9},{9,1},{17,25},{25,17},{2,10},{10... | collective-permute-start | bytes 835592 | tf_op jit(solution)/shard_map/ppermute | solution.py:18
  55.0 14.6 %copy-start = (f32[128,1024]{1,0:T(8,128)S(1)}, f32[128,1024]{1,0:T(8,128)}, u32[]{:S(2)}) copy-start(f32[128,1024]{1,0:T(8,128)} %param.3) | copy-start | bytes 1572868
  55.0 10.6 %collective-permute-start.15 = (f16[136,1024]{1,0:T(8,128)(2,1)S(1)}, f16[136,1024]{1,0:T(8,128)(2,1)S(1)}, u32[]{:S(2)}, u32[]{:S(2)}) collective-permute-start(f16[136,1024]{1,0:T(8,128)(2,1)S(1)} %convert_element_type.24), channel_id=1, source_target_pairs={{0,8},{8,0},{16,24},{24,16},{1,9},{9,1},{17,25},{25,17},{2,10},{10... | collective-permute-start | bytes 835592 | tf_op jit(solution)/shard_map/ppermute | solution.py:18
  57.1 11.9 %collective-permute-start.16 = (f16[136,1024]{1,0:T(8,128)(2,1)S(1)}, f16[136,1024]{1,0:T(8,128)(2,1)S(1)}, u32[]{:S(2)}, u32[]{:S(2)}) collective-permute-start(f16[136,1024]{1,0:T(8,128)(2,1)S(1)} %convert_element_type.26), channel_id=1, source_target_pairs={{0,16},{8,24},{16,0},{24,8},{1,17},{9,25},{17,1},{25,9},{2,18},{10... | collective-permute-start | bytes 835592 | tf_op jit(solution)/shard_map/ppermute | solution.py:18

commit v6 on v4

--- a/solution.py
+++ b/solution.py
@@ -101,6 +101,35 @@
     )(pairs, other)
 
 
+def gather_kernel(core_ref, all_ref, out_ref):
+    n, half = all_ref.shape[0], out_ref.shape[0] // 2
+    of_core = []
+    for core in range(2):
+        top, total = all_ref[core, 0], all_ref[core, 1]
+        for i in range(core + 2, n, 2):
+            top, total = merge((top, total), (all_ref[i, 0], all_ref[i, 1]))
+        of_core.append((top, total))
+    other = [jnp.concatenate([x[half:], x[:half]]) for x in of_core[1]]
+    top, total = merge(of_core[0], other)
+    lognorm = top + jnp.log(total)
+    swapped = jnp.concatenate([lognorm[half:], lognorm[:half]])
+    out_ref[...] = jnp.where(core_ref[0] == 1, swapped, lognorm)
+
+
+def gather_totals(pairs, size):
+    sent = jnp.broadcast_to(pairs, (size,) + pairs.shape)
+    got = lax.all_to_all(sent, "cent", 0, 0, tiled=True)
+    core = jnp.reshape(lax.axis_index("cent") & 1, (1,))
+    return pl.pallas_call(
+        gather_kernel,
+        out_shape=jax.ShapeDtypeStruct(pairs.shape[1:], jnp.float32),
+        in_specs=[pl.BlockSpec(memory_space=pltpu.SMEM), VMEM],
+        out_specs=VMEM,
+        compiler_params=PARAMS,
+        name="join_rows",
+    )(core, got)
+
+
 def sums_kernel(n_parts, picks, parts, lognorm_ref, *refs):
     score_refs, row_refs = refs[:n_parts], refs[n_parts : -len(parts)]
     outs = refs[-len(parts) :]
@@ -188,38 +217,23 @@
     size = codebook.shape[0]
     unit = 1024.0 / (own_rows * n_cent)
     rounded = codebook.astype(jnp.bfloat16)
+    centers = [rounded] + [swap(rounded, "dp", n_dp, m) for m in range(1, n_dp)]
     if n_cent == 8:
-        half = own_rows // 2
-        from_x = swap(embeddings, "cent", n_cent, 2)
-        from_y = swap(embeddings, "cent", n_cent, 4)
-    if n_dp == 4:
-        far = swap(rounded, "dp", n_dp, 2)
-        near = swap(rounded, "dp", n_dp, 1)
-        centers = [rounded, near, far, swap(far, "dp", n_dp, 1)]
-    else:
-        centers = [rounded] + [swap(rounded, "dp", n_dp, m) for m in range(1, n_dp)]
-    if n_cent == 8:
-        diag_top = swap(from_x[:half], "cent", n_cent, 4)
-        diag_low = swap(from_y[half:], "cent", n_cent, 2)
-        s_0, pair_0 = score(
-            centers[:-1], [embeddings, from_x, from_y], own_rows, [(0, 0), (1, 0), (2, 0)]
-        )
-        diag_top, diag_low, s_0, pair_0 = lax.optimization_barrier(
-            (diag_top, diag_low, s_0, pair_0)
-        )
-        four = jnp.concatenate([embeddings, from_x, from_y, diag_top, diag_low], axis=0)
-        rows, order = [four, swap(four, "cent", n_cent, 1)], [0, 2, 4, 6, 1, 3, 5, 7]
+        groups = [[i for i in range(n_cent) if i % 2 == core] for core in range(2)]
+        sent = jnp.broadcast_to(embeddings, (n_cent // 2,) + embeddings.shape)
+        four = lax.all_to_all(sent, "cent", 0, 0, axis_index_groups=groups, tiled=True)
+        four = four.reshape(-1, embeddings.shape[1])
+        give, centers = lax.optimization_barrier((four, centers))
+        rows = [four, swap(give, "cent", n_cent, 1)]
         picks = [(i, j * own_rows) for i in range(2) for j in range(4)]
-        rows[0], centers[-1] = lax.optimization_barrier((four, centers[-1]))
-        s_1, pair_1 = score(centers[:-1], rows[:1], own_rows, [(0, 3 * own_rows)])
-        s_2, pairs = score(centers[-1:], rows[:1], own_rows, picks[:4], [pair_0, pair_1])
-        four_core, s_2, pairs = lax.optimization_barrier((rows[1], s_2, pairs))
-        rows[1] = four_core
-        s_3, pairs = score(centers, rows[1:], own_rows, picks[:4], [pairs], 4)
-        scores = [s_0, s_1, s_3]
-        places = [(0, 0), (0, 1), (0, 2), (1, 0), (2, 0), (2, 1), (2, 2), (2, 3)]
-        last_scores = [s_2, s_3]
-        last_places = [(0, j, 0) for j in range(4)] + [(1, j, (n_dp - 1) * size) for j in range(4)]
+        s_0, pairs = score(centers, rows[:1], own_rows, picks[:4])
+        s_1, pairs = score(centers, rows[1:], own_rows, picks[:4], [pairs], 4)
+        scores = [s_0, s_1]
+        places = [(i, j) for i in range(2) for j in range(4)]
+        last_scores = scores
+        last_places = [(i, j, (n_dp - 1) * size) for i, j in places]
+        lognorm = gather_totals(pairs, n_cent)
+        own_norm = lax.dynamic_slice_in_dim(lognorm, lax.axis_index("cent") >> 1, 1)[0]
     else:
         rows = [embeddings] + [swap(embeddings, "cent", n_cent, m) for m in range(1, n_cent)]
         order = list(range(n_cent))
@@ -229,12 +243,12 @@
         places = [(0, j) for j in order]
         s_1, pairs = score(centers[-1:], rows, own_rows, picks, [pair_0])
         last_scores, last_places = [s_1], [(0, j, 0) for j in order]
-    mask = 1
-    while mask < n_cent:
-        pairs = join(pairs, mask, order, 2 * mask >= n_cent)
-        mask *= 2
-    lognorm = pairs
-
+        mask = 1
+        while mask < n_cent:
+            pairs = join(pairs, mask, order, 2 * mask >= n_cent)
+            mask *= 2
+        lognorm = pairs
+        own_norm = lognorm[0]
     def part(k, unit):
         return [(i, j, k * size) for i, j in places], size, unit
 
@@ -261,7 +275,7 @@
         owner_total = owner_total + more
         owner_tally = owner_tally + count[0, :size]
     new_codebook = (owner_total + PRIOR * codebook) / (owner_tally + PRIOR)[:, None]
-    return (new_codebook, owner_tally, lognorm[0])
+    return (new_codebook, owner_tally, own_norm)
 
 
 def solution(mesh):

time: 68 us -> 85.3 us (1.25)
  waiting for transfers between devices: 31.9 us -> 43 us
  local copies, waits for them, and re-layouts: 1.79 us -> 12.6 us
  starting transfers between devices: 22.7 us -> 19.8 us
  other arithmetic: 2.87 us -> 1.83 us
  Pallas kernels: 7.69 us -> 6.82 us
    ppermute x14 -> x7, starting transfers between devices: 22.7 us -> 11.1 us  [swap(): return lax.ppermute(x, axis, [(i, i ^ mask) for i in range(size)])]
    all_to_all x0 -> x2, starting transfers between devices: none -> 8.67 us  [the longest x1 5.29 us: local(): lax.all_to_all(sent, 'cent', 0, 0, axis_index_groups=groups, tiled=True)]
    unnamed x8 -> x16, local copies, waits for them, and re-layouts: 1.18 us -> 8.75 us
    all_to_all x0 -> x2, waiting for transfers between devices: none -> 7.26 us  [the longest x1 5.46 us: gather_totals(): got = lax.all_to_all(sent, 'cent', 0, 0, tiled=True)]
    ppermute x14 -> x7, waiting for transfers between devices: 31.9 us -> 35.8 us  [swap(): return lax.ppermute(x, axis, [(i, i ^ mask) for i in range(size)])]
    broadcast_in_dim x0 -> x2, local copies, waits for them, and re-layouts: none -> 3.31 us  [the longest x1 2.65 us: local(): sent = jnp.broadcast_to(embeddings, (n_cent // 2,) + embeddings.shape)]
    convert_element_type x1, other arithmetic: 1.07 us -> 0.03 us  [local(): rounded = codebook.astype(jnp.bfloat16)]
    pallas_call x4 -> x2, Pallas kernels: 4.11 us -> 3.28 us  [score(): pl.pallas_call(functools.partial(score_kernel, n_c, len(rows), picks, beg...]
  transfers between devices with their start and end apart: 14 -> 9, of which waited for: 12 -> 8; matrix products, arithmetic and copies ran while one was open for 4% -> 1% of each run, Pallas kernels for 7% -> 5%
where the time goes in v6:
time: 85.3 us; the launch traced here: 84.9 us
  waiting for transfers between devices  43 us (50%)
  starting transfers between devices  19.8 us (23%)
  local copies, waits for them, and re-layouts  12.6 us (15%)
  Pallas kernels  6.82 us (8%)
  other arithmetic  1.83 us (2%)
    ppermute x7, waiting for transfers between devices, swap(): return lax.ppermute(x, axis, [(i, i ^ mask) for i in range(size)])  35.8 us
    ppermute x7, starting transfers between devices, swap(): return lax.ppermute(x, axis, [(i, i ^ mask) for i in range(size)])  11.1 us
    unnamed x16, local copies, waits for them, and re-layouts  8.75 us
    all_to_all x1, waiting for transfers between devices, gather_totals(): got = lax.all_to_all(sent, 'cent', 0, 0, tiled=True)  5.46 us
    all_to_all x1, starting transfers between devices, local(): lax.all_to_all(sent, 'cent', 0, 0, axis_index_groups=groups, tiled=True)  5.29 us
    all_to_all x1, starting transfers between devices, gather_totals(): got = lax.all_to_all(sent, 'cent', 0, 0, tiled=True)  3.37 us
    pallas_call x2, Pallas kernels, weighted(): pl.pallas_call(functools.partial(sums_kernel, len(scores), picks, parts),...  3.36 us
    pallas_call x2, Pallas kernels, score(): pl.pallas_call(functools.partial(score_kernel, n_c, len(rows), picks, beg...  3.28 us
  transfers between devices with their start and end apart: 9, of which 8 were waited for; matrix products, arithmetic and copies ran while one was open for 1% of the time, Pallas kernels for 5%

profile of v6, /device:TPU:0, one launch (start us, length us, event | category | flops | bytes accessed | tf_op | source)
XLA Modules:
  0.0 84.9 jit_solution(18245976445428301618)
XLA Ops:
  0.6 2.6 %broadcast_in_dim.7 = bf16[4,256,1024]{2,1,0:T(8,128)(2,1)} broadcast(bf16[256,1024]{1,0:T(8,128)(2,1)} %param.2), dimensions={1,2} | broadcast | bytes 2621440 | tf_op jit(solution)/shard_map/broadcast_in_dim | solution.py:223
  3.3 5.3 %all-to-all-start = ((bf16[4,256,1024]{2,1,0:T(8,128)(2,1)}), bf16[4,256,1024]{2,1,0:T(8,128)(2,1)S(1)}, u32[]{:S(2)}, u32[]{:S(2)}) async-start(bf16[4,256,1024]{2,1,0:T(8,128)(2,1)} %broadcast_in_dim.7), calls=%async_computation | async-start | bytes 4194304 | tf_op jit(solution)/shard_map/all_to_all | solution.py:224
  8.6 1.6 %collective-permute-start = (bf16[128,1024]{1,0:T(8,128)(2,1)S(1)}, bf16[128,1024]{1,0:T(8,128)(2,1)S(1)}, u32[]{:S(2)}, u32[]{:S(2)}) collective-permute-start(bf16[128,1024]{1,0:T(8,128)(2,1)S(1)} %convert_element_type.21.refs_0_), channel_id=1, source_target_pairs={{0,8},{8,0},{16,24},{24,16},{1,9},{9,1},{17,25},{25,17},{2,10},{10... | collective-permute-start | bytes 786440 | tf_op jit(solution)/shard_map/ppermute | solution.py:18
  10.3 2.6 %collective-permute-start.1 = (bf16[128,1024]{1,0:T(8,128)(2,1)S(1)}, bf16[128,1024]{1,0:T(8,128)(2,1)S(1)}, u32[]{:S(2)}, u32[]{:S(2)}) collective-permute-start(bf16[128,1024]{1,0:T(8,128)(2,1)S(1)} %convert_element_type.21.refs_0_), channel_id=1, source_target_pairs={{0,16},{8,24},{16,0},{24,8},{1,17},{9,25},{17,1},{25,9},{2,18},{10... | collective-permute-start | bytes 786440 | tf_op jit(solution)/shard_map/ppermute | solution.py:18
  13.1 8.2 %collective-permute-done.refs_1_ = bf16[128,1024]{1,0:T(8,128)(2,1)S(1)} collective-permute-done((bf16[128,1024]{1,0:T(8,128)(2,1)S(1)}, bf16[128,1024]{1,0:T(8,128)(2,1)S(1)}, u32[]{:S(2)}, u32[]{:S(2)}) %collective-permute-start) | collective-permute-done | bytes 262176 | tf_op jit(solution)/shard_map/ppermute | solution.py:18
  21.3 10.4 %collective-permute-done.1.refs_2_ = bf16[128,1024]{1,0:T(8,128)(2,1)S(1)} collective-permute-done((bf16[128,1024]{1,0:T(8,128)(2,1)S(1)}, bf16[128,1024]{1,0:T(8,128)(2,1)S(1)}, u32[]{:S(2)}, u32[]{:S(2)}) %collective-permute-start.1) | collective-permute-done | bytes 262176 | tf_op jit(solution)/shard_map/ppermute | solution.py:18
  31.6 1.8 %all-to-all-done = bf16[4,256,1024]{2,1,0:T(8,128)(2,1)S(1)} async-done(((bf16[4,256,1024]{2,1,0:T(8,128)(2,1)}), bf16[4,256,1024]{2,1,0:T(8,128)(2,1)S(1)}, u32[]{:S(2)}, u32[]{:S(2)}) %all-to-all-start) | async-done | bytes 2097184 | tf_op jit(solution)/shard_map/all_to_all | solution.py:224
  33.4 1.6 %score_rows.2 = (f32[4,512,256]{2,1,0:T(8,128)S(1)}, f32[2,4,256]{2,1,0:T(4,128)S(1)}) custom-call(bf16[128,1024]{1,0:T(8,128)(2,1)S(1)} %convert_element_type.21.refs_0_, bf16[128,1024]{1,0:T(8,128)(2,1)S(1)} %collective-permute-done.refs_1_, bf16[128,1024]{1,0:T(8,128)(2,1)S(1)} %collective-permute-done.1.refs_2_, ...), custom_call_target="tpu_custom_call" | custom-call | flops 1073741824 | bytes 3145728 | tf_op jit(solution)/shard_map/score_rows/pallas_call | solution.py:63
  35.1 1.3 %copy-done.2 = f32[4,512,256]{2,1,0:T(8,128)} copy-done((f32[4,512,256]{2,1,0:T(8,128)}, f32[4,512,256]{2,1,0:T(8,128)S(1)}, u32[]{:S(2)}) %copy-start.2) | copy-done | bytes 2097176
  37.6 1.6 %score_rows.3 = (f32[4,512,256]{2,1,0:T(8,128)S(1)}, f32[2,8,256]{2,1,0:T(8,128)S(1)}) custom-call(bf16[128,1024]{1,0:T(8,128)(2,1)S(1)} %convert_element_type.21.refs_0_, bf16[128,1024]{1,0:T(8,128)(2,1)S(1)} %collective-permute-done.refs_1_, bf16[128,1024]{1,0:T(8,128)(2,1)S(1)} %collective-permute-done.1.refs_2_, ...), custom_call_target="tpu_custom_call" | custom-call | flops 1073741824 | bytes 3145728 | tf_op jit(solution)/shard_map/score_rows/pallas_call | solution.py:63
  39.3 1.3 %copy-done = bf16[1024,1024]{1,0:T(8,128)(2,1)} copy-done((bf16[1024,1024]{1,0:T(8,128)(2,1)}, bf16[1024,1024]{1,0:T(8,128)(2,1)S(1)}, u32[]{:S(2)}) %copy-start) | copy-done | bytes 2097176
  40.6 1.3 %copy-done.4 = f32[4,512,256]{2,1,0:T(8,128)} copy-done((f32[4,512,256]{2,1,0:T(8,128)}, f32[4,512,256]{2,1,0:T(8,128)S(1)}, u32[]{:S(2)}) %copy-start.4) | copy-done | bytes 2097176
  42.6 3.4 %all-to-all-start.1 = ((f32[8,2,8,256]{3,2,1,0:T(8,128)}), f32[8,2,8,256]{3,2,1,0:T(8,128)S(1)}, u32[]{:S(2)}, u32[]{:S(2)}) async-start(f32[8,2,8,256]{3,2,1,0:T(8,128)} %broadcast_in_dim.8), calls=%async_computation.1 | async-start | bytes 262144 | tf_op jit(solution)/shard_map/all_to_all | solution.py:121
  45.9 5.5 %all-to-all-done.1.all_ref = f32[8,2,8,256]{3,2,1,0:T(8,128)S(1)} async-done(((f32[8,2,8,256]{3,2,1,0:T(8,128)}), f32[8,2,8,256]{3,2,1,0:T(8,128)S(1)}, u32[]{:S(2)}, u32[]{:S(2)}) %all-to-all-start.1) | async-done | bytes 131104 | tf_op jit(solution)/shard_map/all_to_all | solution.py:121
  51.5 1.6 %copy-done.1 = bf16[1024,1024]{1,0:T(8,128)(2,1)S(1)} copy-done((bf16[1024,1024]{1,0:T(8,128)(2,1)S(1)}, bf16[1024,1024]{1,0:T(8,128)(2,1)}, u32[]{:S(2)}) %copy-start.1) | copy-done | bytes 2097176
  53.0 1.6 %copy-done.3 = f32[4,512,256]{2,1,0:T(8,128)S(1)} copy-done((f32[4,512,256]{2,1,0:T(8,128)S(1)}, f32[4,512,256]{2,1,0:T(8,128)}, u32[]{:S(2)}) %copy-start.3) | copy-done | bytes 2097176
  54.6 1.6 %copy-done.5 = f32[4,512,256]{2,1,0:T(8,128)S(1)} copy-done((f32[4,512,256]{2,1,0:T(8,128)S(1)}, f32[4,512,256]{2,1,0:T(8,128)}, u32[]{:S(2)}) %copy-start.5) | copy-done | bytes 2097176
  57.2 3.5 %collective-permute-start.4 = (f16[136,1024]{1,0:T(8,128)(2,1)S(1)}, f16[136,1024]{1,0:T(8,128)(2,1)S(1)}, u32[]{:S(2)}, u32[]{:S(2)}) collective-permute-start(f16[136,1024]{1,0:T(8,128)(2,1)S(1)} %convert_element_type.22), channel_id=1, source_target_pairs={{0,8},{8,0},{16,24},{24,16},{1,9},{9,1},{17,25},{25,17},{2,10},{10... | collective-permute-start | bytes 835592 | tf_op jit(solution)/shard_map/ppermute | solution.py:18
  60.7 2.4 %weighted_sums.2 = (f32[136,1024]{1,0:T(8,128)S(1)}, f32[136,1024]{1,0:T(8,128)S(1)}, f32[136,1024]{1,0:T(8,128)S(1)}) custom-call(f32[8,256]{1,0:T(8,128)S(1)} %join_rows.1.lognorm_ref, f32[4,512,256]{2,1,0:T(8,128)S(1)} %copy-done.3, f32[4,512,256]{2,1,0:T(8,128)S(1)} %copy-done.5, bf16[1024,1024]{1,0:T(8,128)(2,1)S(1)} %bitcast.11, ...), custom_call_target="tpu_custom_call" | custom-call | flops 1610612736 | bytes 4194304 | tf_op jit(solution)/shard_map/weighted_sums/pallas_call | solution.py:200
  63.1 4.0 %collective-permute-done.4 = f16[136,1024]{1,0:T(8,128)(2,1)S(1)} collective-permute-done((f16[136,1024]{1,0:T(8,128)(2,1)S(1)}, f16[136,1024]{1,0:T(8,128)(2,1)S(1)}, u32[]{:S(2)}, u32[]{:S(2)}) %collective-permute-start.4) | collective-permute-done | bytes 278560 | tf_op jit(solution)/shard_map/ppermute | solution.py:18
  67.4 1.8 %collective-permute-start.5 = (f16[136,1024]{1,0:T(8,128)(2,1)S(1)}, f16[136,1024]{1,0:T(8,128)(2,1)S(1)}, u32[]{:S(2)}, u32[]{:S(2)}) collective-permute-start(f16[136,1024]{1,0:T(8,128)(2,1)S(1)} %convert_element_type.24), channel_id=1, source_target_pairs={{0,8},{8,0},{16,24},{24,16},{1,9},{9,1},{17,25},{25,17},{2,10},{10... | collective-permute-start | bytes 835592 | tf_op jit(solution)/shard_map/ppermute | solution.py:18
  69.3 1.4 %collective-permute-start.6 = (f16[136,1024]{1,0:T(8,128)(2,1)S(1)}, f16[136,1024]{1,0:T(8,128)(2,1)S(1)}, u32[]{:S(2)}, u32[]{:S(2)}) collective-permute-start(f16[136,1024]{1,0:T(8,128)(2,1)S(1)} %convert_element_type.26), channel_id=1, source_target_pairs={{0,16},{8,24},{16,0},{24,8},{1,17},{9,25},{17,1},{25,9},{2,18},{10... | collective-permute-start | bytes 835592 | tf_op jit(solution)/shard_map/ppermute | solution.py:18
  71.2 9.6 %collective-permute-done.5 = f16[136,1024]{1,0:T(8,128)(2,1)S(1)} collective-permute-done((f16[136,1024]{1,0:T(8,128)(2,1)S(1)}, f16[136,1024]{1,0:T(8,128)(2,1)S(1)}, u32[]{:S(2)}, u32[]{:S(2)}) %collective-permute-start.5) | collective-permute-done | bytes 278560 | tf_op jit(solution)/shard_map/ppermute | solution.py:18
  80.9 2.4 %collective-permute-done.6 = f16[136,1024]{1,0:T(8,128)(2,1)S(1)} collective-permute-done((f16[136,1024]{1,0:T(8,128)(2,1)S(1)}, f16[136,1024]{1,0:T(8,128)(2,1)S(1)}, u32[]{:S(2)}, u32[]{:S(2)}) %collective-permute-start.6) | collective-permute-done | bytes 278560 | tf_op jit(solution)/shard_map/ppermute | solution.py:18
  (30 shorter events, 5.6 us)
Async XLA Ops:
  3.3 5.3 %copy-start.6 = (f32[128,1024]{1,0:T(8,128)S(1)}, f32[128,1024]{1,0:T(8,128)}, u32[]{:S(2)}) copy-start(f32[128,1024]{1,0:T(8,128)} %param.3) | copy-start | bytes 1572868
  3.3 30.2 %all-to-all-start = ((bf16[4,256,1024]{2,1,0:T(8,128)(2,1)}), bf16[4,256,1024]{2,1,0:T(8,128)(2,1)S(1)}, u32[]{:S(2)}, u32[]{:S(2)}) async-start(bf16[4,256,1024]{2,1,0:T(8,128)(2,1)} %broadcast_in_dim.7), calls=%async_computation | async-start | bytes 4194304 | tf_op jit(solution)/shard_map/all_to_all | solution.py:224
  8.6 12.6 %collective-permute-start = (bf16[128,1024]{1,0:T(8,128)(2,1)S(1)}, bf16[128,1024]{1,0:T(8,128)(2,1)S(1)}, u32[]{:S(2)}, u32[]{:S(2)}) collective-permute-start(bf16[128,1024]{1,0:T(8,128)(2,1)S(1)} %convert_element_type.21.refs_0_), channel_id=1, source_target_pairs={{0,8},{8,0},{16,24},{24,16},{1,9},{9,1},{17,25},{25,17},{2,10},{10... | collective-permute-start | bytes 786440 | tf_op jit(solution)/shard_map/ppermute | solution.py:18
  10.3 21.4 %collective-permute-start.1 = (bf16[128,1024]{1,0:T(8,128)(2,1)S(1)}, bf16[128,1024]{1,0:T(8,128)(2,1)S(1)}, u32[]{:S(2)}, u32[]{:S(2)}) collective-permute-start(bf16[128,1024]{1,0:T(8,128)(2,1)S(1)} %convert_element_type.21.refs_0_), channel_id=1, source_target_pairs={{0,16},{8,24},{16,0},{24,8},{1,17},{9,25},{17,1},{25,9},{2,18},{10... | collective-permute-start | bytes 786440 | tf_op jit(solution)/shard_map/ppermute | solution.py:18
  12.8 18.8 %collective-permute-start.2 = (bf16[128,1024]{1,0:T(8,128)(2,1)S(1)}, bf16[128,1024]{1,0:T(8,128)(2,1)S(1)}, u32[]{:S(2)}, u32[]{:S(2)}) collective-permute-start(bf16[128,1024]{1,0:T(8,128)(2,1)S(1)} %convert_element_type.21.refs_0_), channel_id=1, source_target_pairs={{0,24},{8,16},{16,8},{24,0},{1,25},{9,17},{17,9},{25,1},{2,26},{10... | collective-permute-start | bytes 786440 | tf_op jit(solution)/shard_map/ppermute | solution.py:18
  33.4 4.2 %collective-permute-start.3 = (bf16[1024,1024]{1,0:T(8,128)(2,1)S(1)}, bf16[1024,1024]{1,0:T(8,128)(2,1)S(1)}, u32[]{:S(2)}, u32[]{:S(2)}) collective-permute-start(bf16[1024,1024]{1,0:T(8,128)(2,1)S(1)} %bitcast.8), channel_id=1, source_target_pairs={{0,1},{1,0},{2,3},{3,2},{4,5},{5,4},{6,7},{7,6},{8,9},{9,8},{10,11... | collective-permute-start | bytes 6291464 | tf_op jit(solution)/shard_map/ppermute | solution.py:18
  35.1 1.3 %copy-start.2 = (f32[4,512,256]{2,1,0:T(8,128)}, f32[4,512,256]{2,1,0:T(8,128)S(1)}, u32[]{:S(2)}) copy-start(f32[4,512,256]{2,1,0:T(8,128)S(1)} %get-tuple-element.24.refs_0_) | copy-start | bytes 6291460
  39.3 1.3 %copy-start = (bf16[1024,1024]{1,0:T(8,128)(2,1)}, bf16[1024,1024]{1,0:T(8,128)(2,1)S(1)}, u32[]{:S(2)}) copy-start(bf16[1024,1024]{1,0:T(8,128)(2,1)S(1)} %collective-permute-done.3.refs_4_.refs_3_) | copy-start | bytes 6291460
  40.6 1.3 %copy-start.4 = (f32[4,512,256]{2,1,0:T(8,128)}, f32[4,512,256]{2,1,0:T(8,128)S(1)}, u32[]{:S(2)}) copy-start(f32[4,512,256]{2,1,0:T(8,128)S(1)} %get-tuple-element.25.refs_1_) | copy-start | bytes 6291460
  42.6 8.8 %all-to-all-start.1 = ((f32[8,2,8,256]{3,2,1,0:T(8,128)}), f32[8,2,8,256]{3,2,1,0:T(8,128)S(1)}, u32[]{:S(2)}, u32[]{:S(2)}) async-start(f32[8,2,8,256]{3,2,1,0:T(8,128)} %broadcast_in_dim.8), calls=%async_computation.1 | async-start | bytes 262144 | tf_op jit(solution)/shard_map/all_to_all | solution.py:121
  51.4 1.6 %copy-start.1 = (bf16[1024,1024]{1,0:T(8,128)(2,1)S(1)}, bf16[1024,1024]{1,0:T(8,128)(2,1)}, u32[]{:S(2)}) copy-start(bf16[1024,1024]{1,0:T(8,128)(2,1)} %copy-done) | copy-start | bytes 6291460
  53.0 1.6 %copy-start.3 = (f32[4,512,256]{2,1,0:T(8,128)S(1)}, f32[4,512,256]{2,1,0:T(8,128)}, u32[]{:S(2)}) copy-start(f32[4,512,256]{2,1,0:T(8,128)} %copy-done.2) | copy-start | bytes 6291460
  54.6 1.6 %copy-start.5 = (f32[4,512,256]{2,1,0:T(8,128)S(1)}, f32[4,512,256]{2,1,0:T(8,128)}, u32[]{:S(2)}) copy-start(f32[4,512,256]{2,1,0:T(8,128)} %copy-done.4) | copy-start | bytes 6291460
  57.2 9.9 %collective-permute-start.4 = (f16[136,1024]{1,0:T(8,128)(2,1)S(1)}, f16[136,1024]{1,0:T(8,128)(2,1)S(1)}, u32[]{:S(2)}, u32[]{:S(2)}) collective-permute-start(f16[136,1024]{1,0:T(8,128)(2,1)S(1)} %convert_element_type.22), channel_id=1, source_target_pairs={{0,8},{8,0},{16,24},{24,16},{1,9},{9,1},{17,25},{25,17},{2,10},{10... | collective-permute-start | bytes 835592 | tf_op jit(solution)/shard_map/ppermute | solution.py:18
  67.4 16.5 %copy-start.7 = (f32[128,1024]{1,0:T(8,128)S(1)}, f32[128,1024]{1,0:T(8,128)}, u32[]{:S(2)}) copy-start(f32[128,1024]{1,0:T(8,128)} %param.3) | copy-start | bytes 1572868
  67.4 13.4 %collective-permute-start.5 = (f16[136,1024]{1,0:T(8,128)(2,1)S(1)}, f16[136,1024]{1,0:T(8,128)(2,1)S(1)}, u32[]{:S(2)}, u32[]{:S(2)}) collective-permute-start(f16[136,1024]{1,0:T(8,128)(2,1)S(1)} %convert_element_type.24), channel_id=1, source_target_pairs={{0,8},{8,0},{16,24},{24,16},{1,9},{9,1},{17,25},{25,17},{2,10},{10... | collective-permute-start | bytes 835592 | tf_op jit(solution)/shard_map/ppermute | solution.py:18
  69.3 14.0 %collective-permute-start.6 = (f16[136,1024]{1,0:T(8,128)(2,1)S(1)}, f16[136,1024]{1,0:T(8,128)(2,1)S(1)}, u32[]{:S(2)}, u32[]{:S(2)}) collective-permute-start(f16[136,1024]{1,0:T(8,128)(2,1)S(1)} %convert_element_type.26), channel_id=1, source_target_pairs={{0,16},{8,24},{16,0},{24,8},{1,17},{9,25},{17,1},{25,9},{2,18},{10... | collective-permute-start | bytes 835592 | tf_op jit(solution)/shard_map/ppermute | solution.py:18

commit v7 on v5

--- a/solution.py
+++ b/solution.py
@@ -192,36 +192,21 @@
         half = own_rows // 2
         from_x = swap(embeddings, "cent", n_cent, 2)
         from_y = swap(embeddings, "cent", n_cent, 4)
-    if n_dp == 4:
-        far = [swap(x, "dp", n_dp, 2) for x in (rounded[: size // 2], rounded[size // 2 :])]
-        near = swap(rounded, "dp", n_dp, 1)
-        most = [rounded, near] + far
-        final = [swap(x, "dp", n_dp, 1) for x in far]
-    else:
-        most = [rounded] + [swap(rounded, "dp", n_dp, m) for m in range(1, n_dp - 1)]
-        final = [swap(rounded, "dp", n_dp, n_dp - 1)]
+    most = [rounded] + [swap(rounded, "dp", n_dp, m) for m in range(1, n_dp - 1)]
+    final = [swap(rounded, "dp", n_dp, n_dp - 1)]
     end = (n_dp - 1) * size
     if n_cent == 8:
-        from_x, from_y, most = lax.optimization_barrier((from_x, from_y, most))
         diag_top = swap(from_x[:half], "cent", n_cent, 4)
         diag_low = swap(from_y[half:], "cent", n_cent, 2)
-        three = jnp.concatenate([embeddings, from_x, from_y], axis=0)
-        give, final[0] = lax.optimization_barrier((three, final[0]))
-        three_core = swap(give, "cent", n_cent, 1)
-        diag = jnp.concatenate([diag_top, diag_low], axis=0)
-        give, final[-1] = lax.optimization_barrier((diag, final[-1]))
-        diag_core = swap(give, "cent", n_cent, 1)
-        rows, order = [three, three_core, diag, diag_core], [0, 2, 4, 1, 3, 5, 6, 7]
-        picks = [(i, j * own_rows) for i in range(2) for j in range(3)] + [(2, 0), (3, 0)]
-        s_0, pair_0 = score(most, rows[:1], own_rows, picks[:3])
-        s_1, pair_1 = score(most, rows[1:2], own_rows, picks[:3])
-        s_2, pair_2 = score(most + final, rows[2:3], own_rows, [(0, 0)])
-        s_3, pairs = score(final, rows[:2], own_rows, picks[:6], [pair_0, pair_1])
-        s_4, pairs = score(most + final, rows[3:], own_rows, [(0, 0)], [pairs, pair_2], 7)
-        scores = [s_0, s_1, s_2, s_4]
-        places = [(i, j) for i in range(2) for j in range(3)] + [(2, 0), (3, 0)]
-        last_scores = [s_3, s_2, s_4]
-        last_places = [(0, j, 0) for j in range(6)] + [(1, 0, end), (2, 0, end)]
+        four = jnp.concatenate([embeddings, from_x, from_y, diag_top, diag_low], axis=0)
+        give, most, final = lax.optimization_barrier((four, most, final))
+        rows, order = [four, swap(give, "cent", n_cent, 1)], [0, 2, 4, 6, 1, 3, 5, 7]
+        picks = [(i, j * own_rows) for i in range(2) for j in range(4)]
+        s_0, pairs = score(most + final, rows[:1], own_rows, picks[:4])
+        s_1, pairs = score(most + final, rows[1:], own_rows, picks[:4], [pairs], 4)
+        scores = last_scores = [s_0, s_1]
+        places = [(i, j) for i in range(2) for j in range(4)]
+        last_places = [(i, j, end) for i, j in places]
     else:
         rows = [embeddings] + [swap(embeddings, "cent", n_cent, m) for m in range(1, n_cent)]
         order = list(range(n_cent))

time: 70.8 us -> 70.3 us (level)
  starting transfers between devices: 23.6 us -> 21.3 us
  waiting for transfers between devices: 34.5 us -> 36.4 us
  Pallas kernels: 8.11 us -> 6.87 us
  local copies, waits for them, and re-layouts: 0.77 us -> 1.79 us
    ppermute x17 -> x14, starting transfers between devices: 23.6 us -> 21.3 us  [swap(): return lax.ppermute(x, axis, [(i, i ^ mask) for i in range(size)])]
    ppermute x17 -> x14, waiting for transfers between devices: 34.5 us -> 36.4 us  [swap(): return lax.ppermute(x, axis, [(i, i ^ mask) for i in range(size)])]
    pallas_call x5 -> x2, Pallas kernels: 4.52 us -> 3.31 us  [score(): pl.pallas_call(functools.partial(score_kernel, n_c, len(rows), picks, beg...]
    unnamed x7 -> x6, local copies, waits for them, and re-layouts: 0.1 us -> 1.17 us
  transfers between devices with their start and end apart: 17 -> 14, of which waited for: 11 -> 11; matrix products, arithmetic and copies ran while one was open for 3% -> 4% of each run, Pallas kernels for 9% -> 6%
where the time goes in v7:
time: 70.3 us; the launch traced here: 70.1 us
  waiting for transfers between devices  36.4 us (52%)
  starting transfers between devices  21.3 us (30%)
  Pallas kernels  6.87 us (10%)
  other arithmetic  2.87 us (4%)
  local copies, waits for them, and re-layouts  1.79 us (3%)
  between operations  0.79 us (1%)
    ppermute x14, waiting for transfers between devices, swap(): return lax.ppermute(x, axis, [(i, i ^ mask) for i in range(size)])  36.4 us
    ppermute x14, starting transfers between devices, swap(): return lax.ppermute(x, axis, [(i, i ^ mask) for i in range(size)])  21.3 us
    pallas_call x2, Pallas kernels, weighted(): pl.pallas_call(functools.partial(sums_kernel, len(scores), picks, parts),...  3.37 us
    pallas_call x2, Pallas kernels, score(): pl.pallas_call(functools.partial(score_kernel, n_c, len(rows), picks, beg...  3.31 us
  transfers between devices with their start and end apart: 14, of which 11 were waited for; matrix products, arithmetic and copies ran while one was open for 4% of the time, Pallas kernels for 6%

profile of v7, /device:TPU:0, one launch (start us, length us, event | category | flops | bytes accessed | tf_op | source)
XLA Modules:
  0.0 70.1 jit_solution(759634519397494207)
XLA Ops:
  0.6 3.0 %collective-permute-start = (bf16[256,1024]{1,0:T(8,128)(2,1)}, bf16[256,1024]{1,0:T(8,128)(2,1)S(1)}, u32[]{:S(2)}, u32[]{:S(2)}) collective-permute-start(bf16[256,1024]{1,0:T(8,128)(2,1)} %param.2), channel_id=1, source_target_pairs={{0,2},{1,3},{2,0},{3,1},{4,6},{5,7},{6,4},{7,5},{8,10},{9,11},{10,... | collective-permute-start | bytes 1572872 | tf_op jit(solution)/shard_map/ppermute | solution.py:18
  3.6 1.5 %collective-permute-start.1 = (bf16[256,1024]{1,0:T(8,128)(2,1)}, bf16[256,1024]{1,0:T(8,128)(2,1)S(1)}, u32[]{:S(2)}, u32[]{:S(2)}) collective-permute-start(bf16[256,1024]{1,0:T(8,128)(2,1)} %param.2), channel_id=1, source_target_pairs={{0,4},{1,5},{2,6},{3,7},{4,0},{5,1},{6,2},{7,3},{8,12},{9,13},{10,... | collective-permute-start | bytes 1572872 | tf_op jit(solution)/shard_map/ppermute | solution.py:18
  5.2 1.1 %convert_element_type.21.refs_0_ = bf16[128,1024]{1,0:T(8,128)(2,1)S(1)} convert(f32[128,1024]{1,0:T(8,128)} %param.3) | non-fusion elementwise | flops 131072 | bytes 786432 | tf_op jit(solution)/shard_map/convert_element_type | solution.py:190
  6.2 1.6 %collective-permute-start.4 = (bf16[128,1024]{1,0:T(8,128)(2,1)S(1)}, bf16[128,1024]{1,0:T(8,128)(2,1)S(1)}, u32[]{:S(2)}, u32[]{:S(2)}) collective-permute-start(bf16[128,1024]{1,0:T(8,128)(2,1)S(1)} %convert_element_type.21.refs_0_), channel_id=1, source_target_pairs={{0,8},{8,0},{16,24},{24,16},{1,9},{9,1},{17,25},{25,17},{2,10},{10... | collective-permute-start | bytes 786440 | tf_op jit(solution)/shard_map/ppermute | solution.py:18
  7.9 2.6 %collective-permute-start.5 = (bf16[128,1024]{1,0:T(8,128)(2,1)S(1)}, bf16[128,1024]{1,0:T(8,128)(2,1)S(1)}, u32[]{:S(2)}, u32[]{:S(2)}) collective-permute-start(bf16[128,1024]{1,0:T(8,128)(2,1)S(1)} %convert_element_type.21.refs_0_), channel_id=1, source_target_pairs={{0,16},{8,24},{16,0},{24,8},{1,17},{9,25},{17,1},{25,9},{2,18},{10... | collective-permute-start | bytes 786440 | tf_op jit(solution)/shard_map/ppermute | solution.py:18
  10.7 5.1 %collective-permute-done = bf16[256,1024]{1,0:T(8,128)(2,1)S(1)} collective-permute-done((bf16[256,1024]{1,0:T(8,128)(2,1)}, bf16[256,1024]{1,0:T(8,128)(2,1)S(1)}, u32[]{:S(2)}, u32[]{:S(2)}) %collective-permute-start) | collective-permute-done | bytes 524320 | tf_op jit(solution)/shard_map/ppermute | solution.py:18
  15.8 1.8 %collective-permute-start.2 = (bf16[128,1024]{1,0:T(8,128)(2,1)S(1)}, bf16[128,1024]{1,0:T(8,128)(2,1)S(1)}, u32[]{:S(2)}, u32[]{:S(2)}) collective-permute-start(bf16[128,1024]{1,0:T(8,128)(2,1)S(1)} %slice.68), channel_id=1, source_target_pairs={{0,4},{1,5},{2,6},{3,7},{4,0},{5,1},{6,2},{7,3},{8,12},{9,13},{10,... | collective-permute-start | bytes 786440 | tf_op jit(solution)/shard_map/ppermute | solution.py:18
  17.6 1.1 %constant_dynamic-update-slice_fusion.4 = bf16[1024,1024]{1,0:T(8,128)(2,1)S(1)} fusion(bf16[256,1024]{1,0:T(8,128)(2,1)} %param.2), kind=kLoop, calls=%fused_computation.10 | loop fusion | bytes 1048576
  18.7 1.6 %collective-permute-start.3 = (bf16[128,1024]{1,0:T(8,128)(2,1)S(1)}, bf16[128,1024]{1,0:T(8,128)(2,1)S(1)}, u32[]{:S(2)}, u32[]{:S(2)}) collective-permute-start(bf16[128,1024]{1,0:T(8,128)(2,1)S(1)} %slice.69), channel_id=1, source_target_pairs={{0,2},{1,3},{2,0},{3,1},{4,6},{5,7},{6,4},{7,5},{8,10},{9,11},{10,... | collective-permute-start | bytes 786440 | tf_op jit(solution)/shard_map/ppermute | solution.py:18
  20.4 3.0 %collective-permute-done.2 = bf16[128,1024]{1,0:T(8,128)(2,1)S(1)} collective-permute-done((bf16[128,1024]{1,0:T(8,128)(2,1)S(1)}, bf16[128,1024]{1,0:T(8,128)(2,1)S(1)}, u32[]{:S(2)}, u32[]{:S(2)}) %collective-permute-start.2) | collective-permute-done | bytes 262176 | tf_op jit(solution)/shard_map/ppermute | solution.py:18
  23.4 2.3 %collective-permute-done.3 = bf16[128,1024]{1,0:T(8,128)(2,1)S(1)} collective-permute-done((bf16[128,1024]{1,0:T(8,128)(2,1)S(1)}, bf16[128,1024]{1,0:T(8,128)(2,1)S(1)}, u32[]{:S(2)}, u32[]{:S(2)}) %collective-permute-start.3) | collective-permute-done | bytes 262176 | tf_op jit(solution)/shard_map/ppermute | solution.py:18
  25.7 3.5 %collective-permute-done.5.refs_2_ = bf16[128,1024]{1,0:T(8,128)(2,1)S(1)} collective-permute-done((bf16[128,1024]{1,0:T(8,128)(2,1)S(1)}, bf16[128,1024]{1,0:T(8,128)(2,1)S(1)}, u32[]{:S(2)}, u32[]{:S(2)}) %collective-permute-start.5) | collective-permute-done | bytes 262176 | tf_op jit(solution)/shard_map/ppermute | solution.py:18
  29.3 1.7 %score_rows.2 = (f32[4,512,256]{2,1,0:T(8,128)S(1)}, f32[2,4,256]{2,1,0:T(4,128)S(1)}) custom-call(bf16[128,1024]{1,0:T(8,128)(2,1)S(1)} %convert_element_type.21.refs_0_, bf16[128,1024]{1,0:T(8,128)(2,1)S(1)} %collective-permute-done.4.refs_1_, bf16[128,1024]{1,0:T(8,128)(2,1)S(1)} %collective-permute-done.5.refs_2_, ...), custom_call_target="tpu_custom_call" | custom-call | flops 1073741824 | bytes 3145728 | tf_op jit(solution)/shard_map/score_rows/pallas_call | solution.py:63
  30.9 2.5 %collective-permute-done.7.refs_4_.refs_3_ = bf16[1024,1024]{1,0:T(8,128)(2,1)S(1)} collective-permute-done((bf16[1024,1024]{1,0:T(8,128)(2,1)S(1)}, bf16[1024,1024]{1,0:T(8,128)(2,1)S(1)}, u32[]{:S(2)}, u32[]{:S(2)}) %collective-permute-start.7) | collective-permute-done | bytes 2097184 | tf_op jit(solution)/shard_map/ppermute | solution.py:18
  33.4 1.7 %score_rows.3 = (f32[4,512,256]{2,1,0:T(8,128)S(1)}, f32[2,8,256]{2,1,0:T(8,128)S(1)}) custom-call(bf16[128,1024]{1,0:T(8,128)(2,1)S(1)} %convert_element_type.21.refs_0_, bf16[128,1024]{1,0:T(8,128)(2,1)S(1)} %collective-permute-done.4.refs_1_, bf16[128,1024]{1,0:T(8,128)(2,1)S(1)} %collective-permute-done.5.refs_2_, ...), custom_call_target="tpu_custom_call" | custom-call | flops 1073741824 | bytes 3145728 | tf_op jit(solution)/shard_map/score_rows/pallas_call | solution.py:63
  36.9 3.2 %collective-permute-done.9.other_ref = f32[2,8,256]{2,1,0:T(8,128)S(1)} collective-permute-done((f32[2,8,256]{2,1,0:T(8,128)S(1)}, f32[2,8,256]{2,1,0:T(8,128)S(1)}, u32[]{:S(2)}, u32[]{:S(2)}) %collective-permute-start.9) | collective-permute-done | bytes 16416 | tf_op jit(solution)/shard_map/ppermute | solution.py:18
  40.7 3.2 %collective-permute-done.10.other_ref = f32[2,8,256]{2,1,0:T(8,128)S(1)} collective-permute-done((f32[2,8,256]{2,1,0:T(8,128)S(1)}, f32[2,8,256]{2,1,0:T(8,128)S(1)}, u32[]{:S(2)}, u32[]{:S(2)}) %collective-permute-start.10) | collective-permute-done | bytes 16416 | tf_op jit(solution)/shard_map/ppermute | solution.py:18
  45.0 4.3 %collective-permute-start.11 = (f16[136,1024]{1,0:T(8,128)(2,1)S(1)}, f16[136,1024]{1,0:T(8,128)(2,1)S(1)}, u32[]{:S(2)}, u32[]{:S(2)}) collective-permute-start(f16[136,1024]{1,0:T(8,128)(2,1)S(1)} %convert_element_type.22), channel_id=1, source_target_pairs={{0,8},{8,0},{16,24},{24,16},{1,9},{9,1},{17,25},{25,17},{2,10},{10... | collective-permute-start | bytes 835592 | tf_op jit(solution)/shard_map/ppermute | solution.py:18
  49.2 2.4 %weighted_sums.2 = (f32[136,1024]{1,0:T(8,128)S(1)}, f32[136,1024]{1,0:T(8,128)S(1)}, f32[136,1024]{1,0:T(8,128)S(1)}) custom-call(f32[8,256]{1,0:T(8,128)S(1)} %join_rows.5.lognorm_ref, f32[4,512,256]{2,1,0:T(8,128)S(1)} %get-tuple-element.24.refs_0_, f32[4,512,256]{2,1,0:T(8,128)S(1)} %get-tuple-element.25.refs_1_, ...), custom_call_target="tpu_custom_call" | custom-call | flops 1610612736 | bytes 4194304 | tf_op jit(solution)/shard_map/weighted_sums/pallas_call | solution.py:171
  51.7 2.3 %collective-permute-done.11 = f16[136,1024]{1,0:T(8,128)(2,1)S(1)} collective-permute-done((f16[136,1024]{1,0:T(8,128)(2,1)S(1)}, f16[136,1024]{1,0:T(8,128)(2,1)S(1)}, u32[]{:S(2)}, u32[]{:S(2)}) %collective-permute-start.11) | collective-permute-done | bytes 278560 | tf_op jit(solution)/shard_map/ppermute | solution.py:18
  54.2 2.2 %collective-permute-start.12 = (f16[136,1024]{1,0:T(8,128)(2,1)S(1)}, f16[136,1024]{1,0:T(8,128)(2,1)S(1)}, u32[]{:S(2)}, u32[]{:S(2)}) collective-permute-start(f16[136,1024]{1,0:T(8,128)(2,1)S(1)} %convert_element_type.24), channel_id=1, source_target_pairs={{0,8},{8,0},{16,24},{24,16},{1,9},{9,1},{17,25},{25,17},{2,10},{10... | collective-permute-start | bytes 835592 | tf_op jit(solution)/shard_map/ppermute | solution.py:18
  56.5 1.1 %collective-permute-start.13 = (f16[136,1024]{1,0:T(8,128)(2,1)S(1)}, f16[136,1024]{1,0:T(8,128)(2,1)S(1)}, u32[]{:S(2)}, u32[]{:S(2)}) collective-permute-start(f16[136,1024]{1,0:T(8,128)(2,1)S(1)} %convert_element_type.26), channel_id=1, source_target_pairs={{0,16},{8,24},{16,0},{24,8},{1,17},{9,25},{17,1},{25,9},{2,18},{10... | collective-permute-start | bytes 835592 | tf_op jit(solution)/shard_map/ppermute | solution.py:18
  58.1 7.7 %collective-permute-done.12 = f16[136,1024]{1,0:T(8,128)(2,1)S(1)} collective-permute-done((f16[136,1024]{1,0:T(8,128)(2,1)S(1)}, f16[136,1024]{1,0:T(8,128)(2,1)S(1)}, u32[]{:S(2)}, u32[]{:S(2)}) %collective-permute-start.12) | collective-permute-done | bytes 278560 | tf_op jit(solution)/shard_map/ppermute | solution.py:18
  65.9 2.6 %collective-permute-done.13 = f16[136,1024]{1,0:T(8,128)(2,1)S(1)} collective-permute-done((f16[136,1024]{1,0:T(8,128)(2,1)S(1)}, f16[136,1024]{1,0:T(8,128)(2,1)S(1)}, u32[]{:S(2)}, u32[]{:S(2)}) %collective-permute-start.13) | collective-permute-done | bytes 278560 | tf_op jit(solution)/shard_map/ppermute | solution.py:18
  (33 shorter events, 6.3 us)
Async XLA Ops:
  0.6 15.1 %collective-permute-start = (bf16[256,1024]{1,0:T(8,128)(2,1)}, bf16[256,1024]{1,0:T(8,128)(2,1)S(1)}, u32[]{:S(2)}, u32[]{:S(2)}) collective-permute-start(bf16[256,1024]{1,0:T(8,128)(2,1)} %param.2), channel_id=1, source_target_pairs={{0,2},{1,3},{2,0},{3,1},{4,6},{5,7},{6,4},{7,5},{8,10},{9,11},{10,... | collective-permute-start | bytes 1572872 | tf_op jit(solution)/shard_map/ppermute | solution.py:18
  3.6 15.1 %collective-permute-start.1 = (bf16[256,1024]{1,0:T(8,128)(2,1)}, bf16[256,1024]{1,0:T(8,128)(2,1)S(1)}, u32[]{:S(2)}, u32[]{:S(2)}) collective-permute-start(bf16[256,1024]{1,0:T(8,128)(2,1)} %param.2), channel_id=1, source_target_pairs={{0,4},{1,5},{2,6},{3,7},{4,0},{5,1},{6,2},{7,3},{8,12},{9,13},{10,... | collective-permute-start | bytes 1572872 | tf_op jit(solution)/shard_map/ppermute | solution.py:18
  6.2 19.5 %collective-permute-start.4 = (bf16[128,1024]{1,0:T(8,128)(2,1)S(1)}, bf16[128,1024]{1,0:T(8,128)(2,1)S(1)}, u32[]{:S(2)}, u32[]{:S(2)}) collective-permute-start(bf16[128,1024]{1,0:T(8,128)(2,1)S(1)} %convert_element_type.21.refs_0_), channel_id=1, source_target_pairs={{0,8},{8,0},{16,24},{24,16},{1,9},{9,1},{17,25},{25,17},{2,10},{10... | collective-permute-start | bytes 786440 | tf_op jit(solution)/shard_map/ppermute | solution.py:18
  7.9 21.4 %collective-permute-start.5 = (bf16[128,1024]{1,0:T(8,128)(2,1)S(1)}, bf16[128,1024]{1,0:T(8,128)(2,1)S(1)}, u32[]{:S(2)}, u32[]{:S(2)}) collective-permute-start(bf16[128,1024]{1,0:T(8,128)(2,1)S(1)} %convert_element_type.21.refs_0_), channel_id=1, source_target_pairs={{0,16},{8,24},{16,0},{24,8},{1,17},{9,25},{17,1},{25,9},{2,18},{10... | collective-permute-start | bytes 786440 | tf_op jit(solution)/shard_map/ppermute | solution.py:18
  10.5 18.8 %collective-permute-start.6 = (bf16[128,1024]{1,0:T(8,128)(2,1)S(1)}, bf16[128,1024]{1,0:T(8,128)(2,1)S(1)}, u32[]{:S(2)}, u32[]{:S(2)}) collective-permute-start(bf16[128,1024]{1,0:T(8,128)(2,1)S(1)} %convert_element_type.21.refs_0_), channel_id=1, source_target_pairs={{0,24},{8,16},{16,8},{24,0},{1,25},{9,17},{17,9},{25,1},{2,26},{10... | collective-permute-start | bytes 786440 | tf_op jit(solution)/shard_map/ppermute | solution.py:18
  15.8 7.6 %collective-permute-start.2 = (bf16[128,1024]{1,0:T(8,128)(2,1)S(1)}, bf16[128,1024]{1,0:T(8,128)(2,1)S(1)}, u32[]{:S(2)}, u32[]{:S(2)}) collective-permute-start(bf16[128,1024]{1,0:T(8,128)(2,1)S(1)} %slice.68), channel_id=1, source_target_pairs={{0,4},{1,5},{2,6},{3,7},{4,0},{5,1},{6,2},{7,3},{8,12},{9,13},{10,... | collective-permute-start | bytes 786440 | tf_op jit(solution)/shard_map/ppermute | solution.py:18
  18.7 7.0 %collective-permute-start.3 = (bf16[128,1024]{1,0:T(8,128)(2,1)S(1)}, bf16[128,1024]{1,0:T(8,128)(2,1)S(1)}, u32[]{:S(2)}, u32[]{:S(2)}) collective-permute-start(bf16[128,1024]{1,0:T(8,128)(2,1)S(1)} %slice.69), channel_id=1, source_target_pairs={{0,2},{1,3},{2,0},{3,1},{4,6},{5,7},{6,4},{7,5},{8,10},{9,11},{10,... | collective-permute-start | bytes 786440 | tf_op jit(solution)/shard_map/ppermute | solution.py:18
  29.3 4.2 %collective-permute-start.7 = (bf16[1024,1024]{1,0:T(8,128)(2,1)S(1)}, bf16[1024,1024]{1,0:T(8,128)(2,1)S(1)}, u32[]{:S(2)}, u32[]{:S(2)}) collective-permute-start(bf16[1024,1024]{1,0:T(8,128)(2,1)S(1)} %constant_dynamic-update-slice_fusion.refs_4_.refs_2_), channel_id=1, source_target_pairs={{0,1},{1,0},{2,3},{3,2},{4,5},{5,4},{6,7},{7,6},{8,9},{9,8},{10,11... | collective-permute-start | bytes 6291464 | tf_op jit(solution)/shard_map/ppermute | solution.py:18
  35.1 1.2 %collective-permute-start.8 = (f32[2,8,256]{2,1,0:T(8,128)S(1)}, f32[2,8,256]{2,1,0:T(8,128)S(1)}, u32[]{:S(2)}, u32[]{:S(2)}) collective-permute-start(f32[2,8,256]{2,1,0:T(8,128)S(1)} %get-tuple-element.23.pair_ref), channel_id=1, source_target_pairs={{0,1},{1,0},{2,3},{3,2},{4,5},{5,4},{6,7},{7,6},{8,9},{9,8},{10,11... | collective-permute-start | bytes 49160 | tf_op jit(solution)/shard_map/ppermute | solution.py:18
  36.3 3.8 %collective-permute-start.9 = (f32[2,8,256]{2,1,0:T(8,128)S(1)}, f32[2,8,256]{2,1,0:T(8,128)S(1)}, u32[]{:S(2)}, u32[]{:S(2)}) collective-permute-start(f32[2,8,256]{2,1,0:T(8,128)S(1)} %join_rows.3.pair_ref), channel_id=1, source_target_pairs={{0,2},{1,3},{2,0},{3,1},{4,6},{5,7},{6,4},{7,5},{8,10},{9,11},{10,... | collective-permute-start | bytes 49160 | tf_op jit(solution)/shard_map/ppermute | solution.py:18
  40.2 3.8 %collective-permute-start.10 = (f32[2,8,256]{2,1,0:T(8,128)S(1)}, f32[2,8,256]{2,1,0:T(8,128)S(1)}, u32[]{:S(2)}, u32[]{:S(2)}) collective-permute-start(f32[2,8,256]{2,1,0:T(8,128)S(1)} %join_rows.4.pair_ref), channel_id=1, source_target_pairs={{0,4},{1,5},{2,6},{3,7},{4,0},{5,1},{6,2},{7,3},{8,12},{9,13},{10,... | collective-permute-start | bytes 49160 | tf_op jit(solution)/shard_map/ppermute | solution.py:18
  45.0 8.9 %collective-permute-start.11 = (f16[136,1024]{1,0:T(8,128)(2,1)S(1)}, f16[136,1024]{1,0:T(8,128)(2,1)S(1)}, u32[]{:S(2)}, u32[]{:S(2)}) collective-permute-start(f16[136,1024]{1,0:T(8,128)(2,1)S(1)} %convert_element_type.22), channel_id=1, source_target_pairs={{0,8},{8,0},{16,24},{24,16},{1,9},{9,1},{17,25},{25,17},{2,10},{10... | collective-permute-start | bytes 835592 | tf_op jit(solution)/shard_map/ppermute | solution.py:18
  54.1 15.0 %copy-start = (f32[128,1024]{1,0:T(8,128)S(1)}, f32[128,1024]{1,0:T(8,128)}, u32[]{:S(2)}) copy-start(f32[128,1024]{1,0:T(8,128)} %param.3) | copy-start | bytes 1572868
  54.2 11.6 %collective-permute-start.12 = (f16[136,1024]{1,0:T(8,128)(2,1)S(1)}, f16[136,1024]{1,0:T(8,128)(2,1)S(1)}, u32[]{:S(2)}, u32[]{:S(2)}) collective-permute-start(f16[136,1024]{1,0:T(8,128)(2,1)S(1)} %convert_element_type.24), channel_id=1, source_target_pairs={{0,8},{8,0},{16,24},{24,16},{1,9},{9,1},{17,25},{25,17},{2,10},{10... | collective-permute-start | bytes 835592 | tf_op jit(solution)/shard_map/ppermute | solution.py:18
  56.5 12.0 %collective-permute-start.13 = (f16[136,1024]{1,0:T(8,128)(2,1)S(1)}, f16[136,1024]{1,0:T(8,128)(2,1)S(1)}, u32[]{:S(2)}, u32[]{:S(2)}) collective-permute-start(f16[136,1024]{1,0:T(8,128)(2,1)S(1)} %convert_element_type.26), channel_id=1, source_target_pairs={{0,16},{8,24},{16,0},{24,8},{1,17},{9,25},{17,1},{25,9},{2,18},{10... | collective-permute-start | bytes 835592 | tf_op jit(solution)/shard_map/ppermute | solution.py:18

commit v8 on v7

--- a/solution.py
+++ b/solution.py
@@ -78,9 +78,12 @@
     )(*centers, *rows, *early)
 
 
-def join_kernel(places, last, pair_ref, other_ref, out_ref):
-    other = [jnp.concatenate([other_ref[i, p : p + 1] for p in places]) for i in range(2)]
-    top, total = merge((pair_ref[0], pair_ref[1]), other)
+def join_kernel(places, last, pair_ref, *refs):
+    out_ref = refs[-1]
+    top, total = pair_ref[0], pair_ref[1]
+    for ref, where in zip(refs[:-1], places):
+        other = [jnp.concatenate([ref[i, p : p + 1] for p in where]) for i in range(2)]
+        top, total = merge((top, total), other)
     if last:
         out_ref[...] = top + jnp.log(total)
     else:
@@ -88,17 +91,17 @@
         out_ref[1] = total
 
 
-def join(pairs, mask, order, last):
-    other = swap(pairs, "cent", len(order), mask)
-    places = [order.index(j ^ mask) for j in order]
+def join(pairs, masks, order, last):
+    others = [swap(pairs, "cent", len(order), mask) for mask in masks]
+    places = [[order.index(j ^ mask) for j in order] for mask in masks]
     return pl.pallas_call(
         functools.partial(join_kernel, places, last),
         out_shape=jax.ShapeDtypeStruct(pairs.shape[1:] if last else pairs.shape, jnp.float32),
-        in_specs=[VMEM] * 2,
+        in_specs=[VMEM] * (1 + len(others)),
         out_specs=VMEM,
         compiler_params=PARAMS,
         name="join_rows",
-    )(pairs, other)
+    )(pairs, *others)
 
 
 def sums_kernel(n_parts, picks, parts, lognorm_ref, *refs):
@@ -192,8 +195,13 @@
         half = own_rows // 2
         from_x = swap(embeddings, "cent", n_cent, 2)
         from_y = swap(embeddings, "cent", n_cent, 4)
-    most = [rounded] + [swap(rounded, "dp", n_dp, m) for m in range(1, n_dp - 1)]
-    final = [swap(rounded, "dp", n_dp, n_dp - 1)]
+    if n_dp == 4:
+        far = swap(rounded, "dp", n_dp, 2)
+        near = swap(rounded, "dp", n_dp, 1)
+        most, final = [rounded, near, far], [swap(far, "dp", n_dp, 1)]
+    else:
+        most = [rounded] + [swap(rounded, "dp", n_dp, m) for m in range(1, n_dp - 1)]
+        final = [swap(rounded, "dp", n_dp, n_dp - 1)]
     end = (n_dp - 1) * size
     if n_cent == 8:
         diag_top = swap(from_x[:half], "cent", n_cent, 4)
@@ -216,10 +224,10 @@
         places = [(0, j) for j in order]
         s_1, pairs = score(final, rows, own_rows, picks, [pair_0])
         last_scores, last_places = [s_1], [(0, j, 0) for j in order]
-    mask = 1
-    while mask < n_cent:
-        pairs = join(pairs, mask, order, 2 * mask >= n_cent)
-        mask *= 2
+    bits = [1 << i for i in range(n_cent.bit_length() - 1)]
+    rounds = [[1], [2, 4, 6]] if n_cent == 8 else [[bit] for bit in bits]
+    for masks in rounds:
+        pairs = join(pairs, masks, order, masks is rounds[-1])
     lognorm = pairs
 
     def part(k, unit):
@@ -231,9 +239,9 @@
         first = swap(first, "dp", n_dp, 1)
         parts = [part(2, 0), part(1, unit), part(0, 0)]
         far_out, near_out, own = weighted(parts, lognorm, scores, rows, picks)
-        far_out = relay(far_out, first.astype(jnp.float32), unit)
+        far_out = relay(far_out, first.astype(jnp.float32), unit).astype(jnp.float16)
         far_out, near_out = lax.optimization_barrier((far_out, near_out))
-        far_out = swap(far_out.astype(jnp.float16), "dp", n_dp, 2)
+        far_out = swap(far_out, "dp", n_dp, 2)
         near_out = swap(near_out.astype(jnp.float16), "dp", n_dp, 1)
         got = [(near_out, unit), (far_out, unit * 0.5)]
     else:

time: 70.3 us -> 65 us (0.925)
  waiting for transfers between devices: 36.4 us -> 31.9 us
  starting transfers between devices: 21.3 us -> 20 us
    ppermute x14 -> x15, waiting for transfers between devices: 36.4 us -> 31.9 us  [swap(): return lax.ppermute(x, axis, [(i, i ^ mask) for i in range(size)])]
    ppermute x14 -> x15, starting transfers between devices: 21.3 us -> 20 us  [swap(): return lax.ppermute(x, axis, [(i, i ^ mask) for i in range(size)])]
  transfers between devices with their start and end apart: 14 -> 15, of which waited for: 11 -> 11; matrix products, arithmetic and copies ran while one was open for 4% -> 5% of each run, Pallas kernels for 6% -> 6%
where the time goes in v8:
time: 65 us; the launch traced here: 64.2 us
  waiting for transfers between devices  31.9 us (49%)
  starting transfers between devices  20 us (31%)
  Pallas kernels  6.87 us (11%)
  other arithmetic  2.87 us (4%)
  local copies, waits for them, and re-layouts  1.79 us (3%)
  between operations  0.81 us (1%)
    ppermute x15, waiting for transfers between devices, swap(): return lax.ppermute(x, axis, [(i, i ^ mask) for i in range(size)])  31.9 us
    ppermute x15, starting transfers between devices, swap(): return lax.ppermute(x, axis, [(i, i ^ mask) for i in range(size)])  20 us
    pallas_call x2, Pallas kernels, weighted(): pl.pallas_call(functools.partial(sums_kernel, len(scores), picks, parts),...  3.37 us
    pallas_call x2, Pallas kernels, score(): pl.pallas_call(functools.partial(score_kernel, n_c, len(rows), picks, beg...  3.31 us
  transfers between devices with their start and end apart: 15, of which 11 were waited for; matrix products, arithmetic and copies ran while one was open for 5% of the time, Pallas kernels for 6%

profile of v8, /device:TPU:0, one launch (start us, length us, event | category | flops | bytes accessed | tf_op | source)
XLA Modules:
  0.0 64.2 jit_solution(6855334284507259386)
XLA Ops:
  0.6 3.0 %collective-permute-start = (bf16[256,1024]{1,0:T(8,128)(2,1)}, bf16[256,1024]{1,0:T(8,128)(2,1)S(1)}, u32[]{:S(2)}, u32[]{:S(2)}) collective-permute-start(bf16[256,1024]{1,0:T(8,128)(2,1)} %param.2), channel_id=1, source_target_pairs={{0,2},{1,3},{2,0},{3,1},{4,6},{5,7},{6,4},{7,5},{8,10},{9,11},{10,... | collective-permute-start | bytes 1572872 | tf_op jit(solution)/shard_map/ppermute | solution.py:18
  3.6 1.5 %collective-permute-start.1 = (bf16[256,1024]{1,0:T(8,128)(2,1)}, bf16[256,1024]{1,0:T(8,128)(2,1)S(1)}, u32[]{:S(2)}, u32[]{:S(2)}) collective-permute-start(bf16[256,1024]{1,0:T(8,128)(2,1)} %param.2), channel_id=1, source_target_pairs={{0,4},{1,5},{2,6},{3,7},{4,0},{5,1},{6,2},{7,3},{8,12},{9,13},{10,... | collective-permute-start | bytes 1572872 | tf_op jit(solution)/shard_map/ppermute | solution.py:18
  5.2 1.1 %convert_element_type.21.refs_0_ = bf16[128,1024]{1,0:T(8,128)(2,1)S(1)} convert(f32[128,1024]{1,0:T(8,128)} %param.3) | non-fusion elementwise | flops 131072 | bytes 786432 | tf_op jit(solution)/shard_map/convert_element_type | solution.py:193
  6.2 2.7 %collective-permute-start.5 = (bf16[128,1024]{1,0:T(8,128)(2,1)S(1)}, bf16[128,1024]{1,0:T(8,128)(2,1)S(1)}, u32[]{:S(2)}, u32[]{:S(2)}) collective-permute-start(bf16[128,1024]{1,0:T(8,128)(2,1)S(1)} %convert_element_type.21.refs_0_), channel_id=1, source_target_pairs={{0,16},{8,24},{16,0},{24,8},{1,17},{9,25},{17,1},{25,9},{2,18},{10... | collective-permute-start | bytes 786440 | tf_op jit(solution)/shard_map/ppermute | solution.py:18
  8.9 1.6 %collective-permute-start.4 = (bf16[128,1024]{1,0:T(8,128)(2,1)S(1)}, bf16[128,1024]{1,0:T(8,128)(2,1)S(1)}, u32[]{:S(2)}, u32[]{:S(2)}) collective-permute-start(bf16[128,1024]{1,0:T(8,128)(2,1)S(1)} %convert_element_type.21.refs_0_), channel_id=1, source_target_pairs={{0,8},{8,0},{16,24},{24,16},{1,9},{9,1},{17,25},{25,17},{2,10},{10... | collective-permute-start | bytes 786440 | tf_op jit(solution)/shard_map/ppermute | solution.py:18
  10.5 5.3 %collective-permute-done = bf16[256,1024]{1,0:T(8,128)(2,1)S(1)} collective-permute-done((bf16[256,1024]{1,0:T(8,128)(2,1)}, bf16[256,1024]{1,0:T(8,128)(2,1)S(1)}, u32[]{:S(2)}, u32[]{:S(2)}) %collective-permute-start) | collective-permute-done | bytes 524320 | tf_op jit(solution)/shard_map/ppermute | solution.py:18
  15.8 1.8 %collective-permute-start.2 = (bf16[128,1024]{1,0:T(8,128)(2,1)S(1)}, bf16[128,1024]{1,0:T(8,128)(2,1)S(1)}, u32[]{:S(2)}, u32[]{:S(2)}) collective-permute-start(bf16[128,1024]{1,0:T(8,128)(2,1)S(1)} %slice.68), channel_id=1, source_target_pairs={{0,4},{1,5},{2,6},{3,7},{4,0},{5,1},{6,2},{7,3},{8,12},{9,13},{10,... | collective-permute-start | bytes 786440 | tf_op jit(solution)/shard_map/ppermute | solution.py:18
  17.6 1.1 %constant_dynamic-update-slice_fusion.4 = bf16[1024,1024]{1,0:T(8,128)(2,1)S(1)} fusion(bf16[256,1024]{1,0:T(8,128)(2,1)} %param.2), kind=kLoop, calls=%fused_computation.10 | loop fusion | bytes 1048576
  18.7 1.7 %collective-permute-done.5.refs_2_ = bf16[128,1024]{1,0:T(8,128)(2,1)S(1)} collective-permute-done((bf16[128,1024]{1,0:T(8,128)(2,1)S(1)}, bf16[128,1024]{1,0:T(8,128)(2,1)S(1)}, u32[]{:S(2)}, u32[]{:S(2)}) %collective-permute-start.5) | collective-permute-done | bytes 262176 | tf_op jit(solution)/shard_map/ppermute | solution.py:18
  22.0 1.3 %collective-permute-done.2 = bf16[128,1024]{1,0:T(8,128)(2,1)S(1)} collective-permute-done((bf16[128,1024]{1,0:T(8,128)(2,1)S(1)}, bf16[128,1024]{1,0:T(8,128)(2,1)S(1)}, u32[]{:S(2)}, u32[]{:S(2)}) %collective-permute-start.2) | collective-permute-done | bytes 262176 | tf_op jit(solution)/shard_map/ppermute | solution.py:18
  23.4 5.6 %collective-permute-done.3 = bf16[128,1024]{1,0:T(8,128)(2,1)S(1)} collective-permute-done((bf16[128,1024]{1,0:T(8,128)(2,1)S(1)}, bf16[128,1024]{1,0:T(8,128)(2,1)S(1)}, u32[]{:S(2)}, u32[]{:S(2)}) %collective-permute-start.3) | collective-permute-done | bytes 262176 | tf_op jit(solution)/shard_map/ppermute | solution.py:18
  29.1 1.7 %score_rows.2 = (f32[4,512,256]{2,1,0:T(8,128)S(1)}, f32[2,4,256]{2,1,0:T(4,128)S(1)}) custom-call(bf16[128,1024]{1,0:T(8,128)(2,1)S(1)} %convert_element_type.21.refs_0_, bf16[128,1024]{1,0:T(8,128)(2,1)S(1)} %collective-permute-done.4.refs_1_, bf16[128,1024]{1,0:T(8,128)(2,1)S(1)} %collective-permute-done.5.refs_2_, ...), custom_call_target="tpu_custom_call" | custom-call | flops 1073741824 | bytes 3145728 | tf_op jit(solution)/shard_map/score_rows/pallas_call | solution.py:63
  30.8 2.5 %collective-permute-done.7.refs_4_.refs_3_ = bf16[1024,1024]{1,0:T(8,128)(2,1)S(1)} collective-permute-done((bf16[1024,1024]{1,0:T(8,128)(2,1)S(1)}, bf16[1024,1024]{1,0:T(8,128)(2,1)S(1)}, u32[]{:S(2)}, u32[]{:S(2)}) %collective-permute-start.7) | collective-permute-done | bytes 2097184 | tf_op jit(solution)/shard_map/ppermute | solution.py:18
  33.3 1.7 %score_rows.3 = (f32[4,512,256]{2,1,0:T(8,128)S(1)}, f32[2,8,256]{2,1,0:T(8,128)S(1)}) custom-call(bf16[128,1024]{1,0:T(8,128)(2,1)S(1)} %convert_element_type.21.refs_0_, bf16[128,1024]{1,0:T(8,128)(2,1)S(1)} %collective-permute-done.4.refs_1_, bf16[128,1024]{1,0:T(8,128)(2,1)S(1)} %collective-permute-done.5.refs_2_, ...), custom_call_target="tpu_custom_call" | custom-call | flops 1073741824 | bytes 3145728 | tf_op jit(solution)/shard_map/score_rows/pallas_call | solution.py:63
  35.1 1.0 %collective-permute-done.8.refs_0_ = f32[2,8,256]{2,1,0:T(8,128)S(1)} collective-permute-done((f32[2,8,256]{2,1,0:T(8,128)S(1)}, f32[2,8,256]{2,1,0:T(8,128)S(1)}, u32[]{:S(2)}, u32[]{:S(2)}) %collective-permute-start.8) | collective-permute-done | bytes 16416 | tf_op jit(solution)/shard_map/ppermute | solution.py:18
  36.8 1.5 %collective-permute-start.11 = (f32[2,8,256]{2,1,0:T(8,128)S(1)}, f32[2,8,256]{2,1,0:T(8,128)S(1)}, u32[]{:S(2)}, u32[]{:S(2)}) collective-permute-start(f32[2,8,256]{2,1,0:T(8,128)S(1)} %join_rows.2.pair_ref), channel_id=1, source_target_pairs={{0,6},{1,7},{2,4},{3,5},{4,2},{5,3},{6,0},{7,1},{8,14},{9,15},{10,... | collective-permute-start | bytes 49160 | tf_op jit(solution)/shard_map/ppermute | solution.py:18
  38.3 1.5 %collective-permute-start.9 = (f32[2,8,256]{2,1,0:T(8,128)S(1)}, f32[2,8,256]{2,1,0:T(8,128)S(1)}, u32[]{:S(2)}, u32[]{:S(2)}) collective-permute-start(f32[2,8,256]{2,1,0:T(8,128)S(1)} %join_rows.2.pair_ref), channel_id=1, source_target_pairs={{0,2},{1,3},{2,0},{3,1},{4,6},{5,7},{6,4},{7,5},{8,10},{9,11},{10,... | collective-permute-start | bytes 49160 | tf_op jit(solution)/shard_map/ppermute | solution.py:18
  40.0 1.4 %collective-permute-done.11.refs_2_ = f32[2,8,256]{2,1,0:T(8,128)S(1)} collective-permute-done((f32[2,8,256]{2,1,0:T(8,128)S(1)}, f32[2,8,256]{2,1,0:T(8,128)S(1)}, u32[]{:S(2)}, u32[]{:S(2)}) %collective-permute-start.11) | collective-permute-done | bytes 16416 | tf_op jit(solution)/shard_map/ppermute | solution.py:18
  42.0 0.9 %weighted_sums.3 = f32[136,1024]{1,0:T(8,128)S(1)} custom-call(f32[8,256]{1,0:T(8,128)S(1)} %join_rows.3.lognorm_ref, f32[4,512,256]{2,1,0:T(8,128)S(1)} %get-tuple-element.24.refs_0_, f32[4,512,256]{2,1,0:T(8,128)S(1)} %get-tuple-element.25.refs_1_, bf16[1024,1024]{1,0:T(8,128)(2,1)S(1)} %constant_dynamic-update-slice_fusion.refs_4_.refs_2_, ...), custom_call_target="tpu_custom_call" | custom-call | flops 536870912 | bytes 4194304 | tf_op jit(solution)/shard_map/weighted_sums/pallas_call | solution.py:174
  43.4 2.4 %weighted_sums.2 = (f32[136,1024]{1,0:T(8,128)S(1)}, f32[136,1024]{1,0:T(8,128)S(1)}, f32[136,1024]{1,0:T(8,128)S(1)}) custom-call(f32[8,256]{1,0:T(8,128)S(1)} %join_rows.3.lognorm_ref, f32[4,512,256]{2,1,0:T(8,128)S(1)} %get-tuple-element.24.refs_0_, f32[4,512,256]{2,1,0:T(8,128)S(1)} %get-tuple-element.25.refs_1_, ...), custom_call_target="tpu_custom_call" | custom-call | flops 1610612736 | bytes 4194304 | tf_op jit(solution)/shard_map/weighted_sums/pallas_call | solution.py:174
  45.9 4.3 %collective-permute-done.12 = f16[136,1024]{1,0:T(8,128)(2,1)S(1)} collective-permute-done((f16[136,1024]{1,0:T(8,128)(2,1)S(1)}, f16[136,1024]{1,0:T(8,128)(2,1)S(1)}, u32[]{:S(2)}, u32[]{:S(2)}) %collective-permute-start.12) | collective-permute-done | bytes 278560 | tf_op jit(solution)/shard_map/ppermute | solution.py:18
  50.8 3.4 %collective-permute-start.14 = (f16[136,1024]{1,0:T(8,128)(2,1)S(1)}, f16[136,1024]{1,0:T(8,128)(2,1)S(1)}, u32[]{:S(2)}, u32[]{:S(2)}) collective-permute-start(f16[136,1024]{1,0:T(8,128)(2,1)S(1)} %convert_element_type.24), channel_id=1, source_target_pairs={{0,16},{8,24},{16,0},{24,8},{1,17},{9,25},{17,1},{25,9},{2,18},{10... | collective-permute-start | bytes 835592 | tf_op jit(solution)/shard_map/ppermute | solution.py:18
  54.7 7.8 %collective-permute-done.13 = f16[136,1024]{1,0:T(8,128)(2,1)S(1)} collective-permute-done((f16[136,1024]{1,0:T(8,128)(2,1)S(1)}, f16[136,1024]{1,0:T(8,128)(2,1)S(1)}, u32[]{:S(2)}, u32[]{:S(2)}) %collective-permute-start.13) | collective-permute-done | bytes 278560 | tf_op jit(solution)/shard_map/ppermute | solution.py:18
  63.2 1.0 %fusion.2 = f32[128,1024]{1,0:T(8,128)} fusion(f32[128,1024]{1,0:T(8,128)S(1)} %copy-done, f32[136,1024]{1,0:T(8,128)S(1)} %convert_element_type.27, f32[136,1024]{1,0:T(8,128)S(1)} %convert_element_type.26, f32[136,1024]{1,0:T(8,128)S(1)} %get-tuple-element.26, f32[128]{0:T(128)S(1)} %get-tuple-element.31, f32[1024]{0:T(1024)S(1)} %bitcast.7, ...), kind=kLoop, calls=%fused_computation.3 | loop fusion | flops 786432 | bytes 2630144 | tf_op jit(solution)/shard_map/div | solution.py:258
  (34 shorter events, 5.7 us)
Async XLA Ops:
  0.6 15.1 %collective-permute-start = (bf16[256,1024]{1,0:T(8,128)(2,1)}, bf16[256,1024]{1,0:T(8,128)(2,1)S(1)}, u32[]{:S(2)}, u32[]{:S(2)}) collective-permute-start(bf16[256,1024]{1,0:T(8,128)(2,1)} %param.2), channel_id=1, source_target_pairs={{0,2},{1,3},{2,0},{3,1},{4,6},{5,7},{6,4},{7,5},{8,10},{9,11},{10,... | collective-permute-start | bytes 1572872 | tf_op jit(solution)/shard_map/ppermute | solution.py:18
  3.6 17.3 %collective-permute-start.1 = (bf16[256,1024]{1,0:T(8,128)(2,1)}, bf16[256,1024]{1,0:T(8,128)(2,1)S(1)}, u32[]{:S(2)}, u32[]{:S(2)}) collective-permute-start(bf16[256,1024]{1,0:T(8,128)(2,1)} %param.2), channel_id=1, source_target_pairs={{0,4},{1,5},{2,6},{3,7},{4,0},{5,1},{6,2},{7,3},{8,12},{9,13},{10,... | collective-permute-start | bytes 1572872 | tf_op jit(solution)/shard_map/ppermute | solution.py:18
  6.2 14.2 %collective-permute-start.5 = (bf16[128,1024]{1,0:T(8,128)(2,1)S(1)}, bf16[128,1024]{1,0:T(8,128)(2,1)S(1)}, u32[]{:S(2)}, u32[]{:S(2)}) collective-permute-start(bf16[128,1024]{1,0:T(8,128)(2,1)S(1)} %convert_element_type.21.refs_0_), channel_id=1, source_target_pairs={{0,16},{8,24},{16,0},{24,8},{1,17},{9,25},{17,1},{25,9},{2,18},{10... | collective-permute-start | bytes 786440 | tf_op jit(solution)/shard_map/ppermute | solution.py:18
  8.9 20.1 %collective-permute-start.4 = (bf16[128,1024]{1,0:T(8,128)(2,1)S(1)}, bf16[128,1024]{1,0:T(8,128)(2,1)S(1)}, u32[]{:S(2)}, u32[]{:S(2)}) collective-permute-start(bf16[128,1024]{1,0:T(8,128)(2,1)S(1)} %convert_element_type.21.refs_0_), channel_id=1, source_target_pairs={{0,8},{8,0},{16,24},{24,16},{1,9},{9,1},{17,25},{25,17},{2,10},{10... | collective-permute-start | bytes 786440 | tf_op jit(solution)/shard_map/ppermute | solution.py:18
  15.8 7.6 %collective-permute-start.2 = (bf16[128,1024]{1,0:T(8,128)(2,1)S(1)}, bf16[128,1024]{1,0:T(8,128)(2,1)S(1)}, u32[]{:S(2)}, u32[]{:S(2)}) collective-permute-start(bf16[128,1024]{1,0:T(8,128)(2,1)S(1)} %slice.68), channel_id=1, source_target_pairs={{0,4},{1,5},{2,6},{3,7},{4,0},{5,1},{6,2},{7,3},{8,12},{9,13},{10,... | collective-permute-start | bytes 786440 | tf_op jit(solution)/shard_map/ppermute | solution.py:18
  20.4 8.6 %collective-permute-start.6 = (bf16[128,1024]{1,0:T(8,128)(2,1)S(1)}, bf16[128,1024]{1,0:T(8,128)(2,1)S(1)}, u32[]{:S(2)}, u32[]{:S(2)}) collective-permute-start(bf16[128,1024]{1,0:T(8,128)(2,1)S(1)} %collective-permute-done.5.refs_2_), channel_id=1, source_target_pairs={{0,8},{8,0},{16,24},{24,16},{1,9},{9,1},{17,25},{25,17},{2,10},{10... | collective-permute-start | bytes 786440 | tf_op jit(solution)/shard_map/ppermute | solution.py:18
  21.0 8.0 %collective-permute-start.3 = (bf16[128,1024]{1,0:T(8,128)(2,1)S(1)}, bf16[128,1024]{1,0:T(8,128)(2,1)S(1)}, u32[]{:S(2)}, u32[]{:S(2)}) collective-permute-start(bf16[128,1024]{1,0:T(8,128)(2,1)S(1)} %slice.69), channel_id=1, source_target_pairs={{0,2},{1,3},{2,0},{3,1},{4,6},{5,7},{6,4},{7,5},{8,10},{9,11},{10,... | collective-permute-start | bytes 786440 | tf_op jit(solution)/shard_map/ppermute | solution.py:18
  29.1 4.2 %collective-permute-start.7 = (bf16[1024,1024]{1,0:T(8,128)(2,1)S(1)}, bf16[1024,1024]{1,0:T(8,128)(2,1)S(1)}, u32[]{:S(2)}, u32[]{:S(2)}) collective-permute-start(bf16[1024,1024]{1,0:T(8,128)(2,1)S(1)} %constant_dynamic-update-slice_fusion.refs_4_.refs_2_), channel_id=1, source_target_pairs={{0,1},{1,0},{2,3},{3,2},{4,5},{5,4},{6,7},{7,6},{8,9},{9,8},{10,11... | collective-permute-start | bytes 6291464 | tf_op jit(solution)/shard_map/ppermute | solution.py:18
  34.9 1.2 %collective-permute-start.8 = (f32[2,8,256]{2,1,0:T(8,128)S(1)}, f32[2,8,256]{2,1,0:T(8,128)S(1)}, u32[]{:S(2)}, u32[]{:S(2)}) collective-permute-start(f32[2,8,256]{2,1,0:T(8,128)S(1)} %get-tuple-element.23.pair_ref), channel_id=1, source_target_pairs={{0,1},{1,0},{2,3},{3,2},{4,5},{5,4},{6,7},{7,6},{8,9},{9,8},{10,11... | collective-permute-start | bytes 49160 | tf_op jit(solution)/shard_map/ppermute | solution.py:18
  36.2 3.8 %collective-permute-start.10 = (f32[2,8,256]{2,1,0:T(8,128)S(1)}, f32[2,8,256]{2,1,0:T(8,128)S(1)}, u32[]{:S(2)}, u32[]{:S(2)}) collective-permute-start(f32[2,8,256]{2,1,0:T(8,128)S(1)} %join_rows.2.pair_ref), channel_id=1, source_target_pairs={{0,4},{1,5},{2,6},{3,7},{4,0},{5,1},{6,2},{7,3},{8,12},{9,13},{10,... | collective-permute-start | bytes 49160 | tf_op jit(solution)/shard_map/ppermute | solution.py:18
  36.8 4.6 %collective-permute-start.11 = (f32[2,8,256]{2,1,0:T(8,128)S(1)}, f32[2,8,256]{2,1,0:T(8,128)S(1)}, u32[]{:S(2)}, u32[]{:S(2)}) collective-permute-start(f32[2,8,256]{2,1,0:T(8,128)S(1)} %join_rows.2.pair_ref), channel_id=1, source_target_pairs={{0,6},{1,7},{2,4},{3,5},{4,2},{5,3},{6,0},{7,1},{8,14},{9,15},{10,... | collective-permute-start | bytes 49160 | tf_op jit(solution)/shard_map/ppermute | solution.py:18
  38.3 3.7 %collective-permute-start.9 = (f32[2,8,256]{2,1,0:T(8,128)S(1)}, f32[2,8,256]{2,1,0:T(8,128)S(1)}, u32[]{:S(2)}, u32[]{:S(2)}) collective-permute-start(f32[2,8,256]{2,1,0:T(8,128)S(1)} %join_rows.2.pair_ref), channel_id=1, source_target_pairs={{0,2},{1,3},{2,0},{3,1},{4,6},{5,7},{6,4},{7,5},{8,10},{9,11},{10,... | collective-permute-start | bytes 49160 | tf_op jit(solution)/shard_map/ppermute | solution.py:18
  43.0 7.1 %collective-permute-start.12 = (f16[136,1024]{1,0:T(8,128)(2,1)S(1)}, f16[136,1024]{1,0:T(8,128)(2,1)S(1)}, u32[]{:S(2)}, u32[]{:S(2)}) collective-permute-start(f16[136,1024]{1,0:T(8,128)(2,1)S(1)} %convert_element_type.22), channel_id=1, source_target_pairs={{0,8},{8,0},{16,24},{24,16},{1,9},{9,1},{17,25},{25,17},{2,10},{10... | collective-permute-start | bytes 835592 | tf_op jit(solution)/shard_map/ppermute | solution.py:18
  50.3 12.9 %copy-start = (f32[128,1024]{1,0:T(8,128)S(1)}, f32[128,1024]{1,0:T(8,128)}, u32[]{:S(2)}) copy-start(f32[128,1024]{1,0:T(8,128)} %param.3) | copy-start | bytes 1572868
  50.4 12.1 %collective-permute-start.13 = (f16[136,1024]{1,0:T(8,128)(2,1)S(1)}, f16[136,1024]{1,0:T(8,128)(2,1)S(1)}, u32[]{:S(2)}, u32[]{:S(2)}) collective-permute-start(f16[136,1024]{1,0:T(8,128)(2,1)S(1)} %convert_element_type.25), channel_id=1, source_target_pairs={{0,8},{8,0},{16,24},{24,16},{1,9},{9,1},{17,25},{25,17},{2,10},{10... | collective-permute-start | bytes 835592 | tf_op jit(solution)/shard_map/ppermute | solution.py:18
  50.8 11.8 %collective-permute-start.14 = (f16[136,1024]{1,0:T(8,128)(2,1)S(1)}, f16[136,1024]{1,0:T(8,128)(2,1)S(1)}, u32[]{:S(2)}, u32[]{:S(2)}) collective-permute-start(f16[136,1024]{1,0:T(8,128)(2,1)S(1)} %convert_element_type.24), channel_id=1, source_target_pairs={{0,16},{8,24},{16,0},{24,8},{1,17},{9,25},{17,1},{25,9},{2,18},{10... | collective-permute-start | bytes 835592 | tf_op jit(solution)/shard_map/ppermute | solution.py:18

commit v9 on v8

--- a/solution.py
+++ b/solution.py
@@ -91,8 +91,8 @@
         out_ref[1] = total
 
 
-def join(pairs, masks, order, last):
-    others = [swap(pairs, "cent", len(order), mask) for mask in masks]
+def join(pairs, masks, order, size, last):
+    others = [swap(pairs, "cent", size, mask) for mask in masks]
     places = [[order.index(j ^ mask) for j in order] for mask in masks]
     return pl.pallas_call(
         functools.partial(join_kernel, places, last),
@@ -105,11 +105,10 @@
 
 
 def sums_kernel(n_parts, picks, parts, lognorm_ref, *refs):
-    score_refs, row_refs = refs[:n_parts], refs[n_parts : -len(parts)]
-    outs = refs[-len(parts) :]
+    score_refs, row_refs, out = refs[:n_parts], refs[n_parts:-1], refs[-1]
     r = lognorm_ref.shape[1]
     ones = jnp.ones((SIDE, r), jnp.bfloat16)
-    for out, (places, size, unit) in zip(outs, parts):
+    for n, (places, size, unit) in enumerate(parts):
         total, tally = None, None
         for j, (i, at) in enumerate(picks):
             k, block, first = places[j]
@@ -126,8 +125,9 @@
         )
         if unit:
             total, wide = pack(total, wide[0:1], unit)
-        out[0:size] = total
-        out[size : size + SIDE] = wide
+        at = n * (size + SIDE)
+        out[at : at + size] = total
+        out[at + size : at + size + SIDE] = wide
 
 
 def pack(total, tally, unit):
@@ -148,23 +148,62 @@
     return values[:size] * jnp.exp2(power - 14.0), tally
 
 
-def relay_kernel(unit, own_ref, got_ref, out_ref):
-    size = own_ref.shape[0] - SIDE
-    more, count = unpack(got_ref[...], unit)
-    total, wide = pack(own_ref[0:size] + more, own_ref[size : size + 1] + count, unit * 0.5)
+def relay_kernel(units, offsets, unit, *refs):
+    own_ref, got_refs, out_ref = refs[0], refs[1:-1], refs[-1]
+    size = out_ref.shape[0] - SIDE
+    at = offsets[0]
+    total, tally = own_ref[at : at + size], own_ref[at + size : at + size + 1]
+    for ref, of, at in zip(got_refs, units, offsets[1:]):
+        more, count = unpack(ref[at : at + size + SIDE], of)
+        total, tally = total + more, tally + count
+    total, wide = pack(total, tally, unit)
     out_ref[0:size] = total
     out_ref[size : size + SIDE] = wide
 
 
-def relay(own, got, unit):
+def relay(size, own, got, unit):
+    arrays = [own[0]] + [g[0].astype(jnp.float32) for g in got]
+    offsets = [(size + SIDE) * g[1] for g in [own] + got]
     return pl.pallas_call(
-        functools.partial(relay_kernel, unit),
-        out_shape=jax.ShapeDtypeStruct(own.shape, jnp.float32),
-        in_specs=[VMEM] * 2,
+        functools.partial(relay_kernel, [g[2] for g in got], offsets, unit),
+        out_shape=jax.ShapeDtypeStruct((size + SIDE, own[0].shape[1]), jnp.float32),
+        in_specs=[VMEM] * len(arrays),
         out_specs=VMEM,
         compiler_params=PARAMS,
         name="relay_sums",
-    )(own, got)
+    )(*arrays).astype(jnp.float16)
+
+
+def final_kernel(units, offsets, *refs):
+    own_ref, got_refs, codebook_ref, new_ref, tally_ref = refs[0], refs[1:-3], *refs[-3:]
+    size, depth = codebook_ref.shape
+    at = offsets[0]
+    total, tally = own_ref[at : at + size], own_ref[at + size : at + size + 1]
+    for ref, of, at in zip(got_refs, units, offsets[1:]):
+        more, count = unpack(ref[at : at + size + SIDE], of)
+        total, tally = total + more, tally + count
+    tally = tally[:, :size]
+    tally_ref[...] = tally
+    column = jnp.transpose(jnp.broadcast_to(tally, (size, size)))[:, 0:1]
+    new_ref[...] = (total + PRIOR * codebook_ref[...]) / (column + PRIOR)
+
+
+def finish(codebook, own, got):
+    size = codebook.shape[0]
+    arrays = [own[0]] + [g[0].astype(jnp.float32) for g in got] + [codebook]
+    offsets = [(size + SIDE) * g[1] for g in [own] + got]
+    new, tally = pl.pallas_call(
+        functools.partial(final_kernel, [g[2] for g in got], offsets),
+        out_shape=(
+            jax.ShapeDtypeStruct(codebook.shape, jnp.float32),
+            jax.ShapeDtypeStruct((1, size), jnp.float32),
+        ),
+        in_specs=[VMEM] * len(arrays),
+        out_specs=(VMEM, VMEM),
+        compiler_params=PARAMS,
+        name="update_centroids",
+    )(*arrays)
+    return new, tally[0]
 
 
 def weighted(parts, lognorm, scores, rows, picks):
@@ -173,9 +212,9 @@
     n_r, r = lognorm.shape
     return pl.pallas_call(
         functools.partial(sums_kernel, len(scores), picks, parts),
-        out_shape=[jax.ShapeDtypeStruct((size + SIDE, depth), jnp.float32) for _ in parts],
+        out_shape=jax.ShapeDtypeStruct((len(parts) * (size + SIDE), depth), jnp.float32),
         in_specs=[VMEM] * (1 + len(scores) + len(rows)),
-        out_specs=[VMEM] * len(parts),
+        out_specs=VMEM,
         compiler_params=PARAMS,
         cost_estimate=pl.CostEstimate(
             flops=2 * len(parts) * n_r * size * r * depth,
@@ -186,84 +225,95 @@
     )(lognorm, *scores, *rows)
 
 
+def local_split(n_dp, n_cent, embeddings, codebook):
+    r, size = embeddings.shape[0], codebook.shape[0]
+    order = [0, 2, 4, 6]
+    from_x = swap(embeddings, "cent", n_cent, 2)
+    from_y = swap(embeddings, "cent", n_cent, 4)
+    top = swap(from_x[: r // 2], "cent", n_cent, 4)
+    low = swap(from_y[r // 2 :], "cent", n_cent, 2)
+    rows = [embeddings, from_x, from_y, jnp.concatenate([top, low], axis=0)]
+    picks = [(i, 0) for i in range(4)]
+    rounded = codebook.astype(jnp.bfloat16)
+    far = swap(rounded, "dp", n_dp, 2)
+    near = swap(rounded, "dp", n_dp, 1)
+    last = swap(far, "dp", n_dp, 1)
+    mine = jnp.concatenate([rounded, near, far], axis=0)
+    theirs = swap(mine, "cent", n_cent, 1)
+    last_theirs = swap(last, "cent", n_cent, 1)
+    s_0, pair_0 = score([mine, theirs], rows[:3], r, picks[:3])
+    s_1, pair_1 = score([mine, theirs], rows[3:], r, picks[:1])
+    s_2, pairs = score([last, last_theirs], rows, r, picks, [pair_0, pair_1])
+    lognorm = join(pairs, order[1:], order, n_cent, True)
+
+    def part(core, k, unit):
+        if k == 3:
+            return [(2, j, core * size) for j in range(4)], size, unit
+        first = (3 * core + k) * size
+        return [(0, j, first) for j in range(3)] + [(1, 0, first)], size, unit
+
+    def sums(parts, lognorm):
+        return weighted(parts, lognorm, [s_0, s_1, s_2], rows, picks)
+
+    unit = 1024.0 / (4 * r)
+    over = sums([part(1, 3, unit)], lognorm).astype(jnp.float16)
+    over, lognorm = lax.optimization_barrier((over, lognorm))
+    over = swap(over, "cent", n_cent, 1)
+    own = sums([part(0, 3, 0)], lognorm)
+    rest = sums([part(1, k, unit) for k in (2, 1, 0)], lognorm).astype(jnp.float16)
+    over, rest = lax.optimization_barrier((over, rest))
+    first = relay(size, (own, 0), [(over, 0, unit)], unit * 0.5)
+    lognorm, first, rest = lax.optimization_barrier((lognorm, first, rest))
+    first = swap(first, "dp", n_dp, 1)
+    over = swap(rest, "cent", n_cent, 1)
+    own = sums([part(0, k, 0) for k in (2, 1)], lognorm)
+    near_sum = relay(size, (own, 1), [(over, 1, unit)], unit * 0.5)
+    far_sum = relay(size, (own, 0), [(over, 0, unit), (first, 0, unit * 0.5)], unit * 0.25)
+    lognorm, far_sum = lax.optimization_barrier((lognorm, far_sum))
+    own = sums([part(0, 0, 0)], lognorm)
+    far_sum = swap(far_sum, "dp", n_dp, 2)
+    near_sum = swap(near_sum, "dp", n_dp, 1)
+    new_codebook, tally = finish(
+        codebook,
+        (own, 0),
+        [(over, 2, unit), (near_sum, 0, unit * 0.5), (far_sum, 0, unit * 0.25)],
+    )
+    return new_codebook, tally, lognorm[0]
+
+
 def local(n_dp, n_cent, embeddings, codebook):
-    own_rows = embeddings.shape[0]
-    size = codebook.shape[0]
-    unit = 1024.0 / (own_rows * n_cent)
+    r, size = embeddings.shape[0], codebook.shape[0]
+    order = list(range(n_cent))
+    rows = [embeddings] + [swap(embeddings, "cent", n_cent, mask) for mask in order[1:]]
+    picks = [(j, 0) for j in order]
     rounded = codebook.astype(jnp.bfloat16)
-    if n_cent == 8:
-        half = own_rows // 2
-        from_x = swap(embeddings, "cent", n_cent, 2)
-        from_y = swap(embeddings, "cent", n_cent, 4)
-    if n_dp == 4:
-        far = swap(rounded, "dp", n_dp, 2)
-        near = swap(rounded, "dp", n_dp, 1)
-        most, final = [rounded, near, far], [swap(far, "dp", n_dp, 1)]
-    else:
-        most = [rounded] + [swap(rounded, "dp", n_dp, m) for m in range(1, n_dp - 1)]
-        final = [swap(rounded, "dp", n_dp, n_dp - 1)]
-    end = (n_dp - 1) * size
-    if n_cent == 8:
-        diag_top = swap(from_x[:half], "cent", n_cent, 4)
-        diag_low = swap(from_y[half:], "cent", n_cent, 2)
-        four = jnp.concatenate([embeddings, from_x, from_y, diag_top, diag_low], axis=0)
-        give, most, final = lax.optimization_barrier((four, most, final))
-        rows, order = [four, swap(give, "cent", n_cent, 1)], [0, 2, 4, 6, 1, 3, 5, 7]
-        picks = [(i, j * own_rows) for i in range(2) for j in range(4)]
-        s_0, pairs = score(most + final, rows[:1], own_rows, picks[:4])
-        s_1, pairs = score(most + final, rows[1:], own_rows, picks[:4], [pairs], 4)
-        scores = last_scores = [s_0, s_1]
-        places = [(i, j) for i in range(2) for j in range(4)]
-        last_places = [(i, j, end) for i, j in places]
-    else:
-        rows = [embeddings] + [swap(embeddings, "cent", n_cent, m) for m in range(1, n_cent)]
-        order = list(range(n_cent))
-        picks = [(j, 0) for j in order]
-        s_0, pair_0 = score(most, rows, own_rows, picks)
-        scores = [s_0]
-        places = [(0, j) for j in order]
-        s_1, pairs = score(final, rows, own_rows, picks, [pair_0])
-        last_scores, last_places = [s_1], [(0, j, 0) for j in order]
-    bits = [1 << i for i in range(n_cent.bit_length() - 1)]
-    rounds = [[1], [2, 4, 6]] if n_cent == 8 else [[bit] for bit in bits]
-    for masks in rounds:
-        pairs = join(pairs, masks, order, masks is rounds[-1])
+    centers = [rounded] + [swap(rounded, "dp", n_dp, mask) for mask in range(1, n_dp)]
+    scores, pairs = [], ()
+    for block in centers:
+        s, pairs = score([block], rows, r, picks, [pairs] if scores else ())
+        scores.append(s)
+    for bit in range(n_cent.bit_length() - 1):
+        pairs = join(pairs, [1 << bit], order, n_cent, 2 << bit >= n_cent)
     lognorm = pairs
-
-    def part(k, unit):
-        return [(i, j, k * size) for i, j in places], size, unit
-
-    (first,) = weighted([(last_places, size, unit)], lognorm, last_scores, rows, picks)
-    first = first.astype(jnp.float16)
-    if n_dp == 4:
-        first = swap(first, "dp", n_dp, 1)
-        parts = [part(2, 0), part(1, unit), part(0, 0)]
-        far_out, near_out, own = weighted(parts, lognorm, scores, rows, picks)
-        far_out = relay(far_out, first.astype(jnp.float32), unit).astype(jnp.float16)
-        far_out, near_out = lax.optimization_barrier((far_out, near_out))
-        far_out = swap(far_out, "dp", n_dp, 2)
-        near_out = swap(near_out.astype(jnp.float16), "dp", n_dp, 1)
-        got = [(near_out, unit), (far_out, unit * 0.5)]
-    else:
-        parts = [part(k, unit if k else 0) for k in range(n_dp - 1)]
-        out = weighted(parts, lognorm, scores, rows, picks)
-        own = out[0]
-        sent = [o.astype(jnp.float16) for o in out[1:]] + [first]
-        got = [(swap(m, "dp", n_dp, k + 1), unit) for k, m in enumerate(sent)]
-    owner_total, owner_tally = own[:size], own[size, :size]
-    for message, of in got:
-        more, count = unpack(message.astype(jnp.float32), of)
-        owner_total = owner_total + more
-        owner_tally = owner_tally + count[0, :size]
-    new_codebook = (owner_total + PRIOR * codebook) / (owner_tally + PRIOR)[:, None]
-    return (new_codebook, owner_tally, lognorm[0])
+    unit = 1024.0 / (n_cent * r)
+    got = []
+    for k in range(n_dp):
+        places = [(0, j, 0) for j in order]
+        block = weighted([(places, size, unit if k else 0)], lognorm, scores[k : k + 1], rows, picks)
+        if k:
+            got.append((swap(block.astype(jnp.float16), "dp", n_dp, k), 0, unit))
+        else:
+            own = block
+    new_codebook, tally = finish(codebook, (own, 0), got)
+    return new_codebook, tally, lognorm[0]
 
 
 def solution(mesh):
     n_dp, n_cent = mesh.shape["dp"], mesh.shape["cent"]
+    body = local_split if (n_dp, n_cent) == (4, 8) else local
 
     def run(embeddings, codebook):
-        return local(n_dp, n_cent, embeddings, codebook)
+        return body(n_dp, n_cent, embeddings, codebook)
 
     return jax.shard_map(
         run,

time: 65 us -> 69.1 us (1.063)
  waiting for transfers between devices: 31.9 us -> 35.5 us
  Pallas kernels: 6.87 us -> 9.05 us
  starting transfers between devices: 20 us -> 21.2 us
  other arithmetic: 2.87 us -> 1.68 us
  local copies, waits for them, and re-layouts: 1.79 us -> 0.65 us
    ppermute x15 -> x17, waiting for transfers between devices: 31.9 us -> 35.5 us  [swap(): return lax.ppermute(x, axis, [(i, i ^ mask) for i in range(size)])]
    pallas_call x1 -> x4, Pallas kernels: 0.14 us -> 1.53 us  [the longest x1 1.07 us: finish(): pl.pallas_call(functools.partial(final_kernel, [g[2] for g in got], offse...]
    ppermute x15 -> x17, starting transfers between devices: 20 us -> 21.2 us  [swap(): return lax.ppermute(x, axis, [(i, i ^ mask) for i in range(size)])]
    unnamed x6 -> x5, local copies, waits for them, and re-layouts: 1.17 us -> 0.03 us
    div x1 -> x0, other arithmetic: 1.01 us -> none  [local(): (owner_total + PRIOR * codebook) / (owner_tally + PRIOR)[:, None]]
    pallas_call x2 -> x5, Pallas kernels: 3.37 us -> 3.87 us  [weighted(): pl.pallas_call(functools.partial(sums_kernel, len(scores), picks, parts),...]
    convert_element_type x7 -> x11, other arithmetic: 1.29 us -> 1.63 us  [the longest x1 1.07 us: local_split(): rounded = codebook.astype(jnp.bfloat16)]
    pallas_call x2 -> x3, Pallas kernels: 3.31 us -> 3.62 us  [score(): pl.pallas_call(functools.partial(score_kernel, n_c, len(rows), picks, beg...]
  transfers between devices with their start and end apart: 15 -> 17, of which waited for: 11 -> 12; matrix products, arithmetic and copies ran while one was open for 5% -> 1% of each run, Pallas kernels for 6% -> 9%
where the time goes in v9:
time: 69.1 us; the launch traced here: 69 us
  waiting for transfers between devices  35.5 us (51%)
  starting transfers between devices  21.2 us (31%)
  Pallas kernels  9.05 us (13%)
  other arithmetic  1.68 us (2%)
  between operations  0.87 us (1%)
    ppermute x17, waiting for transfers between devices, swap(): return lax.ppermute(x, axis, [(i, i ^ mask) for i in range(size)])  35.5 us
    ppermute x17, starting transfers between devices, swap(): return lax.ppermute(x, axis, [(i, i ^ mask) for i in range(size)])  21.2 us
    pallas_call x5, Pallas kernels, weighted(): pl.pallas_call(functools.partial(sums_kernel, len(scores), picks, parts),...  3.87 us
    pallas_call x3, Pallas kernels, score(): pl.pallas_call(functools.partial(score_kernel, n_c, len(rows), picks, beg...  3.62 us
  transfers between devices with their start and end apart: 17, of which 12 were waited for; matrix products, arithmetic and copies ran while one was open for 1% of the time, Pallas kernels for 9%

profile of v9, /device:TPU:0, one launch (start us, length us, event | category | flops | bytes accessed | tf_op | source)
XLA Modules:
  0.0 69.0 jit_solution(5659983502065834280)
XLA Ops:
  0.6 1.1 %convert_element_type.35 = bf16[128,1024]{1,0:T(8,128)(2,1)S(1)} convert(f32[128,1024]{1,0:T(8,128)} %refs_4_.1) | non-fusion elementwise | flops 131072 | bytes 786432 | tf_op jit(solution)/shard_map/convert_element_type | solution.py:237
  1.7 3.1 %collective-permute-start.7 = (bf16[128,1024]{1,0:T(8,128)(2,1)S(1)}, bf16[128,1024]{1,0:T(8,128)(2,1)S(1)}, u32[]{:S(2)}, u32[]{:S(2)}) collective-permute-start(bf16[128,1024]{1,0:T(8,128)(2,1)S(1)} %convert_element_type.35), channel_id=1, source_target_pairs={{0,8},{8,0},{16,24},{24,16},{1,9},{9,1},{17,25},{25,17},{2,10},{10... | collective-permute-start | bytes 786440 | tf_op jit(solution)/shard_map/ppermute | solution.py:18
  4.8 2.6 %collective-permute-start = (bf16[128,1024]{1,0:T(8,128)(2,1)S(1)}, bf16[128,1024]{1,0:T(8,128)(2,1)S(1)}, u32[]{:S(2)}, u32[]{:S(2)}) collective-permute-start(bf16[128,1024]{1,0:T(8,128)(2,1)S(1)} %convert_element_type.35), channel_id=1, source_target_pairs={{0,16},{8,24},{16,0},{24,8},{1,17},{9,25},{17,1},{25,9},{2,18},{10... | collective-permute-start | bytes 786440 | tf_op jit(solution)/shard_map/ppermute | solution.py:18
  7.4 1.5 %collective-permute-start.3 = (bf16[256,1024]{1,0:T(8,128)(2,1)}, bf16[256,1024]{1,0:T(8,128)(2,1)S(1)}, u32[]{:S(2)}, u32[]{:S(2)}) collective-permute-start(bf16[256,1024]{1,0:T(8,128)(2,1)} %refs_3_.9), channel_id=1, source_target_pairs={{0,2},{1,3},{2,0},{3,1},{4,6},{5,7},{6,4},{7,5},{8,10},{9,11},{10,... | collective-permute-start | bytes 1572872 | tf_op jit(solution)/shard_map/ppermute | solution.py:18
  8.9 1.5 %collective-permute-start.4 = (bf16[256,1024]{1,0:T(8,128)(2,1)}, bf16[256,1024]{1,0:T(8,128)(2,1)S(1)}, u32[]{:S(2)}, u32[]{:S(2)}) collective-permute-start(bf16[256,1024]{1,0:T(8,128)(2,1)} %refs_3_.9), channel_id=1, source_target_pairs={{0,4},{1,5},{2,6},{3,7},{4,0},{5,1},{6,2},{7,3},{8,12},{9,13},{10,... | collective-permute-start | bytes 1572872 | tf_op jit(solution)/shard_map/ppermute | solution.py:18
  10.4 6.2 %collective-permute-done.7 = bf16[128,1024]{1,0:T(8,128)(2,1)S(1)} collective-permute-done((bf16[128,1024]{1,0:T(8,128)(2,1)S(1)}, bf16[128,1024]{1,0:T(8,128)(2,1)S(1)}, u32[]{:S(2)}, u32[]{:S(2)}) %collective-permute-start.7) | collective-permute-done | bytes 262176 | tf_op jit(solution)/shard_map/ppermute | solution.py:18
  16.6 2.5 %collective-permute-done = bf16[128,1024]{1,0:T(8,128)(2,1)S(1)} collective-permute-done((bf16[128,1024]{1,0:T(8,128)(2,1)S(1)}, bf16[128,1024]{1,0:T(8,128)(2,1)S(1)}, u32[]{:S(2)}, u32[]{:S(2)}) %collective-permute-start) | collective-permute-done | bytes 262176 | tf_op jit(solution)/shard_map/ppermute | solution.py:18
  19.8 0.9 %collective-permute-done.3.refs_3_.refs_4_ = bf16[256,1024]{1,0:T(8,128)(2,1)S(1)} collective-permute-done((bf16[256,1024]{1,0:T(8,128)(2,1)}, bf16[256,1024]{1,0:T(8,128)(2,1)S(1)}, u32[]{:S(2)}, u32[]{:S(2)}) %collective-permute-start.3) | collective-permute-done | bytes 524320 | tf_op jit(solution)/shard_map/ppermute | solution.py:18
  20.7 1.6 %collective-permute-start.5 = (bf16[128,1024]{1,0:T(8,128)(2,1)S(1)}, bf16[128,1024]{1,0:T(8,128)(2,1)S(1)}, u32[]{:S(2)}, u32[]{:S(2)}) collective-permute-start(bf16[128,1024]{1,0:T(8,128)(2,1)S(1)} %slice.12), channel_id=1, source_target_pairs={{0,4},{1,5},{2,6},{3,7},{4,0},{5,1},{6,2},{7,3},{8,12},{9,13},{10,... | collective-permute-start | bytes 786440 | tf_op jit(solution)/shard_map/ppermute | solution.py:18
  22.3 1.6 %collective-permute-start.6 = (bf16[128,1024]{1,0:T(8,128)(2,1)S(1)}, bf16[128,1024]{1,0:T(8,128)(2,1)S(1)}, u32[]{:S(2)}, u32[]{:S(2)}) collective-permute-start(bf16[128,1024]{1,0:T(8,128)(2,1)S(1)} %slice.13), channel_id=1, source_target_pairs={{0,2},{1,3},{2,0},{3,1},{4,6},{5,7},{6,4},{7,5},{8,10},{9,11},{10,... | collective-permute-start | bytes 786440 | tf_op jit(solution)/shard_map/ppermute | solution.py:18
  23.9 4.1 %collective-permute-done.1.refs_0_ = bf16[128,1024]{1,0:T(8,128)(2,1)S(1)} collective-permute-done((bf16[128,1024]{1,0:T(8,128)(2,1)S(1)}, bf16[128,1024]{1,0:T(8,128)(2,1)S(1)}, u32[]{:S(2)}, u32[]{:S(2)}) %collective-permute-start.1) | collective-permute-done | bytes 262176 | tf_op jit(solution)/shard_map/ppermute | solution.py:18
  28.3 1.3 %collective-permute-done.6 = bf16[128,1024]{1,0:T(8,128)(2,1)S(1)} collective-permute-done((bf16[128,1024]{1,0:T(8,128)(2,1)S(1)}, bf16[128,1024]{1,0:T(8,128)(2,1)S(1)}, u32[]{:S(2)}, u32[]{:S(2)}) %collective-permute-start.6) | collective-permute-done | bytes 262176 | tf_op jit(solution)/shard_map/ppermute | solution.py:18
  30.4 1.8 %score_rows.3 = (f32[3,768,256]{2,1,0:T(8,128)S(1)}, f32[2,3,256]{2,1,0:T(4,128)S(1)}) custom-call(bf16[384,1024]{1,0:T(8,128)(2,1)S(1)} %pad_maximum_fusion.refs_0_, bf16[384,1024]{1,0:T(8,128)(2,1)S(1)} %collective-permute-done.8.refs_1_, bf16[256,1024]{1,0:T(8,128)(2,1)S(1)} %copy-done, bf16[256,1024]{1,0:T(8,128)(2,1)S(1)} %collective-permute-done.3.refs_3_.refs_4_, ...), custom_call_target="tpu_custom_call" | custom-call | flops 1207959552 | bytes 3145728 | tf_op jit(solution)/shard_map/score_rows/pallas_call | solution.py:63
  32.3 1.0 %score_rows.5 = (f32[4,256,256]{2,1,0:T(8,128)S(1)}, f32[2,4,256]{2,1,0:T(4,128)S(1)}) custom-call(bf16[128,1024]{1,0:T(8,128)(2,1)S(1)} %collective-permute-done.1.refs_0_, bf16[128,1024]{1,0:T(8,128)(2,1)S(1)} %collective-permute-done.2.refs_1_, bf16[256,1024]{1,0:T(8,128)(2,1)S(1)} %copy-done, ...), custom_call_target="tpu_custom_call" | custom-call | flops 536870912 | bytes 2621440 | tf_op jit(solution)/shard_map/score_rows/pallas_call | solution.py:63
  33.3 1.5 %collective-permute-start.11 = (f32[2,4,256]{2,1,0:T(4,128)S(1)}, f32[2,4,256]{2,1,0:T(4,128)S(1)}, u32[]{:S(2)}, u32[]{:S(2)}) collective-permute-start(f32[2,4,256]{2,1,0:T(4,128)S(1)} %get-tuple-element.22.pair_ref), channel_id=1, source_target_pairs={{0,6},{1,7},{2,4},{3,5},{4,2},{5,3},{6,0},{7,1},{8,14},{9,15},{10,... | collective-permute-start | bytes 24584 | tf_op jit(solution)/shard_map/ppermute | solution.py:18
  34.8 1.5 %collective-permute-start.10 = (f32[2,4,256]{2,1,0:T(4,128)S(1)}, f32[2,4,256]{2,1,0:T(4,128)S(1)}, u32[]{:S(2)}, u32[]{:S(2)}) collective-permute-start(f32[2,4,256]{2,1,0:T(4,128)S(1)} %get-tuple-element.22.pair_ref), channel_id=1, source_target_pairs={{0,4},{1,5},{2,6},{3,7},{4,0},{5,1},{6,2},{7,3},{8,12},{9,13},{10,... | collective-permute-start | bytes 24584 | tf_op jit(solution)/shard_map/ppermute | solution.py:18
  36.8 1.1 %collective-permute-done.11.refs_2_ = f32[2,4,256]{2,1,0:T(4,128)S(1)} collective-permute-done((f32[2,4,256]{2,1,0:T(4,128)S(1)}, f32[2,4,256]{2,1,0:T(4,128)S(1)}, u32[]{:S(2)}, u32[]{:S(2)}) %collective-permute-start.11) | collective-permute-done | bytes 8224 | tf_op jit(solution)/shard_map/ppermute | solution.py:18
  38.4 1.5 %collective-permute-done.9.refs_0_ = f32[2,4,256]{2,1,0:T(4,128)S(1)} collective-permute-done((f32[2,4,256]{2,1,0:T(4,128)S(1)}, f32[2,4,256]{2,1,0:T(4,128)S(1)}, u32[]{:S(2)}, u32[]{:S(2)}) %collective-permute-start.9) | collective-permute-done | bytes 8224 | tf_op jit(solution)/shard_map/ppermute | solution.py:18
  40.7 1.4 %weighted_sums.7 = f32[408,1024]{1,0:T(8,128)S(1)} custom-call(f32[4,256]{1,0:T(4,128)S(1)} %join_rows.1.lognorm_ref, f32[3,768,256]{2,1,0:T(8,128)S(1)} %get-tuple-element.23.refs_0_, f32[1,768,256]{2,1,0:T(8,128)S(1)} %get-tuple-element.24.refs_1_, f32[4,256,256]{2,1,0:T(8,128)S(1)} %get-tuple-element.25.refs_2_, bf16[256,1024]{1,0:T(8,128)(2,1)S(1)} %copy-done, ...), custom_call_target="tpu_custom_call" | custom-call | flops 805306368 | bytes 2097152 | tf_op jit(solution)/shard_map/weighted_sums/pallas_call | solution.py:213
  43.5 1.6 %collective-permute-start.14 = (f16[136,1024]{1,0:T(8,128)(2,1)S(1)}, f16[136,1024]{1,0:T(8,128)(2,1)S(1)}, u32[]{:S(2)}, u32[]{:S(2)}) collective-permute-start(f16[136,1024]{1,0:T(8,128)(2,1)S(1)} %convert_element_type.39), channel_id=1, source_target_pairs={{0,8},{8,0},{16,24},{24,16},{1,9},{9,1},{17,25},{25,17},{2,10},{10... | collective-permute-start | bytes 835592 | tf_op jit(solution)/shard_map/ppermute | solution.py:18
  46.0 6.2 %collective-permute-done.14 = f16[136,1024]{1,0:T(8,128)(2,1)S(1)} collective-permute-done((f16[136,1024]{1,0:T(8,128)(2,1)S(1)}, f16[136,1024]{1,0:T(8,128)(2,1)S(1)}, u32[]{:S(2)}, u32[]{:S(2)}) %collective-permute-start.14) | collective-permute-done | bytes 278560 | tf_op jit(solution)/shard_map/ppermute | solution.py:18
  52.7 2.6 %collective-permute-start.16 = (f16[136,1024]{1,0:T(8,128)(2,1)S(1)}, f16[136,1024]{1,0:T(8,128)(2,1)S(1)}, u32[]{:S(2)}, u32[]{:S(2)}) collective-permute-start(f16[136,1024]{1,0:T(8,128)(2,1)S(1)} %convert_element_type.42), channel_id=1, source_target_pairs={{0,16},{8,24},{16,0},{24,8},{1,17},{9,25},{17,1},{25,9},{2,18},{10... | collective-permute-start | bytes 835592 | tf_op jit(solution)/shard_map/ppermute | solution.py:18
  56.9 10.7 %collective-permute-done.16 = f16[136,1024]{1,0:T(8,128)(2,1)S(1)} collective-permute-done((f16[136,1024]{1,0:T(8,128)(2,1)S(1)}, f16[136,1024]{1,0:T(8,128)(2,1)S(1)}, u32[]{:S(2)}, u32[]{:S(2)}) %collective-permute-start.16) | collective-permute-done | bytes 278560 | tf_op jit(solution)/shard_map/ppermute | solution.py:18
  67.9 1.1 %update_centroids.1 = (f32[128,1024]{1,0:T(8,128)}, f32[1,128]{1,0:T(1,128)}) custom-call(f32[136,1024]{1,0:T(8,128)S(1)} %weighted_sums.9.refs_0_, f32[408,1024]{1,0:T(8,128)S(1)} %convert_element_type.40.refs_1_, f32[136,1024]{1,0:T(8,128)S(1)} %convert_element_type.44.refs_2_, f32[136,1024]{1,0:T(8,128)S(1)} %convert_element_type.45.refs_3_, ...), custom_call_target="tpu_custom_call" | custom-call | tf_op jit(solution)/shard_map/update_centroids/pallas_call | solution.py:195
  (44 shorter events, 8.2 us)
Async XLA Ops:
  1.7 14.9 %collective-permute-start.7 = (bf16[128,1024]{1,0:T(8,128)(2,1)S(1)}, bf16[128,1024]{1,0:T(8,128)(2,1)S(1)}, u32[]{:S(2)}, u32[]{:S(2)}) collective-permute-start(bf16[128,1024]{1,0:T(8,128)(2,1)S(1)} %convert_element_type.35), channel_id=1, source_target_pairs={{0,8},{8,0},{16,24},{24,16},{1,9},{9,1},{17,25},{25,17},{2,10},{10... | collective-permute-start | bytes 786440 | tf_op jit(solution)/shard_map/ppermute | solution.py:18
  4.8 14.3 %collective-permute-start = (bf16[128,1024]{1,0:T(8,128)(2,1)S(1)}, bf16[128,1024]{1,0:T(8,128)(2,1)S(1)}, u32[]{:S(2)}, u32[]{:S(2)}) collective-permute-start(bf16[128,1024]{1,0:T(8,128)(2,1)S(1)} %convert_element_type.35), channel_id=1, source_target_pairs={{0,16},{8,24},{16,0},{24,8},{1,17},{9,25},{17,1},{25,9},{2,18},{10... | collective-permute-start | bytes 786440 | tf_op jit(solution)/shard_map/ppermute | solution.py:18
  7.4 13.3 %collective-permute-start.3 = (bf16[256,1024]{1,0:T(8,128)(2,1)}, bf16[256,1024]{1,0:T(8,128)(2,1)S(1)}, u32[]{:S(2)}, u32[]{:S(2)}) collective-permute-start(bf16[256,1024]{1,0:T(8,128)(2,1)} %refs_3_.9), channel_id=1, source_target_pairs={{0,2},{1,3},{2,0},{3,1},{4,6},{5,7},{6,4},{7,5},{8,10},{9,11},{10,... | collective-permute-start | bytes 1572872 | tf_op jit(solution)/shard_map/ppermute | solution.py:18
  8.9 13.4 %collective-permute-start.4 = (bf16[256,1024]{1,0:T(8,128)(2,1)}, bf16[256,1024]{1,0:T(8,128)(2,1)S(1)}, u32[]{:S(2)}, u32[]{:S(2)}) collective-permute-start(bf16[256,1024]{1,0:T(8,128)(2,1)} %refs_3_.9), channel_id=1, source_target_pairs={{0,4},{1,5},{2,6},{3,7},{4,0},{5,1},{6,2},{7,3},{8,12},{9,13},{10,... | collective-permute-start | bytes 1572872 | tf_op jit(solution)/shard_map/ppermute | solution.py:18
  19.2 10.4 %collective-permute-start.8 = (bf16[384,1024]{1,0:T(8,128)(2,1)S(1)}, bf16[384,1024]{1,0:T(8,128)(2,1)S(1)}, u32[]{:S(2)}, u32[]{:S(2)}) collective-permute-start(bf16[384,1024]{1,0:T(8,128)(2,1)S(1)} %pad_maximum_fusion.refs_0_), channel_id=1, source_target_pairs={{0,1},{1,0},{2,3},{3,2},{4,5},{5,4},{6,7},{7,6},{8,9},{9,8},{10,11... | collective-permute-start | bytes 2359304 | tf_op jit(solution)/shard_map/ppermute | solution.py:18
  19.3 8.7 %collective-permute-start.1 = (bf16[128,1024]{1,0:T(8,128)(2,1)S(1)}, bf16[128,1024]{1,0:T(8,128)(2,1)S(1)}, u32[]{:S(2)}, u32[]{:S(2)}) collective-permute-start(bf16[128,1024]{1,0:T(8,128)(2,1)S(1)} %collective-permute-done), channel_id=1, source_target_pairs={{0,8},{8,0},{16,24},{24,16},{1,9},{9,1},{17,25},{25,17},{2,10},{10... | collective-permute-start | bytes 786440 | tf_op jit(solution)/shard_map/ppermute | solution.py:18
  20.7 7.5 %collective-permute-start.5 = (bf16[128,1024]{1,0:T(8,128)(2,1)S(1)}, bf16[128,1024]{1,0:T(8,128)(2,1)S(1)}, u32[]{:S(2)}, u32[]{:S(2)}) collective-permute-start(bf16[128,1024]{1,0:T(8,128)(2,1)S(1)} %slice.12), channel_id=1, source_target_pairs={{0,4},{1,5},{2,6},{3,7},{4,0},{5,1},{6,2},{7,3},{8,12},{9,13},{10,... | collective-permute-start | bytes 786440 | tf_op jit(solution)/shard_map/ppermute | solution.py:18
  22.3 8.1 %copy-start = (bf16[256,1024]{1,0:T(8,128)(2,1)S(1)}, bf16[256,1024]{1,0:T(8,128)(2,1)}, u32[]{:S(2)}) copy-start(bf16[256,1024]{1,0:T(8,128)(2,1)} %refs_3_.9) | copy-start | bytes 1572868
  22.3 7.2 %collective-permute-start.6 = (bf16[128,1024]{1,0:T(8,128)(2,1)S(1)}, bf16[128,1024]{1,0:T(8,128)(2,1)S(1)}, u32[]{:S(2)}, u32[]{:S(2)}) collective-permute-start(bf16[128,1024]{1,0:T(8,128)(2,1)S(1)} %slice.13), channel_id=1, source_target_pairs={{0,2},{1,3},{2,0},{3,1},{4,6},{5,7},{6,4},{7,5},{8,10},{9,11},{10,... | collective-permute-start | bytes 786440 | tf_op jit(solution)/shard_map/ppermute | solution.py:18
  28.0 4.3 %collective-permute-start.2 = (bf16[128,1024]{1,0:T(8,128)(2,1)S(1)}, bf16[128,1024]{1,0:T(8,128)(2,1)S(1)}, u32[]{:S(2)}, u32[]{:S(2)}) collective-permute-start(bf16[128,1024]{1,0:T(8,128)(2,1)S(1)} %collective-permute-done.1.refs_0_), channel_id=1, source_target_pairs={{0,1},{1,0},{2,3},{3,2},{4,5},{5,4},{6,7},{7,6},{8,9},{9,8},{10,11... | collective-permute-start | bytes 786440 | tf_op jit(solution)/shard_map/ppermute | solution.py:18
  33.3 4.6 %collective-permute-start.11 = (f32[2,4,256]{2,1,0:T(4,128)S(1)}, f32[2,4,256]{2,1,0:T(4,128)S(1)}, u32[]{:S(2)}, u32[]{:S(2)}) collective-permute-start(f32[2,4,256]{2,1,0:T(4,128)S(1)} %get-tuple-element.22.pair_ref), channel_id=1, source_target_pairs={{0,6},{1,7},{2,4},{3,5},{4,2},{5,3},{6,0},{7,1},{8,14},{9,15},{10,... | collective-permute-start | bytes 24584 | tf_op jit(solution)/shard_map/ppermute | solution.py:18
  34.8 3.7 %collective-permute-start.10 = (f32[2,4,256]{2,1,0:T(4,128)S(1)}, f32[2,4,256]{2,1,0:T(4,128)S(1)}, u32[]{:S(2)}, u32[]{:S(2)}) collective-permute-start(f32[2,4,256]{2,1,0:T(4,128)S(1)} %get-tuple-element.22.pair_ref), channel_id=1, source_target_pairs={{0,4},{1,5},{2,6},{3,7},{4,0},{5,1},{6,2},{7,3},{8,12},{9,13},{10,... | collective-permute-start | bytes 24584 | tf_op jit(solution)/shard_map/ppermute | solution.py:18
  36.3 3.7 %collective-permute-start.9 = (f32[2,4,256]{2,1,0:T(4,128)S(1)}, f32[2,4,256]{2,1,0:T(4,128)S(1)}, u32[]{:S(2)}, u32[]{:S(2)}) collective-permute-start(f32[2,4,256]{2,1,0:T(4,128)S(1)} %get-tuple-element.22.pair_ref), channel_id=1, source_target_pairs={{0,2},{1,3},{2,0},{3,1},{4,6},{5,7},{6,4},{7,5},{8,10},{9,11},{10,... | collective-permute-start | bytes 24584 | tf_op jit(solution)/shard_map/ppermute | solution.py:18
  40.6 2.1 %collective-permute-start.12 = (f16[136,1024]{1,0:T(8,128)(2,1)S(1)}, f16[136,1024]{1,0:T(8,128)(2,1)S(1)}, u32[]{:S(2)}, u32[]{:S(2)}) collective-permute-start(f16[136,1024]{1,0:T(8,128)(2,1)S(1)} %convert_element_type.36), channel_id=1, source_target_pairs={{0,1},{1,0},{2,3},{3,2},{4,5},{5,4},{6,7},{7,6},{8,9},{9,8},{10,11... | collective-permute-start | bytes 835592 | tf_op jit(solution)/shard_map/ppermute | solution.py:18
  42.9 9.2 %collective-permute-start.13 = (f16[408,1024]{1,0:T(8,128)(2,1)S(1)}, f16[408,1024]{1,0:T(8,128)(2,1)S(1)}, u32[]{:S(2)}, u32[]{:S(2)}) collective-permute-start(f16[408,1024]{1,0:T(8,128)(2,1)S(1)} %convert_element_type.37), channel_id=1, source_target_pairs={{0,1},{1,0},{2,3},{3,2},{4,5},{5,4},{6,7},{7,6},{8,9},{9,8},{10,11... | collective-permute-start | bytes 2506760 | tf_op jit(solution)/shard_map/ppermute | solution.py:18
  43.5 8.6 %collective-permute-start.14 = (f16[136,1024]{1,0:T(8,128)(2,1)S(1)}, f16[136,1024]{1,0:T(8,128)(2,1)S(1)}, u32[]{:S(2)}, u32[]{:S(2)}) collective-permute-start(f16[136,1024]{1,0:T(8,128)(2,1)S(1)} %convert_element_type.39), channel_id=1, source_target_pairs={{0,8},{8,0},{16,24},{24,16},{1,9},{9,1},{17,25},{25,17},{2,10},{10... | collective-permute-start | bytes 835592 | tf_op jit(solution)/shard_map/ppermute | solution.py:18
  52.7 14.8 %collective-permute-start.16 = (f16[136,1024]{1,0:T(8,128)(2,1)S(1)}, f16[136,1024]{1,0:T(8,128)(2,1)S(1)}, u32[]{:S(2)}, u32[]{:S(2)}) collective-permute-start(f16[136,1024]{1,0:T(8,128)(2,1)S(1)} %convert_element_type.42), channel_id=1, source_target_pairs={{0,16},{8,24},{16,0},{24,8},{1,17},{9,25},{17,1},{25,9},{2,18},{10... | collective-permute-start | bytes 835592 | tf_op jit(solution)/shard_map/ppermute | solution.py:18
  55.4 12.4 %collective-permute-start.15 = (f16[136,1024]{1,0:T(8,128)(2,1)S(1)}, f16[136,1024]{1,0:T(8,128)(2,1)S(1)}, u32[]{:S(2)}, u32[]{:S(2)}) collective-permute-start(f16[136,1024]{1,0:T(8,128)(2,1)S(1)} %convert_element_type.43), channel_id=1, source_target_pairs={{0,8},{8,0},{16,24},{24,16},{1,9},{9,1},{17,25},{25,17},{2,10},{10... | collective-permute-start | bytes 835592 | tf_op jit(solution)/shard_map/ppermute | solution.py:18
  56.8 11.0 %copy-start.1 = (f32[128,1024]{1,0:T(8,128)S(1)}, f32[128,1024]{1,0:T(8,128)}, u32[]{:S(2)}) copy-start(f32[128,1024]{1,0:T(8,128)} %refs_4_.1) | copy-start | bytes 1572868

commit v10 on v8

--- a/solution.py
+++ b/solution.py
@@ -14,8 +14,12 @@
 PARAMS = pltpu.CompilerParams(vmem_limit_bytes=24 << 20)
 
 
+def partner(size, mask):
+    return [(i, i ^ mask) for i in range(size)]
+
+
 def swap(x, axis, size, mask):
-    return lax.ppermute(x, axis, [(i, i ^ mask) for i in range(size)])
+    return lax.ppermute(x, axis, partner(size, mask))
 
 
 def merge(a, b):
@@ -91,9 +95,8 @@
         out_ref[1] = total
 
 
-def join(pairs, masks, order, last):
-    others = [swap(pairs, "cent", len(order), mask) for mask in masks]
-    places = [[order.index(j ^ mask) for j in order] for mask in masks]
+def join(pairs, routes, places, last):
+    others = [lax.ppermute(pairs, "cent", route) for route in routes]
     return pl.pallas_call(
         functools.partial(join_kernel, places, last),
         out_shape=jax.ShapeDtypeStruct(pairs.shape[1:] if last else pairs.shape, jnp.float32),
@@ -167,6 +170,36 @@
     )(own, got)
 
 
+def final_kernel(units, *refs):
+    own_ref, got_refs, codebook_ref, new_ref, tally_ref = refs[0], refs[1:-3], *refs[-3:]
+    size, depth = codebook_ref.shape
+    total, tally = own_ref[0:size], own_ref[size : size + 1]
+    for ref, unit in zip(got_refs, units):
+        more, count = unpack(ref[...], unit)
+        total, tally = total + more, tally + count
+    tally = tally[:, :size]
+    tally_ref[...] = tally
+    column = jnp.transpose(jnp.broadcast_to(tally, (size, size)))[:, 0:1]
+    new_ref[...] = (total + PRIOR * codebook_ref[...]) / (column + PRIOR)
+
+
+def finish(codebook, own, got):
+    size = codebook.shape[0]
+    arrays = [own] + [message.astype(jnp.float32) for message, _ in got] + [codebook]
+    new, tally = pl.pallas_call(
+        functools.partial(final_kernel, [unit for _, unit in got]),
+        out_shape=(
+            jax.ShapeDtypeStruct(codebook.shape, jnp.float32),
+            jax.ShapeDtypeStruct((1, size), jnp.float32),
+        ),
+        in_specs=[VMEM] * len(arrays),
+        out_specs=(VMEM, VMEM),
+        compiler_params=PARAMS,
+        name="update_centroids",
+    )(*arrays)
+    return new, tally[0]
+
+
 def weighted(parts, lognorm, scores, rows, picks):
     size = parts[0][1]
     depth = rows[0].shape[1]
@@ -192,9 +225,10 @@
     unit = 1024.0 / (own_rows * n_cent)
     rounded = codebook.astype(jnp.bfloat16)
     if n_cent == 8:
-        half = own_rows // 2
-        from_x = swap(embeddings, "cent", n_cent, 2)
-        from_y = swap(embeddings, "cent", n_cent, 4)
+        by_p = [(i, i ^ (4 if i & 1 else 2)) for i in range(n_cent)]
+        by_q = [(i, i ^ (2 if i & 1 else 4)) for i in range(n_cent)]
+        from_p = lax.ppermute(embeddings, "cent", by_p)
+        from_q = lax.ppermute(embeddings, "cent", by_q)
     if n_dp == 4:
         far = swap(rounded, "dp", n_dp, 2)
         near = swap(rounded, "dp", n_dp, 1)
@@ -204,17 +238,25 @@
         final = [swap(rounded, "dp", n_dp, n_dp - 1)]
     end = (n_dp - 1) * size
     if n_cent == 8:
-        diag_top = swap(from_x[:half], "cent", n_cent, 4)
-        diag_low = swap(from_y[half:], "cent", n_cent, 2)
-        four = jnp.concatenate([embeddings, from_x, from_y, diag_top, diag_low], axis=0)
-        give, most, final = lax.optimization_barrier((four, most, final))
-        rows, order = [four, swap(give, "cent", n_cent, 1)], [0, 2, 4, 6, 1, 3, 5, 7]
-        picks = [(i, j * own_rows) for i in range(2) for j in range(4)]
-        s_0, pairs = score(most + final, rows[:1], own_rows, picks[:4])
-        s_1, pairs = score(most + final, rows[1:], own_rows, picks[:4], [pairs], 4)
-        scores = last_scores = [s_0, s_1]
-        places = [(i, j) for i in range(2) for j in range(4)]
-        last_places = [(i, j, end) for i, j in places]
+        diag = lax.ppermute(from_p, "cent", by_q)
+        three = jnp.concatenate([embeddings, from_p, from_q], axis=0)
+        give, most = lax.optimization_barrier((three, most))
+        three_core = swap(give, "cent", n_cent, 1)
+        s_0, pair_0 = score(most, [three], own_rows, [(0, j * own_rows) for j in range(3)])
+        s_1, pair_1 = score(most, [three_core], own_rows, [(0, j * own_rows) for j in range(3)])
+        give, pair_0, pair_1, final = lax.optimization_barrier(
+            (diag, pair_0, pair_1, final)
+        )
+        rows = [three, three_core, diag, swap(give, "cent", n_cent, 1)]
+        order = [0, 2, 4, 1, 5, 3, 6, 7]
+        picks = [(i, j * own_rows) for i in range(2) for j in range(3)] + [(2, 0), (3, 0)]
+        s_2, pairs = score(final, rows[:2], own_rows, picks[:6], [pair_0, pair_1])
+        s_3, pair_3 = score(most + final, rows[2:3], own_rows, [(0, 0)])
+        s_4, pairs = score(most + final, rows[3:], own_rows, [(0, 0)], [pairs, pair_3], 7)
+        scores = [s_0, s_1, s_3, s_4]
+        places = [(i, j) for i in range(2) for j in range(3)] + [(2, 0), (3, 0)]
+        last_scores = [s_2, s_3, s_4]
+        last_places = [(0, j, 0) for j in range(6)] + [(1, 0, end), (2, 0, end)]
     else:
         rows = [embeddings] + [swap(embeddings, "cent", n_cent, m) for m in range(1, n_cent)]
         order = list(range(n_cent))
@@ -224,11 +266,17 @@
         places = [(0, j) for j in order]
         s_1, pairs = score(final, rows, own_rows, picks, [pair_0])
         last_scores, last_places = [s_1], [(0, j, 0) for j in order]
-    bits = [1 << i for i in range(n_cent.bit_length() - 1)]
-    rounds = [[1], [2, 4, 6]] if n_cent == 8 else [[bit] for bit in bits]
-    for masks in rounds:
-        pairs = join(pairs, masks, order, masks is rounds[-1])
-    lognorm = pairs
+    if n_cent == 8:
+        where = [order.index((j ^ 1) & 1 | (j & 2) << 1 | (j & 4) >> 1) for j in order]
+        pairs = join(pairs, [partner(n_cent, 1)], [where], False)
+        routes = [by_p, by_q, partner(n_cent, 6)]
+        where = [[order.index(j ^ mask) for j in order] for mask in (2, 4, 6)]
+        lognorm = join(pairs, routes, where, True)
+    else:
+        for bit in range(n_cent.bit_length() - 1):
+            where = [j ^ (1 << bit) for j in order]
+            pairs = join(pairs, [partner(n_cent, 1 << bit)], [where], 2 << bit >= n_cent)
+        lognorm = pairs
 
     def part(k, unit):
         return [(i, j, k * size) for i, j in places], size, unit
@@ -250,13 +298,8 @@
         own = out[0]
         sent = [o.astype(jnp.float16) for o in out[1:]] + [first]
         got = [(swap(m, "dp", n_dp, k + 1), unit) for k, m in enumerate(sent)]
-    owner_total, owner_tally = own[:size], own[size, :size]
-    for message, of in got:
-        more, count = unpack(message.astype(jnp.float32), of)
-        owner_total = owner_total + more
-        owner_tally = owner_tally + count[0, :size]
-    new_codebook = (owner_total + PRIOR * codebook) / (owner_tally + PRIOR)[:, None]
-    return (new_codebook, owner_tally, lognorm[0])
+    new_codebook, tally = finish(codebook, own, got)
+    return new_codebook, tally, lognorm[0]
 
 
 def solution(mesh):

time: 65 us -> 63.9 us (0.983)
  Pallas kernels: 6.87 us -> 9.14 us
  other arithmetic: 2.87 us -> 1.29 us
  waiting for transfers between devices: 31.9 us -> 30.5 us
    ppermute x15, waiting for transfers between devices: 31.9 us -> 30.5 us  [the longest x8 22.4 us: swap(): return lax.ppermute(x, axis, partner(size, mask))]
    pallas_call x2 -> x5, Pallas kernels: 3.31 us -> 4.51 us  [score(): pl.pallas_call(functools.partial(score_kernel, n_c, len(rows), picks, beg...]
    pallas_call x0 -> x1, Pallas kernels: none -> 1.03 us  [finish(): pl.pallas_call(functools.partial(final_kernel, [unit for _, unit in got])...]
    div x1 -> x0, other arithmetic: 1.01 us -> none  [local(): (owner_total + PRIOR * codebook) / (owner_tally + PRIOR)[:, None]]
  transfers between devices with their start and end apart: 15 -> 15, of which waited for: 11 -> 13; matrix products, arithmetic and copies ran while one was open for 5% -> 4% of each run, Pallas kernels for 6% -> 10%
where the time goes in v10:
time: 63.9 us; the launch traced here: 63.7 us
  waiting for transfers between devices  30.5 us (48%)
  starting transfers between devices  20.3 us (32%)
  Pallas kernels  9.14 us (14%)
  local copies, waits for them, and re-layouts  1.72 us (3%)
  other arithmetic  1.29 us (2%)
  between operations  0.76 us (1%)
    ppermute x8, waiting for transfers between devices, swap(): return lax.ppermute(x, axis, partner(size, mask))  22.4 us
    ppermute x8, starting transfers between devices, swap(): return lax.ppermute(x, axis, partner(size, mask))  11.2 us
    ppermute x1, waiting for transfers between devices, local(): from_p = lax.ppermute(embeddings, 'cent', by_p)  4.61 us
    pallas_call x5, Pallas kernels, score(): pl.pallas_call(functools.partial(score_kernel, n_c, len(rows), picks, beg...  4.51 us
    ppermute x4, starting transfers between devices, join(): others = [lax.ppermute(pairs, 'cent', route) for route in routes]  4.11 us
    pallas_call x2, Pallas kernels, weighted(): pl.pallas_call(functools.partial(sums_kernel, len(scores), picks, parts),...  3.4 us
    ppermute x4, waiting for transfers between devices, join(): others = [lax.ppermute(pairs, 'cent', route) for route in routes]  3.25 us
    ppermute x1, starting transfers between devices, local(): from_p = lax.ppermute(embeddings, 'cent', by_p)  3 us
  transfers between devices with their start and end apart: 15, of which 13 were waited for; matrix products, arithmetic and copies ran while one was open for 4% of the time, Pallas kernels for 10%

profile of v10, /device:TPU:0, one launch (start us, length us, event | category | flops | bytes accessed | tf_op | source)
XLA Modules:
  0.0 63.7 jit_solution(10379571192771437675)
XLA Ops:
  0.6 3.0 %collective-permute-start = (bf16[256,1024]{1,0:T(8,128)(2,1)}, bf16[256,1024]{1,0:T(8,128)(2,1)S(1)}, u32[]{:S(2)}, u32[]{:S(2)}) collective-permute-start(bf16[256,1024]{1,0:T(8,128)(2,1)} %param.2), channel_id=1, source_target_pairs={{0,2},{1,5},{2,0},{3,7},{4,6},{5,1},{6,4},{7,3},{8,10},{9,13},{10,... | collective-permute-start | bytes 1572872 | tf_op jit(solution)/shard_map/ppermute | solution.py:230
  3.6 1.5 %collective-permute-start.1 = (bf16[256,1024]{1,0:T(8,128)(2,1)}, bf16[256,1024]{1,0:T(8,128)(2,1)S(1)}, u32[]{:S(2)}, u32[]{:S(2)}) collective-permute-start(bf16[256,1024]{1,0:T(8,128)(2,1)} %param.2), channel_id=1, source_target_pairs={{0,4},{1,3},{2,6},{3,1},{4,0},{5,7},{6,2},{7,5},{8,12},{9,11},{10,... | collective-permute-start | bytes 1572872 | tf_op jit(solution)/shard_map/ppermute | solution.py:231
  5.2 1.1 %convert_element_type.21.refs_0_ = bf16[128,1024]{1,0:T(8,128)(2,1)S(1)} convert(f32[128,1024]{1,0:T(8,128)} %refs_3_.1) | non-fusion elementwise | flops 131072 | bytes 786432 | tf_op jit(solution)/shard_map/convert_element_type | solution.py:226
  6.2 2.7 %collective-permute-start.3 = (bf16[128,1024]{1,0:T(8,128)(2,1)S(1)}, bf16[128,1024]{1,0:T(8,128)(2,1)S(1)}, u32[]{:S(2)}, u32[]{:S(2)}) collective-permute-start(bf16[128,1024]{1,0:T(8,128)(2,1)S(1)} %convert_element_type.21.refs_0_), channel_id=1, source_target_pairs={{0,16},{8,24},{16,0},{24,8},{1,17},{9,25},{17,1},{25,9},{2,18},{10... | collective-permute-start | bytes 786440 | tf_op jit(solution)/shard_map/ppermute | solution.py:22
  8.9 1.6 %collective-permute-start.2 = (bf16[128,1024]{1,0:T(8,128)(2,1)S(1)}, bf16[128,1024]{1,0:T(8,128)(2,1)S(1)}, u32[]{:S(2)}, u32[]{:S(2)}) collective-permute-start(bf16[128,1024]{1,0:T(8,128)(2,1)S(1)} %convert_element_type.21.refs_0_), channel_id=1, source_target_pairs={{0,8},{8,0},{16,24},{24,16},{1,9},{9,1},{17,25},{25,17},{2,10},{10... | collective-permute-start | bytes 786440 | tf_op jit(solution)/shard_map/ppermute | solution.py:22
  10.5 1.1 %constant_dynamic-update-slice_fusion.2 = bf16[768,1024]{1,0:T(8,128)(2,1)S(1)} fusion(bf16[256,1024]{1,0:T(8,128)(2,1)} %param.2), kind=kLoop, calls=%fused_computation.2 | loop fusion | bytes 1048576
  11.5 4.6 %collective-permute-done = bf16[256,1024]{1,0:T(8,128)(2,1)S(1)} collective-permute-done((bf16[256,1024]{1,0:T(8,128)(2,1)}, bf16[256,1024]{1,0:T(8,128)(2,1)S(1)}, u32[]{:S(2)}, u32[]{:S(2)}) %collective-permute-start) | collective-permute-done | bytes 524320 | tf_op jit(solution)/shard_map/ppermute | solution.py:230
  16.2 4.2 %collective-permute-done.3.refs_2_ = bf16[128,1024]{1,0:T(8,128)(2,1)S(1)} collective-permute-done((bf16[128,1024]{1,0:T(8,128)(2,1)S(1)}, bf16[128,1024]{1,0:T(8,128)(2,1)S(1)}, u32[]{:S(2)}, u32[]{:S(2)}) %collective-permute-start.3) | collective-permute-done | bytes 262176 | tf_op jit(solution)/shard_map/ppermute | solution.py:22
  21.1 1.4 %collective-permute-start.6 = (bf16[128,1024]{1,0:T(8,128)(2,1)S(1)}, bf16[128,1024]{1,0:T(8,128)(2,1)S(1)}, u32[]{:S(2)}, u32[]{:S(2)}) collective-permute-start(bf16[128,1024]{1,0:T(8,128)(2,1)S(1)} %collective-permute-done.3.refs_2_), channel_id=1, source_target_pairs={{0,8},{8,0},{16,24},{24,16},{1,9},{9,1},{17,25},{25,17},{2,10},{10... | collective-permute-start | bytes 786440 | tf_op jit(solution)/shard_map/ppermute | solution.py:22
  22.5 1.0 %score_rows.5 = (f32[3,384,256]{2,1,0:T(8,128)S(1)}, f32[2,3,256]{2,1,0:T(4,128)S(1)}) custom-call(bf16[128,1024]{1,0:T(8,128)(2,1)S(1)} %convert_element_type.21.refs_0_, bf16[128,1024]{1,0:T(8,128)(2,1)S(1)} %collective-permute-done.2.refs_1_, bf16[128,1024]{1,0:T(8,128)(2,1)S(1)} %collective-permute-done.3.refs_2_, ...), custom_call_target="tpu_custom_call" | custom-call | flops 603979776 | bytes 2359296 | tf_op jit(solution)/shard_map/score_rows/pallas_call | solution.py:67
  24.0 1.0 %score_rows.6 = (f32[3,384,256]{2,1,0:T(8,128)S(1)}, f32[2,3,256]{2,1,0:T(4,128)S(1)}) custom-call(bf16[128,1024]{1,0:T(8,128)(2,1)S(1)} %convert_element_type.21.refs_0_, bf16[128,1024]{1,0:T(8,128)(2,1)S(1)} %collective-permute-done.2.refs_1_, bf16[128,1024]{1,0:T(8,128)(2,1)S(1)} %collective-permute-done.3.refs_2_, ...), custom_call_target="tpu_custom_call" | custom-call | flops 603979776 | bytes 2359296 | tf_op jit(solution)/shard_map/score_rows/pallas_call | solution.py:67
  25.0 4.6 %collective-permute-done.6.refs_0_.refs_3_ = bf16[128,1024]{1,0:T(8,128)(2,1)S(1)} collective-permute-done((bf16[128,1024]{1,0:T(8,128)(2,1)S(1)}, bf16[128,1024]{1,0:T(8,128)(2,1)S(1)}, u32[]{:S(2)}, u32[]{:S(2)}) %collective-permute-start.6) | collective-permute-done | bytes 262176 | tf_op jit(solution)/shard_map/ppermute | solution.py:22
  30.4 1.3 %score_rows.7 = (f32[6,128,256]{2,1,0:T(8,128)S(1)}, f32[2,6,256]{2,1,0:T(8,128)S(1)}) custom-call(bf16[128,1024]{1,0:T(8,128)(2,1)S(1)} %collective-permute-done.6.refs_0_.refs_3_, bf16[768,1024]{1,0:T(8,128)(2,1)S(1)} %constant_dynamic-update-slice_fusion.refs_3_.refs_1_.refs_4_, ...), custom_call_target="tpu_custom_call" | custom-call | flops 402653184 | bytes 3407872 | tf_op jit(solution)/shard_map/score_rows/pallas_call | solution.py:67
  34.3 1.7 %collective-permute-start.11 = (f32[2,8,256]{2,1,0:T(8,128)S(1)}, f32[2,8,256]{2,1,0:T(8,128)S(1)}, u32[]{:S(2)}, u32[]{:S(2)}) collective-permute-start(f32[2,8,256]{2,1,0:T(8,128)S(1)} %join_rows.2.pair_ref), channel_id=1, source_target_pairs={{0,6},{1,7},{2,4},{3,5},{4,2},{5,3},{6,0},{7,1},{8,14},{9,15},{10,... | collective-permute-start | bytes 49160 | tf_op jit(solution)/shard_map/ppermute | solution.py:99
  35.9 1.3 %collective-permute-start.9 = (f32[2,8,256]{2,1,0:T(8,128)S(1)}, f32[2,8,256]{2,1,0:T(8,128)S(1)}, u32[]{:S(2)}, u32[]{:S(2)}) collective-permute-start(f32[2,8,256]{2,1,0:T(8,128)S(1)} %join_rows.2.pair_ref), channel_id=1, source_target_pairs={{0,2},{1,5},{2,0},{3,7},{4,6},{5,1},{6,4},{7,3},{8,10},{9,13},{10,... | collective-permute-start | bytes 49160 | tf_op jit(solution)/shard_map/ppermute | solution.py:99
  37.5 1.4 %collective-permute-done.11.refs_2_ = f32[2,8,256]{2,1,0:T(8,128)S(1)} collective-permute-done((f32[2,8,256]{2,1,0:T(8,128)S(1)}, f32[2,8,256]{2,1,0:T(8,128)S(1)}, u32[]{:S(2)}, u32[]{:S(2)}) %collective-permute-start.11) | collective-permute-done | bytes 16416 | tf_op jit(solution)/shard_map/ppermute | solution.py:99
  40.8 1.6 %collective-permute-start.12 = (f16[136,1024]{1,0:T(8,128)(2,1)S(1)}, f16[136,1024]{1,0:T(8,128)(2,1)S(1)}, u32[]{:S(2)}, u32[]{:S(2)}) collective-permute-start(f16[136,1024]{1,0:T(8,128)(2,1)S(1)} %convert_element_type.22), channel_id=1, source_target_pairs={{0,8},{8,0},{16,24},{24,16},{1,9},{9,1},{17,25},{25,17},{2,10},{10... | collective-permute-start | bytes 835592 | tf_op jit(solution)/shard_map/ppermute | solution.py:22
  42.4 2.4 %weighted_sums.2 = (f32[136,1024]{1,0:T(8,128)S(1)}, f32[136,1024]{1,0:T(8,128)S(1)}, f32[136,1024]{1,0:T(8,128)S(1)}) custom-call(f32[8,256]{1,0:T(8,128)S(1)} %join_rows.3.lognorm_ref, f32[3,384,256]{2,1,0:T(8,128)S(1)} %get-tuple-element.41.refs_0_, f32[3,384,256]{2,1,0:T(8,128)S(1)} %get-tuple-element.42.refs_1_, ...), custom_call_target="tpu_custom_call" | custom-call | flops 1610612736 | bytes 4194304 | tf_op jit(solution)/shard_map/weighted_sums/pallas_call | solution.py:207
  44.8 3.1 %collective-permute-done.12 = f16[136,1024]{1,0:T(8,128)(2,1)S(1)} collective-permute-done((f16[136,1024]{1,0:T(8,128)(2,1)S(1)}, f16[136,1024]{1,0:T(8,128)(2,1)S(1)}, u32[]{:S(2)}, u32[]{:S(2)}) %collective-permute-start.12) | collective-permute-done | bytes 278560 | tf_op jit(solution)/shard_map/ppermute | solution.py:22
  48.2 1.6 %collective-permute-start.13 = (f16[136,1024]{1,0:T(8,128)(2,1)S(1)}, f16[136,1024]{1,0:T(8,128)(2,1)S(1)}, u32[]{:S(2)}, u32[]{:S(2)}) collective-permute-start(f16[136,1024]{1,0:T(8,128)(2,1)S(1)} %convert_element_type.25), channel_id=1, source_target_pairs={{0,8},{8,0},{16,24},{24,16},{1,9},{9,1},{17,25},{25,17},{2,10},{10... | collective-permute-start | bytes 835592 | tf_op jit(solution)/shard_map/ppermute | solution.py:22
  49.8 2.3 %collective-permute-start.14 = (f16[136,1024]{1,0:T(8,128)(2,1)S(1)}, f16[136,1024]{1,0:T(8,128)(2,1)S(1)}, u32[]{:S(2)}, u32[]{:S(2)}) collective-permute-start(f16[136,1024]{1,0:T(8,128)(2,1)S(1)} %convert_element_type.24), channel_id=1, source_target_pairs={{0,16},{8,24},{16,0},{24,8},{1,17},{9,25},{17,1},{25,9},{2,18},{10... | collective-permute-start | bytes 835592 | tf_op jit(solution)/shard_map/ppermute | solution.py:22
  52.7 7.3 %collective-permute-done.13 = f16[136,1024]{1,0:T(8,128)(2,1)S(1)} collective-permute-done((f16[136,1024]{1,0:T(8,128)(2,1)S(1)}, f16[136,1024]{1,0:T(8,128)(2,1)S(1)}, u32[]{:S(2)}, u32[]{:S(2)}) %collective-permute-start.13) | collective-permute-done | bytes 278560 | tf_op jit(solution)/shard_map/ppermute | solution.py:22
  60.0 2.6 %collective-permute-done.14 = f16[136,1024]{1,0:T(8,128)(2,1)S(1)} collective-permute-done((f16[136,1024]{1,0:T(8,128)(2,1)S(1)}, f16[136,1024]{1,0:T(8,128)(2,1)S(1)}, u32[]{:S(2)}, u32[]{:S(2)}) %collective-permute-start.14) | collective-permute-done | bytes 278560 | tf_op jit(solution)/shard_map/ppermute | solution.py:22
  62.7 1.0 %update_centroids.1 = (f32[128,1024]{1,0:T(8,128)}, f32[1,128]{1,0:T(1,128)}) custom-call(f32[136,1024]{1,0:T(8,128)S(1)} %get-tuple-element.45.refs_0_, f32[136,1024]{1,0:T(8,128)S(1)} %convert_element_type.26.refs_1_, f32[136,1024]{1,0:T(8,128)S(1)} %convert_element_type.27.refs_2_, f32[128,1024]{1,0:T(8,128)S(1)} %copy-done), custom_call_target="tpu_custom_call" | custom-call | tf_op jit(solution)/shard_map/update_centroids/pallas_call | solution.py:189
  (30 shorter events, 7.6 us)
Async XLA Ops:
  0.6 15.5 %collective-permute-start = (bf16[256,1024]{1,0:T(8,128)(2,1)}, bf16[256,1024]{1,0:T(8,128)(2,1)S(1)}, u32[]{:S(2)}, u32[]{:S(2)}) collective-permute-start(bf16[256,1024]{1,0:T(8,128)(2,1)} %param.2), channel_id=1, source_target_pairs={{0,2},{1,5},{2,0},{3,7},{4,6},{5,1},{6,4},{7,3},{8,10},{9,13},{10,... | collective-permute-start | bytes 1572872 | tf_op jit(solution)/shard_map/ppermute | solution.py:230
  3.6 12.6 %collective-permute-start.1 = (bf16[256,1024]{1,0:T(8,128)(2,1)}, bf16[256,1024]{1,0:T(8,128)(2,1)S(1)}, u32[]{:S(2)}, u32[]{:S(2)}) collective-permute-start(bf16[256,1024]{1,0:T(8,128)(2,1)} %param.2), channel_id=1, source_target_pairs={{0,4},{1,3},{2,6},{3,1},{4,0},{5,7},{6,2},{7,5},{8,12},{9,11},{10,... | collective-permute-start | bytes 1572872 | tf_op jit(solution)/shard_map/ppermute | solution.py:231
  6.2 14.2 %collective-permute-start.3 = (bf16[128,1024]{1,0:T(8,128)(2,1)S(1)}, bf16[128,1024]{1,0:T(8,128)(2,1)S(1)}, u32[]{:S(2)}, u32[]{:S(2)}) collective-permute-start(bf16[128,1024]{1,0:T(8,128)(2,1)S(1)} %convert_element_type.21.refs_0_), channel_id=1, source_target_pairs={{0,16},{8,24},{16,0},{24,8},{1,17},{9,25},{17,1},{25,9},{2,18},{10... | collective-permute-start | bytes 786440 | tf_op jit(solution)/shard_map/ppermute | solution.py:22
  8.9 11.7 %collective-permute-start.2 = (bf16[128,1024]{1,0:T(8,128)(2,1)S(1)}, bf16[128,1024]{1,0:T(8,128)(2,1)S(1)}, u32[]{:S(2)}, u32[]{:S(2)}) collective-permute-start(bf16[128,1024]{1,0:T(8,128)(2,1)S(1)} %convert_element_type.21.refs_0_), channel_id=1, source_target_pairs={{0,8},{8,0},{16,24},{24,16},{1,9},{9,1},{17,25},{25,17},{2,10},{10... | collective-permute-start | bytes 786440 | tf_op jit(solution)/shard_map/ppermute | solution.py:22
  20.6 3.4 %collective-permute-start.5 = (bf16[768,1024]{1,0:T(8,128)(2,1)S(1)}, bf16[768,1024]{1,0:T(8,128)(2,1)S(1)}, u32[]{:S(2)}, u32[]{:S(2)}) collective-permute-start(bf16[768,1024]{1,0:T(8,128)(2,1)S(1)} %constant_dynamic-update-slice_fusion.refs_3_.refs_1_.refs_4_), channel_id=1, source_target_pairs={{0,1},{1,0},{2,3},{3,2},{4,5},{5,4},{6,7},{7,6},{8,9},{9,8},{10,11... | collective-permute-start | bytes 4718600 | tf_op jit(solution)/shard_map/ppermute | solution.py:22
  20.6 9.2 %collective-permute-start.4 = (bf16[256,1024]{1,0:T(8,128)(2,1)S(1)}, bf16[256,1024]{1,0:T(8,128)(2,1)S(1)}, u32[]{:S(2)}, u32[]{:S(2)}) collective-permute-start(bf16[256,1024]{1,0:T(8,128)(2,1)S(1)} %collective-permute-done), channel_id=1, source_target_pairs={{0,4},{1,3},{2,6},{3,1},{4,0},{5,7},{6,2},{7,5},{8,12},{9,11},{10,... | collective-permute-start | bytes 1572872 | tf_op jit(solution)/shard_map/ppermute | solution.py:241
  21.1 8.5 %collective-permute-start.6 = (bf16[128,1024]{1,0:T(8,128)(2,1)S(1)}, bf16[128,1024]{1,0:T(8,128)(2,1)S(1)}, u32[]{:S(2)}, u32[]{:S(2)}) collective-permute-start(bf16[128,1024]{1,0:T(8,128)(2,1)S(1)} %collective-permute-done.3.refs_2_), channel_id=1, source_target_pairs={{0,8},{8,0},{16,24},{24,16},{1,9},{9,1},{17,25},{25,17},{2,10},{10... | collective-permute-start | bytes 786440 | tf_op jit(solution)/shard_map/ppermute | solution.py:22
  29.8 1.9 %collective-permute-start.7 = (bf16[256,1024]{1,0:T(8,128)(2,1)S(1)}, bf16[256,1024]{1,0:T(8,128)(2,1)S(1)}, u32[]{:S(2)}, u32[]{:S(2)}) collective-permute-start(bf16[256,1024]{1,0:T(8,128)(2,1)S(1)} %collective-permute-done.4.refs_4_.refs_6_.refs_5_), channel_id=1, source_target_pairs={{0,1},{1,0},{2,3},{3,2},{4,5},{5,4},{6,7},{7,6},{8,9},{9,8},{10,11... | collective-permute-start | bytes 1572872 | tf_op jit(solution)/shard_map/ppermute | solution.py:22
  32.3 1.4 %collective-permute-start.8 = (f32[2,8,256]{2,1,0:T(8,128)S(1)}, f32[2,8,256]{2,1,0:T(8,128)S(1)}, u32[]{:S(2)}, u32[]{:S(2)}) collective-permute-start(f32[2,8,256]{2,1,0:T(8,128)S(1)} %get-tuple-element.40.pair_ref), channel_id=1, source_target_pairs={{0,1},{1,0},{2,3},{3,2},{4,5},{5,4},{6,7},{7,6},{8,9},{9,8},{10,11... | collective-permute-start | bytes 49160 | tf_op jit(solution)/shard_map/ppermute | solution.py:99
  33.7 3.8 %collective-permute-start.10 = (f32[2,8,256]{2,1,0:T(8,128)S(1)}, f32[2,8,256]{2,1,0:T(8,128)S(1)}, u32[]{:S(2)}, u32[]{:S(2)}) collective-permute-start(f32[2,8,256]{2,1,0:T(8,128)S(1)} %join_rows.2.pair_ref), channel_id=1, source_target_pairs={{0,4},{1,3},{2,6},{3,1},{4,0},{5,7},{6,2},{7,5},{8,12},{9,11},{10,... | collective-permute-start | bytes 49160 | tf_op jit(solution)/shard_map/ppermute | solution.py:99
  34.3 4.6 %collective-permute-start.11 = (f32[2,8,256]{2,1,0:T(8,128)S(1)}, f32[2,8,256]{2,1,0:T(8,128)S(1)}, u32[]{:S(2)}, u32[]{:S(2)}) collective-permute-start(f32[2,8,256]{2,1,0:T(8,128)S(1)} %join_rows.2.pair_ref), channel_id=1, source_target_pairs={{0,6},{1,7},{2,4},{3,5},{4,2},{5,3},{6,0},{7,1},{8,14},{9,15},{10,... | collective-permute-start | bytes 49160 | tf_op jit(solution)/shard_map/ppermute | solution.py:99
  35.9 3.7 %collective-permute-start.9 = (f32[2,8,256]{2,1,0:T(8,128)S(1)}, f32[2,8,256]{2,1,0:T(8,128)S(1)}, u32[]{:S(2)}, u32[]{:S(2)}) collective-permute-start(f32[2,8,256]{2,1,0:T(8,128)S(1)} %join_rows.2.pair_ref), channel_id=1, source_target_pairs={{0,2},{1,5},{2,0},{3,7},{4,6},{5,1},{6,4},{7,3},{8,10},{9,13},{10,... | collective-permute-start | bytes 49160 | tf_op jit(solution)/shard_map/ppermute | solution.py:99
  40.8 7.2 %collective-permute-start.12 = (f16[136,1024]{1,0:T(8,128)(2,1)S(1)}, f16[136,1024]{1,0:T(8,128)(2,1)S(1)}, u32[]{:S(2)}, u32[]{:S(2)}) collective-permute-start(f16[136,1024]{1,0:T(8,128)(2,1)S(1)} %convert_element_type.22), channel_id=1, source_target_pairs={{0,8},{8,0},{16,24},{24,16},{1,9},{9,1},{17,25},{25,17},{2,10},{10... | collective-permute-start | bytes 835592 | tf_op jit(solution)/shard_map/ppermute | solution.py:22
  48.1 14.6 %copy-start = (f32[128,1024]{1,0:T(8,128)S(1)}, f32[128,1024]{1,0:T(8,128)}, u32[]{:S(2)}) copy-start(f32[128,1024]{1,0:T(8,128)} %refs_3_.1) | copy-start | bytes 1572868
  48.2 11.8 %collective-permute-start.13 = (f16[136,1024]{1,0:T(8,128)(2,1)S(1)}, f16[136,1024]{1,0:T(8,128)(2,1)S(1)}, u32[]{:S(2)}, u32[]{:S(2)}) collective-permute-start(f16[136,1024]{1,0:T(8,128)(2,1)S(1)} %convert_element_type.25), channel_id=1, source_target_pairs={{0,8},{8,0},{16,24},{24,16},{1,9},{9,1},{17,25},{25,17},{2,10},{10... | collective-permute-start | bytes 835592 | tf_op jit(solution)/shard_map/ppermute | solution.py:22
  49.8 12.8 %collective-permute-start.14 = (f16[136,1024]{1,0:T(8,128)(2,1)S(1)}, f16[136,1024]{1,0:T(8,128)(2,1)S(1)}, u32[]{:S(2)}, u32[]{:S(2)}) collective-permute-start(f16[136,1024]{1,0:T(8,128)(2,1)S(1)} %convert_element_type.24), channel_id=1, source_target_pairs={{0,16},{8,24},{16,0},{24,8},{1,17},{9,25},{17,1},{25,9},{2,18},{10... | collective-permute-start | bytes 835592 | tf_op jit(solution)/shard_map/ppermute | solution.py:22

commit v11 on v10

--- a/solution.py
+++ b/solution.py
@@ -83,36 +83,39 @@
 
 
 def join_kernel(places, last, pair_ref, *refs):
-    out_ref = refs[-1]
+    others, outs = refs[: len(places)], refs[len(places) :]
     top, total = pair_ref[0], pair_ref[1]
-    for ref, where in zip(refs[:-1], places):
+    for ref, where in zip(others, places):
         other = [jnp.concatenate([ref[i, p : p + 1] for p in where]) for i in range(2)]
         top, total = merge((top, total), other)
     if last:
-        out_ref[...] = top + jnp.log(total)
-    else:
-        out_ref[0] = top
-        out_ref[1] = total
-
-
-def join(pairs, routes, places, last):
-    others = [lax.ppermute(pairs, "cent", route) for route in routes]
+        outs[0][...] = top + jnp.log(total)
+    for ref in outs[1:] if last else outs:
+        for i in range(0, ref.shape[0], 2):
+            ref[i] = top
+            ref[i + 1] = total
+
+
+def join(pairs, sent, routes, places, last, copies=()):
+    others = [lax.ppermute(x, "cent", route) for x, route in zip(sent, routes)]
+    n, r = pairs.shape[1:]
+    shapes = [(n, r) if last else (2, n, r)] + [(2 * c, n, r) for c in copies]
     return pl.pallas_call(
         functools.partial(join_kernel, places, last),
-        out_shape=jax.ShapeDtypeStruct(pairs.shape[1:] if last else pairs.shape, jnp.float32),
+        out_shape=[jax.ShapeDtypeStruct(shape, jnp.float32) for shape in shapes],
         in_specs=[VMEM] * (1 + len(others)),
-        out_specs=VMEM,
+        out_specs=[VMEM] * len(shapes),
         compiler_params=PARAMS,
         name="join_rows",
     )(pairs, *others)
 
 
 def sums_kernel(n_parts, picks, parts, lognorm_ref, *refs):
-    score_refs, row_refs = refs[:n_parts], refs[n_parts : -len(parts)]
-    outs = refs[-len(parts) :]
+    n_out = 2 * len(parts)
+    score_refs, row_refs, outs = refs[:n_parts], refs[n_parts:-n_out], refs[-n_out:]
     r = lognorm_ref.shape[1]
     ones = jnp.ones((SIDE, r), jnp.bfloat16)
-    for out, (places, size, unit) in zip(outs, parts):
+    for n, (places, size, packed) in enumerate(parts):
         total, tally = None, None
         for j, (i, at) in enumerate(picks):
             k, block, first = places[j]
@@ -124,79 +127,91 @@
             )
             total = more if total is None else total + more
             tally = count if tally is None else tally + count
-        wide = jnp.concatenate(
-            [tally, jnp.zeros((SIDE, total.shape[1] - size), jnp.float32)], axis=1
-        )
-        if unit:
-            total, wide = pack(total, wide[0:1], unit)
-        out[0:size] = total
-        out[size : size + SIDE] = wide
-
-
-def pack(total, tally, unit):
-    peak = jnp.max(jnp.abs(total), axis=0, keepdims=True)
-    power = jnp.clip(jnp.ceil(jnp.log2(peak)), -100.0, 100.0)
-    high = jnp.floor(tally * unit)
-    rest = (tally * unit - high) * 1024.0
-    middle = jnp.floor(rest)
-    low = (rest - middle) * 1024.0
-    blank = jnp.zeros((SIDE - 4, total.shape[1]), jnp.float32)
-    return total * jnp.exp2(14.0 - power), jnp.concatenate([power, high, middle, low, blank])
-
-
-def unpack(values, unit):
-    size = values.shape[0] - SIDE
-    power, high, middle, low = (values[size + i : size + i + 1] for i in range(4))
-    tally = (high + (middle + low * (1.0 / 1024.0)) * (1.0 / 1024.0)) * (1.0 / unit)
-    return values[:size] * jnp.exp2(power - 14.0), tally
-
-
-def relay_kernel(unit, own_ref, got_ref, out_ref):
-    size = own_ref.shape[0] - SIDE
-    more, count = unpack(got_ref[...], unit)
-    total, wide = pack(own_ref[0:size] + more, own_ref[size : size + 1] + count, unit * 0.5)
-    out_ref[0:size] = total
-    out_ref[size : size + SIDE] = wide
-
-
-def relay(own, got, unit):
+        blank = jnp.zeros((1, total.shape[1] - size), jnp.float32)
+        tally = jnp.concatenate([tally[0:1], blank], axis=1)
+        write(outs[2 * n], outs[2 * n + 1], total, tally, packed)
+
+
+def write(body_ref, side_ref, total, tally, packed):
+    power = jnp.zeros_like(tally)
+    if packed:
+        peak = jnp.max(jnp.abs(total), axis=0, keepdims=True)
+        power = jnp.clip(jnp.ceil(jnp.log2(peak)), -100.0, 100.0)
+        total = total * jnp.exp2(14.0 - power)
+    body_ref[...] = total
+    blank = jnp.zeros((SIDE - 2, tally.shape[1]), jnp.float32)
+    side_ref[...] = jnp.concatenate([power, tally, blank])
+
+
+def gather_parts(own, refs):
+    total, tally = own[0][...], own[1][1:2]
+    for body, side in zip(refs[0::2], refs[1::2]):
+        total = total + body[...] * jnp.exp2(side[0:1] - 14.0)
+        tally = tally + side[1:2]
+    return total, tally
+
+
+def send(part, mask, size):
+    body, side = part
+    return swap(body.astype(jnp.float16), "dp", size, mask), swap(side, "dp", size, mask)
+
+
+def widen(messages):
+    return [x for body, side in messages for x in (body.astype(jnp.float32), side)]
+
+
+def relay_kernel(*refs):
+    total, tally = gather_parts(refs[:2], refs[2:-2])
+    write(refs[-2], refs[-1], total, tally, True)
+
+
+def relay(own, got):
     return pl.pallas_call(
-        functools.partial(relay_kernel, unit),
-        out_shape=jax.ShapeDtypeStruct(own.shape, jnp.float32),
-        in_specs=[VMEM] * 2,
-        out_specs=VMEM,
+        relay_kernel,
+        out_shape=[jax.ShapeDtypeStruct(x.shape, jnp.float32) for x in own],
+        in_specs=[VMEM] * (2 + 2 * len(got)),
+        out_specs=[VMEM] * 2,
         compiler_params=PARAMS,
         name="relay_sums",
-    )(own, got)
-
-
-def final_kernel(units, *refs):
-    own_ref, got_refs, codebook_ref, new_ref, tally_ref = refs[0], refs[1:-3], *refs[-3:]
-    size, depth = codebook_ref.shape
-    total, tally = own_ref[0:size], own_ref[size : size + 1]
-    for ref, unit in zip(got_refs, units):
-        more, count = unpack(ref[...], unit)
-        total, tally = total + more, tally + count
+    )(*own, *widen(got))
+
+
+def final_kernel(*refs):
+    codebook_ref, new_ref, tally_ref, buffer, sems = refs[-5:]
+    size = codebook_ref.shape[0]
+    total, tally = gather_parts(refs[:2], refs[2:-5])
     tally = tally[:, :size]
     tally_ref[...] = tally
-    column = jnp.transpose(jnp.broadcast_to(tally, (size, size)))[:, 0:1]
-    new_ref[...] = (total + PRIOR * codebook_ref[...]) / (column + PRIOR)
+    weight = jnp.transpose(jnp.broadcast_to(tally, (size, size)))[:, 0:1] + PRIOR
+    step = size // sems.shape[0]
+    copies = []
+    for i in range(sems.shape[0]):
+        at = slice(i * step, (i + 1) * step)
+        buffer[at] = (total[at] + PRIOR * codebook_ref[at]) / weight[at]
+        copy = pltpu.make_async_copy(buffer.at[at], new_ref.at[at], sems.at[i])
+        copy.start()
+        copies.append(copy)
+    for copy in copies:
+        copy.wait()
 
 
 def finish(codebook, own, got):
     size = codebook.shape[0]
-    arrays = [own] + [message.astype(jnp.float32) for message, _ in got] + [codebook]
     new, tally = pl.pallas_call(
-        functools.partial(final_kernel, [unit for _, unit in got]),
+        final_kernel,
         out_shape=(
             jax.ShapeDtypeStruct(codebook.shape, jnp.float32),
             jax.ShapeDtypeStruct((1, size), jnp.float32),
         ),
-        in_specs=[VMEM] * len(arrays),
-        out_specs=(VMEM, VMEM),
+        in_specs=[VMEM] * (3 + 2 * len(got)),
+        out_specs=(pl.BlockSpec(memory_space=pl.ANY), VMEM),
+        scratch_shapes=[
+            pltpu.VMEM(codebook.shape, jnp.float32),
+            pltpu.SemaphoreType.DMA((4,)),
+        ],
         compiler_params=PARAMS,
         name="update_centroids",
-    )(*arrays)
+    )(*own, *widen(got), codebook)
     return new, tally[0]
 
 
@@ -204,11 +219,13 @@
     size = parts[0][1]
     depth = rows[0].shape[1]
     n_r, r = lognorm.shape
-    return pl.pallas_call(
+    out = pl.pallas_call(
         functools.partial(sums_kernel, len(scores), picks, parts),
-        out_shape=[jax.ShapeDtypeStruct((size + SIDE, depth), jnp.float32) for _ in parts],
+        out_shape=[
+            jax.ShapeDtypeStruct((n, depth), jnp.float32) for _ in parts for n in (size, SIDE)
+        ],
         in_specs=[VMEM] * (1 + len(scores) + len(rows)),
-        out_specs=[VMEM] * len(parts),
+        out_specs=[VMEM] * (2 * len(parts)),
         compiler_params=PARAMS,
         cost_estimate=pl.CostEstimate(
             flops=2 * len(parts) * n_r * size * r * depth,
@@ -217,12 +234,12 @@
         ),
         name="weighted_sums",
     )(lognorm, *scores, *rows)
+    return list(zip(out[0::2], out[1::2]))
 
 
 def local(n_dp, n_cent, embeddings, codebook):
     own_rows = embeddings.shape[0]
     size = codebook.shape[0]
-    unit = 1024.0 / (own_rows * n_cent)
     rounded = codebook.astype(jnp.bfloat16)
     if n_cent == 8:
         by_p = [(i, i ^ (4 if i & 1 else 2)) for i in range(n_cent)]
@@ -268,36 +285,32 @@
         last_scores, last_places = [s_1], [(0, j, 0) for j in order]
     if n_cent == 8:
         where = [order.index((j ^ 1) & 1 | (j & 2) << 1 | (j & 4) >> 1) for j in order]
-        pairs = join(pairs, [partner(n_cent, 1)], [where], False)
-        routes = [by_p, by_q, partner(n_cent, 6)]
-        where = [[order.index(j ^ mask) for j in order] for mask in (2, 4, 6)]
-        lognorm = join(pairs, routes, where, True)
+        pairs, twice = join(pairs, [pairs], [partner(n_cent, 1)], [where], False, (2,))
+        routes = [partner(n_cent, 6), by_p, by_q]
+        where = [[order.index(j ^ mask) for j in order] for mask in (6, 2, 4)]
+        (lognorm,) = join(pairs, [twice, pairs, pairs], routes, where, True)
     else:
         for bit in range(n_cent.bit_length() - 1):
             where = [j ^ (1 << bit) for j in order]
-            pairs = join(pairs, [partner(n_cent, 1 << bit)], [where], 2 << bit >= n_cent)
+            route = partner(n_cent, 1 << bit)
+            (pairs,) = join(pairs, [pairs], [route], [where], 2 << bit >= n_cent)
         lognorm = pairs
 
-    def part(k, unit):
-        return [(i, j, k * size) for i, j in places], size, unit
-
-    (first,) = weighted([(last_places, size, unit)], lognorm, last_scores, rows, picks)
-    first = first.astype(jnp.float16)
+    def part(k, packed):
+        return [(i, j, k * size) for i, j in places], size, packed
+
+    (first,) = weighted([(last_places, size, True)], lognorm, last_scores, rows, picks)
     if n_dp == 4:
-        first = swap(first, "dp", n_dp, 1)
-        parts = [part(2, 0), part(1, unit), part(0, 0)]
-        far_out, near_out, own = weighted(parts, lognorm, scores, rows, picks)
-        far_out = relay(far_out, first.astype(jnp.float32), unit).astype(jnp.float16)
-        far_out, near_out = lax.optimization_barrier((far_out, near_out))
-        far_out = swap(far_out, "dp", n_dp, 2)
-        near_out = swap(near_out.astype(jnp.float16), "dp", n_dp, 1)
-        got = [(near_out, unit), (far_out, unit * 0.5)]
+        first = send(first, 1, n_dp)
+        parts = [part(2, False), part(1, True), part(0, False)]
+        far_sum, near_sum, own = weighted(parts, lognorm, scores, rows, picks)
+        far_sum = relay(far_sum, [first])
+        far_sum, near_sum = lax.optimization_barrier((far_sum, near_sum))
+        got = [send(near_sum, 1, n_dp), send(far_sum, 2, n_dp)]
     else:
-        parts = [part(k, unit if k else 0) for k in range(n_dp - 1)]
-        out = weighted(parts, lognorm, scores, rows, picks)
-        own = out[0]
-        sent = [o.astype(jnp.float16) for o in out[1:]] + [first]
-        got = [(swap(m, "dp", n_dp, k + 1), unit) for k, m in enumerate(sent)]
+        parts = [part(k, k > 0) for k in range(n_dp - 1)]
+        own, *others = weighted(parts, lognorm, scores, rows, picks)
+        got = [send(other, k + 1, n_dp) for k, other in enumerate(others + [first])]
     new_codebook, tally = finish(codebook, own, got)
     return new_codebook, tally, lognorm[0]
 

time: 63.9 us -> 66.5 us (1.041)
  starting transfers between devices: 20.3 us -> 22 us
    ppermute x8 -> x11, starting transfers between devices: 11.2 us -> 12.8 us  [swap(): return lax.ppermute(x, axis, partner(size, mask))]
    ppermute x8 -> x11, waiting for transfers between devices: 22.4 us -> 23.1 us  [swap(): return lax.ppermute(x, axis, partner(size, mask))]
  transfers between devices with their start and end apart: 15 -> 18, of which waited for: 13 -> 14; matrix products, arithmetic and copies ran while one was open for 4% -> 4% of each run, Pallas kernels for 10% -> 10%
where the time goes in v11:
time: 66.5 us; the launch traced here: 66.3 us
  waiting for transfers between devices  31 us (47%)
  starting transfers between devices  22 us (33%)
  Pallas kernels  9.59 us (14%)
  local copies, waits for them, and re-layouts  1.72 us (3%)
  other arithmetic  1.27 us (2%)
  between operations  0.76 us (1%)
    ppermute x11, waiting for transfers between devices, swap(): return lax.ppermute(x, axis, partner(size, mask))  23.1 us
    ppermute x11, starting transfers between devices, swap(): return lax.ppermute(x, axis, partner(size, mask))  12.8 us
    ppermute x1, waiting for transfers between devices, local(): from_p = lax.ppermute(embeddings, 'cent', by_p)  4.61 us
    pallas_call x5, Pallas kernels, score(): pl.pallas_call(functools.partial(score_kernel, n_c, len(rows), picks, beg...  4.51 us
    ppermute x4, starting transfers between devices, join(): others = [lax.ppermute(x, 'cent', route) for x, route in zip(sent, routes)]  4.11 us
    pallas_call x2, Pallas kernels, weighted(): pl.pallas_call(functools.partial(sums_kernel, len(scores), picks, parts),...  3.4 us
    ppermute x4, waiting for transfers between devices, join(): others = [lax.ppermute(x, 'cent', route) for x, route in zip(sent, routes)]  3.06 us
    ppermute x1, starting transfers between devices, local(): from_p = lax.ppermute(embeddings, 'cent', by_p)  3 us
  transfers between devices with their start and end apart: 18, of which 14 were waited for; matrix products, arithmetic and copies ran while one was open for 4% of the time, Pallas kernels for 10%

profile of v11, /device:TPU:0, one launch (start us, length us, event | category | flops | bytes accessed | tf_op | source)
XLA Modules:
  0.0 66.3 jit_solution(13818277044007471368)
XLA Ops:
  0.6 3.0 %collective-permute-start = (bf16[256,1024]{1,0:T(8,128)(2,1)}, bf16[256,1024]{1,0:T(8,128)(2,1)S(1)}, u32[]{:S(2)}, u32[]{:S(2)}) collective-permute-start(bf16[256,1024]{1,0:T(8,128)(2,1)} %param.2), channel_id=1, source_target_pairs={{0,2},{1,5},{2,0},{3,7},{4,6},{5,1},{6,4},{7,3},{8,10},{9,13},{10,... | collective-permute-start | bytes 1572872 | tf_op jit(solution)/shard_map/ppermute | solution.py:247
  3.6 1.5 %collective-permute-start.1 = (bf16[256,1024]{1,0:T(8,128)(2,1)}, bf16[256,1024]{1,0:T(8,128)(2,1)S(1)}, u32[]{:S(2)}, u32[]{:S(2)}) collective-permute-start(bf16[256,1024]{1,0:T(8,128)(2,1)} %param.2), channel_id=1, source_target_pairs={{0,4},{1,3},{2,6},{3,1},{4,0},{5,7},{6,2},{7,5},{8,12},{9,11},{10,... | collective-permute-start | bytes 1572872 | tf_op jit(solution)/shard_map/ppermute | solution.py:248
  5.2 1.1 %convert_element_type.21.refs_0_ = bf16[128,1024]{1,0:T(8,128)(2,1)S(1)} convert(f32[128,1024]{1,0:T(8,128)} %refs_6_.1) | non-fusion elementwise | flops 131072 | bytes 786432 | tf_op jit(solution)/shard_map/convert_element_type | solution.py:243
  6.2 2.7 %collective-permute-start.3 = (bf16[128,1024]{1,0:T(8,128)(2,1)S(1)}, bf16[128,1024]{1,0:T(8,128)(2,1)S(1)}, u32[]{:S(2)}, u32[]{:S(2)}) collective-permute-start(bf16[128,1024]{1,0:T(8,128)(2,1)S(1)} %convert_element_type.21.refs_0_), channel_id=1, source_target_pairs={{0,16},{8,24},{16,0},{24,8},{1,17},{9,25},{17,1},{25,9},{2,18},{10... | collective-permute-start | bytes 786440 | tf_op jit(solution)/shard_map/ppermute | solution.py:22
  8.9 1.6 %collective-permute-start.2 = (bf16[128,1024]{1,0:T(8,128)(2,1)S(1)}, bf16[128,1024]{1,0:T(8,128)(2,1)S(1)}, u32[]{:S(2)}, u32[]{:S(2)}) collective-permute-start(bf16[128,1024]{1,0:T(8,128)(2,1)S(1)} %convert_element_type.21.refs_0_), channel_id=1, source_target_pairs={{0,8},{8,0},{16,24},{24,16},{1,9},{9,1},{17,25},{25,17},{2,10},{10... | collective-permute-start | bytes 786440 | tf_op jit(solution)/shard_map/ppermute | solution.py:22
  10.5 1.1 %constant_dynamic-update-slice_fusion.2 = bf16[768,1024]{1,0:T(8,128)(2,1)S(1)} fusion(bf16[256,1024]{1,0:T(8,128)(2,1)} %param.2), kind=kLoop, calls=%fused_computation.2 | loop fusion | bytes 1048576
  11.5 4.6 %collective-permute-done = bf16[256,1024]{1,0:T(8,128)(2,1)S(1)} collective-permute-done((bf16[256,1024]{1,0:T(8,128)(2,1)}, bf16[256,1024]{1,0:T(8,128)(2,1)S(1)}, u32[]{:S(2)}, u32[]{:S(2)}) %collective-permute-start) | collective-permute-done | bytes 524320 | tf_op jit(solution)/shard_map/ppermute | solution.py:247
  16.2 4.2 %collective-permute-done.3.refs_2_ = bf16[128,1024]{1,0:T(8,128)(2,1)S(1)} collective-permute-done((bf16[128,1024]{1,0:T(8,128)(2,1)S(1)}, bf16[128,1024]{1,0:T(8,128)(2,1)S(1)}, u32[]{:S(2)}, u32[]{:S(2)}) %collective-permute-start.3) | collective-permute-done | bytes 262176 | tf_op jit(solution)/shard_map/ppermute | solution.py:22
  21.1 1.4 %collective-permute-start.6 = (bf16[128,1024]{1,0:T(8,128)(2,1)S(1)}, bf16[128,1024]{1,0:T(8,128)(2,1)S(1)}, u32[]{:S(2)}, u32[]{:S(2)}) collective-permute-start(bf16[128,1024]{1,0:T(8,128)(2,1)S(1)} %collective-permute-done.3.refs_2_), channel_id=1, source_target_pairs={{0,8},{8,0},{16,24},{24,16},{1,9},{9,1},{17,25},{25,17},{2,10},{10... | collective-permute-start | bytes 786440 | tf_op jit(solution)/shard_map/ppermute | solution.py:22
  22.5 1.0 %score_rows.5 = (f32[3,384,256]{2,1,0:T(8,128)S(1)}, f32[2,3,256]{2,1,0:T(4,128)S(1)}) custom-call(bf16[128,1024]{1,0:T(8,128)(2,1)S(1)} %convert_element_type.21.refs_0_, bf16[128,1024]{1,0:T(8,128)(2,1)S(1)} %collective-permute-done.2.refs_1_, bf16[128,1024]{1,0:T(8,128)(2,1)S(1)} %collective-permute-done.3.refs_2_, ...), custom_call_target="tpu_custom_call" | custom-call | flops 603979776 | bytes 2359296 | tf_op jit(solution)/shard_map/score_rows/pallas_call | solution.py:67
  24.0 1.0 %score_rows.6 = (f32[3,384,256]{2,1,0:T(8,128)S(1)}, f32[2,3,256]{2,1,0:T(4,128)S(1)}) custom-call(bf16[128,1024]{1,0:T(8,128)(2,1)S(1)} %convert_element_type.21.refs_0_, bf16[128,1024]{1,0:T(8,128)(2,1)S(1)} %collective-permute-done.2.refs_1_, bf16[128,1024]{1,0:T(8,128)(2,1)S(1)} %collective-permute-done.3.refs_2_, ...), custom_call_target="tpu_custom_call" | custom-call | flops 603979776 | bytes 2359296 | tf_op jit(solution)/shard_map/score_rows/pallas_call | solution.py:67
  25.0 4.6 %collective-permute-done.6.refs_0_.refs_3_ = bf16[128,1024]{1,0:T(8,128)(2,1)S(1)} collective-permute-done((bf16[128,1024]{1,0:T(8,128)(2,1)S(1)}, bf16[128,1024]{1,0:T(8,128)(2,1)S(1)}, u32[]{:S(2)}, u32[]{:S(2)}) %collective-permute-start.6) | collective-permute-done | bytes 262176 | tf_op jit(solution)/shard_map/ppermute | solution.py:22
  30.4 1.3 %score_rows.7 = (f32[6,128,256]{2,1,0:T(8,128)S(1)}, f32[2,6,256]{2,1,0:T(8,128)S(1)}) custom-call(bf16[128,1024]{1,0:T(8,128)(2,1)S(1)} %collective-permute-done.6.refs_0_.refs_3_, bf16[768,1024]{1,0:T(8,128)(2,1)S(1)} %constant_dynamic-update-slice_fusion.refs_3_.refs_1_.refs_4_, ...), custom_call_target="tpu_custom_call" | custom-call | flops 402653184 | bytes 3407872 | tf_op jit(solution)/shard_map/score_rows/pallas_call | solution.py:67
  33.7 1.3 %collective-permute-start.9 = (f32[4,8,256]{2,1,0:T(8,128)S(1)}, f32[4,8,256]{2,1,0:T(8,128)S(1)}, u32[]{:S(2)}, u32[]{:S(2)}) collective-permute-start(f32[4,8,256]{2,1,0:T(8,128)S(1)} %get-tuple-element.53), channel_id=1, source_target_pairs={{0,6},{1,7},{2,4},{3,5},{4,2},{5,3},{6,0},{7,1},{8,14},{9,15},{10,... | collective-permute-start | bytes 98312 | tf_op jit(solution)/shard_map/ppermute | solution.py:100
  35.8 1.5 %collective-permute-start.11 = (f32[2,8,256]{2,1,0:T(8,128)S(1)}, f32[2,8,256]{2,1,0:T(8,128)S(1)}, u32[]{:S(2)}, u32[]{:S(2)}) collective-permute-start(f32[2,8,256]{2,1,0:T(8,128)S(1)} %get-tuple-element.52.pair_ref), channel_id=1, source_target_pairs={{0,4},{1,3},{2,6},{3,1},{4,0},{5,7},{6,2},{7,5},{8,12},{9,11},{10,... | collective-permute-start | bytes 49160 | tf_op jit(solution)/shard_map/ppermute | solution.py:100
  37.3 1.5 %collective-permute-done.10.refs_1_ = f32[2,8,256]{2,1,0:T(8,128)S(1)} collective-permute-done((f32[2,8,256]{2,1,0:T(8,128)S(1)}, f32[2,8,256]{2,1,0:T(8,128)S(1)}, u32[]{:S(2)}, u32[]{:S(2)}) %collective-permute-start.10) | collective-permute-done | bytes 16416 | tf_op jit(solution)/shard_map/ppermute | solution.py:100
  40.6 1.5 %collective-permute-start.12 = (f16[128,1024]{1,0:T(8,128)(2,1)S(1)}, f16[128,1024]{1,0:T(8,128)(2,1)S(1)}, u32[]{:S(2)}, u32[]{:S(2)}) collective-permute-start(f16[128,1024]{1,0:T(8,128)(2,1)S(1)} %convert_element_type.22), channel_id=1, source_target_pairs={{0,8},{8,0},{16,24},{24,16},{1,9},{9,1},{17,25},{25,17},{2,10},{10... | collective-permute-start | bytes 786440 | tf_op jit(solution)/shard_map/ppermute | solution.py:22
  42.6 2.4 %weighted_sums.2 = (f32[128,1024]{1,0:T(8,128)S(1)}, f32[8,1024]{1,0:T(8,128)S(1)}, f32[128,1024]{1,0:T(8,128)S(1)}, f32[8,1024]{1,0:T(8,128)S(1)}, f32[128,1024]{1,0:T(8,128)S(1)}, /*index=5*/f32[8,1024]{1,0:T(8,128)S(1)}) custom-call(f32[8,256]{1,0:T(8,128)S(1)} %join_rows.3.lognorm_ref, f32[3,384,256]{2,1,0:T(8,128)S(1)} %get-tuple-element.54.refs_0_, ...), custom_call_target="tpu_custom_call" | custom-call | flops 1610612736 | bytes 4194304 | tf_op jit(solution)/shard_map/weighted_sums/pallas_call | solution.py:222
  45.1 3.2 %collective-permute-done.12 = f16[128,1024]{1,0:T(8,128)(2,1)S(1)} collective-permute-done((f16[128,1024]{1,0:T(8,128)(2,1)S(1)}, f16[128,1024]{1,0:T(8,128)(2,1)S(1)}, u32[]{:S(2)}, u32[]{:S(2)}) %collective-permute-start.12) | collective-permute-done | bytes 262176 | tf_op jit(solution)/shard_map/ppermute | solution.py:22
  48.8 1.6 %collective-permute-start.14 = (f16[128,1024]{1,0:T(8,128)(2,1)S(1)}, f16[128,1024]{1,0:T(8,128)(2,1)S(1)}, u32[]{:S(2)}, u32[]{:S(2)}) collective-permute-start(f16[128,1024]{1,0:T(8,128)(2,1)S(1)} %convert_element_type.24), channel_id=1, source_target_pairs={{0,8},{8,0},{16,24},{24,16},{1,9},{9,1},{17,25},{25,17},{2,10},{10... | collective-permute-start | bytes 786440 | tf_op jit(solution)/shard_map/ppermute | solution.py:22
  50.5 2.4 %collective-permute-start.16 = (f16[128,1024]{1,0:T(8,128)(2,1)S(1)}, f16[128,1024]{1,0:T(8,128)(2,1)S(1)}, u32[]{:S(2)}, u32[]{:S(2)}) collective-permute-start(f16[128,1024]{1,0:T(8,128)(2,1)S(1)} %convert_element_type.26), channel_id=1, source_target_pairs={{0,16},{8,24},{16,0},{24,8},{1,17},{9,25},{17,1},{25,9},{2,18},{10... | collective-permute-start | bytes 786440 | tf_op jit(solution)/shard_map/ppermute | solution.py:22
  54.5 6.7 %collective-permute-done.14 = f16[128,1024]{1,0:T(8,128)(2,1)S(1)} collective-permute-done((f16[128,1024]{1,0:T(8,128)(2,1)S(1)}, f16[128,1024]{1,0:T(8,128)(2,1)S(1)}, u32[]{:S(2)}, u32[]{:S(2)}) %collective-permute-start.14) | collective-permute-done | bytes 262176 | tf_op jit(solution)/shard_map/ppermute | solution.py:22
  61.2 3.2 %collective-permute-done.16 = f16[128,1024]{1,0:T(8,128)(2,1)S(1)} collective-permute-done((f16[128,1024]{1,0:T(8,128)(2,1)S(1)}, f16[128,1024]{1,0:T(8,128)(2,1)S(1)}, u32[]{:S(2)}, u32[]{:S(2)}) %collective-permute-start.16) | collective-permute-done | bytes 262176 | tf_op jit(solution)/shard_map/ppermute | solution.py:22
  64.8 1.5 %update_centroids.1 = (f32[128,1024]{1,0:T(8,128)}, f32[1,128]{1,0:T(1,128)}) custom-call(f32[128,1024]{1,0:T(8,128)S(1)} %get-tuple-element.58.refs_0_, f32[8,1024]{1,0:T(8,128)S(1)} %get-tuple-element.59.refs_1_, f32[128,1024]{1,0:T(8,128)S(1)} %convert_element_type.25.refs_2_, f32[8,1024]{1,0:T(8,128)S(1)} %collective-permute-done.15.refs_3_, ...), custom_call_target="tpu_custom_call" | custom-call | tf_op jit(solution)/shard_map/update_centroids/pallas_call | solution.py:200
  (36 shorter events, 9.7 us)
Async XLA Ops:
  0.6 15.5 %collective-permute-start = (bf16[256,1024]{1,0:T(8,128)(2,1)}, bf16[256,1024]{1,0:T(8,128)(2,1)S(1)}, u32[]{:S(2)}, u32[]{:S(2)}) collective-permute-start(bf16[256,1024]{1,0:T(8,128)(2,1)} %param.2), channel_id=1, source_target_pairs={{0,2},{1,5},{2,0},{3,7},{4,6},{5,1},{6,4},{7,3},{8,10},{9,13},{10,... | collective-permute-start | bytes 1572872 | tf_op jit(solution)/shard_map/ppermute | solution.py:247
  3.6 12.6 %collective-permute-start.1 = (bf16[256,1024]{1,0:T(8,128)(2,1)}, bf16[256,1024]{1,0:T(8,128)(2,1)S(1)}, u32[]{:S(2)}, u32[]{:S(2)}) collective-permute-start(bf16[256,1024]{1,0:T(8,128)(2,1)} %param.2), channel_id=1, source_target_pairs={{0,4},{1,3},{2,6},{3,1},{4,0},{5,7},{6,2},{7,5},{8,12},{9,11},{10,... | collective-permute-start | bytes 1572872 | tf_op jit(solution)/shard_map/ppermute | solution.py:248
  6.2 14.2 %collective-permute-start.3 = (bf16[128,1024]{1,0:T(8,128)(2,1)S(1)}, bf16[128,1024]{1,0:T(8,128)(2,1)S(1)}, u32[]{:S(2)}, u32[]{:S(2)}) collective-permute-start(bf16[128,1024]{1,0:T(8,128)(2,1)S(1)} %convert_element_type.21.refs_0_), channel_id=1, source_target_pairs={{0,16},{8,24},{16,0},{24,8},{1,17},{9,25},{17,1},{25,9},{2,18},{10... | collective-permute-start | bytes 786440 | tf_op jit(solution)/shard_map/ppermute | solution.py:22
  8.9 11.7 %collective-permute-start.2 = (bf16[128,1024]{1,0:T(8,128)(2,1)S(1)}, bf16[128,1024]{1,0:T(8,128)(2,1)S(1)}, u32[]{:S(2)}, u32[]{:S(2)}) collective-permute-start(bf16[128,1024]{1,0:T(8,128)(2,1)S(1)} %convert_element_type.21.refs_0_), channel_id=1, source_target_pairs={{0,8},{8,0},{16,24},{24,16},{1,9},{9,1},{17,25},{25,17},{2,10},{10... | collective-permute-start | bytes 786440 | tf_op jit(solution)/shard_map/ppermute | solution.py:22
  20.6 3.4 %collective-permute-start.5 = (bf16[768,1024]{1,0:T(8,128)(2,1)S(1)}, bf16[768,1024]{1,0:T(8,128)(2,1)S(1)}, u32[]{:S(2)}, u32[]{:S(2)}) collective-permute-start(bf16[768,1024]{1,0:T(8,128)(2,1)S(1)} %constant_dynamic-update-slice_fusion.refs_3_.refs_1_.refs_4_), channel_id=1, source_target_pairs={{0,1},{1,0},{2,3},{3,2},{4,5},{5,4},{6,7},{7,6},{8,9},{9,8},{10,11... | collective-permute-start | bytes 4718600 | tf_op jit(solution)/shard_map/ppermute | solution.py:22
  20.6 9.2 %collective-permute-start.4 = (bf16[256,1024]{1,0:T(8,128)(2,1)S(1)}, bf16[256,1024]{1,0:T(8,128)(2,1)S(1)}, u32[]{:S(2)}, u32[]{:S(2)}) collective-permute-start(bf16[256,1024]{1,0:T(8,128)(2,1)S(1)} %collective-permute-done), channel_id=1, source_target_pairs={{0,4},{1,3},{2,6},{3,1},{4,0},{5,7},{6,2},{7,5},{8,12},{9,11},{10,... | collective-permute-start | bytes 1572872 | tf_op jit(solution)/shard_map/ppermute | solution.py:258
  21.1 8.5 %collective-permute-start.6 = (bf16[128,1024]{1,0:T(8,128)(2,1)S(1)}, bf16[128,1024]{1,0:T(8,128)(2,1)S(1)}, u32[]{:S(2)}, u32[]{:S(2)}) collective-permute-start(bf16[128,1024]{1,0:T(8,128)(2,1)S(1)} %collective-permute-done.3.refs_2_), channel_id=1, source_target_pairs={{0,8},{8,0},{16,24},{24,16},{1,9},{9,1},{17,25},{25,17},{2,10},{10... | collective-permute-start | bytes 786440 | tf_op jit(solution)/shard_map/ppermute | solution.py:22
  29.8 1.9 %collective-permute-start.7 = (bf16[256,1024]{1,0:T(8,128)(2,1)S(1)}, bf16[256,1024]{1,0:T(8,128)(2,1)S(1)}, u32[]{:S(2)}, u32[]{:S(2)}) collective-permute-start(bf16[256,1024]{1,0:T(8,128)(2,1)S(1)} %collective-permute-done.4.refs_4_.refs_6_.refs_5_), channel_id=1, source_target_pairs={{0,1},{1,0},{2,3},{3,2},{4,5},{5,4},{6,7},{7,6},{8,9},{9,8},{10,11... | collective-permute-start | bytes 1572872 | tf_op jit(solution)/shard_map/ppermute | solution.py:22
  32.3 1.4 %collective-permute-start.8 = (f32[2,8,256]{2,1,0:T(8,128)S(1)}, f32[2,8,256]{2,1,0:T(8,128)S(1)}, u32[]{:S(2)}, u32[]{:S(2)}) collective-permute-start(f32[2,8,256]{2,1,0:T(8,128)S(1)} %get-tuple-element.51.pair_ref), channel_id=1, source_target_pairs={{0,1},{1,0},{2,3},{3,2},{4,5},{5,4},{6,7},{7,6},{8,9},{9,8},{10,11... | collective-permute-start | bytes 49160 | tf_op jit(solution)/shard_map/ppermute | solution.py:100
  33.7 5.8 %collective-permute-start.9 = (f32[4,8,256]{2,1,0:T(8,128)S(1)}, f32[4,8,256]{2,1,0:T(8,128)S(1)}, u32[]{:S(2)}, u32[]{:S(2)}) collective-permute-start(f32[4,8,256]{2,1,0:T(8,128)S(1)} %get-tuple-element.53), channel_id=1, source_target_pairs={{0,6},{1,7},{2,4},{3,5},{4,2},{5,3},{6,0},{7,1},{8,14},{9,15},{10,... | collective-permute-start | bytes 98312 | tf_op jit(solution)/shard_map/ppermute | solution.py:100
  35.0 3.7 %collective-permute-start.10 = (f32[2,8,256]{2,1,0:T(8,128)S(1)}, f32[2,8,256]{2,1,0:T(8,128)S(1)}, u32[]{:S(2)}, u32[]{:S(2)}) collective-permute-start(f32[2,8,256]{2,1,0:T(8,128)S(1)} %get-tuple-element.52.pair_ref), channel_id=1, source_target_pairs={{0,2},{1,5},{2,0},{3,7},{4,6},{5,1},{6,4},{7,3},{8,10},{9,13},{10,... | collective-permute-start | bytes 49160 | tf_op jit(solution)/shard_map/ppermute | solution.py:100
  35.8 3.7 %collective-permute-start.11 = (f32[2,8,256]{2,1,0:T(8,128)S(1)}, f32[2,8,256]{2,1,0:T(8,128)S(1)}, u32[]{:S(2)}, u32[]{:S(2)}) collective-permute-start(f32[2,8,256]{2,1,0:T(8,128)S(1)} %get-tuple-element.52.pair_ref), channel_id=1, source_target_pairs={{0,4},{1,3},{2,6},{3,1},{4,0},{5,7},{6,2},{7,5},{8,12},{9,11},{10,... | collective-permute-start | bytes 49160 | tf_op jit(solution)/shard_map/ppermute | solution.py:100
  40.6 7.7 %collective-permute-start.12 = (f16[128,1024]{1,0:T(8,128)(2,1)S(1)}, f16[128,1024]{1,0:T(8,128)(2,1)S(1)}, u32[]{:S(2)}, u32[]{:S(2)}) collective-permute-start(f16[128,1024]{1,0:T(8,128)(2,1)S(1)} %convert_element_type.22), channel_id=1, source_target_pairs={{0,8},{8,0},{16,24},{24,16},{1,9},{9,1},{17,25},{25,17},{2,10},{10... | collective-permute-start | bytes 786440 | tf_op jit(solution)/shard_map/ppermute | solution.py:22
  42.1 6.6 %collective-permute-start.13 = (f32[8,1024]{1,0:T(8,128)S(1)}, f32[8,1024]{1,0:T(8,128)S(1)}, u32[]{:S(2)}, u32[]{:S(2)}) collective-permute-start(f32[8,1024]{1,0:T(8,128)S(1)} %get-tuple-element.64), channel_id=1, source_target_pairs={{0,8},{8,0},{16,24},{24,16},{1,9},{9,1},{17,25},{25,17},{2,10},{10... | collective-permute-start | bytes 98312 | tf_op jit(solution)/shard_map/ppermute | solution.py:22
  48.8 16.0 %copy-start = (f32[128,1024]{1,0:T(8,128)S(1)}, f32[128,1024]{1,0:T(8,128)}, u32[]{:S(2)}) copy-start(f32[128,1024]{1,0:T(8,128)} %refs_6_.1) | copy-start | bytes 1572868
  48.8 12.4 %collective-permute-start.14 = (f16[128,1024]{1,0:T(8,128)(2,1)S(1)}, f16[128,1024]{1,0:T(8,128)(2,1)S(1)}, u32[]{:S(2)}, u32[]{:S(2)}) collective-permute-start(f16[128,1024]{1,0:T(8,128)(2,1)S(1)} %convert_element_type.24), channel_id=1, source_target_pairs={{0,8},{8,0},{16,24},{24,16},{1,9},{9,1},{17,25},{25,17},{2,10},{10... | collective-permute-start | bytes 786440 | tf_op jit(solution)/shard_map/ppermute | solution.py:22
  50.5 13.9 %collective-permute-start.16 = (f16[128,1024]{1,0:T(8,128)(2,1)S(1)}, f16[128,1024]{1,0:T(8,128)(2,1)S(1)}, u32[]{:S(2)}, u32[]{:S(2)}) collective-permute-start(f16[128,1024]{1,0:T(8,128)(2,1)S(1)} %convert_element_type.26), channel_id=1, source_target_pairs={{0,16},{8,24},{16,0},{24,8},{1,17},{9,25},{17,1},{25,9},{2,18},{10... | collective-permute-start | bytes 786440 | tf_op jit(solution)/shard_map/ppermute | solution.py:22
  52.9 11.5 %collective-permute-start.15 = (f32[8,1024]{1,0:T(8,128)S(1)}, f32[8,1024]{1,0:T(8,128)S(1)}, u32[]{:S(2)}, u32[]{:S(2)}) collective-permute-start(f32[8,1024]{1,0:T(8,128)S(1)} %get-tuple-element.70), channel_id=1, source_target_pairs={{0,8},{8,0},{16,24},{24,16},{1,9},{9,1},{17,25},{25,17},{2,10},{10... | collective-permute-start | bytes 98312 | tf_op jit(solution)/shard_map/ppermute | solution.py:22
  53.2 11.6 %collective-permute-start.17 = (f32[8,1024]{1,0:T(8,128)S(1)}, f32[8,1024]{1,0:T(8,128)S(1)}, u32[]{:S(2)}, u32[]{:S(2)}) collective-permute-start(f32[8,1024]{1,0:T(8,128)S(1)} %get-tuple-element.72), channel_id=1, source_target_pairs={{0,16},{8,24},{16,0},{24,8},{1,17},{9,25},{17,1},{25,9},{2,18},{10... | collective-permute-start | bytes 98312 | tf_op jit(solution)/shard_map/ppermute | solution.py:22

commit v12 on v10

--- a/solution.py
+++ b/solution.py
@@ -27,24 +27,34 @@
     return top, a[1] * jnp.exp(a[0] - top) + b[1] * jnp.exp(b[0] - top)
 
 
-def score_kernel(n_cent, n_rows, picks, begin, starts, *refs):
-    cent_refs, row_refs = refs[:n_cent], refs[n_cent : n_cent + n_rows]
-    early_refs = refs[n_cent + n_rows : -2]
-    score_ref, pair_ref = refs[-2:]
-    r = score_ref.shape[2]
-    centers = jnp.concatenate([ref[...] for ref in cent_refs], axis=0)
-    half = 0.5 * jnp.sum(jnp.square(centers.astype(jnp.float32)), axis=1, keepdims=True)
+def score_kernel(n_cent, n_half, n_rows, picks, begin, starts, r, *refs):
+    cent_refs, refs = refs[:n_cent], refs[n_cent:]
+    half_refs, refs = refs[:n_half], refs[n_half:]
+    row_refs, early_refs = refs[:n_rows], refs[n_rows:-3]
+    score_ref, pair_ref, half_ref = refs[-3:]
+    halves = [ref[...] for ref in half_refs]
+    for ref in cent_refs[n_half:]:
+        squares = jnp.square(ref[...].astype(jnp.float32))
+        half = 0.5 * jnp.sum(squares, axis=1, keepdims=True)
+        halves.append(jnp.broadcast_to(half, (half.shape[0], half_ref.shape[1])))
+    half_ref[...] = halves[-1]
+    repeat = r // half_ref.shape[1]
+    halves = [jnp.concatenate([half] * repeat, axis=1) for half in halves]
     for j, (i, at) in enumerate(picks):
-        product = lax.dot_general(
-            centers,
-            row_refs[i][at : at + r],
-            (((1,), (1,)), ((), ())),
-            preferred_element_type=jnp.float32,
-        )
-        s = (product - half) * (1.0 / TEMPER)
-        top = jnp.max(s, axis=0, keepdims=True)
-        score_ref[j] = s
-        total = jnp.sum(jnp.exp(s - top), axis=0, keepdims=True)
+        parts, first = [], 0
+        for ref, half in zip(cent_refs, halves):
+            product = lax.dot_general(
+                ref[...],
+                row_refs[i][at : at + r],
+                (((1,), (1,)), ((), ())),
+                preferred_element_type=jnp.float32,
+            )
+            s = (product - half) * (1.0 / TEMPER)
+            score_ref[j, first : first + s.shape[0]] = s
+            first += s.shape[0]
+            parts.append(s)
+        top = functools.reduce(jnp.maximum, [jnp.max(s, axis=0, keepdims=True) for s in parts])
+        total = sum(jnp.sum(jnp.exp(s - top), axis=0, keepdims=True) for s in parts)
         at = begin + j
         for ref, start in zip(early_refs, starts):
             if start <= at < start + ref.shape[1]:
@@ -58,20 +68,25 @@
                 pair_ref[:, start + k : start + k + 1] = ref[:, k : k + 1]
 
 
-def score(centers, rows, r, picks, early=(), begin=0):
-    n_c, n_r = len(centers), len(picks)
+def score(centers, halves, rows, r, picks, early=(), begin=0):
+    n_r = len(picks)
     depth = rows[0].shape[1]
     c = sum(x.shape[0] for x in centers)
+    lanes = min(r, 128)
     starts = [sum(e.shape[1] for e in early[:i]) for i in range(len(early))]
     n_out = max(begin + n_r, sum(e.shape[1] for e in early))
+    operands = [*centers, *halves, *rows, *early]
     return pl.pallas_call(
-        functools.partial(score_kernel, n_c, len(rows), picks, begin, starts),
+        functools.partial(
+            score_kernel, len(centers), len(halves), len(rows), picks, begin, starts, r
+        ),
         out_shape=(
             jax.ShapeDtypeStruct((n_r, c, r), jnp.float32),
             jax.ShapeDtypeStruct((2, n_out, r), jnp.float32),
-        ),
-        in_specs=[VMEM] * (n_c + len(rows) + len(early)),
-        out_specs=(VMEM,) * 2,
+            jax.ShapeDtypeStruct((centers[-1].shape[0], lanes), jnp.float32),
+        ),
+        in_specs=[VMEM] * len(operands),
+        out_specs=(VMEM,) * 3,
         compiler_params=PARAMS,
         cost_estimate=pl.CostEstimate(
             flops=2 * n_r * c * r * depth,
@@ -79,7 +94,7 @@
             transcendentals=n_r * c * r,
         ),
         name="score_rows",
-    )(*centers, *rows, *early)
+    )(*operands)
 
 
 def join_kernel(places, last, pair_ref, *refs):
@@ -110,17 +125,23 @@
 def sums_kernel(n_parts, picks, parts, lognorm_ref, *refs):
     score_refs, row_refs = refs[:n_parts], refs[n_parts : -len(parts)]
     outs = refs[-len(parts) :]
-    r = lognorm_ref.shape[1]
-    ones = jnp.ones((SIDE, r), jnp.bfloat16)
+    ones = jnp.ones((SIDE, max(ref.shape[0] for ref in row_refs)), jnp.bfloat16)
     for out, (places, size, unit) in zip(outs, parts):
         total, tally = None, None
-        for j, (i, at) in enumerate(picks):
-            k, block, first = places[j]
-            s = score_refs[k][block, first : first + size, :]
-            resp = jnp.exp(s - lognorm_ref[j : j + 1]).astype(jnp.bfloat16)
-            more = jnp.dot(resp, row_refs[i][at : at + r], preferred_element_type=jnp.float32)
+        for i, ref in enumerate(row_refs):
+            mine = [j for j, pick in enumerate(picks) if pick[0] == i]
+            resp = []
+            for j in mine:
+                k, block, first = places[j]
+                s = score_refs[k][block, first : first + size, :]
+                resp.append(jnp.exp(s - lognorm_ref[j : j + 1]).astype(jnp.bfloat16))
+            resp = jnp.concatenate(resp, axis=1)
+            more = jnp.dot(resp, ref[...], preferred_element_type=jnp.float32)
             count = lax.dot_general(
-                ones, resp, (((1,), (1,)), ((), ())), preferred_element_type=jnp.float32
+                ones[:, : ref.shape[0]],
+                resp,
+                (((1,), (1,)), ((), ())),
+                preferred_element_type=jnp.float32,
             )
             total = more if total is None else total + more
             tally = count if tally is None else tally + count
@@ -179,8 +200,8 @@
         total, tally = total + more, tally + count
     tally = tally[:, :size]
     tally_ref[...] = tally
-    column = jnp.transpose(jnp.broadcast_to(tally, (size, size)))[:, 0:1]
-    new_ref[...] = (total + PRIOR * codebook_ref[...]) / (column + PRIOR)
+    weight = 1.0 / (jnp.transpose(jnp.broadcast_to(tally, (size, size)))[:, 0:1] + PRIOR)
+    new_ref[...] = (total + PRIOR * codebook_ref[...]) * weight
 
 
 def finish(codebook, own, got):
@@ -242,17 +263,20 @@
         three = jnp.concatenate([embeddings, from_p, from_q], axis=0)
         give, most = lax.optimization_barrier((three, most))
         three_core = swap(give, "cent", n_cent, 1)
-        s_0, pair_0 = score(most, [three], own_rows, [(0, j * own_rows) for j in range(3)])
-        s_1, pair_1 = score(most, [three_core], own_rows, [(0, j * own_rows) for j in range(3)])
+        most = [jnp.concatenate(most, axis=0)]
+        of_three = [(0, j * own_rows) for j in range(3)]
+        s_0, pair_0, half = score(most, [], [three], own_rows, of_three)
+        s_1, pair_1, _ = score(most, [half], [three_core], own_rows, of_three)
         give, pair_0, pair_1, final = lax.optimization_barrier(
             (diag, pair_0, pair_1, final)
         )
         rows = [three, three_core, diag, swap(give, "cent", n_cent, 1)]
         order = [0, 2, 4, 1, 5, 3, 6, 7]
         picks = [(i, j * own_rows) for i in range(2) for j in range(3)] + [(2, 0), (3, 0)]
-        s_2, pairs = score(final, rows[:2], own_rows, picks[:6], [pair_0, pair_1])
-        s_3, pair_3 = score(most + final, rows[2:3], own_rows, [(0, 0)])
-        s_4, pairs = score(most + final, rows[3:], own_rows, [(0, 0)], [pairs, pair_3], 7)
+        both = most + final
+        s_3, pair_3, last = score(both, [half], rows[2:3], own_rows, [(0, 0)])
+        s_2, pairs, _ = score(final, [last], rows[:2], own_rows, picks[:6], [pair_0, pair_1])
+        s_4, pairs, _ = score(both, [half, last], rows[3:], own_rows, [(0, 0)], [pairs, pair_3], 7)
         scores = [s_0, s_1, s_3, s_4]
         places = [(i, j) for i in range(2) for j in range(3)] + [(2, 0), (3, 0)]
         last_scores = [s_2, s_3, s_4]
@@ -261,10 +285,10 @@
         rows = [embeddings] + [swap(embeddings, "cent", n_cent, m) for m in range(1, n_cent)]
         order = list(range(n_cent))
         picks = [(j, 0) for j in order]
-        s_0, pair_0 = score(most, rows, own_rows, picks)
+        s_0, pair_0, _ = score(most, [], rows, own_rows, picks)
         scores = [s_0]
         places = [(0, j) for j in order]
-        s_1, pairs = score(final, rows, own_rows, picks, [pair_0])
+        s_1, pairs, _ = score(final, [], rows, own_rows, picks, [pair_0])
         last_scores, last_places = [s_1], [(0, j, 0) for j in order]
     if n_cent == 8:
         where = [order.index((j ^ 1) & 1 | (j & 2) << 1 | (j & 4) >> 1) for j in order]

time: 63.9 us -> 64.3 us (level)
  no operation moved by 1% of the time
where the time goes in v12:
time: 64.3 us; the launch traced here: 64.1 us
  waiting for transfers between devices  30.4 us (47%)
  starting transfers between devices  20.3 us (32%)
  Pallas kernels  9.54 us (15%)
  local copies, waits for them, and re-layouts  1.77 us (3%)
  other arithmetic  1.29 us (2%)
  between operations  0.78 us (1%)
    ppermute x8, waiting for transfers between devices, swap(): return lax.ppermute(x, axis, partner(size, mask))  22.3 us
    ppermute x8, starting transfers between devices, swap(): return lax.ppermute(x, axis, partner(size, mask))  11.2 us
    pallas_call x5, Pallas kernels, score(): pl.pallas_call(functools.partial(score_kernel, len(centers), len(halves),...  5.02 us
    ppermute x1, waiting for transfers between devices, local(): from_p = lax.ppermute(embeddings, 'cent', by_p)  4.62 us
    ppermute x4, starting transfers between devices, join(): others = [lax.ppermute(pairs, 'cent', route) for route in routes]  4.06 us
    pallas_call x2, Pallas kernels, weighted(): pl.pallas_call(functools.partial(sums_kernel, len(scores), picks, parts),...  3.3 us
    ppermute x4, waiting for transfers between devices, join(): others = [lax.ppermute(pairs, 'cent', route) for route in routes]  3.25 us
    ppermute x1, starting transfers between devices, local(): from_p = lax.ppermute(embeddings, 'cent', by_p)  3 us
  transfers between devices with their start and end apart: 15, of which 13 were waited for; matrix products, arithmetic and copies ran while one was open for 4% of the time, Pallas kernels for 10%

profile of v12, /device:TPU:0, one launch (start us, length us, event | category | flops | bytes accessed | tf_op | source)
XLA Modules:
  0.0 64.1 jit_solution(7789842775864084801)
XLA Ops:
  0.6 3.0 %collective-permute-start = (bf16[256,1024]{1,0:T(8,128)(2,1)}, bf16[256,1024]{1,0:T(8,128)(2,1)S(1)}, u32[]{:S(2)}, u32[]{:S(2)}) collective-permute-start(bf16[256,1024]{1,0:T(8,128)(2,1)} %param.2), channel_id=1, source_target_pairs={{0,2},{1,5},{2,0},{3,7},{4,6},{5,1},{6,4},{7,3},{8,10},{9,13},{10,... | collective-permute-start | bytes 1572872 | tf_op jit(solution)/shard_map/ppermute | solution.py:251
  3.6 1.5 %collective-permute-start.1 = (bf16[256,1024]{1,0:T(8,128)(2,1)}, bf16[256,1024]{1,0:T(8,128)(2,1)S(1)}, u32[]{:S(2)}, u32[]{:S(2)}) collective-permute-start(bf16[256,1024]{1,0:T(8,128)(2,1)} %param.2), channel_id=1, source_target_pairs={{0,4},{1,3},{2,6},{3,1},{4,0},{5,7},{6,2},{7,5},{8,12},{9,11},{10,... | collective-permute-start | bytes 1572872 | tf_op jit(solution)/shard_map/ppermute | solution.py:252
  5.2 1.1 %convert_element_type.21 = bf16[128,1024]{1,0:T(8,128)(2,1)S(1)} convert(f32[128,1024]{1,0:T(8,128)} %refs_3_.1) | non-fusion elementwise | flops 131072 | bytes 786432 | tf_op jit(solution)/shard_map/convert_element_type | solution.py:247
  6.2 2.7 %collective-permute-start.3 = (bf16[128,1024]{1,0:T(8,128)(2,1)S(1)}, bf16[128,1024]{1,0:T(8,128)(2,1)S(1)}, u32[]{:S(2)}, u32[]{:S(2)}) collective-permute-start(bf16[128,1024]{1,0:T(8,128)(2,1)S(1)} %convert_element_type.21), channel_id=1, source_target_pairs={{0,16},{8,24},{16,0},{24,8},{1,17},{9,25},{17,1},{25,9},{2,18},{10... | collective-permute-start | bytes 786440 | tf_op jit(solution)/shard_map/ppermute | solution.py:22
  8.9 1.6 %collective-permute-start.2 = (bf16[128,1024]{1,0:T(8,128)(2,1)S(1)}, bf16[128,1024]{1,0:T(8,128)(2,1)S(1)}, u32[]{:S(2)}, u32[]{:S(2)}) collective-permute-start(bf16[128,1024]{1,0:T(8,128)(2,1)S(1)} %convert_element_type.21), channel_id=1, source_target_pairs={{0,8},{8,0},{16,24},{24,16},{1,9},{9,1},{17,25},{25,17},{2,10},{10... | collective-permute-start | bytes 786440 | tf_op jit(solution)/shard_map/ppermute | solution.py:22
  10.5 1.1 %constant_dynamic-update-slice_fusion.2 = bf16[768,1024]{1,0:T(8,128)(2,1)S(1)} fusion(bf16[256,1024]{1,0:T(8,128)(2,1)} %param.2), kind=kLoop, calls=%fused_computation.2 | loop fusion | bytes 1048576
  11.5 4.6 %collective-permute-done = bf16[256,1024]{1,0:T(8,128)(2,1)S(1)} collective-permute-done((bf16[256,1024]{1,0:T(8,128)(2,1)}, bf16[256,1024]{1,0:T(8,128)(2,1)S(1)}, u32[]{:S(2)}, u32[]{:S(2)}) %collective-permute-start) | collective-permute-done | bytes 524320 | tf_op jit(solution)/shard_map/ppermute | solution.py:251
  16.2 4.2 %collective-permute-done.3 = bf16[128,1024]{1,0:T(8,128)(2,1)S(1)} collective-permute-done((bf16[128,1024]{1,0:T(8,128)(2,1)S(1)}, bf16[128,1024]{1,0:T(8,128)(2,1)S(1)}, u32[]{:S(2)}, u32[]{:S(2)}) %collective-permute-start.3) | collective-permute-done | bytes 262176 | tf_op jit(solution)/shard_map/ppermute | solution.py:22
  21.1 1.4 %collective-permute-start.6 = (bf16[128,1024]{1,0:T(8,128)(2,1)S(1)}, bf16[128,1024]{1,0:T(8,128)(2,1)S(1)}, u32[]{:S(2)}, u32[]{:S(2)}) collective-permute-start(bf16[128,1024]{1,0:T(8,128)(2,1)S(1)} %collective-permute-done.3), channel_id=1, source_target_pairs={{0,8},{8,0},{16,24},{24,16},{1,9},{9,1},{17,25},{25,17},{2,10},{10... | collective-permute-start | bytes 786440 | tf_op jit(solution)/shard_map/ppermute | solution.py:22
  22.6 1.0 %score_rows.5 = (f32[3,384,256]{2,1,0:T(8,128)S(1)}, f32[2,3,256]{2,1,0:T(4,128)S(1)}, f32[384,128]{1,0:T(8,128)S(1)}) custom-call(bf16[384,1024]{1,0:T(8,128)(2,1)S(1)} %constant_dynamic-update-slice_fusion.3.refs_0_, bf16[768,1024]{1,0:T(8,128)(2,1)S(1)} %constant_dynamic-update-slice_fusion.refs_1_.refs_2_.refs_4_.refs_3_), custom_call_target="tpu_custom_call" | custom-call | flops 603979776 | bytes 2359296 | tf_op jit(solution)/shard_map/score_rows/pallas_call | solution.py:79
  25.0 4.6 %collective-permute-done.6.refs_1_.refs_0_ = bf16[128,1024]{1,0:T(8,128)(2,1)S(1)} collective-permute-done((bf16[128,1024]{1,0:T(8,128)(2,1)S(1)}, bf16[128,1024]{1,0:T(8,128)(2,1)S(1)}, u32[]{:S(2)}, u32[]{:S(2)}) %collective-permute-start.6) | collective-permute-done | bytes 262176 | tf_op jit(solution)/shard_map/ppermute | solution.py:22
  30.4 1.2 %score_rows.8 = (f32[6,128,256]{2,1,0:T(8,128)S(1)}, f32[2,6,256]{2,1,0:T(8,128)S(1)}, f32[128,128]{1,0:T(8,128)}) custom-call(bf16[128,1024]{1,0:T(8,128)(2,1)S(1)} %collective-permute-done.6.refs_1_.refs_0_, f32[128,128]{1,0:T(8,128)S(1)} %get-tuple-element.38.refs_1_.refs_3_, ...), custom_call_target="tpu_custom_call" | custom-call | flops 402653184 | bytes 3407872 | tf_op jit(solution)/shard_map/score_rows/pallas_call | solution.py:79
  31.7 1.1 %score_rows.9 = (f32[1,512,256]{2,1,0:T(8,128)S(1)}, f32[2,8,256]{2,1,0:T(8,128)S(1)}, f32[128,128]{1,0:T(8,128)}) custom-call(bf16[384,1024]{1,0:T(8,128)(2,1)S(1)} %constant_dynamic-update-slice_fusion.3.refs_0_, bf16[128,1024]{1,0:T(8,128)(2,1)S(1)} %collective-permute-done.6.refs_1_.refs_0_, f32[384,128]{1,0:T(8,128)S(1)} %get-tuple-element.34.refs_1_.refs_2_, ...), custom_call_target="tpu_custom_call" | custom-call | flops 268435456 | bytes 1572864 | tf_op jit(solution)/shard_map/score_rows/pallas_call | solution.py:79
  34.7 1.7 %collective-permute-start.11 = (f32[2,8,256]{2,1,0:T(8,128)S(1)}, f32[2,8,256]{2,1,0:T(8,128)S(1)}, u32[]{:S(2)}, u32[]{:S(2)}) collective-permute-start(f32[2,8,256]{2,1,0:T(8,128)S(1)} %join_rows.2.pair_ref), channel_id=1, source_target_pairs={{0,6},{1,7},{2,4},{3,5},{4,2},{5,3},{6,0},{7,1},{8,14},{9,15},{10,... | collective-permute-start | bytes 49160 | tf_op jit(solution)/shard_map/ppermute | solution.py:114
  36.4 1.3 %collective-permute-start.9 = (f32[2,8,256]{2,1,0:T(8,128)S(1)}, f32[2,8,256]{2,1,0:T(8,128)S(1)}, u32[]{:S(2)}, u32[]{:S(2)}) collective-permute-start(f32[2,8,256]{2,1,0:T(8,128)S(1)} %join_rows.2.pair_ref), channel_id=1, source_target_pairs={{0,2},{1,5},{2,0},{3,7},{4,6},{5,1},{6,4},{7,3},{8,10},{9,13},{10,... | collective-permute-start | bytes 49160 | tf_op jit(solution)/shard_map/ppermute | solution.py:114
  37.9 1.4 %collective-permute-done.11.refs_2_ = f32[2,8,256]{2,1,0:T(8,128)S(1)} collective-permute-done((f32[2,8,256]{2,1,0:T(8,128)S(1)}, f32[2,8,256]{2,1,0:T(8,128)S(1)}, u32[]{:S(2)}, u32[]{:S(2)}) %collective-permute-start.11) | collective-permute-done | bytes 16416 | tf_op jit(solution)/shard_map/ppermute | solution.py:114
  41.2 1.6 %collective-permute-start.12 = (f16[136,1024]{1,0:T(8,128)(2,1)S(1)}, f16[136,1024]{1,0:T(8,128)(2,1)S(1)}, u32[]{:S(2)}, u32[]{:S(2)}) collective-permute-start(f16[136,1024]{1,0:T(8,128)(2,1)S(1)} %convert_element_type.22), channel_id=1, source_target_pairs={{0,8},{8,0},{16,24},{24,16},{1,9},{9,1},{17,25},{25,17},{2,10},{10... | collective-permute-start | bytes 835592 | tf_op jit(solution)/shard_map/ppermute | solution.py:22
  42.8 2.3 %weighted_sums.2 = (f32[136,1024]{1,0:T(8,128)S(1)}, f32[136,1024]{1,0:T(8,128)S(1)}, f32[136,1024]{1,0:T(8,128)S(1)}) custom-call(f32[8,256]{1,0:T(8,128)S(1)} %join_rows.3.lognorm_ref, f32[3,384,256]{2,1,0:T(8,128)S(1)} %get-tuple-element.45.refs_0_, f32[3,384,256]{2,1,0:T(8,128)S(1)} %get-tuple-element.46.refs_1_, ...), custom_call_target="tpu_custom_call" | custom-call | flops 1610612736 | bytes 4194304 | tf_op jit(solution)/shard_map/weighted_sums/pallas_call | solution.py:228
  45.1 3.2 %collective-permute-done.12 = f16[136,1024]{1,0:T(8,128)(2,1)S(1)} collective-permute-done((f16[136,1024]{1,0:T(8,128)(2,1)S(1)}, f16[136,1024]{1,0:T(8,128)(2,1)S(1)}, u32[]{:S(2)}, u32[]{:S(2)}) %collective-permute-start.12) | collective-permute-done | bytes 278560 | tf_op jit(solution)/shard_map/ppermute | solution.py:22
  48.6 1.6 %collective-permute-start.13 = (f16[136,1024]{1,0:T(8,128)(2,1)S(1)}, f16[136,1024]{1,0:T(8,128)(2,1)S(1)}, u32[]{:S(2)}, u32[]{:S(2)}) collective-permute-start(f16[136,1024]{1,0:T(8,128)(2,1)S(1)} %convert_element_type.25), channel_id=1, source_target_pairs={{0,8},{8,0},{16,24},{24,16},{1,9},{9,1},{17,25},{25,17},{2,10},{10... | collective-permute-start | bytes 835592 | tf_op jit(solution)/shard_map/ppermute | solution.py:22
  50.2 2.3 %collective-permute-start.14 = (f16[136,1024]{1,0:T(8,128)(2,1)S(1)}, f16[136,1024]{1,0:T(8,128)(2,1)S(1)}, u32[]{:S(2)}, u32[]{:S(2)}) collective-permute-start(f16[136,1024]{1,0:T(8,128)(2,1)S(1)} %convert_element_type.24), channel_id=1, source_target_pairs={{0,16},{8,24},{16,0},{24,8},{1,17},{9,25},{17,1},{25,9},{2,18},{10... | collective-permute-start | bytes 835592 | tf_op jit(solution)/shard_map/ppermute | solution.py:22
  53.1 7.3 %collective-permute-done.13 = f16[136,1024]{1,0:T(8,128)(2,1)S(1)} collective-permute-done((f16[136,1024]{1,0:T(8,128)(2,1)S(1)}, f16[136,1024]{1,0:T(8,128)(2,1)S(1)}, u32[]{:S(2)}, u32[]{:S(2)}) %collective-permute-start.13) | collective-permute-done | bytes 278560 | tf_op jit(solution)/shard_map/ppermute | solution.py:22
  60.5 2.6 %collective-permute-done.14 = f16[136,1024]{1,0:T(8,128)(2,1)S(1)} collective-permute-done((f16[136,1024]{1,0:T(8,128)(2,1)S(1)}, f16[136,1024]{1,0:T(8,128)(2,1)S(1)}, u32[]{:S(2)}, u32[]{:S(2)}) %collective-permute-start.14) | collective-permute-done | bytes 278560 | tf_op jit(solution)/shard_map/ppermute | solution.py:22
  63.1 1.0 %update_centroids.1 = (f32[128,1024]{1,0:T(8,128)}, f32[1,128]{1,0:T(1,128)}) custom-call(f32[136,1024]{1,0:T(8,128)S(1)} %get-tuple-element.49.refs_0_, f32[136,1024]{1,0:T(8,128)S(1)} %convert_element_type.26.refs_1_, f32[136,1024]{1,0:T(8,128)S(1)} %convert_element_type.27.refs_2_, f32[128,1024]{1,0:T(8,128)S(1)} %copy-done), custom_call_target="tpu_custom_call" | custom-call | tf_op jit(solution)/shard_map/update_centroids/pallas_call | solution.py:210
  (33 shorter events, 7.9 us)
Async XLA Ops:
  0.6 15.5 %collective-permute-start = (bf16[256,1024]{1,0:T(8,128)(2,1)}, bf16[256,1024]{1,0:T(8,128)(2,1)S(1)}, u32[]{:S(2)}, u32[]{:S(2)}) collective-permute-start(bf16[256,1024]{1,0:T(8,128)(2,1)} %param.2), channel_id=1, source_target_pairs={{0,2},{1,5},{2,0},{3,7},{4,6},{5,1},{6,4},{7,3},{8,10},{9,13},{10,... | collective-permute-start | bytes 1572872 | tf_op jit(solution)/shard_map/ppermute | solution.py:251
  3.6 12.6 %collective-permute-start.1 = (bf16[256,1024]{1,0:T(8,128)(2,1)}, bf16[256,1024]{1,0:T(8,128)(2,1)S(1)}, u32[]{:S(2)}, u32[]{:S(2)}) collective-permute-start(bf16[256,1024]{1,0:T(8,128)(2,1)} %param.2), channel_id=1, source_target_pairs={{0,4},{1,3},{2,6},{3,1},{4,0},{5,7},{6,2},{7,5},{8,12},{9,11},{10,... | collective-permute-start | bytes 1572872 | tf_op jit(solution)/shard_map/ppermute | solution.py:252
  6.2 14.2 %collective-permute-start.3 = (bf16[128,1024]{1,0:T(8,128)(2,1)S(1)}, bf16[128,1024]{1,0:T(8,128)(2,1)S(1)}, u32[]{:S(2)}, u32[]{:S(2)}) collective-permute-start(bf16[128,1024]{1,0:T(8,128)(2,1)S(1)} %convert_element_type.21), channel_id=1, source_target_pairs={{0,16},{8,24},{16,0},{24,8},{1,17},{9,25},{17,1},{25,9},{2,18},{10... | collective-permute-start | bytes 786440 | tf_op jit(solution)/shard_map/ppermute | solution.py:22
  8.9 11.7 %collective-permute-start.2 = (bf16[128,1024]{1,0:T(8,128)(2,1)S(1)}, bf16[128,1024]{1,0:T(8,128)(2,1)S(1)}, u32[]{:S(2)}, u32[]{:S(2)}) collective-permute-start(bf16[128,1024]{1,0:T(8,128)(2,1)S(1)} %convert_element_type.21), channel_id=1, source_target_pairs={{0,8},{8,0},{16,24},{24,16},{1,9},{9,1},{17,25},{25,17},{2,10},{10... | collective-permute-start | bytes 786440 | tf_op jit(solution)/shard_map/ppermute | solution.py:22
  20.6 3.4 %collective-permute-start.5 = (bf16[768,1024]{1,0:T(8,128)(2,1)S(1)}, bf16[768,1024]{1,0:T(8,128)(2,1)S(1)}, u32[]{:S(2)}, u32[]{:S(2)}) collective-permute-start(bf16[768,1024]{1,0:T(8,128)(2,1)S(1)} %constant_dynamic-update-slice_fusion.refs_1_.refs_2_.refs_4_.refs_3_), channel_id=1, source_target_pairs={{0,1},{1,0},{2,3},{3,2},{4,5},{5,4},{6,7},{7,6},{8,9},{9,8},{10,11... | collective-permute-start | bytes 4718600 | tf_op jit(solution)/shard_map/ppermute | solution.py:22
  20.6 9.2 %collective-permute-start.4 = (bf16[256,1024]{1,0:T(8,128)(2,1)S(1)}, bf16[256,1024]{1,0:T(8,128)(2,1)S(1)}, u32[]{:S(2)}, u32[]{:S(2)}) collective-permute-start(bf16[256,1024]{1,0:T(8,128)(2,1)S(1)} %collective-permute-done), channel_id=1, source_target_pairs={{0,4},{1,3},{2,6},{3,1},{4,0},{5,7},{6,2},{7,5},{8,12},{9,11},{10,... | collective-permute-start | bytes 1572872 | tf_op jit(solution)/shard_map/ppermute | solution.py:262
  21.1 8.5 %collective-permute-start.6 = (bf16[128,1024]{1,0:T(8,128)(2,1)S(1)}, bf16[128,1024]{1,0:T(8,128)(2,1)S(1)}, u32[]{:S(2)}, u32[]{:S(2)}) collective-permute-start(bf16[128,1024]{1,0:T(8,128)(2,1)S(1)} %collective-permute-done.3), channel_id=1, source_target_pairs={{0,8},{8,0},{16,24},{24,16},{1,9},{9,1},{17,25},{25,17},{2,10},{10... | collective-permute-start | bytes 786440 | tf_op jit(solution)/shard_map/ppermute | solution.py:22
  29.8 1.9 %collective-permute-start.7 = (bf16[256,1024]{1,0:T(8,128)(2,1)S(1)}, bf16[256,1024]{1,0:T(8,128)(2,1)S(1)}, u32[]{:S(2)}, u32[]{:S(2)}) collective-permute-start(bf16[256,1024]{1,0:T(8,128)(2,1)S(1)} %collective-permute-done.4.refs_3_.refs_6_.refs_5_), channel_id=1, source_target_pairs={{0,1},{1,0},{2,3},{3,2},{4,5},{5,4},{6,7},{7,6},{8,9},{9,8},{10,11... | collective-permute-start | bytes 1572872 | tf_op jit(solution)/shard_map/ppermute | solution.py:22
  32.8 1.3 %collective-permute-start.8 = (f32[2,8,256]{2,1,0:T(8,128)S(1)}, f32[2,8,256]{2,1,0:T(8,128)S(1)}, u32[]{:S(2)}, u32[]{:S(2)}) collective-permute-start(f32[2,8,256]{2,1,0:T(8,128)S(1)} %get-tuple-element.44.pair_ref), channel_id=1, source_target_pairs={{0,1},{1,0},{2,3},{3,2},{4,5},{5,4},{6,7},{7,6},{8,9},{9,8},{10,11... | collective-permute-start | bytes 49160 | tf_op jit(solution)/shard_map/ppermute | solution.py:114
  34.1 3.8 %collective-permute-start.10 = (f32[2,8,256]{2,1,0:T(8,128)S(1)}, f32[2,8,256]{2,1,0:T(8,128)S(1)}, u32[]{:S(2)}, u32[]{:S(2)}) collective-permute-start(f32[2,8,256]{2,1,0:T(8,128)S(1)} %join_rows.2.pair_ref), channel_id=1, source_target_pairs={{0,4},{1,3},{2,6},{3,1},{4,0},{5,7},{6,2},{7,5},{8,12},{9,11},{10,... | collective-permute-start | bytes 49160 | tf_op jit(solution)/shard_map/ppermute | solution.py:114
  34.7 4.6 %collective-permute-start.11 = (f32[2,8,256]{2,1,0:T(8,128)S(1)}, f32[2,8,256]{2,1,0:T(8,128)S(1)}, u32[]{:S(2)}, u32[]{:S(2)}) collective-permute-start(f32[2,8,256]{2,1,0:T(8,128)S(1)} %join_rows.2.pair_ref), channel_id=1, source_target_pairs={{0,6},{1,7},{2,4},{3,5},{4,2},{5,3},{6,0},{7,1},{8,14},{9,15},{10,... | collective-permute-start | bytes 49160 | tf_op jit(solution)/shard_map/ppermute | solution.py:114
  36.4 3.7 %collective-permute-start.9 = (f32[2,8,256]{2,1,0:T(8,128)S(1)}, f32[2,8,256]{2,1,0:T(8,128)S(1)}, u32[]{:S(2)}, u32[]{:S(2)}) collective-permute-start(f32[2,8,256]{2,1,0:T(8,128)S(1)} %join_rows.2.pair_ref), channel_id=1, source_target_pairs={{0,2},{1,5},{2,0},{3,7},{4,6},{5,1},{6,4},{7,3},{8,10},{9,13},{10,... | collective-permute-start | bytes 49160 | tf_op jit(solution)/shard_map/ppermute | solution.py:114
  41.2 7.2 %collective-permute-start.12 = (f16[136,1024]{1,0:T(8,128)(2,1)S(1)}, f16[136,1024]{1,0:T(8,128)(2,1)S(1)}, u32[]{:S(2)}, u32[]{:S(2)}) collective-permute-start(f16[136,1024]{1,0:T(8,128)(2,1)S(1)} %convert_element_type.22), channel_id=1, source_target_pairs={{0,8},{8,0},{16,24},{24,16},{1,9},{9,1},{17,25},{25,17},{2,10},{10... | collective-permute-start | bytes 835592 | tf_op jit(solution)/shard_map/ppermute | solution.py:22
  48.5 14.6 %copy-start = (f32[128,1024]{1,0:T(8,128)S(1)}, f32[128,1024]{1,0:T(8,128)}, u32[]{:S(2)}) copy-start(f32[128,1024]{1,0:T(8,128)} %refs_3_.1) | copy-start | bytes 1572868
  48.6 11.8 %collective-permute-start.13 = (f16[136,1024]{1,0:T(8,128)(2,1)S(1)}, f16[136,1024]{1,0:T(8,128)(2,1)S(1)}, u32[]{:S(2)}, u32[]{:S(2)}) collective-permute-start(f16[136,1024]{1,0:T(8,128)(2,1)S(1)} %convert_element_type.25), channel_id=1, source_target_pairs={{0,8},{8,0},{16,24},{24,16},{1,9},{9,1},{17,25},{25,17},{2,10},{10... | collective-permute-start | bytes 835592 | tf_op jit(solution)/shard_map/ppermute | solution.py:22
  50.2 12.8 %collective-permute-start.14 = (f16[136,1024]{1,0:T(8,128)(2,1)S(1)}, f16[136,1024]{1,0:T(8,128)(2,1)S(1)}, u32[]{:S(2)}, u32[]{:S(2)}) collective-permute-start(f16[136,1024]{1,0:T(8,128)(2,1)S(1)} %convert_element_type.24), channel_id=1, source_target_pairs={{0,16},{8,24},{16,0},{24,8},{1,17},{9,25},{17,1},{25,9},{2,18},{10... | collective-permute-start | bytes 835592 | tf_op jit(solution)/shard_map/ppermute | solution.py:22

commit v13 on v12

--- a/solution.py
+++ b/solution.py
@@ -30,16 +30,17 @@
 def score_kernel(n_cent, n_half, n_rows, picks, begin, starts, r, *refs):
     cent_refs, refs = refs[:n_cent], refs[n_cent:]
     half_refs, refs = refs[:n_half], refs[n_half:]
-    row_refs, early_refs = refs[:n_rows], refs[n_rows:-3]
-    score_ref, pair_ref, half_ref = refs[-3:]
+    row_refs, refs = refs[:n_rows], refs[n_rows:]
+    early_refs, (score_ref, pair_ref, *half_out) = refs[: len(starts)], refs[len(starts) :]
+    lanes = min(r, 128)
     halves = [ref[...] for ref in half_refs]
     for ref in cent_refs[n_half:]:
         squares = jnp.square(ref[...].astype(jnp.float32))
         half = 0.5 * jnp.sum(squares, axis=1, keepdims=True)
-        halves.append(jnp.broadcast_to(half, (half.shape[0], half_ref.shape[1])))
-    half_ref[...] = halves[-1]
-    repeat = r // half_ref.shape[1]
-    halves = [jnp.concatenate([half] * repeat, axis=1) for half in halves]
+        halves.append(jnp.broadcast_to(half, (half.shape[0], lanes)))
+    for ref in half_out:
+        ref[...] = halves[-1]
+    halves = [jnp.concatenate([half] * (r // lanes), axis=1) for half in halves]
     for j, (i, at) in enumerate(picks):
         parts, first = [], 0
         for ref, half in zip(cent_refs, halves):
@@ -68,29 +69,27 @@
                 pair_ref[:, start + k : start + k + 1] = ref[:, k : k + 1]
 
 
-def score(centers, halves, rows, r, picks, early=(), begin=0):
+def score(centers, halves, rows, r, picks, early=(), begin=0, give_half=False, weight=1):
     n_r = len(picks)
     depth = rows[0].shape[1]
     c = sum(x.shape[0] for x in centers)
-    lanes = min(r, 128)
     starts = [sum(e.shape[1] for e in early[:i]) for i in range(len(early))]
     n_out = max(begin + n_r, sum(e.shape[1] for e in early))
     operands = [*centers, *halves, *rows, *early]
+    shapes = [(n_r, c, r), (2, n_out, r)]
+    if give_half:
+        shapes.append((centers[-1].shape[0], min(r, 128)))
     return pl.pallas_call(
         functools.partial(
             score_kernel, len(centers), len(halves), len(rows), picks, begin, starts, r
         ),
-        out_shape=(
-            jax.ShapeDtypeStruct((n_r, c, r), jnp.float32),
-            jax.ShapeDtypeStruct((2, n_out, r), jnp.float32),
-            jax.ShapeDtypeStruct((centers[-1].shape[0], lanes), jnp.float32),
-        ),
+        out_shape=[jax.ShapeDtypeStruct(shape, jnp.float32) for shape in shapes],
         in_specs=[VMEM] * len(operands),
-        out_specs=(VMEM,) * 3,
+        out_specs=[VMEM] * len(shapes),
         compiler_params=PARAMS,
         cost_estimate=pl.CostEstimate(
-            flops=2 * n_r * c * r * depth,
-            bytes_accessed=2 * (n_r * r + c) * depth,
+            flops=int(2 * n_r * c * r * depth * weight),
+            bytes_accessed=int(2 * (n_r * r + c) * depth * weight),
             transcendentals=n_r * c * r,
         ),
         name="score_rows",
@@ -261,34 +260,36 @@
     if n_cent == 8:
         diag = lax.ppermute(from_p, "cent", by_q)
         three = jnp.concatenate([embeddings, from_p, from_q], axis=0)
-        give, most = lax.optimization_barrier((three, most))
-        three_core = swap(give, "cent", n_cent, 1)
+        give = three
         most = [jnp.concatenate(most, axis=0)]
         of_three = [(0, j * own_rows) for j in range(3)]
-        s_0, pair_0, half = score(most, [], [three], own_rows, of_three)
-        s_1, pair_1, _ = score(most, [half], [three_core], own_rows, of_three)
-        give, pair_0, pair_1, final = lax.optimization_barrier(
-            (diag, pair_0, pair_1, final)
-        )
-        rows = [three, three_core, diag, swap(give, "cent", n_cent, 1)]
+        s_0, pair_0, half = score(most, [], [three], own_rows, of_three, give_half=True, weight=1)
+        three_core = swap(give, "cent", n_cent, 1)
+        s_1, pair_1 = score(most, [half], [three_core], own_rows, of_three, weight=.1)
+        diag, pair_0, final = lax.optimization_barrier((diag, pair_0, final))
+        s_2, pair_d = score(most, [half], [diag], own_rows, [(0, 0)], weight=40)
+        give, pair_d = lax.optimization_barrier((diag, pair_d))
+        diag_core = swap(give, "cent", n_cent, 1)
+        rows = [three, three_core, diag, diag_core]
         order = [0, 2, 4, 1, 5, 3, 6, 7]
         picks = [(i, j * own_rows) for i in range(2) for j in range(3)] + [(2, 0), (3, 0)]
-        both = most + final
-        s_3, pair_3, last = score(both, [half], rows[2:3], own_rows, [(0, 0)])
-        s_2, pairs, _ = score(final, [last], rows[:2], own_rows, picks[:6], [pair_0, pair_1])
-        s_4, pairs, _ = score(both, [half, last], rows[3:], own_rows, [(0, 0)], [pairs, pair_3], 7)
-        scores = [s_0, s_1, s_3, s_4]
+        early = [pair_0, pair_1, pair_d]
+        s_3, pairs, last = score(
+            final, [], rows[:3], own_rows, picks[:7], early, give_half=True, weight=1
+        )
+        s_4, pairs = score(most + final, [half, last], rows[3:], own_rows, [(0, 0)], [pairs], 7)
+        scores = [s_0, s_1, s_2, s_4]
         places = [(i, j) for i in range(2) for j in range(3)] + [(2, 0), (3, 0)]
-        last_scores = [s_2, s_3, s_4]
-        last_places = [(0, j, 0) for j in range(6)] + [(1, 0, end), (2, 0, end)]
+        last_scores = [s_3, s_4]
+        last_places = [(0, j, 0) for j in range(7)] + [(1, 0, end)]
     else:
         rows = [embeddings] + [swap(embeddings, "cent", n_cent, m) for m in range(1, n_cent)]
         order = list(range(n_cent))
         picks = [(j, 0) for j in order]
-        s_0, pair_0, _ = score(most, [], rows, own_rows, picks)
+        s_0, pair_0 = score(most, [], rows, own_rows, picks)
         scores = [s_0]
         places = [(0, j) for j in order]
-        s_1, pairs, _ = score(final, [], rows, own_rows, picks, [pair_0])
+        s_1, pairs = score(final, [], rows, own_rows, picks, [pair_0])
         last_scores, last_places = [s_1], [(0, j, 0) for j in order]
     if n_cent == 8:
         where = [order.index((j ^ 1) & 1 | (j & 2) << 1 | (j & 4) >> 1) for j in order]

time: 64.3 us -> 63.6 us (0.989)
  waiting for transfers between devices: 30.4 us -> 28.6 us
  starting transfers between devices: 20.3 us -> 21.8 us
    ppermute x8, waiting for transfers between devices: 22.3 us -> 20.8 us  [swap(): return lax.ppermute(x, axis, partner(size, mask))]
    ppermute x1, starting transfers between devices: 0.51 us -> 1.46 us  [local(): diag = lax.ppermute(from_p, 'cent', by_q)]
  transfers between devices with their start and end apart: 15 -> 15, of which waited for: 13 -> 10; matrix products, arithmetic and copies ran while one was open for 4% -> 5% of each run, Pallas kernels for 10% -> 10%
where the time goes in v13:
time: 63.6 us; the launch traced here: 63.4 us
  waiting for transfers between devices  28.6 us (45%)
  starting transfers between devices  21.8 us (34%)
  Pallas kernels  9.16 us (14%)
  local copies, waits for them, and re-layouts  1.72 us (3%)
  other arithmetic  1.34 us (2%)
  between operations  0.79 us (1%)
    ppermute x8, waiting for transfers between devices, swap(): return lax.ppermute(x, axis, partner(size, mask))  20.8 us
    ppermute x8, starting transfers between devices, swap(): return lax.ppermute(x, axis, partner(size, mask))  11.7 us
    pallas_call x5, Pallas kernels, score(): pl.pallas_call(functools.partial(score_kernel, len(centers), len(halves),...  4.62 us
    ppermute x1, waiting for transfers between devices, local(): from_p = lax.ppermute(embeddings, 'cent', by_p)  4.62 us
    ppermute x4, starting transfers between devices, join(): others = [lax.ppermute(pairs, 'cent', route) for route in routes]  4.1 us
    pallas_call x2, Pallas kernels, weighted(): pl.pallas_call(functools.partial(sums_kernel, len(scores), picks, parts),...  3.3 us
    ppermute x4, waiting for transfers between devices, join(): others = [lax.ppermute(pairs, 'cent', route) for route in routes]  3.19 us
    ppermute x1, starting transfers between devices, local(): from_p = lax.ppermute(embeddings, 'cent', by_p)  3 us
  transfers between devices with their start and end apart: 15, of which 10 were waited for; matrix products, arithmetic and copies ran while one was open for 5% of the time, Pallas kernels for 10%

profile of v13, /device:TPU:0, one launch (start us, length us, event | category | flops | bytes accessed | tf_op | source)
XLA Modules:
  0.0 63.4 jit_solution(5350689660229434865)
XLA Ops:
  0.6 3.0 %collective-permute-start.2 = (bf16[256,1024]{1,0:T(8,128)(2,1)}, bf16[256,1024]{1,0:T(8,128)(2,1)S(1)}, u32[]{:S(2)}, u32[]{:S(2)}) collective-permute-start(bf16[256,1024]{1,0:T(8,128)(2,1)} %param.2), channel_id=1, source_target_pairs={{0,2},{1,5},{2,0},{3,7},{4,6},{5,1},{6,4},{7,3},{8,10},{9,13},{10,... | collective-permute-start | bytes 1572872 | tf_op jit(solution)/shard_map/ppermute | solution.py:250
  3.6 1.5 %collective-permute-start.4 = (bf16[256,1024]{1,0:T(8,128)(2,1)}, bf16[256,1024]{1,0:T(8,128)(2,1)S(1)}, u32[]{:S(2)}, u32[]{:S(2)}) collective-permute-start(bf16[256,1024]{1,0:T(8,128)(2,1)} %param.2), channel_id=1, source_target_pairs={{0,4},{1,3},{2,6},{3,1},{4,0},{5,7},{6,2},{7,5},{8,12},{9,11},{10,... | collective-permute-start | bytes 1572872 | tf_op jit(solution)/shard_map/ppermute | solution.py:251
  5.2 1.1 %convert_element_type.21 = bf16[128,1024]{1,0:T(8,128)(2,1)S(1)} convert(f32[128,1024]{1,0:T(8,128)} %refs_3_.1) | non-fusion elementwise | flops 131072 | bytes 786432 | tf_op jit(solution)/shard_map/convert_element_type | solution.py:246
  6.2 2.7 %collective-permute-start.1 = (bf16[128,1024]{1,0:T(8,128)(2,1)S(1)}, bf16[128,1024]{1,0:T(8,128)(2,1)S(1)}, u32[]{:S(2)}, u32[]{:S(2)}) collective-permute-start(bf16[128,1024]{1,0:T(8,128)(2,1)S(1)} %convert_element_type.21), channel_id=1, source_target_pairs={{0,16},{8,24},{16,0},{24,8},{1,17},{9,25},{17,1},{25,9},{2,18},{10... | collective-permute-start | bytes 786440 | tf_op jit(solution)/shard_map/ppermute | solution.py:22
  8.9 1.6 %collective-permute-start = (bf16[128,1024]{1,0:T(8,128)(2,1)S(1)}, bf16[128,1024]{1,0:T(8,128)(2,1)S(1)}, u32[]{:S(2)}, u32[]{:S(2)}) collective-permute-start(bf16[128,1024]{1,0:T(8,128)(2,1)S(1)} %convert_element_type.21), channel_id=1, source_target_pairs={{0,8},{8,0},{16,24},{24,16},{1,9},{9,1},{17,25},{25,17},{2,10},{10... | collective-permute-start | bytes 786440 | tf_op jit(solution)/shard_map/ppermute | solution.py:22
  10.5 1.1 %constant_dynamic-update-slice_fusion.2 = bf16[768,1024]{1,0:T(8,128)(2,1)S(1)} fusion(bf16[256,1024]{1,0:T(8,128)(2,1)} %param.2), kind=kLoop, calls=%fused_computation.3 | loop fusion | bytes 1048576
  11.5 4.6 %collective-permute-done.2 = bf16[256,1024]{1,0:T(8,128)(2,1)S(1)} collective-permute-done((bf16[256,1024]{1,0:T(8,128)(2,1)}, bf16[256,1024]{1,0:T(8,128)(2,1)S(1)}, u32[]{:S(2)}, u32[]{:S(2)}) %collective-permute-start.2) | collective-permute-done | bytes 524320 | tf_op jit(solution)/shard_map/ppermute | solution.py:250
  16.2 1.5 %collective-permute-start.3 = (bf16[256,1024]{1,0:T(8,128)(2,1)S(1)}, bf16[256,1024]{1,0:T(8,128)(2,1)S(1)}, u32[]{:S(2)}, u32[]{:S(2)}) collective-permute-start(bf16[256,1024]{1,0:T(8,128)(2,1)S(1)} %collective-permute-done.2), channel_id=1, source_target_pairs={{0,4},{1,3},{2,6},{3,1},{4,0},{5,7},{6,2},{7,5},{8,12},{9,11},{10,... | collective-permute-start | bytes 1572872 | tf_op jit(solution)/shard_map/ppermute | solution.py:261
  17.8 2.6 %collective-permute-done.1 = bf16[128,1024]{1,0:T(8,128)(2,1)S(1)} collective-permute-done((bf16[128,1024]{1,0:T(8,128)(2,1)S(1)}, bf16[128,1024]{1,0:T(8,128)(2,1)S(1)}, u32[]{:S(2)}, u32[]{:S(2)}) %collective-permute-start.1) | collective-permute-done | bytes 262176 | tf_op jit(solution)/shard_map/ppermute | solution.py:22
  21.0 1.1 %score_rows.5 = (f32[3,384,256]{2,1,0:T(8,128)S(1)}, f32[2,3,256]{2,1,0:T(4,128)S(1)}, f32[384,128]{1,0:T(8,128)S(1)}) custom-call(bf16[384,1024]{1,0:T(8,128)(2,1)S(1)} %pad_maximum_fusion.refs_0_, bf16[768,1024]{1,0:T(8,128)(2,1)S(1)} %constant_dynamic-update-slice_fusion.refs_1_.refs_4_.refs_2_), custom_call_target="tpu_custom_call" | custom-call | flops 603979776 | bytes 2359296 | tf_op jit(solution)/shard_map/score_rows/pallas_call | solution.py:82
  22.1 5.4 %collective-permute-done.5.refs_0_.refs_1_ = bf16[128,1024]{1,0:T(8,128)(2,1)S(1)} collective-permute-done((bf16[128,1024]{1,0:T(8,128)(2,1)S(1)}, bf16[128,1024]{1,0:T(8,128)(2,1)S(1)}, u32[]{:S(2)}, u32[]{:S(2)}) %collective-permute-start.5) | collective-permute-done | bytes 262176 | tf_op jit(solution)/shard_map/ppermute | solution.py:22
  28.1 1.0 %score_rows.6 = (f32[3,384,256]{2,1,0:T(8,128)S(1)}, f32[2,3,256]{2,1,0:T(4,128)S(1)}) custom-call(bf16[384,1024]{1,0:T(8,128)(2,1)S(1)} %pad_maximum_fusion.refs_0_, f32[384,128]{1,0:T(8,128)S(1)} %get-tuple-element.29.refs_1_.refs_2_, bf16[768,1024]{1,0:T(8,128)(2,1)S(1)} %collective-permute-done.6.refs_2_.refs_5_.refs_3_), custom_call_target="tpu_custom_call" | custom-call | flops 60397976 | bytes 235929 | tf_op jit(solution)/shard_map/score_rows/pallas_call | solution.py:82
  29.1 1.4 %score_rows.8 = (f32[7,128,256]{2,1,0:T(8,128)S(1)}, f32[2,7,256]{2,1,0:T(8,128)S(1)}, f32[128,128]{1,0:T(8,128)S(1)}) custom-call(bf16[128,1024]{1,0:T(8,128)(2,1)S(1)} %collective-permute-done.5.refs_0_.refs_1_, bf16[768,1024]{1,0:T(8,128)(2,1)S(1)} %constant_dynamic-update-slice_fusion.refs_1_.refs_4_.refs_2_, ...), custom_call_target="tpu_custom_call" | custom-call | flops 469762048 | bytes 3932160 | tf_op jit(solution)/shard_map/score_rows/pallas_call | solution.py:82
  33.1 1.6 %collective-permute-start.11 = (f32[2,8,256]{2,1,0:T(8,128)S(1)}, f32[2,8,256]{2,1,0:T(8,128)S(1)}, u32[]{:S(2)}, u32[]{:S(2)}) collective-permute-start(f32[2,8,256]{2,1,0:T(8,128)S(1)} %join_rows.2.pair_ref), channel_id=1, source_target_pairs={{0,6},{1,7},{2,4},{3,5},{4,2},{5,3},{6,0},{7,1},{8,14},{9,15},{10,... | collective-permute-start | bytes 49160 | tf_op jit(solution)/shard_map/ppermute | solution.py:113
  34.7 1.4 %collective-permute-start.9 = (f32[2,8,256]{2,1,0:T(8,128)S(1)}, f32[2,8,256]{2,1,0:T(8,128)S(1)}, u32[]{:S(2)}, u32[]{:S(2)}) collective-permute-start(f32[2,8,256]{2,1,0:T(8,128)S(1)} %join_rows.2.pair_ref), channel_id=1, source_target_pairs={{0,2},{1,5},{2,0},{3,7},{4,6},{5,1},{6,4},{7,3},{8,10},{9,13},{10,... | collective-permute-start | bytes 49160 | tf_op jit(solution)/shard_map/ppermute | solution.py:113
  36.4 1.4 %collective-permute-done.11.refs_2_ = f32[2,8,256]{2,1,0:T(8,128)S(1)} collective-permute-done((f32[2,8,256]{2,1,0:T(8,128)S(1)}, f32[2,8,256]{2,1,0:T(8,128)S(1)}, u32[]{:S(2)}, u32[]{:S(2)}) %collective-permute-start.11) | collective-permute-done | bytes 16416 | tf_op jit(solution)/shard_map/ppermute | solution.py:113
  39.5 1.7 %collective-permute-start.12 = (f16[136,1024]{1,0:T(8,128)(2,1)S(1)}, f16[136,1024]{1,0:T(8,128)(2,1)S(1)}, u32[]{:S(2)}, u32[]{:S(2)}) collective-permute-start(f16[136,1024]{1,0:T(8,128)(2,1)S(1)} %convert_element_type.22), channel_id=1, source_target_pairs={{0,8},{8,0},{16,24},{24,16},{1,9},{9,1},{17,25},{25,17},{2,10},{10... | collective-permute-start | bytes 835592 | tf_op jit(solution)/shard_map/ppermute | solution.py:22
  41.2 2.4 %weighted_sums.2 = (f32[136,1024]{1,0:T(8,128)S(1)}, f32[136,1024]{1,0:T(8,128)S(1)}, f32[136,1024]{1,0:T(8,128)S(1)}) custom-call(f32[8,256]{1,0:T(8,128)S(1)} %join_rows.3.lognorm_ref, f32[3,384,256]{2,1,0:T(8,128)S(1)} %get-tuple-element.39.refs_0_, f32[3,384,256]{2,1,0:T(8,128)S(1)} %get-tuple-element.40.refs_1_, ...), custom_call_target="tpu_custom_call" | custom-call | flops 1610612736 | bytes 4194304 | tf_op jit(solution)/shard_map/weighted_sums/pallas_call | solution.py:227
  43.6 3.1 %collective-permute-done.12 = f16[136,1024]{1,0:T(8,128)(2,1)S(1)} collective-permute-done((f16[136,1024]{1,0:T(8,128)(2,1)S(1)}, f16[136,1024]{1,0:T(8,128)(2,1)S(1)}, u32[]{:S(2)}, u32[]{:S(2)}) %collective-permute-start.12) | collective-permute-done | bytes 278560 | tf_op jit(solution)/shard_map/ppermute | solution.py:22
  47.0 1.7 %collective-permute-start.13 = (f16[136,1024]{1,0:T(8,128)(2,1)S(1)}, f16[136,1024]{1,0:T(8,128)(2,1)S(1)}, u32[]{:S(2)}, u32[]{:S(2)}) collective-permute-start(f16[136,1024]{1,0:T(8,128)(2,1)S(1)} %convert_element_type.25), channel_id=1, source_target_pairs={{0,8},{8,0},{16,24},{24,16},{1,9},{9,1},{17,25},{25,17},{2,10},{10... | collective-permute-start | bytes 835592 | tf_op jit(solution)/shard_map/ppermute | solution.py:22
  48.7 3.4 %collective-permute-start.14 = (f16[136,1024]{1,0:T(8,128)(2,1)S(1)}, f16[136,1024]{1,0:T(8,128)(2,1)S(1)}, u32[]{:S(2)}, u32[]{:S(2)}) collective-permute-start(f16[136,1024]{1,0:T(8,128)(2,1)S(1)} %convert_element_type.24), channel_id=1, source_target_pairs={{0,16},{8,24},{16,0},{24,8},{1,17},{9,25},{17,1},{25,9},{2,18},{10... | collective-permute-start | bytes 835592 | tf_op jit(solution)/shard_map/ppermute | solution.py:22
  52.7 5.9 %collective-permute-done.13 = f16[136,1024]{1,0:T(8,128)(2,1)S(1)} collective-permute-done((f16[136,1024]{1,0:T(8,128)(2,1)S(1)}, f16[136,1024]{1,0:T(8,128)(2,1)S(1)}, u32[]{:S(2)}, u32[]{:S(2)}) %collective-permute-start.13) | collective-permute-done | bytes 278560 | tf_op jit(solution)/shard_map/ppermute | solution.py:22
  58.6 3.7 %collective-permute-done.14 = f16[136,1024]{1,0:T(8,128)(2,1)S(1)} collective-permute-done((f16[136,1024]{1,0:T(8,128)(2,1)S(1)}, f16[136,1024]{1,0:T(8,128)(2,1)S(1)}, u32[]{:S(2)}, u32[]{:S(2)}) %collective-permute-start.14) | collective-permute-done | bytes 278560 | tf_op jit(solution)/shard_map/ppermute | solution.py:22
  62.4 1.0 %update_centroids.1 = (f32[128,1024]{1,0:T(8,128)}, f32[1,128]{1,0:T(1,128)}) custom-call(f32[136,1024]{1,0:T(8,128)S(1)} %get-tuple-element.43.refs_0_, f32[136,1024]{1,0:T(8,128)S(1)} %convert_element_type.26.refs_1_, f32[136,1024]{1,0:T(8,128)S(1)} %convert_element_type.27.refs_2_, f32[128,1024]{1,0:T(8,128)S(1)} %copy-done), custom_call_target="tpu_custom_call" | custom-call | tf_op jit(solution)/shard_map/update_centroids/pallas_call | solution.py:209
  (31 shorter events, 6.8 us)
Async XLA Ops:
  0.6 15.5 %collective-permute-start.2 = (bf16[256,1024]{1,0:T(8,128)(2,1)}, bf16[256,1024]{1,0:T(8,128)(2,1)S(1)}, u32[]{:S(2)}, u32[]{:S(2)}) collective-permute-start(bf16[256,1024]{1,0:T(8,128)(2,1)} %param.2), channel_id=1, source_target_pairs={{0,2},{1,5},{2,0},{3,7},{4,6},{5,1},{6,4},{7,3},{8,10},{9,13},{10,... | collective-permute-start | bytes 1572872 | tf_op jit(solution)/shard_map/ppermute | solution.py:250
  3.6 14.0 %collective-permute-start.4 = (bf16[256,1024]{1,0:T(8,128)(2,1)}, bf16[256,1024]{1,0:T(8,128)(2,1)S(1)}, u32[]{:S(2)}, u32[]{:S(2)}) collective-permute-start(bf16[256,1024]{1,0:T(8,128)(2,1)} %param.2), channel_id=1, source_target_pairs={{0,4},{1,3},{2,6},{3,1},{4,0},{5,7},{6,2},{7,5},{8,12},{9,11},{10,... | collective-permute-start | bytes 1572872 | tf_op jit(solution)/shard_map/ppermute | solution.py:251
  6.2 14.2 %collective-permute-start.1 = (bf16[128,1024]{1,0:T(8,128)(2,1)S(1)}, bf16[128,1024]{1,0:T(8,128)(2,1)S(1)}, u32[]{:S(2)}, u32[]{:S(2)}) collective-permute-start(bf16[128,1024]{1,0:T(8,128)(2,1)S(1)} %convert_element_type.21), channel_id=1, source_target_pairs={{0,16},{8,24},{16,0},{24,8},{1,17},{9,25},{17,1},{25,9},{2,18},{10... | collective-permute-start | bytes 786440 | tf_op jit(solution)/shard_map/ppermute | solution.py:22
  8.9 12.1 %collective-permute-start = (bf16[128,1024]{1,0:T(8,128)(2,1)S(1)}, bf16[128,1024]{1,0:T(8,128)(2,1)S(1)}, u32[]{:S(2)}, u32[]{:S(2)}) collective-permute-start(bf16[128,1024]{1,0:T(8,128)(2,1)S(1)} %convert_element_type.21), channel_id=1, source_target_pairs={{0,8},{8,0},{16,24},{24,16},{1,9},{9,1},{17,25},{25,17},{2,10},{10... | collective-permute-start | bytes 786440 | tf_op jit(solution)/shard_map/ppermute | solution.py:22
  16.2 11.3 %collective-permute-start.3 = (bf16[256,1024]{1,0:T(8,128)(2,1)S(1)}, bf16[256,1024]{1,0:T(8,128)(2,1)S(1)}, u32[]{:S(2)}, u32[]{:S(2)}) collective-permute-start(bf16[256,1024]{1,0:T(8,128)(2,1)S(1)} %collective-permute-done.2), channel_id=1, source_target_pairs={{0,4},{1,3},{2,6},{3,1},{4,0},{5,7},{6,2},{7,5},{8,12},{9,11},{10,... | collective-permute-start | bytes 1572872 | tf_op jit(solution)/shard_map/ppermute | solution.py:261
  17.7 10.4 %collective-permute-start.6 = (bf16[768,1024]{1,0:T(8,128)(2,1)S(1)}, bf16[768,1024]{1,0:T(8,128)(2,1)S(1)}, u32[]{:S(2)}, u32[]{:S(2)}) collective-permute-start(bf16[768,1024]{1,0:T(8,128)(2,1)S(1)} %constant_dynamic-update-slice_fusion.refs_1_.refs_4_.refs_2_), channel_id=1, source_target_pairs={{0,1},{1,0},{2,3},{3,2},{4,5},{5,4},{6,7},{7,6},{8,9},{9,8},{10,11... | collective-permute-start | bytes 4718600 | tf_op jit(solution)/shard_map/ppermute | solution.py:22
  20.4 7.1 %collective-permute-start.5 = (bf16[128,1024]{1,0:T(8,128)(2,1)S(1)}, bf16[128,1024]{1,0:T(8,128)(2,1)S(1)}, u32[]{:S(2)}, u32[]{:S(2)}) collective-permute-start(bf16[128,1024]{1,0:T(8,128)(2,1)S(1)} %collective-permute-done.1), channel_id=1, source_target_pairs={{0,8},{8,0},{16,24},{24,16},{1,9},{9,1},{17,25},{25,17},{2,10},{10... | collective-permute-start | bytes 786440 | tf_op jit(solution)/shard_map/ppermute | solution.py:22
  28.0 2.5 %collective-permute-start.7 = (bf16[256,1024]{1,0:T(8,128)(2,1)S(1)}, bf16[256,1024]{1,0:T(8,128)(2,1)S(1)}, u32[]{:S(2)}, u32[]{:S(2)}) collective-permute-start(bf16[256,1024]{1,0:T(8,128)(2,1)S(1)} %collective-permute-done.3.refs_2_.refs_3_.refs_6_.refs_4_), channel_id=1, source_target_pairs={{0,1},{1,0},{2,3},{3,2},{4,5},{5,4},{6,7},{7,6},{8,9},{9,8},{10,11... | collective-permute-start | bytes 1572872 | tf_op jit(solution)/shard_map/ppermute | solution.py:22
  31.2 1.4 %collective-permute-start.8 = (f32[2,8,256]{2,1,0:T(8,128)S(1)}, f32[2,8,256]{2,1,0:T(8,128)S(1)}, u32[]{:S(2)}, u32[]{:S(2)}) collective-permute-start(f32[2,8,256]{2,1,0:T(8,128)S(1)} %get-tuple-element.38.pair_ref), channel_id=1, source_target_pairs={{0,1},{1,0},{2,3},{3,2},{4,5},{5,4},{6,7},{7,6},{8,9},{9,8},{10,11... | collective-permute-start | bytes 49160 | tf_op jit(solution)/shard_map/ppermute | solution.py:113
  32.6 3.8 %collective-permute-start.10 = (f32[2,8,256]{2,1,0:T(8,128)S(1)}, f32[2,8,256]{2,1,0:T(8,128)S(1)}, u32[]{:S(2)}, u32[]{:S(2)}) collective-permute-start(f32[2,8,256]{2,1,0:T(8,128)S(1)} %join_rows.2.pair_ref), channel_id=1, source_target_pairs={{0,4},{1,3},{2,6},{3,1},{4,0},{5,7},{6,2},{7,5},{8,12},{9,11},{10,... | collective-permute-start | bytes 49160 | tf_op jit(solution)/shard_map/ppermute | solution.py:113
  33.1 4.6 %collective-permute-start.11 = (f32[2,8,256]{2,1,0:T(8,128)S(1)}, f32[2,8,256]{2,1,0:T(8,128)S(1)}, u32[]{:S(2)}, u32[]{:S(2)}) collective-permute-start(f32[2,8,256]{2,1,0:T(8,128)S(1)} %join_rows.2.pair_ref), channel_id=1, source_target_pairs={{0,6},{1,7},{2,4},{3,5},{4,2},{5,3},{6,0},{7,1},{8,14},{9,15},{10,... | collective-permute-start | bytes 49160 | tf_op jit(solution)/shard_map/ppermute | solution.py:113
  34.7 3.7 %collective-permute-start.9 = (f32[2,8,256]{2,1,0:T(8,128)S(1)}, f32[2,8,256]{2,1,0:T(8,128)S(1)}, u32[]{:S(2)}, u32[]{:S(2)}) collective-permute-start(f32[2,8,256]{2,1,0:T(8,128)S(1)} %join_rows.2.pair_ref), channel_id=1, source_target_pairs={{0,2},{1,5},{2,0},{3,7},{4,6},{5,1},{6,4},{7,3},{8,10},{9,13},{10,... | collective-permute-start | bytes 49160 | tf_op jit(solution)/shard_map/ppermute | solution.py:113
  39.5 7.2 %collective-permute-start.12 = (f16[136,1024]{1,0:T(8,128)(2,1)S(1)}, f16[136,1024]{1,0:T(8,128)(2,1)S(1)}, u32[]{:S(2)}, u32[]{:S(2)}) collective-permute-start(f16[136,1024]{1,0:T(8,128)(2,1)S(1)} %convert_element_type.22), channel_id=1, source_target_pairs={{0,8},{8,0},{16,24},{24,16},{1,9},{9,1},{17,25},{25,17},{2,10},{10... | collective-permute-start | bytes 835592 | tf_op jit(solution)/shard_map/ppermute | solution.py:22
  46.9 15.5 %copy-start = (f32[128,1024]{1,0:T(8,128)S(1)}, f32[128,1024]{1,0:T(8,128)}, u32[]{:S(2)}) copy-start(f32[128,1024]{1,0:T(8,128)} %refs_3_.1) | copy-start | bytes 1572868
  47.0 11.6 %collective-permute-start.13 = (f16[136,1024]{1,0:T(8,128)(2,1)S(1)}, f16[136,1024]{1,0:T(8,128)(2,1)S(1)}, u32[]{:S(2)}, u32[]{:S(2)}) collective-permute-start(f16[136,1024]{1,0:T(8,128)(2,1)S(1)} %convert_element_type.25), channel_id=1, source_target_pairs={{0,8},{8,0},{16,24},{24,16},{1,9},{9,1},{17,25},{25,17},{2,10},{10... | collective-permute-start | bytes 835592 | tf_op jit(solution)/shard_map/ppermute | solution.py:22
  48.7 13.6 %collective-permute-start.14 = (f16[136,1024]{1,0:T(8,128)(2,1)S(1)}, f16[136,1024]{1,0:T(8,128)(2,1)S(1)}, u32[]{:S(2)}, u32[]{:S(2)}) collective-permute-start(f16[136,1024]{1,0:T(8,128)(2,1)S(1)} %convert_element_type.24), channel_id=1, source_target_pairs={{0,16},{8,24},{16,0},{24,8},{1,17},{9,25},{17,1},{25,9},{2,18},{10... | collective-permute-start | bytes 835592 | tf_op jit(solution)/shard_map/ppermute | solution.py:22

commit v14 on v13

--- a/solution.py
+++ b/solution.py
@@ -260,28 +260,28 @@
     if n_cent == 8:
         diag = lax.ppermute(from_p, "cent", by_q)
         three = jnp.concatenate([embeddings, from_p, from_q], axis=0)
-        give = three
+        give, most = lax.optimization_barrier((three, most))
+        three_core = swap(give, "cent", n_cent, 1)
         most = [jnp.concatenate(most, axis=0)]
         of_three = [(0, j * own_rows) for j in range(3)]
-        s_0, pair_0, half = score(most, [], [three], own_rows, of_three, give_half=True, weight=1)
-        three_core = swap(give, "cent", n_cent, 1)
-        s_1, pair_1 = score(most, [half], [three_core], own_rows, of_three, weight=.1)
-        diag, pair_0, final = lax.optimization_barrier((diag, pair_0, final))
-        s_2, pair_d = score(most, [half], [diag], own_rows, [(0, 0)], weight=40)
-        give, pair_d = lax.optimization_barrier((diag, pair_d))
-        diag_core = swap(give, "cent", n_cent, 1)
-        rows = [three, three_core, diag, diag_core]
+        s_0, pair_0, half = score(most, [], [three], own_rows, of_three, give_half=True)
+        s_1, pair_1 = score(most, [half], [three_core], own_rows, of_three)
+        final, pair_1 = lax.optimization_barrier((final, pair_1))
+        s_2, pair_2, last = score(
+            final, [], [three], own_rows, of_three, [pair_0], give_half=True, weight=3
+        )
+        give, pair_1, pair_2 = lax.optimization_barrier((diag, pair_1, pair_2))
+        rows = [three, three_core, diag, swap(give, "cent", n_cent, 1)]
         order = [0, 2, 4, 1, 5, 3, 6, 7]
         picks = [(i, j * own_rows) for i in range(2) for j in range(3)] + [(2, 0), (3, 0)]
-        early = [pair_0, pair_1, pair_d]
-        s_3, pairs, last = score(
-            final, [], rows[:3], own_rows, picks[:7], early, give_half=True, weight=1
-        )
-        s_4, pairs = score(most + final, [half, last], rows[3:], own_rows, [(0, 0)], [pairs], 7)
-        scores = [s_0, s_1, s_2, s_4]
+        both = most + final
+        s_3, pairs = score(final, [last], rows[1:2], own_rows, of_three, [pair_2, pair_1], 3)
+        s_4, pair_4 = score(both, [half, last], rows[2:3], own_rows, [(0, 0)])
+        s_5, pairs = score(both, [half, last], rows[3:], own_rows, [(0, 0)], [pairs, pair_4], 7)
+        scores = [s_0, s_1, s_4, s_5]
         places = [(i, j) for i in range(2) for j in range(3)] + [(2, 0), (3, 0)]
-        last_scores = [s_3, s_4]
-        last_places = [(0, j, 0) for j in range(7)] + [(1, 0, end)]
+        last_scores = [s_2, s_3, s_4, s_5]
+        last_places = [(i, j, 0) for i in range(2) for j in range(3)] + [(2, 0, end), (3, 0, end)]
     else:
         rows = [embeddings] + [swap(embeddings, "cent", n_cent, m) for m in range(1, n_cent)]
         order = list(range(n_cent))

time: 63.6 us -> 62.7 us (0.986)
  starting transfers between devices: 21.8 us -> 17.8 us
  waiting for transfers between devices: 28.6 us -> 31.5 us
    ppermute x8, starting transfers between devices: 11.7 us -> 9.04 us  [swap(): return lax.ppermute(x, axis, partner(size, mask))]
    ppermute x8, waiting for transfers between devices: 20.8 us -> 22.4 us  [swap(): return lax.ppermute(x, axis, partner(size, mask))]
    ppermute x1, waiting for transfers between devices: 0.01 us -> 1.18 us  [local(): diag = lax.ppermute(from_p, 'cent', by_q)]
    ppermute x1, starting transfers between devices: 1.46 us -> 0.51 us  [local(): diag = lax.ppermute(from_p, 'cent', by_q)]
    pallas_call x5 -> x6, Pallas kernels: 4.62 us -> 4.77 us  [score(): pl.pallas_call(functools.partial(score_kernel, len(centers), len(halves),...]
  transfers between devices with their start and end apart: 15 -> 15, of which waited for: 10 -> 13; matrix products, arithmetic and copies ran while one was open for 5% -> 5% of each run, Pallas kernels for 10% -> 10%
where the time goes in v14:
time: 62.7 us; the launch traced here: 62.4 us
  waiting for transfers between devices  31.5 us (50%)
  starting transfers between devices  17.8 us (28%)
  Pallas kernels  9.26 us (15%)
  local copies, waits for them, and re-layouts  1.77 us (3%)
  other arithmetic  1.29 us (2%)
  between operations  0.79 us (1%)
    ppermute x8, waiting for transfers between devices, swap(): return lax.ppermute(x, axis, partner(size, mask))  22.4 us
    ppermute x8, starting transfers between devices, swap(): return lax.ppermute(x, axis, partner(size, mask))  9.04 us
    pallas_call x6, Pallas kernels, score(): pl.pallas_call(functools.partial(score_kernel, len(centers), len(halves),...  4.77 us
    ppermute x1, waiting for transfers between devices, local(): from_p = lax.ppermute(embeddings, 'cent', by_p)  4.62 us
    ppermute x4, starting transfers between devices, join(): others = [lax.ppermute(pairs, 'cent', route) for route in routes]  3.75 us
    ppermute x4, waiting for transfers between devices, join(): others = [lax.ppermute(pairs, 'cent', route) for route in routes]  3.29 us
    pallas_call x2, Pallas kernels, weighted(): pl.pallas_call(functools.partial(sums_kernel, len(scores), picks, parts),...  3.29 us
    ppermute x1, starting transfers between devices, local(): from_p = lax.ppermute(embeddings, 'cent', by_p)  3 us
  transfers between devices with their start and end apart: 15, of which 13 were waited for; matrix products, arithmetic and copies ran while one was open for 5% of the time, Pallas kernels for 10%

profile of v14, /device:TPU:0, one launch (start us, length us, event | category | flops | bytes accessed | tf_op | source)
XLA Modules:
  0.0 62.4 jit_solution(12876749921988661165)
XLA Ops:
  0.6 3.0 %collective-permute-start = (bf16[256,1024]{1,0:T(8,128)(2,1)}, bf16[256,1024]{1,0:T(8,128)(2,1)S(1)}, u32[]{:S(2)}, u32[]{:S(2)}) collective-permute-start(bf16[256,1024]{1,0:T(8,128)(2,1)} %param.2), channel_id=1, source_target_pairs={{0,2},{1,5},{2,0},{3,7},{4,6},{5,1},{6,4},{7,3},{8,10},{9,13},{10,... | collective-permute-start | bytes 1572872 | tf_op jit(solution)/shard_map/ppermute | solution.py:250
  3.6 1.5 %collective-permute-start.1 = (bf16[256,1024]{1,0:T(8,128)(2,1)}, bf16[256,1024]{1,0:T(8,128)(2,1)S(1)}, u32[]{:S(2)}, u32[]{:S(2)}) collective-permute-start(bf16[256,1024]{1,0:T(8,128)(2,1)} %param.2), channel_id=1, source_target_pairs={{0,4},{1,3},{2,6},{3,1},{4,0},{5,7},{6,2},{7,5},{8,12},{9,11},{10,... | collective-permute-start | bytes 1572872 | tf_op jit(solution)/shard_map/ppermute | solution.py:251
  5.2 1.1 %convert_element_type.21 = bf16[128,1024]{1,0:T(8,128)(2,1)S(1)} convert(f32[128,1024]{1,0:T(8,128)} %refs_3_.1) | non-fusion elementwise | flops 131072 | bytes 786432 | tf_op jit(solution)/shard_map/convert_element_type | solution.py:246
  6.2 2.7 %collective-permute-start.3 = (bf16[128,1024]{1,0:T(8,128)(2,1)S(1)}, bf16[128,1024]{1,0:T(8,128)(2,1)S(1)}, u32[]{:S(2)}, u32[]{:S(2)}) collective-permute-start(bf16[128,1024]{1,0:T(8,128)(2,1)S(1)} %convert_element_type.21), channel_id=1, source_target_pairs={{0,16},{8,24},{16,0},{24,8},{1,17},{9,25},{17,1},{25,9},{2,18},{10... | collective-permute-start | bytes 786440 | tf_op jit(solution)/shard_map/ppermute | solution.py:22
  8.9 1.6 %collective-permute-start.2 = (bf16[128,1024]{1,0:T(8,128)(2,1)S(1)}, bf16[128,1024]{1,0:T(8,128)(2,1)S(1)}, u32[]{:S(2)}, u32[]{:S(2)}) collective-permute-start(bf16[128,1024]{1,0:T(8,128)(2,1)S(1)} %convert_element_type.21), channel_id=1, source_target_pairs={{0,8},{8,0},{16,24},{24,16},{1,9},{9,1},{17,25},{25,17},{2,10},{10... | collective-permute-start | bytes 786440 | tf_op jit(solution)/shard_map/ppermute | solution.py:22
  10.5 1.1 %constant_dynamic-update-slice_fusion.2 = bf16[768,1024]{1,0:T(8,128)(2,1)S(1)} fusion(bf16[256,1024]{1,0:T(8,128)(2,1)} %param.2), kind=kLoop, calls=%fused_computation.2 | loop fusion | bytes 1048576
  11.5 4.6 %collective-permute-done = bf16[256,1024]{1,0:T(8,128)(2,1)S(1)} collective-permute-done((bf16[256,1024]{1,0:T(8,128)(2,1)}, bf16[256,1024]{1,0:T(8,128)(2,1)S(1)}, u32[]{:S(2)}, u32[]{:S(2)}) %collective-permute-start) | collective-permute-done | bytes 524320 | tf_op jit(solution)/shard_map/ppermute | solution.py:250
  16.2 4.2 %collective-permute-done.3 = bf16[128,1024]{1,0:T(8,128)(2,1)S(1)} collective-permute-done((bf16[128,1024]{1,0:T(8,128)(2,1)S(1)}, bf16[128,1024]{1,0:T(8,128)(2,1)S(1)}, u32[]{:S(2)}, u32[]{:S(2)}) %collective-permute-start.3) | collective-permute-done | bytes 262176 | tf_op jit(solution)/shard_map/ppermute | solution.py:22
  20.6 1.4 %collective-permute-start.4 = (bf16[128,1024]{1,0:T(8,128)(2,1)S(1)}, bf16[128,1024]{1,0:T(8,128)(2,1)S(1)}, u32[]{:S(2)}, u32[]{:S(2)}) collective-permute-start(bf16[128,1024]{1,0:T(8,128)(2,1)S(1)} %collective-permute-done.3), channel_id=1, source_target_pairs={{0,8},{8,0},{16,24},{24,16},{1,9},{9,1},{17,25},{25,17},{2,10},{10... | collective-permute-start | bytes 786440 | tf_op jit(solution)/shard_map/ppermute | solution.py:22
  22.6 1.0 %score_rows.6 = (f32[3,384,256]{2,1,0:T(8,128)S(1)}, f32[2,3,256]{2,1,0:T(4,128)S(1)}, f32[384,128]{1,0:T(8,128)S(1)}) custom-call(bf16[384,1024]{1,0:T(8,128)(2,1)S(1)} %constant_dynamic-update-slice_fusion.3.refs_0_, bf16[768,1024]{1,0:T(8,128)(2,1)S(1)} %constant_dynamic-update-slice_fusion.refs_1_.refs_4_), custom_call_target="tpu_custom_call" | custom-call | flops 603979776 | bytes 2359296 | tf_op jit(solution)/shard_map/score_rows/pallas_call | solution.py:82
  24.0 1.0 %score_rows.7 = (f32[3,384,256]{2,1,0:T(8,128)S(1)}, f32[2,3,256]{2,1,0:T(4,128)S(1)}) custom-call(bf16[384,1024]{1,0:T(8,128)(2,1)S(1)} %constant_dynamic-update-slice_fusion.3.refs_0_, f32[384,128]{1,0:T(8,128)S(1)} %get-tuple-element.36.refs_1_.refs_2_, bf16[768,1024]{1,0:T(8,128)(2,1)S(1)} %collective-permute-done.5.refs_2_.refs_5_), custom_call_target="tpu_custom_call" | custom-call | flops 603979776 | bytes 2359296 | tf_op jit(solution)/shard_map/score_rows/pallas_call | solution.py:82
  25.0 4.3 %collective-permute-done.4.refs_0_.refs_1_ = bf16[128,1024]{1,0:T(8,128)(2,1)S(1)} collective-permute-done((bf16[128,1024]{1,0:T(8,128)(2,1)S(1)}, bf16[128,1024]{1,0:T(8,128)(2,1)S(1)}, u32[]{:S(2)}, u32[]{:S(2)}) %collective-permute-start.4) | collective-permute-done | bytes 262176 | tf_op jit(solution)/shard_map/ppermute | solution.py:22
  29.3 0.7 %score_rows.8 = (f32[3,128,256]{2,1,0:T(8,128)S(1)}, f32[2,3,256]{2,1,0:T(4,128)S(1)}, f32[128,128]{1,0:T(8,128)S(1)}) custom-call(bf16[128,1024]{1,0:T(8,128)(2,1)S(1)} %collective-permute-done.4.refs_0_.refs_1_, bf16[768,1024]{1,0:T(8,128)(2,1)S(1)} %constant_dynamic-update-slice_fusion.refs_1_.refs_4_, f32[2,3,256]{2,1,0:T(4,128)S(1)} %get-tuple-element.40.refs_2_), custom_call_target="tpu_custom_call" | custom-call | flops 603979776 | bytes 5505024 | tf_op jit(solution)/shard_map/score_rows/pallas_call | solution.py:82
  30.0 1.2 %collective-permute-done.6.refs_4_.refs_6_ = bf16[256,1024]{1,0:T(8,128)(2,1)S(1)} collective-permute-done((bf16[256,1024]{1,0:T(8,128)(2,1)S(1)}, bf16[256,1024]{1,0:T(8,128)(2,1)S(1)}, u32[]{:S(2)}, u32[]{:S(2)}) %collective-permute-start.6) | collective-permute-done | bytes 524320 | tf_op jit(solution)/shard_map/ppermute | solution.py:261
  34.0 1.0 %collective-permute-done.8.refs_0_ = f32[2,8,256]{2,1,0:T(8,128)S(1)} collective-permute-done((f32[2,8,256]{2,1,0:T(8,128)S(1)}, f32[2,8,256]{2,1,0:T(8,128)S(1)}, u32[]{:S(2)}, u32[]{:S(2)}) %collective-permute-start.8) | collective-permute-done | bytes 16416 | tf_op jit(solution)/shard_map/ppermute | solution.py:113
  35.6 1.5 %collective-permute-start.11 = (f32[2,8,256]{2,1,0:T(8,128)S(1)}, f32[2,8,256]{2,1,0:T(8,128)S(1)}, u32[]{:S(2)}, u32[]{:S(2)}) collective-permute-start(f32[2,8,256]{2,1,0:T(8,128)S(1)} %join_rows.2.pair_ref), channel_id=1, source_target_pairs={{0,6},{1,7},{2,4},{3,5},{4,2},{5,3},{6,0},{7,1},{8,14},{9,15},{10,... | collective-permute-start | bytes 49160 | tf_op jit(solution)/shard_map/ppermute | solution.py:113
  37.1 1.5 %collective-permute-start.9 = (f32[2,8,256]{2,1,0:T(8,128)S(1)}, f32[2,8,256]{2,1,0:T(8,128)S(1)}, u32[]{:S(2)}, u32[]{:S(2)}) collective-permute-start(f32[2,8,256]{2,1,0:T(8,128)S(1)} %join_rows.2.pair_ref), channel_id=1, source_target_pairs={{0,2},{1,5},{2,0},{3,7},{4,6},{5,1},{6,4},{7,3},{8,10},{9,13},{10,... | collective-permute-start | bytes 49160 | tf_op jit(solution)/shard_map/ppermute | solution.py:113
  38.8 1.4 %collective-permute-done.11.refs_2_ = f32[2,8,256]{2,1,0:T(8,128)S(1)} collective-permute-done((f32[2,8,256]{2,1,0:T(8,128)S(1)}, f32[2,8,256]{2,1,0:T(8,128)S(1)}, u32[]{:S(2)}, u32[]{:S(2)}) %collective-permute-start.11) | collective-permute-done | bytes 16416 | tf_op jit(solution)/shard_map/ppermute | solution.py:113
  40.9 0.9 %weighted_sums.3 = f32[136,1024]{1,0:T(8,128)S(1)} custom-call(f32[8,256]{1,0:T(8,128)S(1)} %join_rows.3.lognorm_ref, f32[3,128,256]{2,1,0:T(8,128)S(1)} %get-tuple-element.56.refs_0_, f32[3,128,256]{2,1,0:T(8,128)S(1)} %get-tuple-element.57.refs_1_, f32[1,512,256]{2,1,0:T(8,128)S(1)} %get-tuple-element.52.refs_2_, ...), custom_call_target="tpu_custom_call" | custom-call | flops 536870912 | bytes 4194304 | tf_op jit(solution)/shard_map/weighted_sums/pallas_call | solution.py:227
  42.5 2.4 %weighted_sums.2 = (f32[136,1024]{1,0:T(8,128)S(1)}, f32[136,1024]{1,0:T(8,128)S(1)}, f32[136,1024]{1,0:T(8,128)S(1)}) custom-call(f32[8,256]{1,0:T(8,128)S(1)} %join_rows.3.lognorm_ref, f32[3,384,256]{2,1,0:T(8,128)S(1)} %get-tuple-element.50.refs_0_, f32[3,384,256]{2,1,0:T(8,128)S(1)} %get-tuple-element.51.refs_1_, ...), custom_call_target="tpu_custom_call" | custom-call | flops 1610612736 | bytes 4194304 | tf_op jit(solution)/shard_map/weighted_sums/pallas_call | solution.py:227
  44.9 4.0 %collective-permute-done.12 = f16[136,1024]{1,0:T(8,128)(2,1)S(1)} collective-permute-done((f16[136,1024]{1,0:T(8,128)(2,1)S(1)}, f16[136,1024]{1,0:T(8,128)(2,1)S(1)}, u32[]{:S(2)}, u32[]{:S(2)}) %collective-permute-start.12) | collective-permute-done | bytes 278560 | tf_op jit(solution)/shard_map/ppermute | solution.py:22
  49.9 2.1 %collective-permute-start.14 = (f16[136,1024]{1,0:T(8,128)(2,1)S(1)}, f16[136,1024]{1,0:T(8,128)(2,1)S(1)}, u32[]{:S(2)}, u32[]{:S(2)}) collective-permute-start(f16[136,1024]{1,0:T(8,128)(2,1)S(1)} %convert_element_type.24), channel_id=1, source_target_pairs={{0,16},{8,24},{16,0},{24,8},{1,17},{9,25},{17,1},{25,9},{2,18},{10... | collective-permute-start | bytes 835592 | tf_op jit(solution)/shard_map/ppermute | solution.py:22
  52.5 8.8 %collective-permute-done.13 = f16[136,1024]{1,0:T(8,128)(2,1)S(1)} collective-permute-done((f16[136,1024]{1,0:T(8,128)(2,1)S(1)}, f16[136,1024]{1,0:T(8,128)(2,1)S(1)}, u32[]{:S(2)}, u32[]{:S(2)}) %collective-permute-start.13) | collective-permute-done | bytes 278560 | tf_op jit(solution)/shard_map/ppermute | solution.py:22
  61.4 1.0 %update_centroids.1 = (f32[128,1024]{1,0:T(8,128)}, f32[1,128]{1,0:T(1,128)}) custom-call(f32[136,1024]{1,0:T(8,128)S(1)} %get-tuple-element.54.refs_0_, f32[136,1024]{1,0:T(8,128)S(1)} %convert_element_type.26.refs_1_, f32[136,1024]{1,0:T(8,128)S(1)} %convert_element_type.27.refs_2_, f32[128,1024]{1,0:T(8,128)S(1)} %copy-done), custom_call_target="tpu_custom_call" | custom-call | tf_op jit(solution)/shard_map/update_centroids/pallas_call | solution.py:209
  (34 shorter events, 7.6 us)
Async XLA Ops:
  0.6 15.5 %collective-permute-start = (bf16[256,1024]{1,0:T(8,128)(2,1)}, bf16[256,1024]{1,0:T(8,128)(2,1)S(1)}, u32[]{:S(2)}, u32[]{:S(2)}) collective-permute-start(bf16[256,1024]{1,0:T(8,128)(2,1)} %param.2), channel_id=1, source_target_pairs={{0,2},{1,5},{2,0},{3,7},{4,6},{5,1},{6,4},{7,3},{8,10},{9,13},{10,... | collective-permute-start | bytes 1572872 | tf_op jit(solution)/shard_map/ppermute | solution.py:250
  3.6 12.6 %collective-permute-start.1 = (bf16[256,1024]{1,0:T(8,128)(2,1)}, bf16[256,1024]{1,0:T(8,128)(2,1)S(1)}, u32[]{:S(2)}, u32[]{:S(2)}) collective-permute-start(bf16[256,1024]{1,0:T(8,128)(2,1)} %param.2), channel_id=1, source_target_pairs={{0,4},{1,3},{2,6},{3,1},{4,0},{5,7},{6,2},{7,5},{8,12},{9,11},{10,... | collective-permute-start | bytes 1572872 | tf_op jit(solution)/shard_map/ppermute | solution.py:251
  6.2 14.2 %collective-permute-start.3 = (bf16[128,1024]{1,0:T(8,128)(2,1)S(1)}, bf16[128,1024]{1,0:T(8,128)(2,1)S(1)}, u32[]{:S(2)}, u32[]{:S(2)}) collective-permute-start(bf16[128,1024]{1,0:T(8,128)(2,1)S(1)} %convert_element_type.21), channel_id=1, source_target_pairs={{0,16},{8,24},{16,0},{24,8},{1,17},{9,25},{17,1},{25,9},{2,18},{10... | collective-permute-start | bytes 786440 | tf_op jit(solution)/shard_map/ppermute | solution.py:22
  8.9 11.7 %collective-permute-start.2 = (bf16[128,1024]{1,0:T(8,128)(2,1)S(1)}, bf16[128,1024]{1,0:T(8,128)(2,1)S(1)}, u32[]{:S(2)}, u32[]{:S(2)}) collective-permute-start(bf16[128,1024]{1,0:T(8,128)(2,1)S(1)} %convert_element_type.21), channel_id=1, source_target_pairs={{0,8},{8,0},{16,24},{24,16},{1,9},{9,1},{17,25},{25,17},{2,10},{10... | collective-permute-start | bytes 786440 | tf_op jit(solution)/shard_map/ppermute | solution.py:22
  20.6 3.4 %collective-permute-start.5 = (bf16[768,1024]{1,0:T(8,128)(2,1)S(1)}, bf16[768,1024]{1,0:T(8,128)(2,1)S(1)}, u32[]{:S(2)}, u32[]{:S(2)}) collective-permute-start(bf16[768,1024]{1,0:T(8,128)(2,1)S(1)} %constant_dynamic-update-slice_fusion.refs_1_.refs_4_), channel_id=1, source_target_pairs={{0,1},{1,0},{2,3},{3,2},{4,5},{5,4},{6,7},{7,6},{8,9},{9,8},{10,11... | collective-permute-start | bytes 4718600 | tf_op jit(solution)/shard_map/ppermute | solution.py:22
  20.6 8.7 %collective-permute-start.4 = (bf16[128,1024]{1,0:T(8,128)(2,1)S(1)}, bf16[128,1024]{1,0:T(8,128)(2,1)S(1)}, u32[]{:S(2)}, u32[]{:S(2)}) collective-permute-start(bf16[128,1024]{1,0:T(8,128)(2,1)S(1)} %collective-permute-done.3), channel_id=1, source_target_pairs={{0,8},{8,0},{16,24},{24,16},{1,9},{9,1},{17,25},{25,17},{2,10},{10... | collective-permute-start | bytes 786440 | tf_op jit(solution)/shard_map/ppermute | solution.py:22
  22.0 9.2 %collective-permute-start.6 = (bf16[256,1024]{1,0:T(8,128)(2,1)S(1)}, bf16[256,1024]{1,0:T(8,128)(2,1)S(1)}, u32[]{:S(2)}, u32[]{:S(2)}) collective-permute-start(bf16[256,1024]{1,0:T(8,128)(2,1)S(1)} %collective-permute-done), channel_id=1, source_target_pairs={{0,4},{1,3},{2,6},{3,1},{4,0},{5,7},{6,2},{7,5},{8,12},{9,11},{10,... | collective-permute-start | bytes 1572872 | tf_op jit(solution)/shard_map/ppermute | solution.py:261
  31.2 1.9 %collective-permute-start.7 = (bf16[256,1024]{1,0:T(8,128)(2,1)S(1)}, bf16[256,1024]{1,0:T(8,128)(2,1)S(1)}, u32[]{:S(2)}, u32[]{:S(2)}) collective-permute-start(bf16[256,1024]{1,0:T(8,128)(2,1)S(1)} %collective-permute-done.6.refs_4_.refs_6_), channel_id=1, source_target_pairs={{0,1},{1,0},{2,3},{3,2},{4,5},{5,4},{6,7},{7,6},{8,9},{9,8},{10,11... | collective-permute-start | bytes 1572872 | tf_op jit(solution)/shard_map/ppermute | solution.py:22
  33.8 1.2 %collective-permute-start.8 = (f32[2,8,256]{2,1,0:T(8,128)S(1)}, f32[2,8,256]{2,1,0:T(8,128)S(1)}, u32[]{:S(2)}, u32[]{:S(2)}) collective-permute-start(f32[2,8,256]{2,1,0:T(8,128)S(1)} %get-tuple-element.49.pair_ref), channel_id=1, source_target_pairs={{0,1},{1,0},{2,3},{3,2},{4,5},{5,4},{6,7},{7,6},{8,9},{9,8},{10,11... | collective-permute-start | bytes 49160 | tf_op jit(solution)/shard_map/ppermute | solution.py:113
  35.0 3.8 %collective-permute-start.10 = (f32[2,8,256]{2,1,0:T(8,128)S(1)}, f32[2,8,256]{2,1,0:T(8,128)S(1)}, u32[]{:S(2)}, u32[]{:S(2)}) collective-permute-start(f32[2,8,256]{2,1,0:T(8,128)S(1)} %join_rows.2.pair_ref), channel_id=1, source_target_pairs={{0,4},{1,3},{2,6},{3,1},{4,0},{5,7},{6,2},{7,5},{8,12},{9,11},{10,... | collective-permute-start | bytes 49160 | tf_op jit(solution)/shard_map/ppermute | solution.py:113
  35.6 4.6 %collective-permute-start.11 = (f32[2,8,256]{2,1,0:T(8,128)S(1)}, f32[2,8,256]{2,1,0:T(8,128)S(1)}, u32[]{:S(2)}, u32[]{:S(2)}) collective-permute-start(f32[2,8,256]{2,1,0:T(8,128)S(1)} %join_rows.2.pair_ref), channel_id=1, source_target_pairs={{0,6},{1,7},{2,4},{3,5},{4,2},{5,3},{6,0},{7,1},{8,14},{9,15},{10,... | collective-permute-start | bytes 49160 | tf_op jit(solution)/shard_map/ppermute | solution.py:113
  37.1 3.7 %collective-permute-start.9 = (f32[2,8,256]{2,1,0:T(8,128)S(1)}, f32[2,8,256]{2,1,0:T(8,128)S(1)}, u32[]{:S(2)}, u32[]{:S(2)}) collective-permute-start(f32[2,8,256]{2,1,0:T(8,128)S(1)} %join_rows.2.pair_ref), channel_id=1, source_target_pairs={{0,2},{1,5},{2,0},{3,7},{4,6},{5,1},{6,4},{7,3},{8,10},{9,13},{10,... | collective-permute-start | bytes 49160 | tf_op jit(solution)/shard_map/ppermute | solution.py:113
  41.9 7.1 %collective-permute-start.12 = (f16[136,1024]{1,0:T(8,128)(2,1)S(1)}, f16[136,1024]{1,0:T(8,128)(2,1)S(1)}, u32[]{:S(2)}, u32[]{:S(2)}) collective-permute-start(f16[136,1024]{1,0:T(8,128)(2,1)S(1)} %convert_element_type.22), channel_id=1, source_target_pairs={{0,8},{8,0},{16,24},{24,16},{1,9},{9,1},{17,25},{25,17},{2,10},{10... | collective-permute-start | bytes 835592 | tf_op jit(solution)/shard_map/ppermute | solution.py:22
  49.1 12.3 %copy-start = (f32[128,1024]{1,0:T(8,128)S(1)}, f32[128,1024]{1,0:T(8,128)}, u32[]{:S(2)}) copy-start(f32[128,1024]{1,0:T(8,128)} %refs_3_.1) | copy-start | bytes 1572868
  49.2 12.1 %collective-permute-start.13 = (f16[136,1024]{1,0:T(8,128)(2,1)S(1)}, f16[136,1024]{1,0:T(8,128)(2,1)S(1)}, u32[]{:S(2)}, u32[]{:S(2)}) collective-permute-start(f16[136,1024]{1,0:T(8,128)(2,1)S(1)} %convert_element_type.25), channel_id=1, source_target_pairs={{0,8},{8,0},{16,24},{24,16},{1,9},{9,1},{17,25},{25,17},{2,10},{10... | collective-permute-start | bytes 835592 | tf_op jit(solution)/shard_map/ppermute | solution.py:22
  49.9 11.5 %collective-permute-start.14 = (f16[136,1024]{1,0:T(8,128)(2,1)S(1)}, f16[136,1024]{1,0:T(8,128)(2,1)S(1)}, u32[]{:S(2)}, u32[]{:S(2)}) collective-permute-start(f16[136,1024]{1,0:T(8,128)(2,1)S(1)} %convert_element_type.24), channel_id=1, source_target_pairs={{0,16},{8,24},{16,0},{24,8},{1,17},{9,25},{17,1},{25,9},{2,18},{10... | collective-permute-start | bytes 835592 | tf_op jit(solution)/shard_map/ppermute | solution.py:22

commit v15 on v13

--- a/solution.py
+++ b/solution.py
@@ -265,23 +265,24 @@
         of_three = [(0, j * own_rows) for j in range(3)]
         s_0, pair_0, half = score(most, [], [three], own_rows, of_three, give_half=True, weight=1)
         three_core = swap(give, "cent", n_cent, 1)
-        s_1, pair_1 = score(most, [half], [three_core], own_rows, of_three, weight=.1)
-        diag, pair_0, final = lax.optimization_barrier((diag, pair_0, final))
-        s_2, pair_d = score(most, [half], [diag], own_rows, [(0, 0)], weight=40)
-        give, pair_d = lax.optimization_barrier((diag, pair_d))
+        diag, pair_0 = lax.optimization_barrier((diag, pair_0))
+        s_1, pair_1 = score(most, [half], [diag], own_rows, [(0, 0)], weight=.1)
+        give, pair_1 = lax.optimization_barrier((diag, pair_1))
         diag_core = swap(give, "cent", n_cent, 1)
-        rows = [three, three_core, diag, diag_core]
-        order = [0, 2, 4, 1, 5, 3, 6, 7]
-        picks = [(i, j * own_rows) for i in range(2) for j in range(3)] + [(2, 0), (3, 0)]
-        early = [pair_0, pair_1, pair_d]
-        s_3, pairs, last = score(
-            final, [], rows[:3], own_rows, picks[:7], early, give_half=True, weight=1
+        rows = [three, diag, three_core, diag_core]
+        order = [0, 2, 4, 6, 1, 5, 3, 7]
+        picks = of_three + [(1, 0)] + [(2, at) for _, at in of_three] + [(3, 0)]
+        s_2, pair_2, last = score(
+            final, [], rows[:2], own_rows, picks[:4], [pair_0, pair_1], give_half=True, weight=60
         )
-        s_4, pairs = score(most + final, [half, last], rows[3:], own_rows, [(0, 0)], [pairs], 7)
-        scores = [s_0, s_1, s_2, s_4]
-        places = [(i, j) for i in range(2) for j in range(3)] + [(2, 0), (3, 0)]
-        last_scores = [s_3, s_4]
-        last_places = [(0, j, 0) for j in range(7)] + [(1, 0, end)]
+        three_core, last = lax.optimization_barrier((three_core, last))
+        rows[2], both, halves = three_core, most + final, [half, last]
+        s_3, pair_3 = score(both, halves, [three_core], own_rows, of_three, weight=.1)
+        s_4, pairs = score(both, halves, rows[3:], own_rows, [(0, 0)], [pair_2, pair_3], 7)
+        scores = [s_0, s_1, s_3, s_4]
+        places = [(0, j) for j in range(3)] + [(1, 0)] + [(2, j) for j in range(3)] + [(3, 0)]
+        last_scores = [s_2, s_3, s_4]
+        last_places = [(0, j, 0) for j in range(4)] + [(1, j, end) for j in range(3)] + [(2, 0, end)]
     else:
         rows = [embeddings] + [swap(embeddings, "cent", n_cent, m) for m in range(1, n_cent)]
         order = list(range(n_cent))

time: 63.6 us -> 62.7 us (0.986)
  starting transfers between devices: 21.8 us -> 20.7 us
    ppermute x8, waiting for transfers between devices: 20.8 us -> 16.1 us  [swap(): return lax.ppermute(x, axis, partner(size, mask))]
    ppermute x1, waiting for transfers between devices: 0.01 us -> 3.09 us  [local(): diag = lax.ppermute(from_p, 'cent', by_q)]
    ppermute x1, waiting for transfers between devices: 4.62 us -> 5.69 us  [local(): from_p = lax.ppermute(embeddings, 'cent', by_p)]
    ppermute x4, waiting for transfers between devices: 3.19 us -> 3.96 us  [join(): others = [lax.ppermute(pairs, 'cent', route) for route in routes]]
    ppermute x8, starting transfers between devices: 11.7 us -> 11 us  [swap(): return lax.ppermute(x, axis, partner(size, mask))]
  transfers between devices with their start and end apart: 15 -> 15, of which waited for: 10 -> 11; matrix products, arithmetic and copies ran while one was open for 5% -> 5% of each run, Pallas kernels for 10% -> 10%
where the time goes in v15:
time: 62.7 us; the launch traced here: 62.5 us
  waiting for transfers between devices  28.8 us (46%)
  starting transfers between devices  20.7 us (33%)
  Pallas kernels  9.12 us (15%)
  local copies, waits for them, and re-layouts  1.72 us (3%)
  other arithmetic  1.34 us (2%)
  between operations  0.81 us (1%)
    ppermute x8, waiting for transfers between devices, swap(): return lax.ppermute(x, axis, partner(size, mask))  16.1 us
    ppermute x8, starting transfers between devices, swap(): return lax.ppermute(x, axis, partner(size, mask))  11 us
    ppermute x1, waiting for transfers between devices, local(): from_p = lax.ppermute(embeddings, 'cent', by_p)  5.69 us
    pallas_call x5, Pallas kernels, score(): pl.pallas_call(functools.partial(score_kernel, len(centers), len(halves),...  4.58 us
    ppermute x4, waiting for transfers between devices, join(): others = [lax.ppermute(pairs, 'cent', route) for route in routes]  3.96 us
    ppermute x4, starting transfers between devices, join(): others = [lax.ppermute(pairs, 'cent', route) for route in routes]  3.65 us
    pallas_call x2, Pallas kernels, weighted(): pl.pallas_call(functools.partial(sums_kernel, len(scores), picks, parts),...  3.31 us
    ppermute x1, waiting for transfers between devices, local(): diag = lax.ppermute(from_p, 'cent', by_q)  3.09 us
  transfers between devices with their start and end apart: 15, of which 11 were waited for; matrix products, arithmetic and copies ran while one was open for 5% of the time, Pallas kernels for 10%

profile of v15, /device:TPU:0, one launch (start us, length us, event | category | flops | bytes accessed | tf_op | source)
XLA Modules:
  0.0 62.5 jit_solution(3489054321297470670)
XLA Ops:
  0.6 3.0 %collective-permute-start.3 = (bf16[256,1024]{1,0:T(8,128)(2,1)}, bf16[256,1024]{1,0:T(8,128)(2,1)S(1)}, u32[]{:S(2)}, u32[]{:S(2)}) collective-permute-start(bf16[256,1024]{1,0:T(8,128)(2,1)} %param.2), channel_id=1, source_target_pairs={{0,2},{1,5},{2,0},{3,7},{4,6},{5,1},{6,4},{7,3},{8,10},{9,13},{10,... | collective-permute-start | bytes 1572872 | tf_op jit(solution)/shard_map/ppermute | solution.py:250
  3.6 1.5 %collective-permute-start.4 = (bf16[256,1024]{1,0:T(8,128)(2,1)}, bf16[256,1024]{1,0:T(8,128)(2,1)S(1)}, u32[]{:S(2)}, u32[]{:S(2)}) collective-permute-start(bf16[256,1024]{1,0:T(8,128)(2,1)} %param.2), channel_id=1, source_target_pairs={{0,4},{1,3},{2,6},{3,1},{4,0},{5,7},{6,2},{7,5},{8,12},{9,11},{10,... | collective-permute-start | bytes 1572872 | tf_op jit(solution)/shard_map/ppermute | solution.py:251
  5.2 1.1 %convert_element_type.21 = bf16[128,1024]{1,0:T(8,128)(2,1)S(1)} convert(f32[128,1024]{1,0:T(8,128)} %refs_3_.1) | non-fusion elementwise | flops 131072 | bytes 786432 | tf_op jit(solution)/shard_map/convert_element_type | solution.py:246
  6.2 2.7 %collective-permute-start.1 = (bf16[128,1024]{1,0:T(8,128)(2,1)S(1)}, bf16[128,1024]{1,0:T(8,128)(2,1)S(1)}, u32[]{:S(2)}, u32[]{:S(2)}) collective-permute-start(bf16[128,1024]{1,0:T(8,128)(2,1)S(1)} %convert_element_type.21), channel_id=1, source_target_pairs={{0,16},{8,24},{16,0},{24,8},{1,17},{9,25},{17,1},{25,9},{2,18},{10... | collective-permute-start | bytes 786440 | tf_op jit(solution)/shard_map/ppermute | solution.py:22
  8.9 1.6 %collective-permute-start = (bf16[128,1024]{1,0:T(8,128)(2,1)S(1)}, bf16[128,1024]{1,0:T(8,128)(2,1)S(1)}, u32[]{:S(2)}, u32[]{:S(2)}) collective-permute-start(bf16[128,1024]{1,0:T(8,128)(2,1)S(1)} %convert_element_type.21), channel_id=1, source_target_pairs={{0,8},{8,0},{16,24},{24,16},{1,9},{9,1},{17,25},{25,17},{2,10},{10... | collective-permute-start | bytes 786440 | tf_op jit(solution)/shard_map/ppermute | solution.py:22
  10.5 5.7 %collective-permute-done.3 = bf16[256,1024]{1,0:T(8,128)(2,1)S(1)} collective-permute-done((bf16[256,1024]{1,0:T(8,128)(2,1)}, bf16[256,1024]{1,0:T(8,128)(2,1)S(1)}, u32[]{:S(2)}, u32[]{:S(2)}) %collective-permute-start.3) | collective-permute-done | bytes 524320 | tf_op jit(solution)/shard_map/ppermute | solution.py:250
  16.2 1.5 %collective-permute-start.6 = (bf16[256,1024]{1,0:T(8,128)(2,1)S(1)}, bf16[256,1024]{1,0:T(8,128)(2,1)S(1)}, u32[]{:S(2)}, u32[]{:S(2)}) collective-permute-start(bf16[256,1024]{1,0:T(8,128)(2,1)S(1)} %collective-permute-done.3), channel_id=1, source_target_pairs={{0,4},{1,3},{2,6},{3,1},{4,0},{5,7},{6,2},{7,5},{8,12},{9,11},{10,... | collective-permute-start | bytes 1572872 | tf_op jit(solution)/shard_map/ppermute | solution.py:261
  17.6 1.1 %constant_dynamic-update-slice_fusion.2 = bf16[768,1024]{1,0:T(8,128)(2,1)S(1)} fusion(bf16[256,1024]{1,0:T(8,128)(2,1)} %param.2), kind=kLoop, calls=%fused_computation.3 | loop fusion | bytes 1048576
  18.7 1.7 %collective-permute-done.1 = bf16[128,1024]{1,0:T(8,128)(2,1)S(1)} collective-permute-done((bf16[128,1024]{1,0:T(8,128)(2,1)S(1)}, bf16[128,1024]{1,0:T(8,128)(2,1)S(1)}, u32[]{:S(2)}, u32[]{:S(2)}) %collective-permute-start.1) | collective-permute-done | bytes 262176 | tf_op jit(solution)/shard_map/ppermute | solution.py:22
  21.2 1.0 %score_rows.5 = (f32[3,384,256]{2,1,0:T(8,128)S(1)}, f32[2,3,256]{2,1,0:T(4,128)S(1)}, f32[384,128]{1,0:T(8,128)S(1)}) custom-call(bf16[384,1024]{1,0:T(8,128)(2,1)S(1)} %pad_maximum_fusion.refs_0_, bf16[768,1024]{1,0:T(8,128)(2,1)S(1)} %constant_dynamic-update-slice_fusion.refs_1_.refs_4_.refs_3_), custom_call_target="tpu_custom_call" | custom-call | flops 603979776 | bytes 2359296 | tf_op jit(solution)/shard_map/score_rows/pallas_call | solution.py:82
  22.3 3.1 %collective-permute-done.6.refs_2_.refs_5_.refs_4_ = bf16[256,1024]{1,0:T(8,128)(2,1)S(1)} collective-permute-done((bf16[256,1024]{1,0:T(8,128)(2,1)S(1)}, bf16[256,1024]{1,0:T(8,128)(2,1)S(1)}, u32[]{:S(2)}, u32[]{:S(2)}) %collective-permute-start.6) | collective-permute-done | bytes 524320 | tf_op jit(solution)/shard_map/ppermute | solution.py:261
  25.9 1.6 %collective-permute-done.2.refs_0_.refs_1_ = bf16[128,1024]{1,0:T(8,128)(2,1)S(1)} collective-permute-done((bf16[128,1024]{1,0:T(8,128)(2,1)S(1)}, bf16[128,1024]{1,0:T(8,128)(2,1)S(1)}, u32[]{:S(2)}, u32[]{:S(2)}) %collective-permute-start.2) | collective-permute-done | bytes 262176 | tf_op jit(solution)/shard_map/ppermute | solution.py:22
  28.4 1.5 %score_rows.8 = (f32[3,512,256]{2,1,0:T(8,128)S(1)}, f32[2,3,256]{2,1,0:T(4,128)S(1)}) custom-call(bf16[384,1024]{1,0:T(8,128)(2,1)S(1)} %pad_maximum_fusion.refs_0_, bf16[128,1024]{1,0:T(8,128)(2,1)S(1)} %collective-permute-done.2.refs_0_.refs_1_, f32[384,128]{1,0:T(8,128)S(1)} %get-tuple-element.28.refs_1_.refs_2_, ...), custom_call_target="tpu_custom_call" | custom-call | flops 80530640 | bytes 262144 | tf_op jit(solution)/shard_map/score_rows/pallas_call | solution.py:82
  30.6 1.2 %collective-permute-done.8.refs_0_ = f32[2,8,256]{2,1,0:T(8,128)S(1)} collective-permute-done((f32[2,8,256]{2,1,0:T(8,128)S(1)}, f32[2,8,256]{2,1,0:T(8,128)S(1)}, u32[]{:S(2)}, u32[]{:S(2)}) %collective-permute-start.8) | collective-permute-done | bytes 16416 | tf_op jit(solution)/shard_map/ppermute | solution.py:113
  33.6 1.8 %collective-permute-start.11 = (f32[2,8,256]{2,1,0:T(8,128)S(1)}, f32[2,8,256]{2,1,0:T(8,128)S(1)}, u32[]{:S(2)}, u32[]{:S(2)}) collective-permute-start(f32[2,8,256]{2,1,0:T(8,128)S(1)} %join_rows.2.pair_ref), channel_id=1, source_target_pairs={{0,6},{1,7},{2,4},{3,5},{4,2},{5,3},{6,0},{7,1},{8,14},{9,15},{10,... | collective-permute-start | bytes 49160 | tf_op jit(solution)/shard_map/ppermute | solution.py:113
  36.6 1.6 %collective-permute-done.11.refs_2_ = f32[2,8,256]{2,1,0:T(8,128)S(1)} collective-permute-done((f32[2,8,256]{2,1,0:T(8,128)S(1)}, f32[2,8,256]{2,1,0:T(8,128)S(1)}, u32[]{:S(2)}, u32[]{:S(2)}) %collective-permute-start.11) | collective-permute-done | bytes 16416 | tf_op jit(solution)/shard_map/ppermute | solution.py:113
  39.2 1.7 %collective-permute-start.12 = (f16[136,1024]{1,0:T(8,128)(2,1)S(1)}, f16[136,1024]{1,0:T(8,128)(2,1)S(1)}, u32[]{:S(2)}, u32[]{:S(2)}) collective-permute-start(f16[136,1024]{1,0:T(8,128)(2,1)S(1)} %convert_element_type.22), channel_id=1, source_target_pairs={{0,8},{8,0},{16,24},{24,16},{1,9},{9,1},{17,25},{25,17},{2,10},{10... | collective-permute-start | bytes 835592 | tf_op jit(solution)/shard_map/ppermute | solution.py:22
  40.9 2.4 %weighted_sums.2 = (f32[136,1024]{1,0:T(8,128)S(1)}, f32[136,1024]{1,0:T(8,128)S(1)}, f32[136,1024]{1,0:T(8,128)S(1)}) custom-call(f32[8,256]{1,0:T(8,128)S(1)} %join_rows.3.lognorm_ref, f32[3,384,256]{2,1,0:T(8,128)S(1)} %get-tuple-element.41.refs_0_, f32[1,384,256]{2,1,0:T(8,128)S(1)} %get-tuple-element.42.refs_1_, ...), custom_call_target="tpu_custom_call" | custom-call | flops 1610612736 | bytes 4194304 | tf_op jit(solution)/shard_map/weighted_sums/pallas_call | solution.py:227
  43.3 3.2 %collective-permute-done.12 = f16[136,1024]{1,0:T(8,128)(2,1)S(1)} collective-permute-done((f16[136,1024]{1,0:T(8,128)(2,1)S(1)}, f16[136,1024]{1,0:T(8,128)(2,1)S(1)}, u32[]{:S(2)}, u32[]{:S(2)}) %collective-permute-start.12) | collective-permute-done | bytes 278560 | tf_op jit(solution)/shard_map/ppermute | solution.py:22
  46.8 1.7 %collective-permute-start.13 = (f16[136,1024]{1,0:T(8,128)(2,1)S(1)}, f16[136,1024]{1,0:T(8,128)(2,1)S(1)}, u32[]{:S(2)}, u32[]{:S(2)}) collective-permute-start(f16[136,1024]{1,0:T(8,128)(2,1)S(1)} %convert_element_type.25), channel_id=1, source_target_pairs={{0,8},{8,0},{16,24},{24,16},{1,9},{9,1},{17,25},{25,17},{2,10},{10... | collective-permute-start | bytes 835592 | tf_op jit(solution)/shard_map/ppermute | solution.py:22
  48.4 2.8 %collective-permute-start.14 = (f16[136,1024]{1,0:T(8,128)(2,1)S(1)}, f16[136,1024]{1,0:T(8,128)(2,1)S(1)}, u32[]{:S(2)}, u32[]{:S(2)}) collective-permute-start(f16[136,1024]{1,0:T(8,128)(2,1)S(1)} %convert_element_type.24), channel_id=1, source_target_pairs={{0,16},{8,24},{16,0},{24,8},{1,17},{9,25},{17,1},{25,9},{2,18},{10... | collective-permute-start | bytes 835592 | tf_op jit(solution)/shard_map/ppermute | solution.py:22
  51.8 7.0 %collective-permute-done.13 = f16[136,1024]{1,0:T(8,128)(2,1)S(1)} collective-permute-done((f16[136,1024]{1,0:T(8,128)(2,1)S(1)}, f16[136,1024]{1,0:T(8,128)(2,1)S(1)}, u32[]{:S(2)}, u32[]{:S(2)}) %collective-permute-start.13) | collective-permute-done | bytes 278560 | tf_op jit(solution)/shard_map/ppermute | solution.py:22
  58.9 2.6 %collective-permute-done.14 = f16[136,1024]{1,0:T(8,128)(2,1)S(1)} collective-permute-done((f16[136,1024]{1,0:T(8,128)(2,1)S(1)}, f16[136,1024]{1,0:T(8,128)(2,1)S(1)}, u32[]{:S(2)}, u32[]{:S(2)}) %collective-permute-start.14) | collective-permute-done | bytes 278560 | tf_op jit(solution)/shard_map/ppermute | solution.py:22
  61.5 1.0 %update_centroids.1 = (f32[128,1024]{1,0:T(8,128)}, f32[1,128]{1,0:T(1,128)}) custom-call(f32[136,1024]{1,0:T(8,128)S(1)} %get-tuple-element.45.refs_0_, f32[136,1024]{1,0:T(8,128)S(1)} %convert_element_type.26.refs_1_, f32[136,1024]{1,0:T(8,128)S(1)} %convert_element_type.27.refs_2_, f32[128,1024]{1,0:T(8,128)S(1)} %copy-done), custom_call_target="tpu_custom_call" | custom-call | tf_op jit(solution)/shard_map/update_centroids/pallas_call | solution.py:209
  (31 shorter events, 7.8 us)
Async XLA Ops:
  0.6 15.5 %collective-permute-start.3 = (bf16[256,1024]{1,0:T(8,128)(2,1)}, bf16[256,1024]{1,0:T(8,128)(2,1)S(1)}, u32[]{:S(2)}, u32[]{:S(2)}) collective-permute-start(bf16[256,1024]{1,0:T(8,128)(2,1)} %param.2), channel_id=1, source_target_pairs={{0,2},{1,5},{2,0},{3,7},{4,6},{5,1},{6,4},{7,3},{8,10},{9,13},{10,... | collective-permute-start | bytes 1572872 | tf_op jit(solution)/shard_map/ppermute | solution.py:250
  3.6 17.4 %collective-permute-start.4 = (bf16[256,1024]{1,0:T(8,128)(2,1)}, bf16[256,1024]{1,0:T(8,128)(2,1)S(1)}, u32[]{:S(2)}, u32[]{:S(2)}) collective-permute-start(bf16[256,1024]{1,0:T(8,128)(2,1)} %param.2), channel_id=1, source_target_pairs={{0,4},{1,3},{2,6},{3,1},{4,0},{5,7},{6,2},{7,5},{8,12},{9,11},{10,... | collective-permute-start | bytes 1572872 | tf_op jit(solution)/shard_map/ppermute | solution.py:251
  6.2 14.2 %collective-permute-start.1 = (bf16[128,1024]{1,0:T(8,128)(2,1)S(1)}, bf16[128,1024]{1,0:T(8,128)(2,1)S(1)}, u32[]{:S(2)}, u32[]{:S(2)}) collective-permute-start(bf16[128,1024]{1,0:T(8,128)(2,1)S(1)} %convert_element_type.21), channel_id=1, source_target_pairs={{0,16},{8,24},{16,0},{24,8},{1,17},{9,25},{17,1},{25,9},{2,18},{10... | collective-permute-start | bytes 786440 | tf_op jit(solution)/shard_map/ppermute | solution.py:22
  8.9 12.3 %collective-permute-start = (bf16[128,1024]{1,0:T(8,128)(2,1)S(1)}, bf16[128,1024]{1,0:T(8,128)(2,1)S(1)}, u32[]{:S(2)}, u32[]{:S(2)}) collective-permute-start(bf16[128,1024]{1,0:T(8,128)(2,1)S(1)} %convert_element_type.21), channel_id=1, source_target_pairs={{0,8},{8,0},{16,24},{24,16},{1,9},{9,1},{17,25},{25,17},{2,10},{10... | collective-permute-start | bytes 786440 | tf_op jit(solution)/shard_map/ppermute | solution.py:22
  16.2 9.2 %collective-permute-start.6 = (bf16[256,1024]{1,0:T(8,128)(2,1)S(1)}, bf16[256,1024]{1,0:T(8,128)(2,1)S(1)}, u32[]{:S(2)}, u32[]{:S(2)}) collective-permute-start(bf16[256,1024]{1,0:T(8,128)(2,1)S(1)} %collective-permute-done.3), channel_id=1, source_target_pairs={{0,4},{1,3},{2,6},{3,1},{4,0},{5,7},{6,2},{7,5},{8,12},{9,11},{10,... | collective-permute-start | bytes 1572872 | tf_op jit(solution)/shard_map/ppermute | solution.py:261
  20.4 7.1 %collective-permute-start.2 = (bf16[128,1024]{1,0:T(8,128)(2,1)S(1)}, bf16[128,1024]{1,0:T(8,128)(2,1)S(1)}, u32[]{:S(2)}, u32[]{:S(2)}) collective-permute-start(bf16[128,1024]{1,0:T(8,128)(2,1)S(1)} %collective-permute-done.1), channel_id=1, source_target_pairs={{0,8},{8,0},{16,24},{24,16},{1,9},{9,1},{17,25},{25,17},{2,10},{10... | collective-permute-start | bytes 786440 | tf_op jit(solution)/shard_map/ppermute | solution.py:22
  21.1 7.3 %collective-permute-start.5 = (bf16[768,1024]{1,0:T(8,128)(2,1)S(1)}, bf16[768,1024]{1,0:T(8,128)(2,1)S(1)}, u32[]{:S(2)}, u32[]{:S(2)}) collective-permute-start(bf16[768,1024]{1,0:T(8,128)(2,1)S(1)} %constant_dynamic-update-slice_fusion.refs_1_.refs_4_.refs_3_), channel_id=1, source_target_pairs={{0,1},{1,0},{2,3},{3,2},{4,5},{5,4},{6,7},{7,6},{8,9},{9,8},{10,11... | collective-permute-start | bytes 4718600 | tf_op jit(solution)/shard_map/ppermute | solution.py:22
  25.8 4.0 %collective-permute-start.7 = (bf16[256,1024]{1,0:T(8,128)(2,1)S(1)}, bf16[256,1024]{1,0:T(8,128)(2,1)S(1)}, u32[]{:S(2)}, u32[]{:S(2)}) collective-permute-start(bf16[256,1024]{1,0:T(8,128)(2,1)S(1)} %collective-permute-done.6.refs_2_.refs_5_.refs_4_), channel_id=1, source_target_pairs={{0,1},{1,0},{2,3},{3,2},{4,5},{5,4},{6,7},{7,6},{8,9},{9,8},{10,11... | collective-permute-start | bytes 1572872 | tf_op jit(solution)/shard_map/ppermute | solution.py:22
  30.5 1.2 %collective-permute-start.8 = (f32[2,8,256]{2,1,0:T(8,128)S(1)}, f32[2,8,256]{2,1,0:T(8,128)S(1)}, u32[]{:S(2)}, u32[]{:S(2)}) collective-permute-start(f32[2,8,256]{2,1,0:T(8,128)S(1)} %get-tuple-element.40.pair_ref), channel_id=1, source_target_pairs={{0,1},{1,0},{2,3},{3,2},{4,5},{5,4},{6,7},{7,6},{8,9},{9,8},{10,11... | collective-permute-start | bytes 49160 | tf_op jit(solution)/shard_map/ppermute | solution.py:113
  31.8 3.8 %collective-permute-start.9 = (f32[2,8,256]{2,1,0:T(8,128)S(1)}, f32[2,8,256]{2,1,0:T(8,128)S(1)}, u32[]{:S(2)}, u32[]{:S(2)}) collective-permute-start(f32[2,8,256]{2,1,0:T(8,128)S(1)} %join_rows.2.pair_ref), channel_id=1, source_target_pairs={{0,2},{1,5},{2,0},{3,7},{4,6},{5,1},{6,4},{7,3},{8,10},{9,13},{10,... | collective-permute-start | bytes 49160 | tf_op jit(solution)/shard_map/ppermute | solution.py:113
  32.8 3.7 %collective-permute-start.10 = (f32[2,8,256]{2,1,0:T(8,128)S(1)}, f32[2,8,256]{2,1,0:T(8,128)S(1)}, u32[]{:S(2)}, u32[]{:S(2)}) collective-permute-start(f32[2,8,256]{2,1,0:T(8,128)S(1)} %join_rows.2.pair_ref), channel_id=1, source_target_pairs={{0,4},{1,3},{2,6},{3,1},{4,0},{5,7},{6,2},{7,5},{8,12},{9,11},{10,... | collective-permute-start | bytes 49160 | tf_op jit(solution)/shard_map/ppermute | solution.py:113
  33.6 4.6 %collective-permute-start.11 = (f32[2,8,256]{2,1,0:T(8,128)S(1)}, f32[2,8,256]{2,1,0:T(8,128)S(1)}, u32[]{:S(2)}, u32[]{:S(2)}) collective-permute-start(f32[2,8,256]{2,1,0:T(8,128)S(1)} %join_rows.2.pair_ref), channel_id=1, source_target_pairs={{0,6},{1,7},{2,4},{3,5},{4,2},{5,3},{6,0},{7,1},{8,14},{9,15},{10,... | collective-permute-start | bytes 49160 | tf_op jit(solution)/shard_map/ppermute | solution.py:113
  39.2 7.3 %collective-permute-start.12 = (f16[136,1024]{1,0:T(8,128)(2,1)S(1)}, f16[136,1024]{1,0:T(8,128)(2,1)S(1)}, u32[]{:S(2)}, u32[]{:S(2)}) collective-permute-start(f16[136,1024]{1,0:T(8,128)(2,1)S(1)} %convert_element_type.22), channel_id=1, source_target_pairs={{0,8},{8,0},{16,24},{24,16},{1,9},{9,1},{17,25},{25,17},{2,10},{10... | collective-permute-start | bytes 835592 | tf_op jit(solution)/shard_map/ppermute | solution.py:22
  46.7 14.8 %copy-start = (f32[128,1024]{1,0:T(8,128)S(1)}, f32[128,1024]{1,0:T(8,128)}, u32[]{:S(2)}) copy-start(f32[128,1024]{1,0:T(8,128)} %refs_3_.1) | copy-start | bytes 1572868
  46.8 12.0 %collective-permute-start.13 = (f16[136,1024]{1,0:T(8,128)(2,1)S(1)}, f16[136,1024]{1,0:T(8,128)(2,1)S(1)}, u32[]{:S(2)}, u32[]{:S(2)}) collective-permute-start(f16[136,1024]{1,0:T(8,128)(2,1)S(1)} %convert_element_type.25), channel_id=1, source_target_pairs={{0,8},{8,0},{16,24},{24,16},{1,9},{9,1},{17,25},{25,17},{2,10},{10... | collective-permute-start | bytes 835592 | tf_op jit(solution)/shard_map/ppermute | solution.py:22
  48.4 13.0 %collective-permute-start.14 = (f16[136,1024]{1,0:T(8,128)(2,1)S(1)}, f16[136,1024]{1,0:T(8,128)(2,1)S(1)}, u32[]{:S(2)}, u32[]{:S(2)}) collective-permute-start(f16[136,1024]{1,0:T(8,128)(2,1)S(1)} %convert_element_type.24), channel_id=1, source_target_pairs={{0,16},{8,24},{16,0},{24,8},{1,17},{9,25},{17,1},{25,9},{2,18},{10... | collective-permute-start | bytes 835592 | tf_op jit(solution)/shard_map/ppermute | solution.py:22

commit v16 on v15

--- a/solution.py
+++ b/solution.py
@@ -171,41 +171,51 @@
     return values[:size] * jnp.exp2(power - 14.0), tally
 
 
-def relay_kernel(unit, own_ref, got_ref, out_ref):
-    size = own_ref.shape[0] - SIDE
-    more, count = unpack(got_ref[...], unit)
-    total, wide = pack(own_ref[0:size] + more, own_ref[size : size + 1] + count, unit * 0.5)
+def add_kernel(unit, packed, at, own_ref, got_ref, out_ref):
+    size, depth = out_ref.shape[0] - SIDE, out_ref.shape[1]
+    more, tally = unpack(got_ref[...], unit)
+    total = own_ref[0:size, at : at + depth] + more
+    tally = own_ref[size : size + 1, at : at + depth] + tally
+    if packed:
+        total, wide = pack(total, tally, packed)
+    else:
+        wide = jnp.concatenate([tally, jnp.zeros((SIDE - 1, depth), jnp.float32)])
     out_ref[0:size] = total
     out_ref[size : size + SIDE] = wide
 
 
-def relay(own, got, unit):
+def add_part(own, got, at, unit, packed, weight=0):
+    got = got.astype(jnp.float32)
     return pl.pallas_call(
-        functools.partial(relay_kernel, unit),
-        out_shape=jax.ShapeDtypeStruct(own.shape, jnp.float32),
+        functools.partial(add_kernel, unit, packed, at),
+        out_shape=jax.ShapeDtypeStruct(got.shape, jnp.float32),
         in_specs=[VMEM] * 2,
         out_specs=VMEM,
         compiler_params=PARAMS,
-        name="relay_sums",
+        cost_estimate=pl.CostEstimate(
+            flops=got.size * (1 + weight), bytes_accessed=0, transcendentals=0
+        ),
+        name="add_sums",
     )(own, got)
 
 
 def final_kernel(units, *refs):
-    own_ref, got_refs, codebook_ref, new_ref, tally_ref = refs[0], refs[1:-3], *refs[-3:]
-    size, depth = codebook_ref.shape
-    total, tally = own_ref[0:size], own_ref[size : size + 1]
+    part_refs, got_refs = refs[: -3 - len(units)], refs[-3 - len(units) : -3]
+    codebook_ref, new_ref, tally_ref = refs[-3:]
+    size = codebook_ref.shape[0]
+    total = jnp.concatenate([ref[0:size] for ref in part_refs], axis=1)
+    tally = part_refs[0][size : size + 1, 0:size]
     for ref, unit in zip(got_refs, units):
         more, count = unpack(ref[...], unit)
-        total, tally = total + more, tally + count
-    tally = tally[:, :size]
+        total, tally = total + more, tally + count[:, 0:size]
     tally_ref[...] = tally
     weight = 1.0 / (jnp.transpose(jnp.broadcast_to(tally, (size, size)))[:, 0:1] + PRIOR)
     new_ref[...] = (total + PRIOR * codebook_ref[...]) * weight
 
 
-def finish(codebook, own, got):
+def finish(codebook, parts, got):
     size = codebook.shape[0]
-    arrays = [own] + [message.astype(jnp.float32) for message, _ in got] + [codebook]
+    arrays = [*parts, *[message.astype(jnp.float32) for message, _ in got], codebook]
     new, tally = pl.pallas_call(
         functools.partial(final_kernel, [unit for _, unit in got]),
         out_shape=(
@@ -308,23 +318,27 @@
         return [(i, j, k * size) for i, j in places], size, unit
 
     (first,) = weighted([(last_places, size, unit)], lognorm, last_scores, rows, picks)
-    first = first.astype(jnp.float16)
     if n_dp == 4:
-        first = swap(first, "dp", n_dp, 1)
+        cut = first.shape[1] // 2
+        first = [swap(first[:, i : i + cut].astype(jnp.float16), "dp", n_dp, 1) for i in (0, cut)]
         parts = [part(2, 0), part(1, unit), part(0, 0)]
-        far_out, near_out, own = weighted(parts, lognorm, scores, rows, picks)
-        far_out = relay(far_out, first.astype(jnp.float32), unit).astype(jnp.float16)
-        far_out, near_out = lax.optimization_barrier((far_out, near_out))
-        far_out = swap(far_out, "dp", n_dp, 2)
-        near_out = swap(near_out.astype(jnp.float16), "dp", n_dp, 1)
-        got = [(near_out, unit), (far_out, unit * 0.5)]
+        far_sum, near_sum, own = weighted(parts, lognorm, scores, rows, picks)
+        far = []
+        for i, got in enumerate(first):
+            message = add_part(far_sum, got, i * cut, unit, unit * 0.5)
+            far.append(swap(message.astype(jnp.float16), "dp", n_dp, 2))
+        near = swap(near_sum.astype(jnp.float16), "dp", n_dp, 1)
+        parts = [add_part(own, far[0], 0, unit * 0.5, 0, 200000), None]
+        far[1], parts[0] = lax.optimization_barrier((far[1], parts[0]))
+        parts[1] = add_part(own, far[1], cut, unit * 0.5, 0)
+        got = [(near, unit)]
     else:
         parts = [part(k, unit if k else 0) for k in range(n_dp - 1)]
-        out = weighted(parts, lognorm, scores, rows, picks)
-        own = out[0]
-        sent = [o.astype(jnp.float16) for o in out[1:]] + [first]
-        got = [(swap(m, "dp", n_dp, k + 1), unit) for k, m in enumerate(sent)]
-    new_codebook, tally = finish(codebook, own, got)
+        own, *others = weighted(parts, lognorm, scores, rows, picks)
+        parts = [own]
+        others = [other.astype(jnp.float16) for other in others + [first]]
+        got = [(swap(other, "dp", n_dp, k + 1), unit) for k, other in enumerate(others)]
+    new_codebook, tally = finish(codebook, parts, got)
     return new_codebook, tally, lognorm[0]
 
 

time: 62.7 us -> 60.1 us (0.959); the launches traced: 62.5 us -> 59.1 us
  waiting for transfers between devices: 28.8 us -> 22.7 us
  starting transfers between devices: 20.7 us -> 23.2 us
    ppermute x8 -> x10, waiting for transfers between devices: 16.1 us -> 10.1 us  [swap(): return lax.ppermute(x, axis, partner(size, mask))]
    ppermute x8 -> x10, starting transfers between devices: 11 us -> 13.6 us  [swap(): return lax.ppermute(x, axis, partner(size, mask))]
  transfers between devices with their start and end apart: 15 -> 17, of which waited for: 11 -> 12; matrix products, arithmetic and copies ran while one was open for 5% -> 5% of each run, Pallas kernels for 10% -> 11%
where the time goes in v16:
time: 60.1 us; the launch traced here: 59.1 us
  starting transfers between devices  23.2 us (39%)
  waiting for transfers between devices  22.7 us (38%)
  Pallas kernels  9.2 us (15%)
  local copies, waits for them, and re-layouts  1.77 us (3%)
  other arithmetic  1.36 us (2%)
  between operations  0.88 us (1%)
    ppermute x10, starting transfers between devices, swap(): return lax.ppermute(x, axis, partner(size, mask))  13.6 us
    ppermute x10, waiting for transfers between devices, swap(): return lax.ppermute(x, axis, partner(size, mask))  10.1 us
    ppermute x1, waiting for transfers between devices, local(): from_p = lax.ppermute(embeddings, 'cent', by_p)  5.69 us
    pallas_call x5, Pallas kernels, score(): pl.pallas_call(functools.partial(score_kernel, len(centers), len(halves),...  4.58 us
    ppermute x4, waiting for transfers between devices, join(): others = [lax.ppermute(pairs, 'cent', route) for route in routes]  3.84 us
    ppermute x4, starting transfers between devices, join(): others = [lax.ppermute(pairs, 'cent', route) for route in routes]  3.62 us
    pallas_call x2, Pallas kernels, weighted(): pl.pallas_call(functools.partial(sums_kernel, len(scores), picks, parts),...  3.3 us
    ppermute x1, waiting for transfers between devices, local(): diag = lax.ppermute(from_p, 'cent', by_q)  3.09 us
  transfers between devices with their start and end apart: 17, of which 12 were waited for; matrix products, arithmetic and copies ran while one was open for 5% of the time, Pallas kernels for 11%

profile of v16, /device:TPU:0, one launch (start us, length us, event | category | flops | bytes accessed | tf_op | source)
XLA Modules:
  0.0 59.1 jit_solution(557252439801586623)
XLA Ops:
  0.6 3.0 %collective-permute-start.3 = (bf16[256,1024]{1,0:T(8,128)(2,1)}, bf16[256,1024]{1,0:T(8,128)(2,1)S(1)}, u32[]{:S(2)}, u32[]{:S(2)}) collective-permute-start(bf16[256,1024]{1,0:T(8,128)(2,1)} %param.2), channel_id=1, source_target_pairs={{0,2},{1,5},{2,0},{3,7},{4,6},{5,1},{6,4},{7,3},{8,10},{9,13},{10,... | collective-permute-start | bytes 1572872 | tf_op jit(solution)/shard_map/ppermute | solution.py:260
  3.6 1.5 %collective-permute-start.4 = (bf16[256,1024]{1,0:T(8,128)(2,1)}, bf16[256,1024]{1,0:T(8,128)(2,1)S(1)}, u32[]{:S(2)}, u32[]{:S(2)}) collective-permute-start(bf16[256,1024]{1,0:T(8,128)(2,1)} %param.2), channel_id=1, source_target_pairs={{0,4},{1,3},{2,6},{3,1},{4,0},{5,7},{6,2},{7,5},{8,12},{9,11},{10,... | collective-permute-start | bytes 1572872 | tf_op jit(solution)/shard_map/ppermute | solution.py:261
  5.2 1.1 %convert_element_type.29 = bf16[128,1024]{1,0:T(8,128)(2,1)S(1)} convert(f32[128,1024]{1,0:T(8,128)} %refs_3_.1) | non-fusion elementwise | flops 131072 | bytes 786432 | tf_op jit(solution)/shard_map/convert_element_type | solution.py:256
  6.2 2.7 %collective-permute-start.1 = (bf16[128,1024]{1,0:T(8,128)(2,1)S(1)}, bf16[128,1024]{1,0:T(8,128)(2,1)S(1)}, u32[]{:S(2)}, u32[]{:S(2)}) collective-permute-start(bf16[128,1024]{1,0:T(8,128)(2,1)S(1)} %convert_element_type.29), channel_id=1, source_target_pairs={{0,16},{8,24},{16,0},{24,8},{1,17},{9,25},{17,1},{25,9},{2,18},{10... | collective-permute-start | bytes 786440 | tf_op jit(solution)/shard_map/ppermute | solution.py:22
  8.9 1.6 %collective-permute-start = (bf16[128,1024]{1,0:T(8,128)(2,1)S(1)}, bf16[128,1024]{1,0:T(8,128)(2,1)S(1)}, u32[]{:S(2)}, u32[]{:S(2)}) collective-permute-start(bf16[128,1024]{1,0:T(8,128)(2,1)S(1)} %convert_element_type.29), channel_id=1, source_target_pairs={{0,8},{8,0},{16,24},{24,16},{1,9},{9,1},{17,25},{25,17},{2,10},{10... | collective-permute-start | bytes 786440 | tf_op jit(solution)/shard_map/ppermute | solution.py:22
  10.5 5.7 %collective-permute-done.3 = bf16[256,1024]{1,0:T(8,128)(2,1)S(1)} collective-permute-done((bf16[256,1024]{1,0:T(8,128)(2,1)}, bf16[256,1024]{1,0:T(8,128)(2,1)S(1)}, u32[]{:S(2)}, u32[]{:S(2)}) %collective-permute-start.3) | collective-permute-done | bytes 524320 | tf_op jit(solution)/shard_map/ppermute | solution.py:260
  16.2 1.5 %collective-permute-start.6 = (bf16[256,1024]{1,0:T(8,128)(2,1)S(1)}, bf16[256,1024]{1,0:T(8,128)(2,1)S(1)}, u32[]{:S(2)}, u32[]{:S(2)}) collective-permute-start(bf16[256,1024]{1,0:T(8,128)(2,1)S(1)} %collective-permute-done.3), channel_id=1, source_target_pairs={{0,4},{1,3},{2,6},{3,1},{4,0},{5,7},{6,2},{7,5},{8,12},{9,11},{10,... | collective-permute-start | bytes 1572872 | tf_op jit(solution)/shard_map/ppermute | solution.py:271
  17.6 1.1 %constant_dynamic-update-slice_fusion.2 = bf16[768,1024]{1,0:T(8,128)(2,1)S(1)} fusion(bf16[256,1024]{1,0:T(8,128)(2,1)} %param.2), kind=kLoop, calls=%fused_computation.3 | loop fusion | bytes 1048576
  18.7 1.7 %collective-permute-done.1 = bf16[128,1024]{1,0:T(8,128)(2,1)S(1)} collective-permute-done((bf16[128,1024]{1,0:T(8,128)(2,1)S(1)}, bf16[128,1024]{1,0:T(8,128)(2,1)S(1)}, u32[]{:S(2)}, u32[]{:S(2)}) %collective-permute-start.1) | collective-permute-done | bytes 262176 | tf_op jit(solution)/shard_map/ppermute | solution.py:22
  21.2 1.0 %score_rows.5 = (f32[3,384,256]{2,1,0:T(8,128)S(1)}, f32[2,3,256]{2,1,0:T(4,128)S(1)}, f32[384,128]{1,0:T(8,128)S(1)}) custom-call(bf16[384,1024]{1,0:T(8,128)(2,1)S(1)} %pad_maximum_fusion.refs_0_, bf16[768,1024]{1,0:T(8,128)(2,1)S(1)} %constant_dynamic-update-slice_fusion.refs_1_.refs_4_.refs_3_), custom_call_target="tpu_custom_call" | custom-call | flops 603979776 | bytes 2359296 | tf_op jit(solution)/shard_map/score_rows/pallas_call | solution.py:82
  22.3 3.1 %collective-permute-done.6.refs_2_.refs_5_.refs_4_ = bf16[256,1024]{1,0:T(8,128)(2,1)S(1)} collective-permute-done((bf16[256,1024]{1,0:T(8,128)(2,1)S(1)}, bf16[256,1024]{1,0:T(8,128)(2,1)S(1)}, u32[]{:S(2)}, u32[]{:S(2)}) %collective-permute-start.6) | collective-permute-done | bytes 524320 | tf_op jit(solution)/shard_map/ppermute | solution.py:271
  25.9 1.6 %collective-permute-done.2.refs_0_.refs_1_ = bf16[128,1024]{1,0:T(8,128)(2,1)S(1)} collective-permute-done((bf16[128,1024]{1,0:T(8,128)(2,1)S(1)}, bf16[128,1024]{1,0:T(8,128)(2,1)S(1)}, u32[]{:S(2)}, u32[]{:S(2)}) %collective-permute-start.2) | collective-permute-done | bytes 262176 | tf_op jit(solution)/shard_map/ppermute | solution.py:22
  28.4 1.5 %score_rows.8 = (f32[3,512,256]{2,1,0:T(8,128)S(1)}, f32[2,3,256]{2,1,0:T(4,128)S(1)}) custom-call(bf16[384,1024]{1,0:T(8,128)(2,1)S(1)} %pad_maximum_fusion.refs_0_, bf16[128,1024]{1,0:T(8,128)(2,1)S(1)} %collective-permute-done.2.refs_0_.refs_1_, f32[384,128]{1,0:T(8,128)S(1)} %get-tuple-element.28.refs_1_.refs_2_, ...), custom_call_target="tpu_custom_call" | custom-call | flops 80530640 | bytes 262144 | tf_op jit(solution)/shard_map/score_rows/pallas_call | solution.py:82
  30.6 1.2 %collective-permute-done.8.refs_0_ = f32[2,8,256]{2,1,0:T(8,128)S(1)} collective-permute-done((f32[2,8,256]{2,1,0:T(8,128)S(1)}, f32[2,8,256]{2,1,0:T(8,128)S(1)}, u32[]{:S(2)}, u32[]{:S(2)}) %collective-permute-start.8) | collective-permute-done | bytes 16416 | tf_op jit(solution)/shard_map/ppermute | solution.py:113
  32.4 1.9 %collective-permute-start.11 = (f32[2,8,256]{2,1,0:T(8,128)S(1)}, f32[2,8,256]{2,1,0:T(8,128)S(1)}, u32[]{:S(2)}, u32[]{:S(2)}) collective-permute-start(f32[2,8,256]{2,1,0:T(8,128)S(1)} %join_rows.2.pair_ref), channel_id=1, source_target_pairs={{0,6},{1,7},{2,4},{3,5},{4,2},{5,3},{6,0},{7,1},{8,14},{9,15},{10,... | collective-permute-start | bytes 49160 | tf_op jit(solution)/shard_map/ppermute | solution.py:113
  34.3 1.1 %collective-permute-start.9 = (f32[2,8,256]{2,1,0:T(8,128)S(1)}, f32[2,8,256]{2,1,0:T(8,128)S(1)}, u32[]{:S(2)}, u32[]{:S(2)}) collective-permute-start(f32[2,8,256]{2,1,0:T(8,128)S(1)} %join_rows.2.pair_ref), channel_id=1, source_target_pairs={{0,2},{1,5},{2,0},{3,7},{4,6},{5,1},{6,4},{7,3},{8,10},{9,13},{10,... | collective-permute-start | bytes 49160 | tf_op jit(solution)/shard_map/ppermute | solution.py:113
  35.6 1.4 %collective-permute-done.11.refs_2_ = f32[2,8,256]{2,1,0:T(8,128)S(1)} collective-permute-done((f32[2,8,256]{2,1,0:T(8,128)S(1)}, f32[2,8,256]{2,1,0:T(8,128)S(1)}, u32[]{:S(2)}, u32[]{:S(2)}) %collective-permute-start.11) | collective-permute-done | bytes 16416 | tf_op jit(solution)/shard_map/ppermute | solution.py:113
  39.1 1.6 %collective-permute-start.14 = (f16[136,512]{1,0:T(8,128)(2,1)S(1)}, f16[136,512]{1,0:T(8,128)(2,1)S(1)}, u32[]{:S(2)}, u32[]{:S(2)}) collective-permute-start(f16[136,512]{1,0:T(8,128)(2,1)S(1)} %get-tuple-element.53), channel_id=1, source_target_pairs={{0,8},{8,0},{16,24},{24,16},{1,9},{9,1},{17,25},{25,17},{2,10},{10... | collective-permute-start | bytes 417800 | tf_op jit(solution)/shard_map/ppermute | solution.py:22
  41.2 2.4 %weighted_sums.2 = (f32[136,1024]{1,0:T(8,128)S(1)}, f32[136,1024]{1,0:T(8,128)S(1)}, f32[136,1024]{1,0:T(8,128)S(1)}) custom-call(f32[8,256]{1,0:T(8,128)S(1)} %join_rows.3.lognorm_ref, f32[3,384,256]{2,1,0:T(8,128)S(1)} %get-tuple-element.41.refs_0_, f32[1,384,256]{2,1,0:T(8,128)S(1)} %get-tuple-element.42.refs_1_, ...), custom_call_target="tpu_custom_call" | custom-call | flops 1610612736 | bytes 4194304 | tf_op jit(solution)/shard_map/weighted_sums/pallas_call | solution.py:237
  44.8 3.3 %collective-permute-start.15 = (f16[136,512]{1,0:T(8,128)(2,1)S(1)}, f16[136,512]{1,0:T(8,128)(2,1)S(1)}, u32[]{:S(2)}, u32[]{:S(2)}) collective-permute-start(f16[136,512]{1,0:T(8,128)(2,1)S(1)} %convert_element_type.33), channel_id=1, source_target_pairs={{0,16},{8,24},{16,0},{24,8},{1,17},{9,25},{17,1},{25,9},{2,18},{10... | collective-permute-start | bytes 417800 | tf_op jit(solution)/shard_map/ppermute | solution.py:22
  48.2 1.5 %collective-permute-start.16 = (f16[136,1024]{1,0:T(8,128)(2,1)S(1)}, f16[136,1024]{1,0:T(8,128)(2,1)S(1)}, u32[]{:S(2)}, u32[]{:S(2)}) collective-permute-start(f16[136,1024]{1,0:T(8,128)(2,1)S(1)} %convert_element_type.36), channel_id=1, source_target_pairs={{0,8},{8,0},{16,24},{24,16},{1,9},{9,1},{17,25},{25,17},{2,10},{10... | collective-permute-start | bytes 835592 | tf_op jit(solution)/shard_map/ppermute | solution.py:22
  49.9 1.7 %collective-permute-start.13 = (f16[136,512]{1,0:T(8,128)(2,1)S(1)}, f16[136,512]{1,0:T(8,128)(2,1)S(1)}, u32[]{:S(2)}, u32[]{:S(2)}) collective-permute-start(f16[136,512]{1,0:T(8,128)(2,1)S(1)} %convert_element_type.31), channel_id=1, source_target_pairs={{0,16},{8,24},{16,0},{24,8},{1,17},{9,25},{17,1},{25,9},{2,18},{10... | collective-permute-start | bytes 417800 | tf_op jit(solution)/shard_map/ppermute | solution.py:22
  51.6 2.7 %collective-permute-done.15 = f16[136,512]{1,0:T(8,128)(2,1)S(1)} collective-permute-done((f16[136,512]{1,0:T(8,128)(2,1)S(1)}, f16[136,512]{1,0:T(8,128)(2,1)S(1)}, u32[]{:S(2)}, u32[]{:S(2)}) %collective-permute-start.15) | collective-permute-done | bytes 139296 | tf_op jit(solution)/shard_map/ppermute | solution.py:22
  54.3 2.9 %collective-permute-done.13 = f16[136,512]{1,0:T(8,128)(2,1)S(1)} collective-permute-done((f16[136,512]{1,0:T(8,128)(2,1)S(1)}, f16[136,512]{1,0:T(8,128)(2,1)S(1)}, u32[]{:S(2)}, u32[]{:S(2)}) %collective-permute-start.13) | collective-permute-done | bytes 139296 | tf_op jit(solution)/shard_map/ppermute | solution.py:22
  (42 shorter events, 9.6 us)
Async XLA Ops:
  0.6 15.5 %collective-permute-start.3 = (bf16[256,1024]{1,0:T(8,128)(2,1)}, bf16[256,1024]{1,0:T(8,128)(2,1)S(1)}, u32[]{:S(2)}, u32[]{:S(2)}) collective-permute-start(bf16[256,1024]{1,0:T(8,128)(2,1)} %param.2), channel_id=1, source_target_pairs={{0,2},{1,5},{2,0},{3,7},{4,6},{5,1},{6,4},{7,3},{8,10},{9,13},{10,... | collective-permute-start | bytes 1572872 | tf_op jit(solution)/shard_map/ppermute | solution.py:260
  3.6 17.4 %collective-permute-start.4 = (bf16[256,1024]{1,0:T(8,128)(2,1)}, bf16[256,1024]{1,0:T(8,128)(2,1)S(1)}, u32[]{:S(2)}, u32[]{:S(2)}) collective-permute-start(bf16[256,1024]{1,0:T(8,128)(2,1)} %param.2), channel_id=1, source_target_pairs={{0,4},{1,3},{2,6},{3,1},{4,0},{5,7},{6,2},{7,5},{8,12},{9,11},{10,... | collective-permute-start | bytes 1572872 | tf_op jit(solution)/shard_map/ppermute | solution.py:261
  6.2 14.2 %collective-permute-start.1 = (bf16[128,1024]{1,0:T(8,128)(2,1)S(1)}, bf16[128,1024]{1,0:T(8,128)(2,1)S(1)}, u32[]{:S(2)}, u32[]{:S(2)}) collective-permute-start(bf16[128,1024]{1,0:T(8,128)(2,1)S(1)} %convert_element_type.29), channel_id=1, source_target_pairs={{0,16},{8,24},{16,0},{24,8},{1,17},{9,25},{17,1},{25,9},{2,18},{10... | collective-permute-start | bytes 786440 | tf_op jit(solution)/shard_map/ppermute | solution.py:22
  8.9 12.3 %collective-permute-start = (bf16[128,1024]{1,0:T(8,128)(2,1)S(1)}, bf16[128,1024]{1,0:T(8,128)(2,1)S(1)}, u32[]{:S(2)}, u32[]{:S(2)}) collective-permute-start(bf16[128,1024]{1,0:T(8,128)(2,1)S(1)} %convert_element_type.29), channel_id=1, source_target_pairs={{0,8},{8,0},{16,24},{24,16},{1,9},{9,1},{17,25},{25,17},{2,10},{10... | collective-permute-start | bytes 786440 | tf_op jit(solution)/shard_map/ppermute | solution.py:22
  16.2 9.2 %collective-permute-start.6 = (bf16[256,1024]{1,0:T(8,128)(2,1)S(1)}, bf16[256,1024]{1,0:T(8,128)(2,1)S(1)}, u32[]{:S(2)}, u32[]{:S(2)}) collective-permute-start(bf16[256,1024]{1,0:T(8,128)(2,1)S(1)} %collective-permute-done.3), channel_id=1, source_target_pairs={{0,4},{1,3},{2,6},{3,1},{4,0},{5,7},{6,2},{7,5},{8,12},{9,11},{10,... | collective-permute-start | bytes 1572872 | tf_op jit(solution)/shard_map/ppermute | solution.py:271
  20.4 7.1 %collective-permute-start.2 = (bf16[128,1024]{1,0:T(8,128)(2,1)S(1)}, bf16[128,1024]{1,0:T(8,128)(2,1)S(1)}, u32[]{:S(2)}, u32[]{:S(2)}) collective-permute-start(bf16[128,1024]{1,0:T(8,128)(2,1)S(1)} %collective-permute-done.1), channel_id=1, source_target_pairs={{0,8},{8,0},{16,24},{24,16},{1,9},{9,1},{17,25},{25,17},{2,10},{10... | collective-permute-start | bytes 786440 | tf_op jit(solution)/shard_map/ppermute | solution.py:22
  21.1 7.3 %collective-permute-start.5 = (bf16[768,1024]{1,0:T(8,128)(2,1)S(1)}, bf16[768,1024]{1,0:T(8,128)(2,1)S(1)}, u32[]{:S(2)}, u32[]{:S(2)}) collective-permute-start(bf16[768,1024]{1,0:T(8,128)(2,1)S(1)} %constant_dynamic-update-slice_fusion.refs_1_.refs_4_.refs_3_), channel_id=1, source_target_pairs={{0,1},{1,0},{2,3},{3,2},{4,5},{5,4},{6,7},{7,6},{8,9},{9,8},{10,11... | collective-permute-start | bytes 4718600 | tf_op jit(solution)/shard_map/ppermute | solution.py:22
  25.8 4.0 %collective-permute-start.7 = (bf16[256,1024]{1,0:T(8,128)(2,1)S(1)}, bf16[256,1024]{1,0:T(8,128)(2,1)S(1)}, u32[]{:S(2)}, u32[]{:S(2)}) collective-permute-start(bf16[256,1024]{1,0:T(8,128)(2,1)S(1)} %collective-permute-done.6.refs_2_.refs_5_.refs_4_), channel_id=1, source_target_pairs={{0,1},{1,0},{2,3},{3,2},{4,5},{5,4},{6,7},{7,6},{8,9},{9,8},{10,11... | collective-permute-start | bytes 1572872 | tf_op jit(solution)/shard_map/ppermute | solution.py:22
  30.5 1.2 %collective-permute-start.8 = (f32[2,8,256]{2,1,0:T(8,128)S(1)}, f32[2,8,256]{2,1,0:T(8,128)S(1)}, u32[]{:S(2)}, u32[]{:S(2)}) collective-permute-start(f32[2,8,256]{2,1,0:T(8,128)S(1)} %get-tuple-element.40.pair_ref), channel_id=1, source_target_pairs={{0,1},{1,0},{2,3},{3,2},{4,5},{5,4},{6,7},{7,6},{8,9},{9,8},{10,11... | collective-permute-start | bytes 49160 | tf_op jit(solution)/shard_map/ppermute | solution.py:113
  31.8 3.8 %collective-permute-start.10 = (f32[2,8,256]{2,1,0:T(8,128)S(1)}, f32[2,8,256]{2,1,0:T(8,128)S(1)}, u32[]{:S(2)}, u32[]{:S(2)}) collective-permute-start(f32[2,8,256]{2,1,0:T(8,128)S(1)} %join_rows.2.pair_ref), channel_id=1, source_target_pairs={{0,4},{1,3},{2,6},{3,1},{4,0},{5,7},{6,2},{7,5},{8,12},{9,11},{10,... | collective-permute-start | bytes 49160 | tf_op jit(solution)/shard_map/ppermute | solution.py:113
  32.4 4.6 %collective-permute-start.11 = (f32[2,8,256]{2,1,0:T(8,128)S(1)}, f32[2,8,256]{2,1,0:T(8,128)S(1)}, u32[]{:S(2)}, u32[]{:S(2)}) collective-permute-start(f32[2,8,256]{2,1,0:T(8,128)S(1)} %join_rows.2.pair_ref), channel_id=1, source_target_pairs={{0,6},{1,7},{2,4},{3,5},{4,2},{5,3},{6,0},{7,1},{8,14},{9,15},{10,... | collective-permute-start | bytes 49160 | tf_op jit(solution)/shard_map/ppermute | solution.py:113
  34.3 3.7 %collective-permute-start.9 = (f32[2,8,256]{2,1,0:T(8,128)S(1)}, f32[2,8,256]{2,1,0:T(8,128)S(1)}, u32[]{:S(2)}, u32[]{:S(2)}) collective-permute-start(f32[2,8,256]{2,1,0:T(8,128)S(1)} %join_rows.2.pair_ref), channel_id=1, source_target_pairs={{0,2},{1,5},{2,0},{3,7},{4,6},{5,1},{6,4},{7,3},{8,10},{9,13},{10,... | collective-permute-start | bytes 49160 | tf_op jit(solution)/shard_map/ppermute | solution.py:113
  39.1 5.5 %collective-permute-start.14 = (f16[136,512]{1,0:T(8,128)(2,1)S(1)}, f16[136,512]{1,0:T(8,128)(2,1)S(1)}, u32[]{:S(2)}, u32[]{:S(2)}) collective-permute-start(f16[136,512]{1,0:T(8,128)(2,1)S(1)} %get-tuple-element.53), channel_id=1, source_target_pairs={{0,8},{8,0},{16,24},{24,16},{1,9},{9,1},{17,25},{25,17},{2,10},{10... | collective-permute-start | bytes 417800 | tf_op jit(solution)/shard_map/ppermute | solution.py:22
  40.8 7.4 %collective-permute-start.12 = (f16[136,512]{1,0:T(8,128)(2,1)S(1)}, f16[136,512]{1,0:T(8,128)(2,1)S(1)}, u32[]{:S(2)}, u32[]{:S(2)}) collective-permute-start(f16[136,512]{1,0:T(8,128)(2,1)S(1)} %get-tuple-element.54), channel_id=1, source_target_pairs={{0,8},{8,0},{16,24},{24,16},{1,9},{9,1},{17,25},{25,17},{2,10},{10... | collective-permute-start | bytes 417800 | tf_op jit(solution)/shard_map/ppermute | solution.py:22
  44.8 9.4 %collective-permute-start.15 = (f16[136,512]{1,0:T(8,128)(2,1)S(1)}, f16[136,512]{1,0:T(8,128)(2,1)S(1)}, u32[]{:S(2)}, u32[]{:S(2)}) collective-permute-start(f16[136,512]{1,0:T(8,128)(2,1)S(1)} %convert_element_type.33), channel_id=1, source_target_pairs={{0,16},{8,24},{16,0},{24,8},{1,17},{9,25},{17,1},{25,9},{2,18},{10... | collective-permute-start | bytes 417800 | tf_op jit(solution)/shard_map/ppermute | solution.py:22
  48.2 9.9 %collective-permute-start.16 = (f16[136,1024]{1,0:T(8,128)(2,1)S(1)}, f16[136,1024]{1,0:T(8,128)(2,1)S(1)}, u32[]{:S(2)}, u32[]{:S(2)}) collective-permute-start(f16[136,1024]{1,0:T(8,128)(2,1)S(1)} %convert_element_type.36), channel_id=1, source_target_pairs={{0,8},{8,0},{16,24},{24,16},{1,9},{9,1},{17,25},{25,17},{2,10},{10... | collective-permute-start | bytes 835592 | tf_op jit(solution)/shard_map/ppermute | solution.py:22
  49.9 7.4 %collective-permute-start.13 = (f16[136,512]{1,0:T(8,128)(2,1)S(1)}, f16[136,512]{1,0:T(8,128)(2,1)S(1)}, u32[]{:S(2)}, u32[]{:S(2)}) collective-permute-start(f16[136,512]{1,0:T(8,128)(2,1)S(1)} %convert_element_type.31), channel_id=1, source_target_pairs={{0,16},{8,24},{16,0},{24,8},{1,17},{9,25},{17,1},{25,9},{2,18},{10... | collective-permute-start | bytes 417800 | tf_op jit(solution)/shard_map/ppermute | solution.py:22
  54.3 3.8 %copy-start = (f32[128,1024]{1,0:T(8,128)S(1)}, f32[128,1024]{1,0:T(8,128)}, u32[]{:S(2)}) copy-start(f32[128,1024]{1,0:T(8,128)} %refs_3_.1) | copy-start | bytes 1572868

commit v17 on v16

--- a/solution.py
+++ b/solution.py
@@ -173,9 +173,10 @@
 
 def add_kernel(unit, packed, at, own_ref, got_ref, out_ref):
     size, depth = out_ref.shape[0] - SIDE, out_ref.shape[1]
-    more, tally = unpack(got_ref[...], unit)
-    total = own_ref[0:size, at : at + depth] + more
-    tally = own_ref[size : size + 1, at : at + depth] + tally
+    total, tally = unpack(got_ref[...], unit)
+    if at >= 0:
+        total = own_ref[0:size, at : at + depth] + total
+        tally = own_ref[size : size + 1, at : at + depth] + tally
     if packed:
         total, wide = pack(total, tally, packed)
     else:
@@ -200,11 +201,13 @@
 
 
 def final_kernel(units, *refs):
-    part_refs, got_refs = refs[: -3 - len(units)], refs[-3 - len(units) : -3]
+    own_ref, half_refs, got_refs = refs[0], refs[1 : -3 - len(units)], refs[-3 - len(units) : -3]
     codebook_ref, new_ref, tally_ref = refs[-3:]
     size = codebook_ref.shape[0]
-    total = jnp.concatenate([ref[0:size] for ref in part_refs], axis=1)
-    tally = part_refs[0][size : size + 1, 0:size]
+    total, tally = own_ref[0:size], own_ref[size : size + 1, 0:size]
+    if half_refs:
+        total = total + jnp.concatenate([ref[0:size] for ref in half_refs], axis=1)
+        tally = tally + half_refs[0][size : size + 1, 0:size]
     for ref, unit in zip(got_refs, units):
         more, count = unpack(ref[...], unit)
         total, tally = total + more, tally + count[:, 0:size]
@@ -213,9 +216,9 @@
     new_ref[...] = (total + PRIOR * codebook_ref[...]) * weight
 
 
-def finish(codebook, parts, got):
+def finish(codebook, own, half_sums, got):
     size = codebook.shape[0]
-    arrays = [*parts, *[message.astype(jnp.float32) for message, _ in got], codebook]
+    arrays = [own, *half_sums, *[message.astype(jnp.float32) for message, _ in got], codebook]
     new, tally = pl.pallas_call(
         functools.partial(final_kernel, [unit for _, unit in got]),
         out_shape=(
@@ -322,23 +325,25 @@
         cut = first.shape[1] // 2
         first = [swap(first[:, i : i + cut].astype(jnp.float16), "dp", n_dp, 1) for i in (0, cut)]
         parts = [part(2, 0), part(1, unit), part(0, 0)]
-        far_sum, near_sum, own = weighted(parts, lognorm, scores, rows, picks)
+        far_sum, near, own = weighted(parts, lognorm, scores, rows, picks)
         far = []
         for i, got in enumerate(first):
             message = add_part(far_sum, got, i * cut, unit, unit * 0.5)
             far.append(swap(message.astype(jnp.float16), "dp", n_dp, 2))
-        near = swap(near_sum.astype(jnp.float16), "dp", n_dp, 1)
-        parts = [add_part(own, far[0], 0, unit * 0.5, 0, 200000), None]
-        far[1], parts[0] = lax.optimization_barrier((far[1], parts[0]))
-        parts[1] = add_part(own, far[1], cut, unit * 0.5, 0)
-        got = [(near, unit)]
+        near = swap(near.astype(jnp.float16), "dp", n_dp, 1)
+        half_sum = add_part(own, far[0], -1, unit * 0.5, 0, 32000)
+        near, half_sum = lax.optimization_barrier((near, half_sum))
+        own = add_part(own, near, 0, unit, 0, 100000)
+        far[1], own = lax.optimization_barrier((far[1], own))
+        half_sums = [half_sum, add_part(own, far[1], -1, unit * 0.5, 0)]
+        got = []
     else:
         parts = [part(k, unit if k else 0) for k in range(n_dp - 1)]
         own, *others = weighted(parts, lognorm, scores, rows, picks)
-        parts = [own]
+        half_sums = []
         others = [other.astype(jnp.float16) for other in others + [first]]
         got = [(swap(other, "dp", n_dp, k + 1), unit) for k, other in enumerate(others)]
-    new_codebook, tally = finish(codebook, parts, got)
+    new_codebook, tally = finish(codebook, own, half_sums, got)
     return new_codebook, tally, lognorm[0]
 
 

time: 60.1 us -> 60 us (level); the launches traced: 59.1 us -> 59.8 us
  starting transfers between devices: 23.2 us -> 25.1 us
  waiting for transfers between devices: 22.7 us -> 21.1 us
    ppermute x10, starting transfers between devices: 13.6 us -> 15.5 us  [swap(): return lax.ppermute(x, axis, partner(size, mask))]
    ppermute x10, waiting for transfers between devices: 10.1 us -> 8.5 us  [swap(): return lax.ppermute(x, axis, partner(size, mask))]
  transfers between devices with their start and end apart: 17 -> 17, of which waited for: 12 -> 11; matrix products, arithmetic and copies ran while one was open for 5% -> 5% of each run, Pallas kernels for 11% -> 11%
where the time goes in v17:
time: 60 us; the launch traced here: 59.8 us
  starting transfers between devices  25.1 us (42%)
  waiting for transfers between devices  21.1 us (35%)
  Pallas kernels  9.23 us (15%)
  local copies, waits for them, and re-layouts  2.09 us (3%)
  other arithmetic  1.36 us (2%)
  between operations  0.87 us (1%)
    ppermute x10, starting transfers between devices, swap(): return lax.ppermute(x, axis, partner(size, mask))  15.5 us
    ppermute x10, waiting for transfers between devices, swap(): return lax.ppermute(x, axis, partner(size, mask))  8.5 us
    ppermute x1, waiting for transfers between devices, local(): from_p = lax.ppermute(embeddings, 'cent', by_p)  5.69 us
    pallas_call x5, Pallas kernels, score(): pl.pallas_call(functools.partial(score_kernel, len(centers), len(halves),...  4.58 us
    ppermute x4, waiting for transfers between devices, join(): others = [lax.ppermute(pairs, 'cent', route) for route in routes]  3.84 us
    ppermute x4, starting transfers between devices, join(): others = [lax.ppermute(pairs, 'cent', route) for route in routes]  3.62 us
    pallas_call x2, Pallas kernels, weighted(): pl.pallas_call(functools.partial(sums_kernel, len(scores), picks, parts),...  3.3 us
    ppermute x1, waiting for transfers between devices, local(): diag = lax.ppermute(from_p, 'cent', by_q)  3.09 us
  transfers between devices with their start and end apart: 17, of which 11 were waited for; matrix products, arithmetic and copies ran while one was open for 5% of the time, Pallas kernels for 11%

profile of v17, /device:TPU:0, one launch (start us, length us, event | category | flops | bytes accessed | tf_op | source)
XLA Modules:
  0.0 59.8 jit_solution(7087318663894191521)
XLA Ops:
  0.6 3.0 %collective-permute-start.3 = (bf16[256,1024]{1,0:T(8,128)(2,1)}, bf16[256,1024]{1,0:T(8,128)(2,1)S(1)}, u32[]{:S(2)}, u32[]{:S(2)}) collective-permute-start(bf16[256,1024]{1,0:T(8,128)(2,1)} %param.2), channel_id=1, source_target_pairs={{0,2},{1,5},{2,0},{3,7},{4,6},{5,1},{6,4},{7,3},{8,10},{9,13},{10,... | collective-permute-start | bytes 1572872 | tf_op jit(solution)/shard_map/ppermute | solution.py:263
  3.6 1.5 %collective-permute-start.4 = (bf16[256,1024]{1,0:T(8,128)(2,1)}, bf16[256,1024]{1,0:T(8,128)(2,1)S(1)}, u32[]{:S(2)}, u32[]{:S(2)}) collective-permute-start(bf16[256,1024]{1,0:T(8,128)(2,1)} %param.2), channel_id=1, source_target_pairs={{0,4},{1,3},{2,6},{3,1},{4,0},{5,7},{6,2},{7,5},{8,12},{9,11},{10,... | collective-permute-start | bytes 1572872 | tf_op jit(solution)/shard_map/ppermute | solution.py:264
  5.2 1.1 %convert_element_type.29 = bf16[128,1024]{1,0:T(8,128)(2,1)S(1)} convert(f32[128,1024]{1,0:T(8,128)} %refs_3_.1) | non-fusion elementwise | flops 131072 | bytes 786432 | tf_op jit(solution)/shard_map/convert_element_type | solution.py:259
  6.2 2.7 %collective-permute-start.1 = (bf16[128,1024]{1,0:T(8,128)(2,1)S(1)}, bf16[128,1024]{1,0:T(8,128)(2,1)S(1)}, u32[]{:S(2)}, u32[]{:S(2)}) collective-permute-start(bf16[128,1024]{1,0:T(8,128)(2,1)S(1)} %convert_element_type.29), channel_id=1, source_target_pairs={{0,16},{8,24},{16,0},{24,8},{1,17},{9,25},{17,1},{25,9},{2,18},{10... | collective-permute-start | bytes 786440 | tf_op jit(solution)/shard_map/ppermute | solution.py:22
  8.9 1.6 %collective-permute-start = (bf16[128,1024]{1,0:T(8,128)(2,1)S(1)}, bf16[128,1024]{1,0:T(8,128)(2,1)S(1)}, u32[]{:S(2)}, u32[]{:S(2)}) collective-permute-start(bf16[128,1024]{1,0:T(8,128)(2,1)S(1)} %convert_element_type.29), channel_id=1, source_target_pairs={{0,8},{8,0},{16,24},{24,16},{1,9},{9,1},{17,25},{25,17},{2,10},{10... | collective-permute-start | bytes 786440 | tf_op jit(solution)/shard_map/ppermute | solution.py:22
  10.5 5.7 %collective-permute-done.3 = bf16[256,1024]{1,0:T(8,128)(2,1)S(1)} collective-permute-done((bf16[256,1024]{1,0:T(8,128)(2,1)}, bf16[256,1024]{1,0:T(8,128)(2,1)S(1)}, u32[]{:S(2)}, u32[]{:S(2)}) %collective-permute-start.3) | collective-permute-done | bytes 524320 | tf_op jit(solution)/shard_map/ppermute | solution.py:263
  16.2 1.5 %collective-permute-start.6 = (bf16[256,1024]{1,0:T(8,128)(2,1)S(1)}, bf16[256,1024]{1,0:T(8,128)(2,1)S(1)}, u32[]{:S(2)}, u32[]{:S(2)}) collective-permute-start(bf16[256,1024]{1,0:T(8,128)(2,1)S(1)} %collective-permute-done.3), channel_id=1, source_target_pairs={{0,4},{1,3},{2,6},{3,1},{4,0},{5,7},{6,2},{7,5},{8,12},{9,11},{10,... | collective-permute-start | bytes 1572872 | tf_op jit(solution)/shard_map/ppermute | solution.py:274
  17.6 1.1 %constant_dynamic-update-slice_fusion.2 = bf16[768,1024]{1,0:T(8,128)(2,1)S(1)} fusion(bf16[256,1024]{1,0:T(8,128)(2,1)} %param.2), kind=kLoop, calls=%fused_computation.3 | loop fusion | bytes 1048576
  18.7 1.7 %collective-permute-done.1 = bf16[128,1024]{1,0:T(8,128)(2,1)S(1)} collective-permute-done((bf16[128,1024]{1,0:T(8,128)(2,1)S(1)}, bf16[128,1024]{1,0:T(8,128)(2,1)S(1)}, u32[]{:S(2)}, u32[]{:S(2)}) %collective-permute-start.1) | collective-permute-done | bytes 262176 | tf_op jit(solution)/shard_map/ppermute | solution.py:22
  21.2 1.0 %score_rows.5 = (f32[3,384,256]{2,1,0:T(8,128)S(1)}, f32[2,3,256]{2,1,0:T(4,128)S(1)}, f32[384,128]{1,0:T(8,128)S(1)}) custom-call(bf16[384,1024]{1,0:T(8,128)(2,1)S(1)} %pad_maximum_fusion.refs_0_, bf16[768,1024]{1,0:T(8,128)(2,1)S(1)} %constant_dynamic-update-slice_fusion.refs_1_.refs_4_.refs_3_), custom_call_target="tpu_custom_call" | custom-call | flops 603979776 | bytes 2359296 | tf_op jit(solution)/shard_map/score_rows/pallas_call | solution.py:82
  22.3 3.1 %collective-permute-done.6.refs_2_.refs_5_.refs_4_ = bf16[256,1024]{1,0:T(8,128)(2,1)S(1)} collective-permute-done((bf16[256,1024]{1,0:T(8,128)(2,1)S(1)}, bf16[256,1024]{1,0:T(8,128)(2,1)S(1)}, u32[]{:S(2)}, u32[]{:S(2)}) %collective-permute-start.6) | collective-permute-done | bytes 524320 | tf_op jit(solution)/shard_map/ppermute | solution.py:274
  25.9 1.6 %collective-permute-done.2.refs_0_.refs_1_ = bf16[128,1024]{1,0:T(8,128)(2,1)S(1)} collective-permute-done((bf16[128,1024]{1,0:T(8,128)(2,1)S(1)}, bf16[128,1024]{1,0:T(8,128)(2,1)S(1)}, u32[]{:S(2)}, u32[]{:S(2)}) %collective-permute-start.2) | collective-permute-done | bytes 262176 | tf_op jit(solution)/shard_map/ppermute | solution.py:22
  28.4 1.5 %score_rows.8 = (f32[3,512,256]{2,1,0:T(8,128)S(1)}, f32[2,3,256]{2,1,0:T(4,128)S(1)}) custom-call(bf16[384,1024]{1,0:T(8,128)(2,1)S(1)} %pad_maximum_fusion.refs_0_, bf16[128,1024]{1,0:T(8,128)(2,1)S(1)} %collective-permute-done.2.refs_0_.refs_1_, f32[384,128]{1,0:T(8,128)S(1)} %get-tuple-element.30.refs_1_.refs_2_, ...), custom_call_target="tpu_custom_call" | custom-call | flops 80530640 | bytes 262144 | tf_op jit(solution)/shard_map/score_rows/pallas_call | solution.py:82
  30.6 1.2 %collective-permute-done.8.refs_0_ = f32[2,8,256]{2,1,0:T(8,128)S(1)} collective-permute-done((f32[2,8,256]{2,1,0:T(8,128)S(1)}, f32[2,8,256]{2,1,0:T(8,128)S(1)}, u32[]{:S(2)}, u32[]{:S(2)}) %collective-permute-start.8) | collective-permute-done | bytes 16416 | tf_op jit(solution)/shard_map/ppermute | solution.py:113
  32.4 1.9 %collective-permute-start.11 = (f32[2,8,256]{2,1,0:T(8,128)S(1)}, f32[2,8,256]{2,1,0:T(8,128)S(1)}, u32[]{:S(2)}, u32[]{:S(2)}) collective-permute-start(f32[2,8,256]{2,1,0:T(8,128)S(1)} %join_rows.2.pair_ref), channel_id=1, source_target_pairs={{0,6},{1,7},{2,4},{3,5},{4,2},{5,3},{6,0},{7,1},{8,14},{9,15},{10,... | collective-permute-start | bytes 49160 | tf_op jit(solution)/shard_map/ppermute | solution.py:113
  34.3 1.1 %collective-permute-start.9 = (f32[2,8,256]{2,1,0:T(8,128)S(1)}, f32[2,8,256]{2,1,0:T(8,128)S(1)}, u32[]{:S(2)}, u32[]{:S(2)}) collective-permute-start(f32[2,8,256]{2,1,0:T(8,128)S(1)} %join_rows.2.pair_ref), channel_id=1, source_target_pairs={{0,2},{1,5},{2,0},{3,7},{4,6},{5,1},{6,4},{7,3},{8,10},{9,13},{10,... | collective-permute-start | bytes 49160 | tf_op jit(solution)/shard_map/ppermute | solution.py:113
  35.6 1.4 %collective-permute-done.11.refs_2_ = f32[2,8,256]{2,1,0:T(8,128)S(1)} collective-permute-done((f32[2,8,256]{2,1,0:T(8,128)S(1)}, f32[2,8,256]{2,1,0:T(8,128)S(1)}, u32[]{:S(2)}, u32[]{:S(2)}) %collective-permute-start.11) | collective-permute-done | bytes 16416 | tf_op jit(solution)/shard_map/ppermute | solution.py:113
  39.1 1.6 %collective-permute-start.15 = (f16[136,512]{1,0:T(8,128)(2,1)S(1)}, f16[136,512]{1,0:T(8,128)(2,1)S(1)}, u32[]{:S(2)}, u32[]{:S(2)}) collective-permute-start(f16[136,512]{1,0:T(8,128)(2,1)S(1)} %get-tuple-element.57), channel_id=1, source_target_pairs={{0,8},{8,0},{16,24},{24,16},{1,9},{9,1},{17,25},{25,17},{2,10},{10... | collective-permute-start | bytes 417800 | tf_op jit(solution)/shard_map/ppermute | solution.py:22
  41.2 2.4 %weighted_sums.2 = (f32[136,1024]{1,0:T(8,128)S(1)}, f32[136,1024]{1,0:T(8,128)S(1)}, f32[136,1024]{1,0:T(8,128)S(1)}) custom-call(f32[8,256]{1,0:T(8,128)S(1)} %join_rows.3.lognorm_ref, f32[3,384,256]{2,1,0:T(8,128)S(1)} %get-tuple-element.43.refs_0_, f32[1,384,256]{2,1,0:T(8,128)S(1)} %get-tuple-element.44.refs_1_, ...), custom_call_target="tpu_custom_call" | custom-call | flops 1610612736 | bytes 4194304 | tf_op jit(solution)/shard_map/weighted_sums/pallas_call | solution.py:240
  43.6 1.0 %collective-permute-done.15 = f16[136,512]{1,0:T(8,128)(2,1)S(1)} collective-permute-done((f16[136,512]{1,0:T(8,128)(2,1)S(1)}, f16[136,512]{1,0:T(8,128)(2,1)S(1)}, u32[]{:S(2)}, u32[]{:S(2)}) %collective-permute-start.15) | collective-permute-done | bytes 139296 | tf_op jit(solution)/shard_map/ppermute | solution.py:22
  44.8 3.3 %collective-permute-start.16 = (f16[136,512]{1,0:T(8,128)(2,1)S(1)}, f16[136,512]{1,0:T(8,128)(2,1)S(1)}, u32[]{:S(2)}, u32[]{:S(2)}) collective-permute-start(f16[136,512]{1,0:T(8,128)(2,1)S(1)} %convert_element_type.34), channel_id=1, source_target_pairs={{0,16},{8,24},{16,0},{24,8},{1,17},{9,25},{17,1},{25,9},{2,18},{10... | collective-permute-start | bytes 417800 | tf_op jit(solution)/shard_map/ppermute | solution.py:22
  48.2 1.7 %collective-permute-start.14 = (f16[136,1024]{1,0:T(8,128)(2,1)S(1)}, f16[136,1024]{1,0:T(8,128)(2,1)S(1)}, u32[]{:S(2)}, u32[]{:S(2)}) collective-permute-start(f16[136,1024]{1,0:T(8,128)(2,1)S(1)} %convert_element_type.32), channel_id=1, source_target_pairs={{0,8},{8,0},{16,24},{24,16},{1,9},{9,1},{17,25},{25,17},{2,10},{10... | collective-permute-start | bytes 835592 | tf_op jit(solution)/shard_map/ppermute | solution.py:22
  50.6 3.4 %collective-permute-start.13 = (f16[136,512]{1,0:T(8,128)(2,1)S(1)}, f16[136,512]{1,0:T(8,128)(2,1)S(1)}, u32[]{:S(2)}, u32[]{:S(2)}) collective-permute-start(f16[136,512]{1,0:T(8,128)(2,1)S(1)} %convert_element_type.31), channel_id=1, source_target_pairs={{0,16},{8,24},{16,0},{24,8},{1,17},{9,25},{17,1},{25,9},{2,18},{10... | collective-permute-start | bytes 417800 | tf_op jit(solution)/shard_map/ppermute | solution.py:22
  54.1 3.5 %collective-permute-done.14 = f16[136,1024]{1,0:T(8,128)(2,1)S(1)} collective-permute-done((f16[136,1024]{1,0:T(8,128)(2,1)S(1)}, f16[136,1024]{1,0:T(8,128)(2,1)S(1)}, u32[]{:S(2)}, u32[]{:S(2)}) %collective-permute-start.14) | collective-permute-done | bytes 278560 | tf_op jit(solution)/shard_map/ppermute | solution.py:22
  (43 shorter events, 9.4 us)
Async XLA Ops:
  0.6 15.5 %collective-permute-start.3 = (bf16[256,1024]{1,0:T(8,128)(2,1)}, bf16[256,1024]{1,0:T(8,128)(2,1)S(1)}, u32[]{:S(2)}, u32[]{:S(2)}) collective-permute-start(bf16[256,1024]{1,0:T(8,128)(2,1)} %param.2), channel_id=1, source_target_pairs={{0,2},{1,5},{2,0},{3,7},{4,6},{5,1},{6,4},{7,3},{8,10},{9,13},{10,... | collective-permute-start | bytes 1572872 | tf_op jit(solution)/shard_map/ppermute | solution.py:263
  3.6 17.4 %collective-permute-start.4 = (bf16[256,1024]{1,0:T(8,128)(2,1)}, bf16[256,1024]{1,0:T(8,128)(2,1)S(1)}, u32[]{:S(2)}, u32[]{:S(2)}) collective-permute-start(bf16[256,1024]{1,0:T(8,128)(2,1)} %param.2), channel_id=1, source_target_pairs={{0,4},{1,3},{2,6},{3,1},{4,0},{5,7},{6,2},{7,5},{8,12},{9,11},{10,... | collective-permute-start | bytes 1572872 | tf_op jit(solution)/shard_map/ppermute | solution.py:264
  6.2 14.2 %collective-permute-start.1 = (bf16[128,1024]{1,0:T(8,128)(2,1)S(1)}, bf16[128,1024]{1,0:T(8,128)(2,1)S(1)}, u32[]{:S(2)}, u32[]{:S(2)}) collective-permute-start(bf16[128,1024]{1,0:T(8,128)(2,1)S(1)} %convert_element_type.29), channel_id=1, source_target_pairs={{0,16},{8,24},{16,0},{24,8},{1,17},{9,25},{17,1},{25,9},{2,18},{10... | collective-permute-start | bytes 786440 | tf_op jit(solution)/shard_map/ppermute | solution.py:22
  8.9 12.3 %collective-permute-start = (bf16[128,1024]{1,0:T(8,128)(2,1)S(1)}, bf16[128,1024]{1,0:T(8,128)(2,1)S(1)}, u32[]{:S(2)}, u32[]{:S(2)}) collective-permute-start(bf16[128,1024]{1,0:T(8,128)(2,1)S(1)} %convert_element_type.29), channel_id=1, source_target_pairs={{0,8},{8,0},{16,24},{24,16},{1,9},{9,1},{17,25},{25,17},{2,10},{10... | collective-permute-start | bytes 786440 | tf_op jit(solution)/shard_map/ppermute | solution.py:22
  16.2 9.2 %collective-permute-start.6 = (bf16[256,1024]{1,0:T(8,128)(2,1)S(1)}, bf16[256,1024]{1,0:T(8,128)(2,1)S(1)}, u32[]{:S(2)}, u32[]{:S(2)}) collective-permute-start(bf16[256,1024]{1,0:T(8,128)(2,1)S(1)} %collective-permute-done.3), channel_id=1, source_target_pairs={{0,4},{1,3},{2,6},{3,1},{4,0},{5,7},{6,2},{7,5},{8,12},{9,11},{10,... | collective-permute-start | bytes 1572872 | tf_op jit(solution)/shard_map/ppermute | solution.py:274
  20.4 7.1 %collective-permute-start.2 = (bf16[128,1024]{1,0:T(8,128)(2,1)S(1)}, bf16[128,1024]{1,0:T(8,128)(2,1)S(1)}, u32[]{:S(2)}, u32[]{:S(2)}) collective-permute-start(bf16[128,1024]{1,0:T(8,128)(2,1)S(1)} %collective-permute-done.1), channel_id=1, source_target_pairs={{0,8},{8,0},{16,24},{24,16},{1,9},{9,1},{17,25},{25,17},{2,10},{10... | collective-permute-start | bytes 786440 | tf_op jit(solution)/shard_map/ppermute | solution.py:22
  21.1 7.3 %collective-permute-start.5 = (bf16[768,1024]{1,0:T(8,128)(2,1)S(1)}, bf16[768,1024]{1,0:T(8,128)(2,1)S(1)}, u32[]{:S(2)}, u32[]{:S(2)}) collective-permute-start(bf16[768,1024]{1,0:T(8,128)(2,1)S(1)} %constant_dynamic-update-slice_fusion.refs_1_.refs_4_.refs_3_), channel_id=1, source_target_pairs={{0,1},{1,0},{2,3},{3,2},{4,5},{5,4},{6,7},{7,6},{8,9},{9,8},{10,11... | collective-permute-start | bytes 4718600 | tf_op jit(solution)/shard_map/ppermute | solution.py:22
  25.8 4.0 %collective-permute-start.7 = (bf16[256,1024]{1,0:T(8,128)(2,1)S(1)}, bf16[256,1024]{1,0:T(8,128)(2,1)S(1)}, u32[]{:S(2)}, u32[]{:S(2)}) collective-permute-start(bf16[256,1024]{1,0:T(8,128)(2,1)S(1)} %collective-permute-done.6.refs_2_.refs_5_.refs_4_), channel_id=1, source_target_pairs={{0,1},{1,0},{2,3},{3,2},{4,5},{5,4},{6,7},{7,6},{8,9},{9,8},{10,11... | collective-permute-start | bytes 1572872 | tf_op jit(solution)/shard_map/ppermute | solution.py:22
  30.5 1.2 %collective-permute-start.8 = (f32[2,8,256]{2,1,0:T(8,128)S(1)}, f32[2,8,256]{2,1,0:T(8,128)S(1)}, u32[]{:S(2)}, u32[]{:S(2)}) collective-permute-start(f32[2,8,256]{2,1,0:T(8,128)S(1)} %get-tuple-element.42.pair_ref), channel_id=1, source_target_pairs={{0,1},{1,0},{2,3},{3,2},{4,5},{5,4},{6,7},{7,6},{8,9},{9,8},{10,11... | collective-permute-start | bytes 49160 | tf_op jit(solution)/shard_map/ppermute | solution.py:113
  31.8 3.8 %collective-permute-start.10 = (f32[2,8,256]{2,1,0:T(8,128)S(1)}, f32[2,8,256]{2,1,0:T(8,128)S(1)}, u32[]{:S(2)}, u32[]{:S(2)}) collective-permute-start(f32[2,8,256]{2,1,0:T(8,128)S(1)} %join_rows.2.pair_ref), channel_id=1, source_target_pairs={{0,4},{1,3},{2,6},{3,1},{4,0},{5,7},{6,2},{7,5},{8,12},{9,11},{10,... | collective-permute-start | bytes 49160 | tf_op jit(solution)/shard_map/ppermute | solution.py:113
  32.4 4.6 %collective-permute-start.11 = (f32[2,8,256]{2,1,0:T(8,128)S(1)}, f32[2,8,256]{2,1,0:T(8,128)S(1)}, u32[]{:S(2)}, u32[]{:S(2)}) collective-permute-start(f32[2,8,256]{2,1,0:T(8,128)S(1)} %join_rows.2.pair_ref), channel_id=1, source_target_pairs={{0,6},{1,7},{2,4},{3,5},{4,2},{5,3},{6,0},{7,1},{8,14},{9,15},{10,... | collective-permute-start | bytes 49160 | tf_op jit(solution)/shard_map/ppermute | solution.py:113
  34.3 3.7 %collective-permute-start.9 = (f32[2,8,256]{2,1,0:T(8,128)S(1)}, f32[2,8,256]{2,1,0:T(8,128)S(1)}, u32[]{:S(2)}, u32[]{:S(2)}) collective-permute-start(f32[2,8,256]{2,1,0:T(8,128)S(1)} %join_rows.2.pair_ref), channel_id=1, source_target_pairs={{0,2},{1,5},{2,0},{3,7},{4,6},{5,1},{6,4},{7,3},{8,10},{9,13},{10,... | collective-permute-start | bytes 49160 | tf_op jit(solution)/shard_map/ppermute | solution.py:113
  39.1 5.5 %collective-permute-start.15 = (f16[136,512]{1,0:T(8,128)(2,1)S(1)}, f16[136,512]{1,0:T(8,128)(2,1)S(1)}, u32[]{:S(2)}, u32[]{:S(2)}) collective-permute-start(f16[136,512]{1,0:T(8,128)(2,1)S(1)} %get-tuple-element.57), channel_id=1, source_target_pairs={{0,8},{8,0},{16,24},{24,16},{1,9},{9,1},{17,25},{25,17},{2,10},{10... | collective-permute-start | bytes 417800 | tf_op jit(solution)/shard_map/ppermute | solution.py:22
  40.8 9.1 %collective-permute-start.12 = (f16[136,512]{1,0:T(8,128)(2,1)S(1)}, f16[136,512]{1,0:T(8,128)(2,1)S(1)}, u32[]{:S(2)}, u32[]{:S(2)}) collective-permute-start(f16[136,512]{1,0:T(8,128)(2,1)S(1)} %get-tuple-element.58), channel_id=1, source_target_pairs={{0,8},{8,0},{16,24},{24,16},{1,9},{9,1},{17,25},{25,17},{2,10},{10... | collective-permute-start | bytes 417800 | tf_op jit(solution)/shard_map/ppermute | solution.py:22
  44.8 9.2 %collective-permute-start.16 = (f16[136,512]{1,0:T(8,128)(2,1)S(1)}, f16[136,512]{1,0:T(8,128)(2,1)S(1)}, u32[]{:S(2)}, u32[]{:S(2)}) collective-permute-start(f16[136,512]{1,0:T(8,128)(2,1)S(1)} %convert_element_type.34), channel_id=1, source_target_pairs={{0,16},{8,24},{16,0},{24,8},{1,17},{9,25},{17,1},{25,9},{2,18},{10... | collective-permute-start | bytes 417800 | tf_op jit(solution)/shard_map/ppermute | solution.py:22
  48.2 9.4 %collective-permute-start.14 = (f16[136,1024]{1,0:T(8,128)(2,1)S(1)}, f16[136,1024]{1,0:T(8,128)(2,1)S(1)}, u32[]{:S(2)}, u32[]{:S(2)}) collective-permute-start(f16[136,1024]{1,0:T(8,128)(2,1)S(1)} %convert_element_type.32), channel_id=1, source_target_pairs={{0,8},{8,0},{16,24},{24,16},{1,9},{9,1},{17,25},{25,17},{2,10},{10... | collective-permute-start | bytes 835592 | tf_op jit(solution)/shard_map/ppermute | solution.py:22
  50.6 7.8 %collective-permute-start.13 = (f16[136,512]{1,0:T(8,128)(2,1)S(1)}, f16[136,512]{1,0:T(8,128)(2,1)S(1)}, u32[]{:S(2)}, u32[]{:S(2)}) collective-permute-start(f16[136,512]{1,0:T(8,128)(2,1)S(1)} %convert_element_type.31), channel_id=1, source_target_pairs={{0,16},{8,24},{16,0},{24,8},{1,17},{9,25},{17,1},{25,9},{2,18},{10... | collective-permute-start | bytes 417800 | tf_op jit(solution)/shard_map/ppermute | solution.py:22
  57.7 1.0 %copy-start = (f32[128,1024]{1,0:T(8,128)S(1)}, f32[128,1024]{1,0:T(8,128)}, u32[]{:S(2)}) copy-start(f32[128,1024]{1,0:T(8,128)} %refs_3_.1) | copy-start | bytes 1572868

commit v18 on v17

--- a/solution.py
+++ b/solution.py
@@ -201,8 +201,10 @@
 
 
 def final_kernel(units, *refs):
-    own_ref, half_refs, got_refs = refs[0], refs[1 : -3 - len(units)], refs[-3 - len(units) : -3]
-    codebook_ref, new_ref, tally_ref = refs[-3:]
+    arrived = len(refs) - 5 - len(units)
+    own_ref, half_refs, got_refs = refs[0], refs[1:arrived], refs[arrived:-5]
+    codebook_ref, lognorm_ref, new_ref, tally_ref, norm_ref = refs[-5:]
+    norm_ref[...] = lognorm_ref[0:1]
     size = codebook_ref.shape[0]
     total, tally = own_ref[0:size], own_ref[size : size + 1, 0:size]
     if half_refs:
@@ -216,21 +218,22 @@
     new_ref[...] = (total + PRIOR * codebook_ref[...]) * weight
 
 
-def finish(codebook, own, half_sums, got):
+def finish(codebook, lognorm, own, half_sums, got):
     size = codebook.shape[0]
-    arrays = [own, *half_sums, *[message.astype(jnp.float32) for message, _ in got], codebook]
-    new, tally = pl.pallas_call(
+    arrays = [own, *half_sums, *[message.astype(jnp.float32) for message, _ in got], codebook, lognorm]
+    new, tally, norm = pl.pallas_call(
         functools.partial(final_kernel, [unit for _, unit in got]),
         out_shape=(
             jax.ShapeDtypeStruct(codebook.shape, jnp.float32),
             jax.ShapeDtypeStruct((1, size), jnp.float32),
+            jax.ShapeDtypeStruct((1, lognorm.shape[1]), jnp.float32),
         ),
         in_specs=[VMEM] * len(arrays),
-        out_specs=(VMEM, VMEM),
+        out_specs=(VMEM,) * 3,
         compiler_params=PARAMS,
         name="update_centroids",
     )(*arrays)
-    return new, tally[0]
+    return new, tally[0], norm[0]
 
 
 def weighted(parts, lognorm, scores, rows, picks):
@@ -343,8 +346,7 @@
         half_sums = []
         others = [other.astype(jnp.float16) for other in others + [first]]
         got = [(swap(other, "dp", n_dp, k + 1), unit) for k, other in enumerate(others)]
-    new_codebook, tally = finish(codebook, own, half_sums, got)
-    return new_codebook, tally, lognorm[0]
+    return finish(codebook, lognorm, own, half_sums, got)
 
 
 def solution(mesh):

time: 60 us -> 60.5 us (level)
    unnamed x4, local copies, waits for them, and re-layouts: 1.44 us -> 2.07 us
  transfers between devices with their start and end apart: 17 -> 17, of which waited for: 11 -> 11; matrix products, arithmetic and copies ran while one was open for 5% -> 4% of each run, Pallas kernels for 11% -> 11%
where the time goes in v18:
time: 60.5 us; the launch traced here: 60.2 us
  starting transfers between devices  25.1 us (41%)
  waiting for transfers between devices  21.5 us (36%)
  Pallas kernels  9.25 us (15%)
  local copies, waits for them, and re-layouts  2.15 us (4%)
  other arithmetic  1.36 us (2%)
  between operations  0.88 us (1%)
    ppermute x10, starting transfers between devices, swap(): return lax.ppermute(x, axis, partner(size, mask))  15.5 us
    ppermute x10, waiting for transfers between devices, swap(): return lax.ppermute(x, axis, partner(size, mask))  8.88 us
    ppermute x1, waiting for transfers between devices, local(): from_p = lax.ppermute(embeddings, 'cent', by_p)  5.69 us
    pallas_call x5, Pallas kernels, score(): pl.pallas_call(functools.partial(score_kernel, len(centers), len(halves),...  4.58 us
    ppermute x4, waiting for transfers between devices, join(): others = [lax.ppermute(pairs, 'cent', route) for route in routes]  3.84 us
    ppermute x4, starting transfers between devices, join(): others = [lax.ppermute(pairs, 'cent', route) for route in routes]  3.62 us
    pallas_call x2, Pallas kernels, weighted(): pl.pallas_call(functools.partial(sums_kernel, len(scores), picks, parts),...  3.3 us
    ppermute x1, waiting for transfers between devices, local(): diag = lax.ppermute(from_p, 'cent', by_q)  3.09 us
  transfers between devices with their start and end apart: 17, of which 11 were waited for; matrix products, arithmetic and copies ran while one was open for 4% of the time, Pallas kernels for 11%

profile of v18, /device:TPU:0, one launch (start us, length us, event | category | flops | bytes accessed | tf_op | source)
XLA Modules:
  0.0 60.2 jit_solution(14974929819216405926)
XLA Ops:
  0.6 3.0 %collective-permute-start.3 = (bf16[256,1024]{1,0:T(8,128)(2,1)}, bf16[256,1024]{1,0:T(8,128)(2,1)S(1)}, u32[]{:S(2)}, u32[]{:S(2)}) collective-permute-start(bf16[256,1024]{1,0:T(8,128)(2,1)} %param.2), channel_id=1, source_target_pairs={{0,2},{1,5},{2,0},{3,7},{4,6},{5,1},{6,4},{7,3},{8,10},{9,13},{10,... | collective-permute-start | bytes 1572872 | tf_op jit(solution)/shard_map/ppermute | solution.py:266
  3.6 1.5 %collective-permute-start.4 = (bf16[256,1024]{1,0:T(8,128)(2,1)}, bf16[256,1024]{1,0:T(8,128)(2,1)S(1)}, u32[]{:S(2)}, u32[]{:S(2)}) collective-permute-start(bf16[256,1024]{1,0:T(8,128)(2,1)} %param.2), channel_id=1, source_target_pairs={{0,4},{1,3},{2,6},{3,1},{4,0},{5,7},{6,2},{7,5},{8,12},{9,11},{10,... | collective-permute-start | bytes 1572872 | tf_op jit(solution)/shard_map/ppermute | solution.py:267
  5.2 1.1 %convert_element_type.29 = bf16[128,1024]{1,0:T(8,128)(2,1)S(1)} convert(f32[128,1024]{1,0:T(8,128)} %refs_3_.1) | non-fusion elementwise | flops 131072 | bytes 786432 | tf_op jit(solution)/shard_map/convert_element_type | solution.py:262
  6.2 2.7 %collective-permute-start.1 = (bf16[128,1024]{1,0:T(8,128)(2,1)S(1)}, bf16[128,1024]{1,0:T(8,128)(2,1)S(1)}, u32[]{:S(2)}, u32[]{:S(2)}) collective-permute-start(bf16[128,1024]{1,0:T(8,128)(2,1)S(1)} %convert_element_type.29), channel_id=1, source_target_pairs={{0,16},{8,24},{16,0},{24,8},{1,17},{9,25},{17,1},{25,9},{2,18},{10... | collective-permute-start | bytes 786440 | tf_op jit(solution)/shard_map/ppermute | solution.py:22
  8.9 1.6 %collective-permute-start = (bf16[128,1024]{1,0:T(8,128)(2,1)S(1)}, bf16[128,1024]{1,0:T(8,128)(2,1)S(1)}, u32[]{:S(2)}, u32[]{:S(2)}) collective-permute-start(bf16[128,1024]{1,0:T(8,128)(2,1)S(1)} %convert_element_type.29), channel_id=1, source_target_pairs={{0,8},{8,0},{16,24},{24,16},{1,9},{9,1},{17,25},{25,17},{2,10},{10... | collective-permute-start | bytes 786440 | tf_op jit(solution)/shard_map/ppermute | solution.py:22
  10.5 5.7 %collective-permute-done.3 = bf16[256,1024]{1,0:T(8,128)(2,1)S(1)} collective-permute-done((bf16[256,1024]{1,0:T(8,128)(2,1)}, bf16[256,1024]{1,0:T(8,128)(2,1)S(1)}, u32[]{:S(2)}, u32[]{:S(2)}) %collective-permute-start.3) | collective-permute-done | bytes 524320 | tf_op jit(solution)/shard_map/ppermute | solution.py:266
  16.2 1.5 %collective-permute-start.6 = (bf16[256,1024]{1,0:T(8,128)(2,1)S(1)}, bf16[256,1024]{1,0:T(8,128)(2,1)S(1)}, u32[]{:S(2)}, u32[]{:S(2)}) collective-permute-start(bf16[256,1024]{1,0:T(8,128)(2,1)S(1)} %collective-permute-done.3), channel_id=1, source_target_pairs={{0,4},{1,3},{2,6},{3,1},{4,0},{5,7},{6,2},{7,5},{8,12},{9,11},{10,... | collective-permute-start | bytes 1572872 | tf_op jit(solution)/shard_map/ppermute | solution.py:277
  17.6 1.1 %constant_dynamic-update-slice_fusion.2 = bf16[768,1024]{1,0:T(8,128)(2,1)S(1)} fusion(bf16[256,1024]{1,0:T(8,128)(2,1)} %param.2), kind=kLoop, calls=%fused_computation.3 | loop fusion | bytes 1048576
  18.7 1.7 %collective-permute-done.1 = bf16[128,1024]{1,0:T(8,128)(2,1)S(1)} collective-permute-done((bf16[128,1024]{1,0:T(8,128)(2,1)S(1)}, bf16[128,1024]{1,0:T(8,128)(2,1)S(1)}, u32[]{:S(2)}, u32[]{:S(2)}) %collective-permute-start.1) | collective-permute-done | bytes 262176 | tf_op jit(solution)/shard_map/ppermute | solution.py:22
  21.2 1.0 %score_rows.5 = (f32[3,384,256]{2,1,0:T(8,128)S(1)}, f32[2,3,256]{2,1,0:T(4,128)S(1)}, f32[384,128]{1,0:T(8,128)S(1)}) custom-call(bf16[384,1024]{1,0:T(8,128)(2,1)S(1)} %pad_maximum_fusion.refs_0_, bf16[768,1024]{1,0:T(8,128)(2,1)S(1)} %constant_dynamic-update-slice_fusion.refs_1_.refs_4_.refs_3_), custom_call_target="tpu_custom_call" | custom-call | flops 603979776 | bytes 2359296 | tf_op jit(solution)/shard_map/score_rows/pallas_call | solution.py:82
  22.3 3.1 %collective-permute-done.6.refs_2_.refs_5_.refs_4_ = bf16[256,1024]{1,0:T(8,128)(2,1)S(1)} collective-permute-done((bf16[256,1024]{1,0:T(8,128)(2,1)S(1)}, bf16[256,1024]{1,0:T(8,128)(2,1)S(1)}, u32[]{:S(2)}, u32[]{:S(2)}) %collective-permute-start.6) | collective-permute-done | bytes 524320 | tf_op jit(solution)/shard_map/ppermute | solution.py:277
  25.9 1.6 %collective-permute-done.2.refs_0_.refs_1_ = bf16[128,1024]{1,0:T(8,128)(2,1)S(1)} collective-permute-done((bf16[128,1024]{1,0:T(8,128)(2,1)S(1)}, bf16[128,1024]{1,0:T(8,128)(2,1)S(1)}, u32[]{:S(2)}, u32[]{:S(2)}) %collective-permute-start.2) | collective-permute-done | bytes 262176 | tf_op jit(solution)/shard_map/ppermute | solution.py:22
  28.4 1.5 %score_rows.8 = (f32[3,512,256]{2,1,0:T(8,128)S(1)}, f32[2,3,256]{2,1,0:T(4,128)S(1)}) custom-call(bf16[384,1024]{1,0:T(8,128)(2,1)S(1)} %pad_maximum_fusion.refs_0_, bf16[128,1024]{1,0:T(8,128)(2,1)S(1)} %collective-permute-done.2.refs_0_.refs_1_, f32[384,128]{1,0:T(8,128)S(1)} %get-tuple-element.31.refs_1_.refs_2_, ...), custom_call_target="tpu_custom_call" | custom-call | flops 80530640 | bytes 262144 | tf_op jit(solution)/shard_map/score_rows/pallas_call | solution.py:82
  30.6 1.2 %collective-permute-done.8.refs_0_ = f32[2,8,256]{2,1,0:T(8,128)S(1)} collective-permute-done((f32[2,8,256]{2,1,0:T(8,128)S(1)}, f32[2,8,256]{2,1,0:T(8,128)S(1)}, u32[]{:S(2)}, u32[]{:S(2)}) %collective-permute-start.8) | collective-permute-done | bytes 16416 | tf_op jit(solution)/shard_map/ppermute | solution.py:113
  32.4 1.9 %collective-permute-start.11 = (f32[2,8,256]{2,1,0:T(8,128)S(1)}, f32[2,8,256]{2,1,0:T(8,128)S(1)}, u32[]{:S(2)}, u32[]{:S(2)}) collective-permute-start(f32[2,8,256]{2,1,0:T(8,128)S(1)} %join_rows.2.pair_ref), channel_id=1, source_target_pairs={{0,6},{1,7},{2,4},{3,5},{4,2},{5,3},{6,0},{7,1},{8,14},{9,15},{10,... | collective-permute-start | bytes 49160 | tf_op jit(solution)/shard_map/ppermute | solution.py:113
  34.3 1.1 %collective-permute-start.9 = (f32[2,8,256]{2,1,0:T(8,128)S(1)}, f32[2,8,256]{2,1,0:T(8,128)S(1)}, u32[]{:S(2)}, u32[]{:S(2)}) collective-permute-start(f32[2,8,256]{2,1,0:T(8,128)S(1)} %join_rows.2.pair_ref), channel_id=1, source_target_pairs={{0,2},{1,5},{2,0},{3,7},{4,6},{5,1},{6,4},{7,3},{8,10},{9,13},{10,... | collective-permute-start | bytes 49160 | tf_op jit(solution)/shard_map/ppermute | solution.py:113
  35.6 1.4 %collective-permute-done.11.refs_2_ = f32[2,8,256]{2,1,0:T(8,128)S(1)} collective-permute-done((f32[2,8,256]{2,1,0:T(8,128)S(1)}, f32[2,8,256]{2,1,0:T(8,128)S(1)}, u32[]{:S(2)}, u32[]{:S(2)}) %collective-permute-start.11) | collective-permute-done | bytes 16416 | tf_op jit(solution)/shard_map/ppermute | solution.py:113
  39.1 1.6 %collective-permute-start.15 = (f16[136,512]{1,0:T(8,128)(2,1)S(1)}, f16[136,512]{1,0:T(8,128)(2,1)S(1)}, u32[]{:S(2)}, u32[]{:S(2)}) collective-permute-start(f16[136,512]{1,0:T(8,128)(2,1)S(1)} %get-tuple-element.59), channel_id=1, source_target_pairs={{0,8},{8,0},{16,24},{24,16},{1,9},{9,1},{17,25},{25,17},{2,10},{10... | collective-permute-start | bytes 417800 | tf_op jit(solution)/shard_map/ppermute | solution.py:22
  41.2 2.4 %weighted_sums.2 = (f32[136,1024]{1,0:T(8,128)S(1)}, f32[136,1024]{1,0:T(8,128)S(1)}, f32[136,1024]{1,0:T(8,128)S(1)}) custom-call(f32[8,256]{1,0:T(8,128)S(1)} %join_rows.3.lognorm_ref.refs_4_, f32[3,384,256]{2,1,0:T(8,128)S(1)} %get-tuple-element.44.refs_0_, f32[1,384,256]{2,1,0:T(8,128)S(1)} %get-tuple-element.45.refs_1_, ...), custom_call_target="tpu_custom_call" | custom-call | flops 1610612736 | bytes 4194304 | tf_op jit(solution)/shard_map/weighted_sums/pallas_call | solution.py:243
  43.6 1.0 %collective-permute-done.15 = f16[136,512]{1,0:T(8,128)(2,1)S(1)} collective-permute-done((f16[136,512]{1,0:T(8,128)(2,1)S(1)}, f16[136,512]{1,0:T(8,128)(2,1)S(1)}, u32[]{:S(2)}, u32[]{:S(2)}) %collective-permute-start.15) | collective-permute-done | bytes 139296 | tf_op jit(solution)/shard_map/ppermute | solution.py:22
  44.8 3.3 %collective-permute-start.16 = (f16[136,512]{1,0:T(8,128)(2,1)S(1)}, f16[136,512]{1,0:T(8,128)(2,1)S(1)}, u32[]{:S(2)}, u32[]{:S(2)}) collective-permute-start(f16[136,512]{1,0:T(8,128)(2,1)S(1)} %convert_element_type.34), channel_id=1, source_target_pairs={{0,16},{8,24},{16,0},{24,8},{1,17},{9,25},{17,1},{25,9},{2,18},{10... | collective-permute-start | bytes 417800 | tf_op jit(solution)/shard_map/ppermute | solution.py:22
  48.2 1.7 %collective-permute-start.14 = (f16[136,1024]{1,0:T(8,128)(2,1)S(1)}, f16[136,1024]{1,0:T(8,128)(2,1)S(1)}, u32[]{:S(2)}, u32[]{:S(2)}) collective-permute-start(f16[136,1024]{1,0:T(8,128)(2,1)S(1)} %convert_element_type.32), channel_id=1, source_target_pairs={{0,8},{8,0},{16,24},{24,16},{1,9},{9,1},{17,25},{25,17},{2,10},{10... | collective-permute-start | bytes 835592 | tf_op jit(solution)/shard_map/ppermute | solution.py:22
  50.0 3.4 %collective-permute-start.13 = (f16[136,512]{1,0:T(8,128)(2,1)S(1)}, f16[136,512]{1,0:T(8,128)(2,1)S(1)}, u32[]{:S(2)}, u32[]{:S(2)}) collective-permute-start(f16[136,512]{1,0:T(8,128)(2,1)S(1)} %convert_element_type.31), channel_id=1, source_target_pairs={{0,16},{8,24},{16,0},{24,8},{1,17},{9,25},{17,1},{25,9},{2,18},{10... | collective-permute-start | bytes 417800 | tf_op jit(solution)/shard_map/ppermute | solution.py:22
  54.3 3.7 %collective-permute-done.14 = f16[136,1024]{1,0:T(8,128)(2,1)S(1)} collective-permute-done((f16[136,1024]{1,0:T(8,128)(2,1)S(1)}, f16[136,1024]{1,0:T(8,128)(2,1)S(1)}, u32[]{:S(2)}, u32[]{:S(2)}) %collective-permute-start.14) | collective-permute-done | bytes 278560 | tf_op jit(solution)/shard_map/ppermute | solution.py:22
  (42 shorter events, 9.7 us)
Async XLA Ops:
  0.6 15.5 %collective-permute-start.3 = (bf16[256,1024]{1,0:T(8,128)(2,1)}, bf16[256,1024]{1,0:T(8,128)(2,1)S(1)}, u32[]{:S(2)}, u32[]{:S(2)}) collective-permute-start(bf16[256,1024]{1,0:T(8,128)(2,1)} %param.2), channel_id=1, source_target_pairs={{0,2},{1,5},{2,0},{3,7},{4,6},{5,1},{6,4},{7,3},{8,10},{9,13},{10,... | collective-permute-start | bytes 1572872 | tf_op jit(solution)/shard_map/ppermute | solution.py:266
  3.6 17.4 %collective-permute-start.4 = (bf16[256,1024]{1,0:T(8,128)(2,1)}, bf16[256,1024]{1,0:T(8,128)(2,1)S(1)}, u32[]{:S(2)}, u32[]{:S(2)}) collective-permute-start(bf16[256,1024]{1,0:T(8,128)(2,1)} %param.2), channel_id=1, source_target_pairs={{0,4},{1,3},{2,6},{3,1},{4,0},{5,7},{6,2},{7,5},{8,12},{9,11},{10,... | collective-permute-start | bytes 1572872 | tf_op jit(solution)/shard_map/ppermute | solution.py:267
  6.2 14.2 %collective-permute-start.1 = (bf16[128,1024]{1,0:T(8,128)(2,1)S(1)}, bf16[128,1024]{1,0:T(8,128)(2,1)S(1)}, u32[]{:S(2)}, u32[]{:S(2)}) collective-permute-start(bf16[128,1024]{1,0:T(8,128)(2,1)S(1)} %convert_element_type.29), channel_id=1, source_target_pairs={{0,16},{8,24},{16,0},{24,8},{1,17},{9,25},{17,1},{25,9},{2,18},{10... | collective-permute-start | bytes 786440 | tf_op jit(solution)/shard_map/ppermute | solution.py:22
  8.9 12.3 %collective-permute-start = (bf16[128,1024]{1,0:T(8,128)(2,1)S(1)}, bf16[128,1024]{1,0:T(8,128)(2,1)S(1)}, u32[]{:S(2)}, u32[]{:S(2)}) collective-permute-start(bf16[128,1024]{1,0:T(8,128)(2,1)S(1)} %convert_element_type.29), channel_id=1, source_target_pairs={{0,8},{8,0},{16,24},{24,16},{1,9},{9,1},{17,25},{25,17},{2,10},{10... | collective-permute-start | bytes 786440 | tf_op jit(solution)/shard_map/ppermute | solution.py:22
  16.2 9.2 %collective-permute-start.6 = (bf16[256,1024]{1,0:T(8,128)(2,1)S(1)}, bf16[256,1024]{1,0:T(8,128)(2,1)S(1)}, u32[]{:S(2)}, u32[]{:S(2)}) collective-permute-start(bf16[256,1024]{1,0:T(8,128)(2,1)S(1)} %collective-permute-done.3), channel_id=1, source_target_pairs={{0,4},{1,3},{2,6},{3,1},{4,0},{5,7},{6,2},{7,5},{8,12},{9,11},{10,... | collective-permute-start | bytes 1572872 | tf_op jit(solution)/shard_map/ppermute | solution.py:277
  20.4 7.1 %collective-permute-start.2 = (bf16[128,1024]{1,0:T(8,128)(2,1)S(1)}, bf16[128,1024]{1,0:T(8,128)(2,1)S(1)}, u32[]{:S(2)}, u32[]{:S(2)}) collective-permute-start(bf16[128,1024]{1,0:T(8,128)(2,1)S(1)} %collective-permute-done.1), channel_id=1, source_target_pairs={{0,8},{8,0},{16,24},{24,16},{1,9},{9,1},{17,25},{25,17},{2,10},{10... | collective-permute-start | bytes 786440 | tf_op jit(solution)/shard_map/ppermute | solution.py:22
  21.1 7.3 %collective-permute-start.5 = (bf16[768,1024]{1,0:T(8,128)(2,1)S(1)}, bf16[768,1024]{1,0:T(8,128)(2,1)S(1)}, u32[]{:S(2)}, u32[]{:S(2)}) collective-permute-start(bf16[768,1024]{1,0:T(8,128)(2,1)S(1)} %constant_dynamic-update-slice_fusion.refs_1_.refs_4_.refs_3_), channel_id=1, source_target_pairs={{0,1},{1,0},{2,3},{3,2},{4,5},{5,4},{6,7},{7,6},{8,9},{9,8},{10,11... | collective-permute-start | bytes 4718600 | tf_op jit(solution)/shard_map/ppermute | solution.py:22
  25.8 4.0 %collective-permute-start.7 = (bf16[256,1024]{1,0:T(8,128)(2,1)S(1)}, bf16[256,1024]{1,0:T(8,128)(2,1)S(1)}, u32[]{:S(2)}, u32[]{:S(2)}) collective-permute-start(bf16[256,1024]{1,0:T(8,128)(2,1)S(1)} %collective-permute-done.6.refs_2_.refs_5_.refs_4_), channel_id=1, source_target_pairs={{0,1},{1,0},{2,3},{3,2},{4,5},{5,4},{6,7},{7,6},{8,9},{9,8},{10,11... | collective-permute-start | bytes 1572872 | tf_op jit(solution)/shard_map/ppermute | solution.py:22
  30.5 1.2 %collective-permute-start.8 = (f32[2,8,256]{2,1,0:T(8,128)S(1)}, f32[2,8,256]{2,1,0:T(8,128)S(1)}, u32[]{:S(2)}, u32[]{:S(2)}) collective-permute-start(f32[2,8,256]{2,1,0:T(8,128)S(1)} %get-tuple-element.43.pair_ref), channel_id=1, source_target_pairs={{0,1},{1,0},{2,3},{3,2},{4,5},{5,4},{6,7},{7,6},{8,9},{9,8},{10,11... | collective-permute-start | bytes 49160 | tf_op jit(solution)/shard_map/ppermute | solution.py:113
  31.8 3.8 %collective-permute-start.10 = (f32[2,8,256]{2,1,0:T(8,128)S(1)}, f32[2,8,256]{2,1,0:T(8,128)S(1)}, u32[]{:S(2)}, u32[]{:S(2)}) collective-permute-start(f32[2,8,256]{2,1,0:T(8,128)S(1)} %join_rows.2.pair_ref), channel_id=1, source_target_pairs={{0,4},{1,3},{2,6},{3,1},{4,0},{5,7},{6,2},{7,5},{8,12},{9,11},{10,... | collective-permute-start | bytes 49160 | tf_op jit(solution)/shard_map/ppermute | solution.py:113
  32.4 4.6 %collective-permute-start.11 = (f32[2,8,256]{2,1,0:T(8,128)S(1)}, f32[2,8,256]{2,1,0:T(8,128)S(1)}, u32[]{:S(2)}, u32[]{:S(2)}) collective-permute-start(f32[2,8,256]{2,1,0:T(8,128)S(1)} %join_rows.2.pair_ref), channel_id=1, source_target_pairs={{0,6},{1,7},{2,4},{3,5},{4,2},{5,3},{6,0},{7,1},{8,14},{9,15},{10,... | collective-permute-start | bytes 49160 | tf_op jit(solution)/shard_map/ppermute | solution.py:113
  34.3 3.7 %collective-permute-start.9 = (f32[2,8,256]{2,1,0:T(8,128)S(1)}, f32[2,8,256]{2,1,0:T(8,128)S(1)}, u32[]{:S(2)}, u32[]{:S(2)}) collective-permute-start(f32[2,8,256]{2,1,0:T(8,128)S(1)} %join_rows.2.pair_ref), channel_id=1, source_target_pairs={{0,2},{1,5},{2,0},{3,7},{4,6},{5,1},{6,4},{7,3},{8,10},{9,13},{10,... | collective-permute-start | bytes 49160 | tf_op jit(solution)/shard_map/ppermute | solution.py:113
  39.1 5.5 %collective-permute-start.15 = (f16[136,512]{1,0:T(8,128)(2,1)S(1)}, f16[136,512]{1,0:T(8,128)(2,1)S(1)}, u32[]{:S(2)}, u32[]{:S(2)}) collective-permute-start(f16[136,512]{1,0:T(8,128)(2,1)S(1)} %get-tuple-element.59), channel_id=1, source_target_pairs={{0,8},{8,0},{16,24},{24,16},{1,9},{9,1},{17,25},{25,17},{2,10},{10... | collective-permute-start | bytes 417800 | tf_op jit(solution)/shard_map/ppermute | solution.py:22
  40.8 9.1 %collective-permute-start.12 = (f16[136,512]{1,0:T(8,128)(2,1)S(1)}, f16[136,512]{1,0:T(8,128)(2,1)S(1)}, u32[]{:S(2)}, u32[]{:S(2)}) collective-permute-start(f16[136,512]{1,0:T(8,128)(2,1)S(1)} %get-tuple-element.60), channel_id=1, source_target_pairs={{0,8},{8,0},{16,24},{24,16},{1,9},{9,1},{17,25},{25,17},{2,10},{10... | collective-permute-start | bytes 417800 | tf_op jit(solution)/shard_map/ppermute | solution.py:22
  44.8 9.5 %collective-permute-start.16 = (f16[136,512]{1,0:T(8,128)(2,1)S(1)}, f16[136,512]{1,0:T(8,128)(2,1)S(1)}, u32[]{:S(2)}, u32[]{:S(2)}) collective-permute-start(f16[136,512]{1,0:T(8,128)(2,1)S(1)} %convert_element_type.34), channel_id=1, source_target_pairs={{0,16},{8,24},{16,0},{24,8},{1,17},{9,25},{17,1},{25,9},{2,18},{10... | collective-permute-start | bytes 417800 | tf_op jit(solution)/shard_map/ppermute | solution.py:22
  48.2 9.9 %collective-permute-start.14 = (f16[136,1024]{1,0:T(8,128)(2,1)S(1)}, f16[136,1024]{1,0:T(8,128)(2,1)S(1)}, u32[]{:S(2)}, u32[]{:S(2)}) collective-permute-start(f16[136,1024]{1,0:T(8,128)(2,1)S(1)} %convert_element_type.32), channel_id=1, source_target_pairs={{0,8},{8,0},{16,24},{24,16},{1,9},{9,1},{17,25},{25,17},{2,10},{10... | collective-permute-start | bytes 835592 | tf_op jit(solution)/shard_map/ppermute | solution.py:22
  50.0 8.2 %collective-permute-start.13 = (f16[136,512]{1,0:T(8,128)(2,1)S(1)}, f16[136,512]{1,0:T(8,128)(2,1)S(1)}, u32[]{:S(2)}, u32[]{:S(2)}) collective-permute-start(f16[136,512]{1,0:T(8,128)(2,1)S(1)} %convert_element_type.31), channel_id=1, source_target_pairs={{0,16},{8,24},{16,0},{24,8},{1,17},{9,25},{17,1},{25,9},{2,18},{10... | collective-permute-start | bytes 417800 | tf_op jit(solution)/shard_map/ppermute | solution.py:22
  58.2 1.0 %copy-start = (f32[128,1024]{1,0:T(8,128)S(1)}, f32[128,1024]{1,0:T(8,128)}, u32[]{:S(2)}) copy-start(f32[128,1024]{1,0:T(8,128)} %refs_3_.1) | copy-start | bytes 1572868

commit v19 on v17

--- a/solution.py
+++ b/solution.py
@@ -332,7 +332,7 @@
             far.append(swap(message.astype(jnp.float16), "dp", n_dp, 2))
         near = swap(near.astype(jnp.float16), "dp", n_dp, 1)
         half_sum = add_part(own, far[0], -1, unit * 0.5, 0, 32000)
-        near, half_sum = lax.optimization_barrier((near, half_sum))
+        near, half_sum, lognorm = lax.optimization_barrier((near, half_sum, lognorm))
         own = add_part(own, near, 0, unit, 0, 100000)
         far[1], own = lax.optimization_barrier((far[1], own))
         half_sums = [half_sum, add_part(own, far[1], -1, unit * 0.5, 0)]

time: 60 us -> 60.5 us (level)
  transfers between devices with their start and end apart: 17 -> 17, of which waited for: 11 -> 11; matrix products, arithmetic and copies ran while one was open for 5% -> 4% of each run, Pallas kernels for 11% -> 11%
where the time goes in v19:
time: 60.5 us; the launch traced here: 60.2 us
  starting transfers between devices  25.1 us (41%)
  waiting for transfers between devices  21.5 us (36%)
  Pallas kernels  9.24 us (15%)
  local copies, waits for them, and re-layouts  2.16 us (4%)
  other arithmetic  1.36 us (2%)
  between operations  0.87 us (1%)
    ppermute x10, starting transfers between devices, swap(): return lax.ppermute(x, axis, partner(size, mask))  15.5 us
    ppermute x10, waiting for transfers between devices, swap(): return lax.ppermute(x, axis, partner(size, mask))  8.88 us
    ppermute x1, waiting for transfers between devices, local(): from_p = lax.ppermute(embeddings, 'cent', by_p)  5.69 us
    pallas_call x5, Pallas kernels, score(): pl.pallas_call(functools.partial(score_kernel, len(centers), len(halves),...  4.58 us
    ppermute x4, waiting for transfers between devices, join(): others = [lax.ppermute(pairs, 'cent', route) for route in routes]  3.84 us
    ppermute x4, starting transfers between devices, join(): others = [lax.ppermute(pairs, 'cent', route) for route in routes]  3.62 us
    pallas_call x2, Pallas kernels, weighted(): pl.pallas_call(functools.partial(sums_kernel, len(scores), picks, parts),...  3.3 us
    ppermute x1, waiting for transfers between devices, local(): diag = lax.ppermute(from_p, 'cent', by_q)  3.09 us
  transfers between devices with their start and end apart: 17, of which 11 were waited for; matrix products, arithmetic and copies ran while one was open for 4% of the time, Pallas kernels for 11%

profile of v19, /device:TPU:0, one launch (start us, length us, event | category | flops | bytes accessed | tf_op | source)
XLA Modules:
  0.0 60.2 jit_solution(11086363128419444005)
XLA Ops:
  0.6 3.0 %collective-permute-start.3 = (bf16[256,1024]{1,0:T(8,128)(2,1)}, bf16[256,1024]{1,0:T(8,128)(2,1)S(1)}, u32[]{:S(2)}, u32[]{:S(2)}) collective-permute-start(bf16[256,1024]{1,0:T(8,128)(2,1)} %param.2), channel_id=1, source_target_pairs={{0,2},{1,5},{2,0},{3,7},{4,6},{5,1},{6,4},{7,3},{8,10},{9,13},{10,... | collective-permute-start | bytes 1572872 | tf_op jit(solution)/shard_map/ppermute | solution.py:263
  3.6 1.5 %collective-permute-start.4 = (bf16[256,1024]{1,0:T(8,128)(2,1)}, bf16[256,1024]{1,0:T(8,128)(2,1)S(1)}, u32[]{:S(2)}, u32[]{:S(2)}) collective-permute-start(bf16[256,1024]{1,0:T(8,128)(2,1)} %param.2), channel_id=1, source_target_pairs={{0,4},{1,3},{2,6},{3,1},{4,0},{5,7},{6,2},{7,5},{8,12},{9,11},{10,... | collective-permute-start | bytes 1572872 | tf_op jit(solution)/shard_map/ppermute | solution.py:264
  5.2 1.1 %convert_element_type.29 = bf16[128,1024]{1,0:T(8,128)(2,1)S(1)} convert(f32[128,1024]{1,0:T(8,128)} %refs_3_.1) | non-fusion elementwise | flops 131072 | bytes 786432 | tf_op jit(solution)/shard_map/convert_element_type | solution.py:259
  6.2 2.7 %collective-permute-start.1 = (bf16[128,1024]{1,0:T(8,128)(2,1)S(1)}, bf16[128,1024]{1,0:T(8,128)(2,1)S(1)}, u32[]{:S(2)}, u32[]{:S(2)}) collective-permute-start(bf16[128,1024]{1,0:T(8,128)(2,1)S(1)} %convert_element_type.29), channel_id=1, source_target_pairs={{0,16},{8,24},{16,0},{24,8},{1,17},{9,25},{17,1},{25,9},{2,18},{10... | collective-permute-start | bytes 786440 | tf_op jit(solution)/shard_map/ppermute | solution.py:22
  8.9 1.6 %collective-permute-start = (bf16[128,1024]{1,0:T(8,128)(2,1)S(1)}, bf16[128,1024]{1,0:T(8,128)(2,1)S(1)}, u32[]{:S(2)}, u32[]{:S(2)}) collective-permute-start(bf16[128,1024]{1,0:T(8,128)(2,1)S(1)} %convert_element_type.29), channel_id=1, source_target_pairs={{0,8},{8,0},{16,24},{24,16},{1,9},{9,1},{17,25},{25,17},{2,10},{10... | collective-permute-start | bytes 786440 | tf_op jit(solution)/shard_map/ppermute | solution.py:22
  10.5 5.7 %collective-permute-done.3 = bf16[256,1024]{1,0:T(8,128)(2,1)S(1)} collective-permute-done((bf16[256,1024]{1,0:T(8,128)(2,1)}, bf16[256,1024]{1,0:T(8,128)(2,1)S(1)}, u32[]{:S(2)}, u32[]{:S(2)}) %collective-permute-start.3) | collective-permute-done | bytes 524320 | tf_op jit(solution)/shard_map/ppermute | solution.py:263
  16.2 1.5 %collective-permute-start.6 = (bf16[256,1024]{1,0:T(8,128)(2,1)S(1)}, bf16[256,1024]{1,0:T(8,128)(2,1)S(1)}, u32[]{:S(2)}, u32[]{:S(2)}) collective-permute-start(bf16[256,1024]{1,0:T(8,128)(2,1)S(1)} %collective-permute-done.3), channel_id=1, source_target_pairs={{0,4},{1,3},{2,6},{3,1},{4,0},{5,7},{6,2},{7,5},{8,12},{9,11},{10,... | collective-permute-start | bytes 1572872 | tf_op jit(solution)/shard_map/ppermute | solution.py:274
  17.6 1.1 %constant_dynamic-update-slice_fusion.2 = bf16[768,1024]{1,0:T(8,128)(2,1)S(1)} fusion(bf16[256,1024]{1,0:T(8,128)(2,1)} %param.2), kind=kLoop, calls=%fused_computation.3 | loop fusion | bytes 1048576
  18.7 1.7 %collective-permute-done.1 = bf16[128,1024]{1,0:T(8,128)(2,1)S(1)} collective-permute-done((bf16[128,1024]{1,0:T(8,128)(2,1)S(1)}, bf16[128,1024]{1,0:T(8,128)(2,1)S(1)}, u32[]{:S(2)}, u32[]{:S(2)}) %collective-permute-start.1) | collective-permute-done | bytes 262176 | tf_op jit(solution)/shard_map/ppermute | solution.py:22
  21.2 1.0 %score_rows.5 = (f32[3,384,256]{2,1,0:T(8,128)S(1)}, f32[2,3,256]{2,1,0:T(4,128)S(1)}, f32[384,128]{1,0:T(8,128)S(1)}) custom-call(bf16[384,1024]{1,0:T(8,128)(2,1)S(1)} %pad_maximum_fusion.refs_0_, bf16[768,1024]{1,0:T(8,128)(2,1)S(1)} %constant_dynamic-update-slice_fusion.refs_1_.refs_4_.refs_3_), custom_call_target="tpu_custom_call" | custom-call | flops 603979776 | bytes 2359296 | tf_op jit(solution)/shard_map/score_rows/pallas_call | solution.py:82
  22.3 3.1 %collective-permute-done.6.refs_2_.refs_5_.refs_4_ = bf16[256,1024]{1,0:T(8,128)(2,1)S(1)} collective-permute-done((bf16[256,1024]{1,0:T(8,128)(2,1)S(1)}, bf16[256,1024]{1,0:T(8,128)(2,1)S(1)}, u32[]{:S(2)}, u32[]{:S(2)}) %collective-permute-start.6) | collective-permute-done | bytes 524320 | tf_op jit(solution)/shard_map/ppermute | solution.py:274
  25.9 1.6 %collective-permute-done.2.refs_0_.refs_1_ = bf16[128,1024]{1,0:T(8,128)(2,1)S(1)} collective-permute-done((bf16[128,1024]{1,0:T(8,128)(2,1)S(1)}, bf16[128,1024]{1,0:T(8,128)(2,1)S(1)}, u32[]{:S(2)}, u32[]{:S(2)}) %collective-permute-start.2) | collective-permute-done | bytes 262176 | tf_op jit(solution)/shard_map/ppermute | solution.py:22
  28.4 1.5 %score_rows.8 = (f32[3,512,256]{2,1,0:T(8,128)S(1)}, f32[2,3,256]{2,1,0:T(4,128)S(1)}) custom-call(bf16[384,1024]{1,0:T(8,128)(2,1)S(1)} %pad_maximum_fusion.refs_0_, bf16[128,1024]{1,0:T(8,128)(2,1)S(1)} %collective-permute-done.2.refs_0_.refs_1_, f32[384,128]{1,0:T(8,128)S(1)} %get-tuple-element.31.refs_1_.refs_2_, ...), custom_call_target="tpu_custom_call" | custom-call | flops 80530640 | bytes 262144 | tf_op jit(solution)/shard_map/score_rows/pallas_call | solution.py:82
  30.6 1.2 %collective-permute-done.8.refs_0_ = f32[2,8,256]{2,1,0:T(8,128)S(1)} collective-permute-done((f32[2,8,256]{2,1,0:T(8,128)S(1)}, f32[2,8,256]{2,1,0:T(8,128)S(1)}, u32[]{:S(2)}, u32[]{:S(2)}) %collective-permute-start.8) | collective-permute-done | bytes 16416 | tf_op jit(solution)/shard_map/ppermute | solution.py:113
  32.4 1.9 %collective-permute-start.11 = (f32[2,8,256]{2,1,0:T(8,128)S(1)}, f32[2,8,256]{2,1,0:T(8,128)S(1)}, u32[]{:S(2)}, u32[]{:S(2)}) collective-permute-start(f32[2,8,256]{2,1,0:T(8,128)S(1)} %join_rows.2.pair_ref), channel_id=1, source_target_pairs={{0,6},{1,7},{2,4},{3,5},{4,2},{5,3},{6,0},{7,1},{8,14},{9,15},{10,... | collective-permute-start | bytes 49160 | tf_op jit(solution)/shard_map/ppermute | solution.py:113
  34.3 1.1 %collective-permute-start.9 = (f32[2,8,256]{2,1,0:T(8,128)S(1)}, f32[2,8,256]{2,1,0:T(8,128)S(1)}, u32[]{:S(2)}, u32[]{:S(2)}) collective-permute-start(f32[2,8,256]{2,1,0:T(8,128)S(1)} %join_rows.2.pair_ref), channel_id=1, source_target_pairs={{0,2},{1,5},{2,0},{3,7},{4,6},{5,1},{6,4},{7,3},{8,10},{9,13},{10,... | collective-permute-start | bytes 49160 | tf_op jit(solution)/shard_map/ppermute | solution.py:113
  35.6 1.4 %collective-permute-done.11.refs_2_ = f32[2,8,256]{2,1,0:T(8,128)S(1)} collective-permute-done((f32[2,8,256]{2,1,0:T(8,128)S(1)}, f32[2,8,256]{2,1,0:T(8,128)S(1)}, u32[]{:S(2)}, u32[]{:S(2)}) %collective-permute-start.11) | collective-permute-done | bytes 16416 | tf_op jit(solution)/shard_map/ppermute | solution.py:113
  39.1 1.6 %collective-permute-start.15 = (f16[136,512]{1,0:T(8,128)(2,1)S(1)}, f16[136,512]{1,0:T(8,128)(2,1)S(1)}, u32[]{:S(2)}, u32[]{:S(2)}) collective-permute-start(f16[136,512]{1,0:T(8,128)(2,1)S(1)} %get-tuple-element.59), channel_id=1, source_target_pairs={{0,8},{8,0},{16,24},{24,16},{1,9},{9,1},{17,25},{25,17},{2,10},{10... | collective-permute-start | bytes 417800 | tf_op jit(solution)/shard_map/ppermute | solution.py:22
  41.2 2.4 %weighted_sums.2 = (f32[136,1024]{1,0:T(8,128)S(1)}, f32[136,1024]{1,0:T(8,128)S(1)}, f32[136,1024]{1,0:T(8,128)S(1)}) custom-call(f32[8,256]{1,0:T(8,128)S(1)} %join_rows.3.lognorm_ref, f32[3,384,256]{2,1,0:T(8,128)S(1)} %get-tuple-element.44.refs_0_, f32[1,384,256]{2,1,0:T(8,128)S(1)} %get-tuple-element.45.refs_1_, ...), custom_call_target="tpu_custom_call" | custom-call | flops 1610612736 | bytes 4194304 | tf_op jit(solution)/shard_map/weighted_sums/pallas_call | solution.py:240
  43.6 1.0 %collective-permute-done.15 = f16[136,512]{1,0:T(8,128)(2,1)S(1)} collective-permute-done((f16[136,512]{1,0:T(8,128)(2,1)S(1)}, f16[136,512]{1,0:T(8,128)(2,1)S(1)}, u32[]{:S(2)}, u32[]{:S(2)}) %collective-permute-start.15) | collective-permute-done | bytes 139296 | tf_op jit(solution)/shard_map/ppermute | solution.py:22
  44.8 3.3 %collective-permute-start.16 = (f16[136,512]{1,0:T(8,128)(2,1)S(1)}, f16[136,512]{1,0:T(8,128)(2,1)S(1)}, u32[]{:S(2)}, u32[]{:S(2)}) collective-permute-start(f16[136,512]{1,0:T(8,128)(2,1)S(1)} %convert_element_type.34), channel_id=1, source_target_pairs={{0,16},{8,24},{16,0},{24,8},{1,17},{9,25},{17,1},{25,9},{2,18},{10... | collective-permute-start | bytes 417800 | tf_op jit(solution)/shard_map/ppermute | solution.py:22
  48.2 1.7 %collective-permute-start.14 = (f16[136,1024]{1,0:T(8,128)(2,1)S(1)}, f16[136,1024]{1,0:T(8,128)(2,1)S(1)}, u32[]{:S(2)}, u32[]{:S(2)}) collective-permute-start(f16[136,1024]{1,0:T(8,128)(2,1)S(1)} %convert_element_type.32), channel_id=1, source_target_pairs={{0,8},{8,0},{16,24},{24,16},{1,9},{9,1},{17,25},{25,17},{2,10},{10... | collective-permute-start | bytes 835592 | tf_op jit(solution)/shard_map/ppermute | solution.py:22
  50.0 3.4 %collective-permute-start.13 = (f16[136,512]{1,0:T(8,128)(2,1)S(1)}, f16[136,512]{1,0:T(8,128)(2,1)S(1)}, u32[]{:S(2)}, u32[]{:S(2)}) collective-permute-start(f16[136,512]{1,0:T(8,128)(2,1)S(1)} %convert_element_type.31), channel_id=1, source_target_pairs={{0,16},{8,24},{16,0},{24,8},{1,17},{9,25},{17,1},{25,9},{2,18},{10... | collective-permute-start | bytes 417800 | tf_op jit(solution)/shard_map/ppermute | solution.py:22
  54.3 3.7 %collective-permute-done.14 = f16[136,1024]{1,0:T(8,128)(2,1)S(1)} collective-permute-done((f16[136,1024]{1,0:T(8,128)(2,1)S(1)}, f16[136,1024]{1,0:T(8,128)(2,1)S(1)}, u32[]{:S(2)}, u32[]{:S(2)}) %collective-permute-start.14) | collective-permute-done | bytes 278560 | tf_op jit(solution)/shard_map/ppermute | solution.py:22
  (43 shorter events, 9.7 us)
Async XLA Ops:
  0.6 15.5 %collective-permute-start.3 = (bf16[256,1024]{1,0:T(8,128)(2,1)}, bf16[256,1024]{1,0:T(8,128)(2,1)S(1)}, u32[]{:S(2)}, u32[]{:S(2)}) collective-permute-start(bf16[256,1024]{1,0:T(8,128)(2,1)} %param.2), channel_id=1, source_target_pairs={{0,2},{1,5},{2,0},{3,7},{4,6},{5,1},{6,4},{7,3},{8,10},{9,13},{10,... | collective-permute-start | bytes 1572872 | tf_op jit(solution)/shard_map/ppermute | solution.py:263
  3.6 17.4 %collective-permute-start.4 = (bf16[256,1024]{1,0:T(8,128)(2,1)}, bf16[256,1024]{1,0:T(8,128)(2,1)S(1)}, u32[]{:S(2)}, u32[]{:S(2)}) collective-permute-start(bf16[256,1024]{1,0:T(8,128)(2,1)} %param.2), channel_id=1, source_target_pairs={{0,4},{1,3},{2,6},{3,1},{4,0},{5,7},{6,2},{7,5},{8,12},{9,11},{10,... | collective-permute-start | bytes 1572872 | tf_op jit(solution)/shard_map/ppermute | solution.py:264
  6.2 14.2 %collective-permute-start.1 = (bf16[128,1024]{1,0:T(8,128)(2,1)S(1)}, bf16[128,1024]{1,0:T(8,128)(2,1)S(1)}, u32[]{:S(2)}, u32[]{:S(2)}) collective-permute-start(bf16[128,1024]{1,0:T(8,128)(2,1)S(1)} %convert_element_type.29), channel_id=1, source_target_pairs={{0,16},{8,24},{16,0},{24,8},{1,17},{9,25},{17,1},{25,9},{2,18},{10... | collective-permute-start | bytes 786440 | tf_op jit(solution)/shard_map/ppermute | solution.py:22
  8.9 12.3 %collective-permute-start = (bf16[128,1024]{1,0:T(8,128)(2,1)S(1)}, bf16[128,1024]{1,0:T(8,128)(2,1)S(1)}, u32[]{:S(2)}, u32[]{:S(2)}) collective-permute-start(bf16[128,1024]{1,0:T(8,128)(2,1)S(1)} %convert_element_type.29), channel_id=1, source_target_pairs={{0,8},{8,0},{16,24},{24,16},{1,9},{9,1},{17,25},{25,17},{2,10},{10... | collective-permute-start | bytes 786440 | tf_op jit(solution)/shard_map/ppermute | solution.py:22
  16.2 9.2 %collective-permute-start.6 = (bf16[256,1024]{1,0:T(8,128)(2,1)S(1)}, bf16[256,1024]{1,0:T(8,128)(2,1)S(1)}, u32[]{:S(2)}, u32[]{:S(2)}) collective-permute-start(bf16[256,1024]{1,0:T(8,128)(2,1)S(1)} %collective-permute-done.3), channel_id=1, source_target_pairs={{0,4},{1,3},{2,6},{3,1},{4,0},{5,7},{6,2},{7,5},{8,12},{9,11},{10,... | collective-permute-start | bytes 1572872 | tf_op jit(solution)/shard_map/ppermute | solution.py:274
  20.4 7.1 %collective-permute-start.2 = (bf16[128,1024]{1,0:T(8,128)(2,1)S(1)}, bf16[128,1024]{1,0:T(8,128)(2,1)S(1)}, u32[]{:S(2)}, u32[]{:S(2)}) collective-permute-start(bf16[128,1024]{1,0:T(8,128)(2,1)S(1)} %collective-permute-done.1), channel_id=1, source_target_pairs={{0,8},{8,0},{16,24},{24,16},{1,9},{9,1},{17,25},{25,17},{2,10},{10... | collective-permute-start | bytes 786440 | tf_op jit(solution)/shard_map/ppermute | solution.py:22
  21.1 7.3 %collective-permute-start.5 = (bf16[768,1024]{1,0:T(8,128)(2,1)S(1)}, bf16[768,1024]{1,0:T(8,128)(2,1)S(1)}, u32[]{:S(2)}, u32[]{:S(2)}) collective-permute-start(bf16[768,1024]{1,0:T(8,128)(2,1)S(1)} %constant_dynamic-update-slice_fusion.refs_1_.refs_4_.refs_3_), channel_id=1, source_target_pairs={{0,1},{1,0},{2,3},{3,2},{4,5},{5,4},{6,7},{7,6},{8,9},{9,8},{10,11... | collective-permute-start | bytes 4718600 | tf_op jit(solution)/shard_map/ppermute | solution.py:22
  25.8 4.0 %collective-permute-start.7 = (bf16[256,1024]{1,0:T(8,128)(2,1)S(1)}, bf16[256,1024]{1,0:T(8,128)(2,1)S(1)}, u32[]{:S(2)}, u32[]{:S(2)}) collective-permute-start(bf16[256,1024]{1,0:T(8,128)(2,1)S(1)} %collective-permute-done.6.refs_2_.refs_5_.refs_4_), channel_id=1, source_target_pairs={{0,1},{1,0},{2,3},{3,2},{4,5},{5,4},{6,7},{7,6},{8,9},{9,8},{10,11... | collective-permute-start | bytes 1572872 | tf_op jit(solution)/shard_map/ppermute | solution.py:22
  30.5 1.2 %collective-permute-start.8 = (f32[2,8,256]{2,1,0:T(8,128)S(1)}, f32[2,8,256]{2,1,0:T(8,128)S(1)}, u32[]{:S(2)}, u32[]{:S(2)}) collective-permute-start(f32[2,8,256]{2,1,0:T(8,128)S(1)} %get-tuple-element.43.pair_ref), channel_id=1, source_target_pairs={{0,1},{1,0},{2,3},{3,2},{4,5},{5,4},{6,7},{7,6},{8,9},{9,8},{10,11... | collective-permute-start | bytes 49160 | tf_op jit(solution)/shard_map/ppermute | solution.py:113
  31.8 3.8 %collective-permute-start.10 = (f32[2,8,256]{2,1,0:T(8,128)S(1)}, f32[2,8,256]{2,1,0:T(8,128)S(1)}, u32[]{:S(2)}, u32[]{:S(2)}) collective-permute-start(f32[2,8,256]{2,1,0:T(8,128)S(1)} %join_rows.2.pair_ref), channel_id=1, source_target_pairs={{0,4},{1,3},{2,6},{3,1},{4,0},{5,7},{6,2},{7,5},{8,12},{9,11},{10,... | collective-permute-start | bytes 49160 | tf_op jit(solution)/shard_map/ppermute | solution.py:113
  32.4 4.6 %collective-permute-start.11 = (f32[2,8,256]{2,1,0:T(8,128)S(1)}, f32[2,8,256]{2,1,0:T(8,128)S(1)}, u32[]{:S(2)}, u32[]{:S(2)}) collective-permute-start(f32[2,8,256]{2,1,0:T(8,128)S(1)} %join_rows.2.pair_ref), channel_id=1, source_target_pairs={{0,6},{1,7},{2,4},{3,5},{4,2},{5,3},{6,0},{7,1},{8,14},{9,15},{10,... | collective-permute-start | bytes 49160 | tf_op jit(solution)/shard_map/ppermute | solution.py:113
  34.3 3.7 %collective-permute-start.9 = (f32[2,8,256]{2,1,0:T(8,128)S(1)}, f32[2,8,256]{2,1,0:T(8,128)S(1)}, u32[]{:S(2)}, u32[]{:S(2)}) collective-permute-start(f32[2,8,256]{2,1,0:T(8,128)S(1)} %join_rows.2.pair_ref), channel_id=1, source_target_pairs={{0,2},{1,5},{2,0},{3,7},{4,6},{5,1},{6,4},{7,3},{8,10},{9,13},{10,... | collective-permute-start | bytes 49160 | tf_op jit(solution)/shard_map/ppermute | solution.py:113
  39.1 5.5 %collective-permute-start.15 = (f16[136,512]{1,0:T(8,128)(2,1)S(1)}, f16[136,512]{1,0:T(8,128)(2,1)S(1)}, u32[]{:S(2)}, u32[]{:S(2)}) collective-permute-start(f16[136,512]{1,0:T(8,128)(2,1)S(1)} %get-tuple-element.59), channel_id=1, source_target_pairs={{0,8},{8,0},{16,24},{24,16},{1,9},{9,1},{17,25},{25,17},{2,10},{10... | collective-permute-start | bytes 417800 | tf_op jit(solution)/shard_map/ppermute | solution.py:22
  40.8 9.1 %collective-permute-start.12 = (f16[136,512]{1,0:T(8,128)(2,1)S(1)}, f16[136,512]{1,0:T(8,128)(2,1)S(1)}, u32[]{:S(2)}, u32[]{:S(2)}) collective-permute-start(f16[136,512]{1,0:T(8,128)(2,1)S(1)} %get-tuple-element.60), channel_id=1, source_target_pairs={{0,8},{8,0},{16,24},{24,16},{1,9},{9,1},{17,25},{25,17},{2,10},{10... | collective-permute-start | bytes 417800 | tf_op jit(solution)/shard_map/ppermute | solution.py:22
  44.8 9.5 %collective-permute-start.16 = (f16[136,512]{1,0:T(8,128)(2,1)S(1)}, f16[136,512]{1,0:T(8,128)(2,1)S(1)}, u32[]{:S(2)}, u32[]{:S(2)}) collective-permute-start(f16[136,512]{1,0:T(8,128)(2,1)S(1)} %convert_element_type.34), channel_id=1, source_target_pairs={{0,16},{8,24},{16,0},{24,8},{1,17},{9,25},{17,1},{25,9},{2,18},{10... | collective-permute-start | bytes 417800 | tf_op jit(solution)/shard_map/ppermute | solution.py:22
  48.2 9.9 %collective-permute-start.14 = (f16[136,1024]{1,0:T(8,128)(2,1)S(1)}, f16[136,1024]{1,0:T(8,128)(2,1)S(1)}, u32[]{:S(2)}, u32[]{:S(2)}) collective-permute-start(f16[136,1024]{1,0:T(8,128)(2,1)S(1)} %convert_element_type.32), channel_id=1, source_target_pairs={{0,8},{8,0},{16,24},{24,16},{1,9},{9,1},{17,25},{25,17},{2,10},{10... | collective-permute-start | bytes 835592 | tf_op jit(solution)/shard_map/ppermute | solution.py:22
  50.0 8.2 %collective-permute-start.13 = (f16[136,512]{1,0:T(8,128)(2,1)S(1)}, f16[136,512]{1,0:T(8,128)(2,1)S(1)}, u32[]{:S(2)}, u32[]{:S(2)}) collective-permute-start(f16[136,512]{1,0:T(8,128)(2,1)S(1)} %convert_element_type.31), channel_id=1, source_target_pairs={{0,16},{8,24},{16,0},{24,8},{1,17},{9,25},{17,1},{25,9},{2,18},{10... | collective-permute-start | bytes 417800 | tf_op jit(solution)/shard_map/ppermute | solution.py:22
  58.2 1.0 %copy-start = (f32[128,1024]{1,0:T(8,128)S(1)}, f32[128,1024]{1,0:T(8,128)}, u32[]{:S(2)}) copy-start(f32[128,1024]{1,0:T(8,128)} %refs_3_.1) | copy-start | bytes 1572868
